TPU v7x, 32 devices: a whole 2x2x4 slice. The times are simulated.
32 devices in a mesh: grp: 2 (over core), row: 16 (over z, y, x), col: 1.
Axes of the slice: x: 2, y: 2, z: 4, core: 2. Of those that a mesh axis runs over, the one named last changes fastest.
Arguments:
- pair_rep: bfloat16 [256, 128, 128], P(('grp', 'row'), 'col'), parts along dimension 0, may hold values from -6 to 6
- w_left: bfloat16 [128, 128], replicated, may hold values from -0.5 to 0.5
- w_left_gate: bfloat16 [128, 128], replicated, may hold values from -0.5 to 0.5
- w_right: bfloat16 [128, 128], replicated, may hold values from -0.5 to 0.5
- w_right_gate: bfloat16 [128, 128], replicated, may hold values from -0.5 to 0.5
- w_tri_gate: bfloat16 [128, 128], replicated, may hold values from -0.5 to 0.5
- w_tri_out: bfloat16 [128, 128], replicated, may hold values from -0.5 to 0.5
- w_query: bfloat16 [128, 128], replicated, may hold values from -1 to 1
- w_key: bfloat16 [128, 128], replicated, may hold values from -1 to 1
- w_value: bfloat16 [128, 128], replicated, may hold values from -0.5 to 0.5
- w_bias: bfloat16 [128, 4], replicated, may hold values from -54 to 54
- w_att_gate: bfloat16 [128, 128], replicated, may hold values from -0.5 to 0.5
- w_att_out: bfloat16 [128, 128], replicated, may hold values from -0.5 to 0.5
Outputs:
- updated_pair: bfloat16 [256, 128, 128], P(('grp', 'row'), 'col'), parts along dimension 0
There are 2 independent parts, one for each index of `grp`. A program takes and returns all parts, laid end to end along the dimension named above; an argument that names none is the same for every part. Nothing has to cross between parts.
All inputs are finite; a program needn't handle non-finite values.
Results may differ from a plain program's by a relative error of at most 0.023.
The roundings to bfloat16 on the way count: a program that leaves them out, or rounds other values in their place, can miss the bound.
Values may be sent and summed in bfloat16 or wider, within the bound.
No kernel may reach another device: no remote copies, remote signals or barrier semaphores. Data moves between devices by JAX's collectives and lax.ppermute only.
A program may use at most 64 MiB of HBM per device.

v0:
```python
import jax
import jax.numpy as jnp
from jax import lax
from jax.sharding import PartitionSpec as P

HEADS = 4
HEAD_DIM = 32


def layer_norm(values, reduce_axes):
    average = jnp.mean(values, axis=reduce_axes, keepdims=True)
    centered = values - average
    variance = jnp.mean(centered * centered, axis=reduce_axes, keepdims=True)
    return centered * lax.rsqrt(variance + 1e-05)


def project(source, weight):
    return jnp.dot(source, weight, preferred_element_type=jnp.float32)


def channel_major(source, weight):
    return jnp.einsum("ijc,cm->mij", source, weight, preferred_element_type=jnp.float32)


def body(
    pair_rep,
    w_left,
    w_left_gate,
    w_right,
    w_right_gate,
    w_tri_gate,
    w_tri_out,
    w_query,
    w_key,
    w_value,
    w_bias,
    w_att_gate,
    w_att_out,
):
    col_count = pair_rep.shape[1]
    normed = layer_norm(pair_rep.astype(jnp.float32), -1).astype(jnp.bfloat16)
    left_act = (
        jax.nn.sigmoid(channel_major(normed, w_left_gate)) * channel_major(normed, w_left)
    ).astype(jnp.bfloat16)
    right_act = (
        jax.nn.sigmoid(channel_major(normed, w_right_gate)) * channel_major(normed, w_right)
    ).astype(jnp.bfloat16)
    stacked = jnp.stack((left_act, right_act))
    spread = lax.all_to_all(stacked, "row", split_axis=1, concat_axis=2, tiled=True)
    partial_sums = jnp.einsum(
        "cik,cjk->cij", spread[0], spread[1], preferred_element_type=jnp.float32
    )
    summed = lax.psum_scatter(partial_sums, "col", scatter_dimension=2, tiled=True).astype(
        jnp.bfloat16
    )
    returned = lax.all_to_all(summed, "row", split_axis=1, concat_axis=0, tiled=True)
    tri_norm = layer_norm(returned.astype(jnp.float32), 0).astype(jnp.bfloat16)
    update = jnp.einsum("cij,cd->ijd", tri_norm, w_tri_out, preferred_element_type=jnp.float32)
    first_pass = pair_rep.astype(jnp.float32) + jax.nn.sigmoid(project(normed, w_tri_gate)) * update
    att_norm = layer_norm(first_pass, -1).astype(jnp.bfloat16)
    queries = project(att_norm, w_query).astype(jnp.bfloat16)
    key_proj = project(att_norm, w_key).astype(jnp.bfloat16)
    value_proj = project(att_norm, w_value).astype(jnp.bfloat16)
    att_gate = jax.nn.sigmoid(project(att_norm, w_att_gate))
    bias_local = jnp.einsum(
        "ijc,ch->hij", att_norm, w_bias, preferred_element_type=jnp.float32
    ).astype(jnp.bfloat16)
    every_row = lax.all_gather(bias_local, "row", axis=1, tiled=True)
    bias_full = lax.all_to_all(every_row, "col", split_axis=1, concat_axis=2, tiled=True).astype(
        jnp.float32
    )
    key_value = lax.all_gather(jnp.stack((key_proj, value_proj)), "col", axis=2, tiled=True)
    total_keys = key_value.shape[2]
    score_scale = 1.0 / HEAD_DIM**0.5

    def attend_row(row_items):
        query_row = row_items[0].reshape(col_count, HEADS, HEAD_DIM)
        key_row = row_items[1].reshape(total_keys, HEADS, HEAD_DIM)
        value_row = row_items[2].reshape(total_keys, HEADS, HEAD_DIM)
        scores = (
            jnp.einsum("jhd,khd->hjk", query_row, key_row, preferred_element_type=jnp.float32)
            * score_scale
            + bias_full
        )
        row_peak = jnp.max(scores, axis=-1, keepdims=True)
        shifted = jnp.exp(scores - row_peak)
        row_total = jnp.sum(shifted, axis=-1, keepdims=True)
        weights = (shifted / row_total).astype(jnp.bfloat16)
        return jnp.einsum(
            "hjk,khd->jhd", weights, value_row, preferred_element_type=jnp.float32
        ).reshape(col_count, HEADS * HEAD_DIM)

    attended = lax.map(attend_row, (queries, key_value[0], key_value[1]))
    gated = (attended * att_gate).astype(jnp.bfloat16)
    return (first_pass + project(gated, w_att_out)).astype(jnp.bfloat16)


def solution(mesh):
    in_specs = (
        P(("grp", "row"), "col", None),
        P(),
        P(),
        P(),
        P(),
        P(),
        P(),
        P(),
        P(),
        P(),
        P(),
        P(),
        P(),
    )
    out_specs = P(("grp", "row"), "col", None)
    return jax.shard_map(body, mesh=mesh, in_specs=in_specs, out_specs=out_specs, check_vma=False)
```

profile of v0, /device:TPU:0, one launch (start us, length us, event | category | flops | bytes accessed | tf_op | source)
XLA Modules:
  0.0 90.9 jit_solution(12280398900959615245)
XLA Ops:
  0.0 1.1 %copy.34 = bf16[8,128,128]{1,2,0:T(8,128)(2,1)S(1)} copy(bf16[8,128,128]{2,1,0:T(8,128)(2,1)} %param.15) | data formatting | bytes 524288 | tf_op args[0]
  1.3 0.6 copy-done.7
  2.0 0.3 fusion.14
  2.3 0.4 copy-done.8
  2.7 0.3 fusion.11
  3.1 0.4 copy-done.1
  3.5 0.3 fusion.25
  3.8 0.5 copy-done.2
  4.2 0.3 fusion.24
  4.6 0.3 copy.45
  4.9 23.2 %all_to_all.24 = bf16[2,128,8,128]{3,2,0,1:T(8,128)(2,1)S(1)} all-to-all(bf16[2,128,8,128]{3,2,0,1:T(8,128)(2,1)S(1)} %copy.45), channel_id=1, replica_groups=mesh['grp'=2,'row'=16,'col'=1] {'row'}, dimensions={1} | all-to-all | bytes 1048576 | tf_op jit(solution)/shard_map/all_to_all | solution.py:49
  28.3 0.3 convolution_convert_fusion.3
  28.6 0.9 copy.47
  29.5 4.0 %all-to-all-start.1 = ((bf16[8,128,128]{2,0,1:T(8,128)(2,1)}), bf16[8,128,128]{2,0,1:T(8,128)(2,1)S(1)}, u32[]{:S(2)}, u32[]{:S(2)}) async-start(bf16[8,128,128]{2,0,1:T(8,128)(2,1)} %copy.47), calls=%async_computation.1 | async-start | bytes 524288 | tf_op jit(solution)/shard_map/all_to_all | solution.py:56
  33.5 0.3 fusion.17
  33.9 8.7 %all-to-all-done.1 = bf16[8,128,128]{2,0,1:T(8,128)(2,1)S(1)} async-done(((bf16[8,128,128]{2,0,1:T(8,128)(2,1)}), bf16[8,128,128]{2,0,1:T(8,128)(2,1)S(1)}, u32[]{:S(2)}, u32[]{:S(2)}) %all-to-all-start.1) | async-done | bytes 262176 | tf_op jit(solution)/shard_map/all_to_all | solution.py:56
  42.8 0.3 fusion.58
  43.3 0.6 copy-done.6
  44.0 38.3 %all_gather.4 = bf16[4,128,128]{2,0,1:T(4,128)(2,1)S(1)} all-gather(bf16[4,8,128]{2,0,1:T(4,128)(2,1)S(1)} %fusion.26), channel_id=1, replica_groups=mesh['grp'=2,'row'=16,'col'=1] {'row'}, dimensions={1}, use_global_device_ids=true | all-gather | bytes 139264 | tf_op jit(solution)/shard_map/all_gather | solution.py:68
  82.4 0.6 copy-done.3
  83.1 0.3 convolution_convert_fusion
  83.3 0.5 copy-done.4
  83.8 0.3 convolution_convert_fusion.1
  84.1 0.5 copy-done.5
  84.6 0.3 convolution_convert_fusion.2
  84.9 4.7 %while.10 = (s32[]{:T(128)}, f32[8,128,128]{1,2,0:T(8,128)S(1)}, bf16[8,128,128]{1,2,0:T(8,128)(2,1)S(1)}, bf16[8,128,128]{1,2,0:T(8,128)(2,1)S(1)}, bf16[8,128,...) while((s32[]{:T(128)}, f32[8,128,128]{1,2,0:T(8,128)S(1)}, ...), condition=%wide.region_9.0_spmd, body=%wide.region_6.9_spmd.sunk | while | flops 8848128 | bytes 1544281 | solution.py:93
  86.1 0.2 fusion.82
  86.6 0.2 fusion.82
  88.4 0.2 fusion.82
  89.0 0.2 fusion.82
  89.6 0.5 fusion.23
  90.1 0.9 copy.53
  (77 shorter events, 4.3 us)
Async XLA Ops:
  0.0 42.8 %copy-start = (bf16[128,128]{1,0:T(8,128)(2,1)S(1)}, bf16[128,128]{1,0:T(8,128)(2,1)}, u32[]{:S(2)}) copy-start(bf16[128,128]{1,0:T(8,128)(2,1)} %param.21) | copy-start | bytes 98308
  1.2 0.8 copy-start.7
  2.0 0.8 copy-start.8
  2.7 0.8 copy-start.1
  3.5 0.8 copy-start.2
  29.5 4.0 %copy-start.9 = (bf16[128,128]{1,0:T(8,128)(2,1)S(1)}, bf16[128,128]{1,0:T(8,128)(2,1)}, u32[]{:S(2)}) copy-start(bf16[128,128]{1,0:T(8,128)(2,1)} %param.20) | copy-start | bytes 98308
  29.5 13.1 %all-to-all-start.1 = ((bf16[8,128,128]{2,0,1:T(8,128)(2,1)}), bf16[8,128,128]{2,0,1:T(8,128)(2,1)S(1)}, u32[]{:S(2)}, u32[]{:S(2)}) async-start(bf16[8,128,128]{2,0,1:T(8,128)(2,1)} %copy.47), calls=%async_computation.1 | async-start | bytes 524288 | tf_op jit(solution)/shard_map/all_to_all | solution.py:56
  43.2 0.7 copy-start.6
  82.3 0.8 copy-start.3
  83.1 0.8 copy-start.4
  83.8 0.8 copy-start.5
  84.8 4.7 %copy-start.10 = (bf16[128,128]{1,0:T(8,128)(2,1)S(1)}, bf16[128,128]{1,0:T(8,128)(2,1)}, u32[]{:S(2)}) copy-start(bf16[128,128]{1,0:T(8,128)(2,1)} %param.27) | copy-start | bytes 98308
  84.9 4.7 %copy-start.11 = (bf16[128,128]{1,0:T(8,128)(2,1)S(1)}, bf16[128,128]{1,0:T(8,128)(2,1)}, u32[]{:S(2)}) copy-start(bf16[128,128]{1,0:T(8,128)(2,1)} %param.26) | copy-start | bytes 98308
where the time goes:
time: 91.8 us; the launch traced here: 90.9 us
  blocking collectives  61.5 us (67%)
  waiting for transfers between devices  8.73 us (10%)
  local copies, waits for them, and re-layouts  7.84 us (9%)
  matrix products  7.03 us (8%)
  starting transfers between devices  4.02 us (4%)
  other arithmetic  1.17 us (1%)
    all_gather x1, blocking collectives, body(): every_row = lax.all_gather(bias_local, 'row', axis=1, tiled=True)  38.3 us
    all_to_all x1, blocking collectives, body(): lax.all_to_all(stacked, 'row', split_axis=1, concat_axis=2, tiled=True)  23.2 us
    all_to_all x1, waiting for transfers between devices, body(): lax.all_to_all(summed, 'row', split_axis=1, concat_axis=0, tiled=True)  8.73 us
    unnamed x25, local copies, waits for them, and re-layouts  5.31 us
    all_to_all x1, starting transfers between devices, body(): lax.all_to_all(summed, 'row', split_axis=1, concat_axis=0, tiled=True)  4.02 us
    dot_general x8, matrix products, attend_row(): jnp.einsum('jhd,khd->hjk', query_row, key_row, preferred_element_type=jnp...  1.9 us
  transfers between devices with their start and end apart: 1, of which 1 were waited for; matrix products, arithmetic and copies ran while one was open for 0% of the time, Pallas kernels for 0%

commit v1 on v0

--- a/solution.py
+++ b/solution.py
@@ -65,7 +65,9 @@
     bias_local = jnp.einsum(
         "ijc,ch->hij", att_norm, w_bias, preferred_element_type=jnp.float32
     ).astype(jnp.bfloat16)
-    every_row = lax.all_gather(bias_local, "row", axis=1, tiled=True)
+    row_parts = lax.axis_size("row")
+    copies = jnp.broadcast_to(bias_local[None], (row_parts, *bias_local.shape))
+    every_row = lax.all_to_all(copies, "row", split_axis=0, concat_axis=2, tiled=True)[0]
     bias_full = lax.all_to_all(every_row, "col", split_axis=1, concat_axis=2, tiled=True).astype(
         jnp.float32
     )

time: 91.8 us -> 66.3 us (0.72)
  blocking collectives: 61.5 us -> 23.2 us
  waiting for transfers between devices: 8.73 us -> 14.7 us
  starting transfers between devices: 4.02 us -> 7.7 us
  local copies, waits for them, and re-layouts: 7.84 us -> 10.7 us
    all_gather x1 -> x0, blocking collectives: 38.3 us -> none  [body(): every_row = lax.all_gather(bias_local, 'row', axis=1, tiled=True)]
    all_to_all x0 -> x1, waiting for transfers between devices: none -> 6 us  [body(): lax.all_to_all(copies, 'row', split_axis=0, concat_axis=2, tiled=True)[0]]
    all_to_all x0 -> x1, starting transfers between devices: none -> 3.67 us  [body(): lax.all_to_all(copies, 'row', split_axis=0, concat_axis=2, tiled=True)[0]]
    dynamic_slice x16 -> x40, local copies, waits for them, and re-layouts: 0.14 us -> 2.87 us  [body(): attended = lax.map(attend_row, (queries, key_value[0], key_value[1]))]
  transfers between devices with their start and end apart: 1 -> 2, of which waited for: 1 -> 2; matrix products, arithmetic and copies ran while one was open for 0% -> 2% of each run, Pallas kernels for 0% -> 0%
where the time goes in v1:
time: 66.3 us; the launch traced here: 65.5 us
  blocking collectives  23.2 us (35%)
  waiting for transfers between devices  14.7 us (22%)
  local copies, waits for them, and re-layouts  10.7 us (16%)
  starting transfers between devices  7.7 us (12%)
  matrix products  7.14 us (11%)
  other arithmetic  1.18 us (2%)
    all_to_all x1, blocking collectives, body(): lax.all_to_all(stacked, 'row', split_axis=1, concat_axis=2, tiled=True)  23.2 us
    all_to_all x1, waiting for transfers between devices, body(): lax.all_to_all(summed, 'row', split_axis=1, concat_axis=0, tiled=True)  8.73 us
    all_to_all x1, waiting for transfers between devices, body(): lax.all_to_all(copies, 'row', split_axis=0, concat_axis=2, tiled=True)[0]  6 us
    unnamed x25, local copies, waits for them, and re-layouts  4.7 us
    all_to_all x1, starting transfers between devices, body(): lax.all_to_all(summed, 'row', split_axis=1, concat_axis=0, tiled=True)  4.02 us
    all_to_all x1, starting transfers between devices, body(): lax.all_to_all(copies, 'row', split_axis=0, concat_axis=2, tiled=True)[0]  3.67 us
    dynamic_slice x40, local copies, waits for them, and re-layouts, body(): attended = lax.map(attend_row, (queries, key_value[0], key_value[1]))  2.87 us
    dot_general x8, matrix products, attend_row(): jnp.einsum('jhd,khd->hjk', query_row, key_row, preferred_element_type=jnp...  1.99 us
  transfers between devices with their start and end apart: 2, of which 2 were waited for; matrix products, arithmetic and copies ran while one was open for 2% of the time, Pallas kernels for 0%

profile of v1, /device:TPU:0, one launch (start us, length us, event | category | flops | bytes accessed | tf_op | source)
XLA Modules:
  0.0 65.5 jit_solution(8839790977481703368)
XLA Ops:
  0.0 1.1 %copy.58 = bf16[8,128,128]{1,2,0:T(8,128)(2,1)S(1)} copy(bf16[8,128,128]{2,1,0:T(8,128)(2,1)} %param.15) | data formatting | bytes 524288 | tf_op args[0]
  1.3 0.6 copy-done.7
  2.0 0.3 fusion.14
  2.3 0.4 copy-done.8
  2.7 0.3 fusion.11
  3.1 0.4 copy-done.1
  3.5 0.3 fusion.25
  3.8 0.5 copy-done.2
  4.2 0.3 fusion.24
  4.6 0.3 copy.69
  4.9 23.2 %all_to_all.33 = bf16[2,128,8,128]{3,2,0,1:T(8,128)(2,1)S(1)} all-to-all(bf16[2,128,8,128]{3,2,0,1:T(8,128)(2,1)S(1)} %copy.69), channel_id=1, replica_groups=mesh['grp'=2,'row'=16,'col'=1] {'row'}, dimensions={1} | all-to-all | bytes 1048576 | tf_op jit(solution)/shard_map/all_to_all | solution.py:49
  28.3 0.3 convolution_convert_fusion.3
  28.6 0.9 %copy.71 = bf16[8,128,128]{2,0,1:T(8,128)(2,1)} copy(bf16[8,128,128]{2,1,0:T(8,128)(2,1)S(1)} %convolution_convert_fusion.3) | data formatting | bytes 524288 | tf_op jit(solution)/shard_map/convert_element_type | solution.py:53
  29.5 4.0 %all-to-all-start.1 = ((bf16[8,128,128]{2,0,1:T(8,128)(2,1)}), bf16[8,128,128]{2,0,1:T(8,128)(2,1)S(1)}, u32[]{:S(2)}, u32[]{:S(2)}) async-start(bf16[8,128,128]{2,0,1:T(8,128)(2,1)} %copy.71), calls=%async_computation.1 | async-start | bytes 524288 | tf_op jit(solution)/shard_map/all_to_all | solution.py:56
  33.5 0.3 fusion.17
  33.9 8.7 %all-to-all-done.1 = bf16[8,128,128]{2,0,1:T(8,128)(2,1)S(1)} async-done(((bf16[8,128,128]{2,0,1:T(8,128)(2,1)}), bf16[8,128,128]{2,0,1:T(8,128)(2,1)S(1)}, u32[]{:S(2)}, u32[]{:S(2)}) %all-to-all-start.1) | async-done | bytes 262176 | tf_op jit(solution)/shard_map/all_to_all | solution.py:56
  42.8 0.3 fusion.58
  43.3 0.6 copy-done.6
  44.0 0.7 %broadcast_in_dim.8 = bf16[16,4,8,128]{3,2,1,0:T(8,128)(2,1)} broadcast(bf16[4,8,128]{2,1,0:T(8,128)(2,1)S(1)} %copy.78), dimensions={1,2,3} | broadcast | bytes 139264 | tf_op jit(solution)/shard_map/broadcast_in_dim | solution.py:69
  44.7 3.7 %all-to-all-start.2 = ((bf16[16,4,8,128]{3,2,1,0:T(8,128)(2,1)}), bf16[16,4,8,128]{3,2,1,0:T(8,128)(2,1)S(1)}, u32[]{:S(2)}, u32[]{:S(2)}) async-start(bf16[16,4,8,128]{3,2,1,0:T(8,128)(2,1)} %broadcast_in_dim.8), calls=%async_computation.2 | async-start | bytes 262144 | tf_op jit(solution)/shard_map/all_to_all | solution.py:70
  48.4 0.3 convolution_convert_fusion
  48.7 0.5 copy-done.4
  49.2 0.3 convolution_convert_fusion.1
  49.4 0.5 copy-done.5
  49.9 0.3 convolution_convert_fusion.2
  50.2 6.0 %all-to-all-done.2 = bf16[16,4,8,128]{3,2,1,0:T(8,128)(2,1)S(1)} async-done(((bf16[16,4,8,128]{3,2,1,0:T(8,128)(2,1)}), bf16[16,4,8,128]{3,2,1,0:T(8,128)(2,1)S(1)}, u32[]{:S(2)}, u32[]{:S(2)}) %all-to-all-start.2) | async-done | bytes 131104 | tf_op jit(solution)/shard_map/all_to_all | solution.py:70
  56.4 7.7 %while.10 = (s32[]{:T(128)}, f32[8,128,128]{1,2,0:T(8,128)S(1)}, bf16[8,128,128]{2,1,0:T(8,128)(2,1)S(1)}, bf16[8,128,128]{2,1,0:T(8,128)(2,1)S(1)}, bf16[8,128,...) while((s32[]{:T(128)}, f32[8,128,128]{1,2,0:T(8,128)S(1)}, ...), condition=%wide.region_9.0_spmd, body=%wide.region_6.9_spmd.sunk | while | flops 8848128 | bytes 1740889 | solution.py:95
  58.6 0.2 fusion.82
  59.5 0.2 fusion.82
  63.4 0.2 fusion.82
  64.1 0.5 fusion.23
  64.6 0.9 %copy.88 = bf16[8,128,128]{2,1,0:T(8,128)(2,1)} copy(bf16[8,128,128]{1,2,0:T(8,128)(2,1)S(1)} %fusion.23) | data formatting | bytes 524288 | tf_op jit(solution)/shard_map/convert_element_type | solution.py:97
  (105 shorter events, 7.4 us)
Async XLA Ops:
  0.0 42.8 %copy-start = (bf16[128,128]{1,0:T(8,128)(2,1)S(1)}, bf16[128,128]{1,0:T(8,128)(2,1)}, u32[]{:S(2)}) copy-start(bf16[128,128]{1,0:T(8,128)(2,1)} %param.21) | copy-start | bytes 98308
  1.2 0.8 %copy-start.7 = (bf16[128,128]{1,0:T(8,128)(2,1)S(1)}, bf16[128,128]{1,0:T(8,128)(2,1)}, u32[]{:S(2)}) copy-start(bf16[128,128]{1,0:T(8,128)(2,1)} %param.17) | copy-start | bytes 98308
  2.0 0.8 %copy-start.8 = (bf16[128,128]{1,0:T(8,128)(2,1)S(1)}, bf16[128,128]{1,0:T(8,128)(2,1)}, u32[]{:S(2)}) copy-start(bf16[128,128]{1,0:T(8,128)(2,1)} %param.19) | copy-start | bytes 98308
  2.7 0.8 %copy-start.1 = (bf16[128,128]{1,0:T(8,128)(2,1)S(1)}, bf16[128,128]{1,0:T(8,128)(2,1)}, u32[]{:S(2)}) copy-start(bf16[128,128]{1,0:T(8,128)(2,1)} %param.16) | copy-start | bytes 98308
  3.5 0.8 %copy-start.2 = (bf16[128,128]{1,0:T(8,128)(2,1)S(1)}, bf16[128,128]{1,0:T(8,128)(2,1)}, u32[]{:S(2)}) copy-start(bf16[128,128]{1,0:T(8,128)(2,1)} %param.18) | copy-start | bytes 98308
  29.5 4.0 %copy-start.9 = (bf16[128,128]{1,0:T(8,128)(2,1)S(1)}, bf16[128,128]{1,0:T(8,128)(2,1)}, u32[]{:S(2)}) copy-start(bf16[128,128]{1,0:T(8,128)(2,1)} %param.20) | copy-start | bytes 98308
  29.5 13.1 %all-to-all-start.1 = ((bf16[8,128,128]{2,0,1:T(8,128)(2,1)}), bf16[8,128,128]{2,0,1:T(8,128)(2,1)S(1)}, u32[]{:S(2)}, u32[]{:S(2)}) async-start(bf16[8,128,128]{2,0,1:T(8,128)(2,1)} %copy.71), calls=%async_computation.1 | async-start | bytes 524288 | tf_op jit(solution)/shard_map/all_to_all | solution.py:56
  43.2 0.7 %copy-start.6 = (bf16[128,4]{0,1:T(4,128)(2,1)S(1)}, bf16[128,4]{0,1:T(4,128)(2,1)}, u32[]{:S(2)}) copy-start(bf16[128,4]{0,1:T(4,128)(2,1)} %param.25) | copy-start | bytes 3076
  44.7 3.7 %copy-start.3 = (bf16[128,128]{1,0:T(8,128)(2,1)S(1)}, bf16[128,128]{1,0:T(8,128)(2,1)}, u32[]{:S(2)}) copy-start(bf16[128,128]{1,0:T(8,128)(2,1)} %param.23) | copy-start | bytes 98308
  44.7 11.5 %all-to-all-start.2 = ((bf16[16,4,8,128]{3,2,1,0:T(8,128)(2,1)}), bf16[16,4,8,128]{3,2,1,0:T(8,128)(2,1)S(1)}, u32[]{:S(2)}, u32[]{:S(2)}) async-start(bf16[16,4,8,128]{3,2,1,0:T(8,128)(2,1)} %broadcast_in_dim.8), calls=%async_computation.2 | async-start | bytes 262144 | tf_op jit(solution)/shard_map/all_to_all | solution.py:70
  48.4 0.8 %copy-start.4 = (bf16[128,128]{1,0:T(8,128)(2,1)S(1)}, bf16[128,128]{1,0:T(8,128)(2,1)}, u32[]{:S(2)}) copy-start(bf16[128,128]{1,0:T(8,128)(2,1)} %param.22) | copy-start | bytes 98308
  49.2 0.8 %copy-start.5 = (bf16[128,128]{1,0:T(8,128)(2,1)S(1)}, bf16[128,128]{1,0:T(8,128)(2,1)}, u32[]{:S(2)}) copy-start(bf16[128,128]{1,0:T(8,128)(2,1)} %param.24) | copy-start | bytes 98308
  56.3 7.7 %copy-start.10 = (bf16[128,128]{1,0:T(8,128)(2,1)S(1)}, bf16[128,128]{1,0:T(8,128)(2,1)}, u32[]{:S(2)}) copy-start(bf16[128,128]{1,0:T(8,128)(2,1)} %param.27) | copy-start | bytes 98308
  56.3 7.7 %copy-start.11 = (bf16[128,128]{1,0:T(8,128)(2,1)S(1)}, bf16[128,128]{1,0:T(8,128)(2,1)}, u32[]{:S(2)}) copy-start(bf16[128,128]{1,0:T(8,128)(2,1)} %param.26) | copy-start | bytes 98308

commit v2 on v1

--- a/solution.py
+++ b/solution.py
@@ -66,8 +66,13 @@
         "ijc,ch->hij", att_norm, w_bias, preferred_element_type=jnp.float32
     ).astype(jnp.bfloat16)
     row_parts = lax.axis_size("row")
-    copies = jnp.broadcast_to(bias_local[None], (row_parts, *bias_local.shape))
-    every_row = lax.all_to_all(copies, "row", split_axis=0, concat_axis=2, tiled=True)[0]
+    pieces = [bias_local]
+    for shift in range(1, row_parts):
+        pairs = [(r, (r + row_parts - shift) % row_parts) for r in range(row_parts)]
+        pieces.append(lax.ppermute(bias_local, "row", pairs))
+    twice = jnp.concatenate(pieces + pieces, axis=1)
+    first = (row_parts - lax.axis_index("row")) * bias_local.shape[1]
+    every_row = lax.dynamic_slice_in_dim(twice, first, row_parts * bias_local.shape[1], axis=1)
     bias_full = lax.all_to_all(every_row, "col", split_axis=1, concat_axis=2, tiled=True).astype(
         jnp.float32
     )

time: 66.3 us -> 84.5 us (1.27)
  starting transfers between devices: 7.7 us -> 28.5 us
  local copies, waits for them, and re-layouts: 10.7 us -> 7.12 us
  waiting for transfers between devices: 14.7 us -> 15.9 us
    ppermute x0 -> x15, starting transfers between devices: none -> 24.5 us  [body(): pieces.append(lax.ppermute(bias_local, 'row', pairs))]
    ppermute x0 -> x15, waiting for transfers between devices: none -> 7.17 us  [body(): pieces.append(lax.ppermute(bias_local, 'row', pairs))]
    all_to_all x1 -> x0, waiting for transfers between devices: 6 us -> none  [body(): lax.all_to_all(copies, 'row', split_axis=0, concat_axis=2, tiled=True)[0]]
    all_to_all x1 -> x0, starting transfers between devices: 3.67 us -> none  [body(): lax.all_to_all(copies, 'row', split_axis=0, concat_axis=2, tiled=True)[0]]
    dynamic_slice x40 -> x16, local copies, waits for them, and re-layouts: 2.87 us -> 0.14 us  [body(): attended = lax.map(attend_row, (queries, key_value[0], key_value[1]))]
    unnamed x25 -> x55, local copies, waits for them, and re-layouts: 4.7 us -> 4.56 us
  transfers between devices with their start and end apart: 2 -> 16, of which waited for: 2 -> 4; matrix products, arithmetic and copies ran while one was open for 2% -> 2% of each run, Pallas kernels for 0% -> 0%
where the time goes in v2:
time: 84.5 us; the launch traced here: 83.8 us
  starting transfers between devices  28.5 us (34%)
  blocking collectives  23.2 us (27%)
  waiting for transfers between devices  15.9 us (19%)
  local copies, waits for them, and re-layouts  7.12 us (8%)
  matrix products  7.03 us (8%)
  other arithmetic  1.21 us (1%)
    ppermute x15, starting transfers between devices, body(): pieces.append(lax.ppermute(bias_local, 'row', pairs))  24.5 us
    all_to_all x1, blocking collectives, body(): lax.all_to_all(stacked, 'row', split_axis=1, concat_axis=2, tiled=True)  23.2 us
    all_to_all x1, waiting for transfers between devices, body(): lax.all_to_all(summed, 'row', split_axis=1, concat_axis=0, tiled=True)  8.72 us
    ppermute x15, waiting for transfers between devices, body(): pieces.append(lax.ppermute(bias_local, 'row', pairs))  7.17 us
    unnamed x55, local copies, waits for them, and re-layouts  4.56 us
    all_to_all x1, starting transfers between devices, body(): lax.all_to_all(summed, 'row', split_axis=1, concat_axis=0, tiled=True)  4.02 us
    dot_general x8, matrix products, attend_row(): jnp.einsum('jhd,khd->hjk', query_row, key_row, preferred_element_type=jnp...  1.9 us
  transfers between devices with their start and end apart: 16, of which 4 were waited for; matrix products, arithmetic and copies ran while one was open for 2% of the time, Pallas kernels for 0%

profile of v2, /device:TPU:0, one launch (start us, length us, event | category | flops | bytes accessed | tf_op | source)
XLA Modules:
  0.0 83.8 jit_solution(5378629834259494535)
XLA Ops:
  0.0 1.1 %copy.36 = bf16[8,128,128]{1,2,0:T(8,128)(2,1)S(1)} copy(bf16[8,128,128]{2,1,0:T(8,128)(2,1)} %param.15) | data formatting | bytes 524288 | tf_op args[0]
  1.3 0.6 copy-done.7
  2.3 0.4 copy-done.8
  3.1 0.4 copy-done.1
  3.8 0.5 copy-done.2
  4.9 23.2 %all_to_all.24 = bf16[2,128,8,128]{3,2,0,1:T(8,128)(2,1)S(1)} all-to-all(bf16[2,128,8,128]{3,2,0,1:T(8,128)(2,1)S(1)} %copy.47), channel_id=1, replica_groups=mesh['grp'=2,'row'=16,'col'=1] {'row'}, dimensions={1} | all-to-all | bytes 1048576 | tf_op jit(solution)/shard_map/all_to_all | solution.py:49
  28.6 0.9 %copy.49 = bf16[8,128,128]{2,0,1:T(8,128)(2,1)} copy(bf16[8,128,128]{2,1,0:T(8,128)(2,1)S(1)} %convolution_convert_fusion.3) | data formatting | bytes 524288 | tf_op jit(solution)/shard_map/convert_element_type | solution.py:53
  29.5 4.0 %all-to-all-start.1 = ((bf16[8,128,128]{2,0,1:T(8,128)(2,1)}), bf16[8,128,128]{2,0,1:T(8,128)(2,1)S(1)}, u32[]{:S(2)}, u32[]{:S(2)}) async-start(bf16[8,128,128]{2,0,1:T(8,128)(2,1)} %copy.49), calls=%async_computation.1 | async-start | bytes 524288 | tf_op jit(solution)/shard_map/all_to_all | solution.py:56
  33.5 0.3 fusion.17
  33.9 8.7 %all-to-all-done.1 = bf16[8,128,128]{2,0,1:T(8,128)(2,1)S(1)} async-done(((bf16[8,128,128]{2,0,1:T(8,128)(2,1)}), bf16[8,128,128]{2,0,1:T(8,128)(2,1)S(1)}, u32[]{:S(2)}, u32[]{:S(2)}) %all-to-all-start.1) | async-done | bytes 262176 | tf_op jit(solution)/shard_map/all_to_all | solution.py:56
  43.3 0.6 copy-done.6
  44.0 2.2 %collective-permute-start = (bf16[4,8,128]{2,0,1:T(4,128)(2,1)S(1)}, bf16[4,8,128]{2,0,1:T(4,128)(2,1)S(1)}, u32[]{:S(2)}, u32[]{:S(2)}) collective-permute-start(bf16[4,8,128]{2,0,1:T(4,128)(2,1)S(1)} %get-tuple-element.67), channel_id=1, source_target_pairs={{0,15},{1,0},{2,1},{3,2},{4,3},{5,4},{6,5},{7,6},{8,7},{9,8},{10,9... | collective-permute-start | bytes 24584 | tf_op jit(solution)/shard_map/ppermute | solution.py:72
  46.2 1.1 %collective-permute-start.1 = (bf16[4,8,128]{2,0,1:T(4,128)(2,1)S(1)}, bf16[4,8,128]{2,0,1:T(4,128)(2,1)S(1)}, u32[]{:S(2)}, u32[]{:S(2)}) collective-permute-start(bf16[4,8,128]{2,0,1:T(4,128)(2,1)S(1)} %get-tuple-element.67), channel_id=1, source_target_pairs={{0,14},{1,15},{2,0},{3,1},{4,2},{5,3},{6,4},{7,5},{8,6},{9,7},{10,... | collective-permute-start | bytes 24584 | tf_op jit(solution)/shard_map/ppermute | solution.py:72
  47.3 0.8 %collective-permute-start.2 = (bf16[4,8,128]{2,0,1:T(4,128)(2,1)S(1)}, bf16[4,8,128]{2,0,1:T(4,128)(2,1)S(1)}, u32[]{:S(2)}, u32[]{:S(2)}) collective-permute-start(bf16[4,8,128]{2,0,1:T(4,128)(2,1)S(1)} %get-tuple-element.67), channel_id=1, source_target_pairs={{0,13},{1,14},{2,15},{3,0},{4,1},{5,2},{6,3},{7,4},{8,5},{9,6},{10... | collective-permute-start | bytes 24584 | tf_op jit(solution)/shard_map/ppermute | solution.py:72
  48.2 1.5 %collective-permute-start.3 = (bf16[4,8,128]{2,0,1:T(4,128)(2,1)S(1)}, bf16[4,8,128]{2,0,1:T(4,128)(2,1)S(1)}, u32[]{:S(2)}, u32[]{:S(2)}) collective-permute-start(bf16[4,8,128]{2,0,1:T(4,128)(2,1)S(1)} %get-tuple-element.67), channel_id=1, source_target_pairs={{0,12},{1,13},{2,14},{3,15},{4,0},{5,1},{6,2},{7,3},{8,4},{9,5},{1... | collective-permute-start | bytes 24584 | tf_op jit(solution)/shard_map/ppermute | solution.py:72
  49.7 1.9 %collective-permute-start.4 = (bf16[4,8,128]{2,0,1:T(4,128)(2,1)S(1)}, bf16[4,8,128]{2,0,1:T(4,128)(2,1)S(1)}, u32[]{:S(2)}, u32[]{:S(2)}) collective-permute-start(bf16[4,8,128]{2,0,1:T(4,128)(2,1)S(1)} %get-tuple-element.67), channel_id=1, source_target_pairs={{0,11},{1,12},{2,13},{3,14},{4,15},{5,0},{6,1},{7,2},{8,3},{9,4},{... | collective-permute-start | bytes 24584 | tf_op jit(solution)/shard_map/ppermute | solution.py:72
  52.2 0.5 copy-done.5
  53.0 1.9 %collective-permute-start.5 = (bf16[4,8,128]{2,0,1:T(4,128)(2,1)S(1)}, bf16[4,8,128]{2,0,1:T(4,128)(2,1)S(1)}, u32[]{:S(2)}, u32[]{:S(2)}) collective-permute-start(bf16[4,8,128]{2,0,1:T(4,128)(2,1)S(1)} %get-tuple-element.67), channel_id=1, source_target_pairs={{0,10},{1,11},{2,12},{3,13},{4,14},{5,15},{6,0},{7,1},{8,2},{9,3},... | collective-permute-start | bytes 24584 | tf_op jit(solution)/shard_map/ppermute | solution.py:72
  54.9 1.4 %collective-permute-start.6 = (bf16[4,8,128]{2,0,1:T(4,128)(2,1)S(1)}, bf16[4,8,128]{2,0,1:T(4,128)(2,1)S(1)}, u32[]{:S(2)}, u32[]{:S(2)}) collective-permute-start(bf16[4,8,128]{2,0,1:T(4,128)(2,1)S(1)} %get-tuple-element.67), channel_id=1, source_target_pairs={{0,9},{1,10},{2,11},{3,12},{4,13},{5,14},{6,15},{7,0},{8,1},{9,2},... | collective-permute-start | bytes 24584 | tf_op jit(solution)/shard_map/ppermute | solution.py:72
  56.3 1.3 %collective-permute-start.7 = (bf16[4,8,128]{2,0,1:T(4,128)(2,1)S(1)}, bf16[4,8,128]{2,0,1:T(4,128)(2,1)S(1)}, u32[]{:S(2)}, u32[]{:S(2)}) collective-permute-start(bf16[4,8,128]{2,0,1:T(4,128)(2,1)S(1)} %get-tuple-element.67), channel_id=1, source_target_pairs={{0,8},{1,9},{2,10},{3,11},{4,12},{5,13},{6,14},{7,15},{8,0},{9,1},... | collective-permute-start | bytes 24584 | tf_op jit(solution)/shard_map/ppermute | solution.py:72
  57.7 3.3 %collective-permute-start.8 = (bf16[4,8,128]{2,0,1:T(4,128)(2,1)S(1)}, bf16[4,8,128]{2,0,1:T(4,128)(2,1)S(1)}, u32[]{:S(2)}, u32[]{:S(2)}) collective-permute-start(bf16[4,8,128]{2,0,1:T(4,128)(2,1)S(1)} %get-tuple-element.67), channel_id=1, source_target_pairs={{0,7},{1,8},{2,9},{3,10},{4,11},{5,12},{6,13},{7,14},{8,15},{9,0},... | collective-permute-start | bytes 24584 | tf_op jit(solution)/shard_map/ppermute | solution.py:72
  61.0 1.9 %collective-permute-start.9 = (bf16[4,8,128]{2,0,1:T(4,128)(2,1)S(1)}, bf16[4,8,128]{2,0,1:T(4,128)(2,1)S(1)}, u32[]{:S(2)}, u32[]{:S(2)}) collective-permute-start(bf16[4,8,128]{2,0,1:T(4,128)(2,1)S(1)} %get-tuple-element.67), channel_id=1, source_target_pairs={{0,6},{1,7},{2,8},{3,9},{4,10},{5,11},{6,12},{7,13},{8,14},{9,15},... | collective-permute-start | bytes 24584 | tf_op jit(solution)/shard_map/ppermute | solution.py:72
  62.9 0.6 collective-permute-start.10
  63.5 1.5 %collective-permute-start.11 = (bf16[4,8,128]{2,0,1:T(4,128)(2,1)S(1)}, bf16[4,8,128]{2,0,1:T(4,128)(2,1)S(1)}, u32[]{:S(2)}, u32[]{:S(2)}) collective-permute-start(bf16[4,8,128]{2,0,1:T(4,128)(2,1)S(1)} %get-tuple-element.67), channel_id=1, source_target_pairs={{0,4},{1,5},{2,6},{3,7},{4,8},{5,9},{6,10},{7,11},{8,12},{9,13},{1... | collective-permute-start | bytes 24584 | tf_op jit(solution)/shard_map/ppermute | solution.py:72
  65.1 3.3 %collective-permute-start.12 = (bf16[4,8,128]{2,0,1:T(4,128)(2,1)S(1)}, bf16[4,8,128]{2,0,1:T(4,128)(2,1)S(1)}, u32[]{:S(2)}, u32[]{:S(2)}) collective-permute-start(bf16[4,8,128]{2,0,1:T(4,128)(2,1)S(1)} %get-tuple-element.67), channel_id=1, source_target_pairs={{0,3},{1,4},{2,5},{3,6},{4,7},{5,8},{6,9},{7,10},{8,11},{9,12},{10... | collective-permute-start | bytes 24584 | tf_op jit(solution)/shard_map/ppermute | solution.py:72
  68.4 1.5 %collective-permute-start.13 = (bf16[4,8,128]{2,0,1:T(4,128)(2,1)S(1)}, bf16[4,8,128]{2,0,1:T(4,128)(2,1)S(1)}, u32[]{:S(2)}, u32[]{:S(2)}) collective-permute-start(bf16[4,8,128]{2,0,1:T(4,128)(2,1)S(1)} %get-tuple-element.67), channel_id=1, source_target_pairs={{0,2},{1,3},{2,4},{3,5},{4,6},{5,7},{6,8},{7,9},{8,10},{9,11},{10,... | collective-permute-start | bytes 24584 | tf_op jit(solution)/shard_map/ppermute | solution.py:72
  70.1 1.7 %collective-permute-done.12 = bf16[4,8,128]{2,0,1:T(4,128)(2,1)S(1)} collective-permute-done((bf16[4,8,128]{2,0,1:T(4,128)(2,1)S(1)}, bf16[4,8,128]{2,0,1:T(4,128)(2,1)S(1)}, u32[]{:S(2)}, u32[]{:S(2)}) %collective-permute-start.12) | collective-permute-done | bytes 8224 | tf_op jit(solution)/shard_map/ppermute | solution.py:72
  71.8 3.0 %collective-permute-done.13 = bf16[4,8,128]{2,0,1:T(4,128)(2,1)S(1)} collective-permute-done((bf16[4,8,128]{2,0,1:T(4,128)(2,1)S(1)}, bf16[4,8,128]{2,0,1:T(4,128)(2,1)S(1)}, u32[]{:S(2)}, u32[]{:S(2)}) %collective-permute-start.13) | collective-permute-done | bytes 8224 | tf_op jit(solution)/shard_map/ppermute | solution.py:72
  74.8 2.4 %collective-permute-done.14 = bf16[4,8,128]{2,0,1:T(4,128)(2,1)S(1)} collective-permute-done((bf16[4,8,128]{2,0,1:T(4,128)(2,1)S(1)}, bf16[4,8,128]{2,0,1:T(4,128)(2,1)S(1)}, u32[]{:S(2)}, u32[]{:S(2)}) %collective-permute-start.14) | collective-permute-done | bytes 8224 | tf_op jit(solution)/shard_map/ppermute | solution.py:72
  77.7 4.7 %while.10 = (s32[]{:T(128)}, f32[8,128,128]{1,2,0:T(8,128)S(1)}, bf16[8,128,128]{1,2,0:T(8,128)(2,1)S(1)}, bf16[8,128,128]{1,2,0:T(8,128)(2,1)S(1)}, bf16[8,128,...) while((s32[]{:T(128)}, f32[8,128,128]{1,2,0:T(8,128)S(1)}, ...), condition=%wide.region_9.0_spmd, body=%wide.region_6.9_spmd.sunk | while | flops 8848128 | bytes 1544281 | solution.py:100
  82.4 0.5 fusion.23
  83.0 0.9 %copy.56 = bf16[8,128,128]{2,1,0:T(8,128)(2,1)} copy(bf16[8,128,128]{1,2,0:T(8,128)(2,1)S(1)} %fusion.23) | data formatting | bytes 524288 | tf_op jit(solution)/shard_map/convert_element_type | solution.py:102
  (138 shorter events, 8.7 us)
Async XLA Ops:
  0.0 42.8 %copy-start = (bf16[128,128]{1,0:T(8,128)(2,1)S(1)}, bf16[128,128]{1,0:T(8,128)(2,1)}, u32[]{:S(2)}) copy-start(bf16[128,128]{1,0:T(8,128)(2,1)} %param.21) | copy-start | bytes 98308
  1.2 0.8 copy-start.7
  2.0 0.8 copy-start.8
  2.7 0.8 copy-start.1
  3.5 0.8 copy-start.2
  29.5 4.1 %copy-start.9 = (bf16[128,128]{1,0:T(8,128)(2,1)S(1)}, bf16[128,128]{1,0:T(8,128)(2,1)}, u32[]{:S(2)}) copy-start(bf16[128,128]{1,0:T(8,128)(2,1)} %param.20) | copy-start | bytes 98308
  29.5 13.1 %all-to-all-start.1 = ((bf16[8,128,128]{2,0,1:T(8,128)(2,1)}), bf16[8,128,128]{2,0,1:T(8,128)(2,1)S(1)}, u32[]{:S(2)}, u32[]{:S(2)}) async-start(bf16[8,128,128]{2,0,1:T(8,128)(2,1)} %copy.49), calls=%async_computation.1 | async-start | bytes 524288 | tf_op jit(solution)/shard_map/all_to_all | solution.py:56
  43.2 0.7 copy-start.6
  43.9 7.8 %copy-start.3 = (bf16[128,128]{1,0:T(8,128)(2,1)S(1)}, bf16[128,128]{1,0:T(8,128)(2,1)}, u32[]{:S(2)}) copy-start(bf16[128,128]{1,0:T(8,128)(2,1)} %param.23) | copy-start | bytes 98308
  44.0 7.9 %copy-start.4 = (bf16[128,128]{1,0:T(8,128)(2,1)S(1)}, bf16[128,128]{1,0:T(8,128)(2,1)}, u32[]{:S(2)}) copy-start(bf16[128,128]{1,0:T(8,128)(2,1)} %param.22) | copy-start | bytes 98308
  44.0 9.0 %collective-permute-start = (bf16[4,8,128]{2,0,1:T(4,128)(2,1)S(1)}, bf16[4,8,128]{2,0,1:T(4,128)(2,1)S(1)}, u32[]{:S(2)}, u32[]{:S(2)}) collective-permute-start(bf16[4,8,128]{2,0,1:T(4,128)(2,1)S(1)} %get-tuple-element.67), channel_id=1, source_target_pairs={{0,15},{1,0},{2,1},{3,2},{4,3},{5,4},{6,5},{7,6},{8,7},{9,8},{10,9... | collective-permute-start | bytes 24584 | tf_op jit(solution)/shard_map/ppermute | solution.py:72
  46.2 8.6 %collective-permute-start.1 = (bf16[4,8,128]{2,0,1:T(4,128)(2,1)S(1)}, bf16[4,8,128]{2,0,1:T(4,128)(2,1)S(1)}, u32[]{:S(2)}, u32[]{:S(2)}) collective-permute-start(bf16[4,8,128]{2,0,1:T(4,128)(2,1)S(1)} %get-tuple-element.67), channel_id=1, source_target_pairs={{0,14},{1,15},{2,0},{3,1},{4,2},{5,3},{6,4},{7,5},{8,6},{9,7},{10,... | collective-permute-start | bytes 24584 | tf_op jit(solution)/shard_map/ppermute | solution.py:72
  47.3 9.0 %collective-permute-start.2 = (bf16[4,8,128]{2,0,1:T(4,128)(2,1)S(1)}, bf16[4,8,128]{2,0,1:T(4,128)(2,1)S(1)}, u32[]{:S(2)}, u32[]{:S(2)}) collective-permute-start(bf16[4,8,128]{2,0,1:T(4,128)(2,1)S(1)} %get-tuple-element.67), channel_id=1, source_target_pairs={{0,13},{1,14},{2,15},{3,0},{4,1},{5,2},{6,3},{7,4},{8,5},{9,6},{10... | collective-permute-start | bytes 24584 | tf_op jit(solution)/shard_map/ppermute | solution.py:72
  48.2 9.5 %collective-permute-start.3 = (bf16[4,8,128]{2,0,1:T(4,128)(2,1)S(1)}, bf16[4,8,128]{2,0,1:T(4,128)(2,1)S(1)}, u32[]{:S(2)}, u32[]{:S(2)}) collective-permute-start(bf16[4,8,128]{2,0,1:T(4,128)(2,1)S(1)} %get-tuple-element.67), channel_id=1, source_target_pairs={{0,12},{1,13},{2,14},{3,15},{4,0},{5,1},{6,2},{7,3},{8,4},{9,5},{1... | collective-permute-start | bytes 24584 | tf_op jit(solution)/shard_map/ppermute | solution.py:72
  49.7 11.3 %collective-permute-start.4 = (bf16[4,8,128]{2,0,1:T(4,128)(2,1)S(1)}, bf16[4,8,128]{2,0,1:T(4,128)(2,1)S(1)}, u32[]{:S(2)}, u32[]{:S(2)}) collective-permute-start(bf16[4,8,128]{2,0,1:T(4,128)(2,1)S(1)} %get-tuple-element.67), channel_id=1, source_target_pairs={{0,11},{1,12},{2,13},{3,14},{4,15},{5,0},{6,1},{7,2},{8,3},{9,4},{... | collective-permute-start | bytes 24584 | tf_op jit(solution)/shard_map/ppermute | solution.py:72
  51.9 0.8 copy-start.5
  53.0 9.9 %collective-permute-start.5 = (bf16[4,8,128]{2,0,1:T(4,128)(2,1)S(1)}, bf16[4,8,128]{2,0,1:T(4,128)(2,1)S(1)}, u32[]{:S(2)}, u32[]{:S(2)}) collective-permute-start(bf16[4,8,128]{2,0,1:T(4,128)(2,1)S(1)} %get-tuple-element.67), channel_id=1, source_target_pairs={{0,10},{1,11},{2,12},{3,13},{4,14},{5,15},{6,0},{7,1},{8,2},{9,3},... | collective-permute-start | bytes 24584 | tf_op jit(solution)/shard_map/ppermute | solution.py:72
  54.9 8.7 %collective-permute-start.6 = (bf16[4,8,128]{2,0,1:T(4,128)(2,1)S(1)}, bf16[4,8,128]{2,0,1:T(4,128)(2,1)S(1)}, u32[]{:S(2)}, u32[]{:S(2)}) collective-permute-start(bf16[4,8,128]{2,0,1:T(4,128)(2,1)S(1)} %get-tuple-element.67), channel_id=1, source_target_pairs={{0,9},{1,10},{2,11},{3,12},{4,13},{5,14},{6,15},{7,0},{8,1},{9,2},... | collective-permute-start | bytes 24584 | tf_op jit(solution)/shard_map/ppermute | solution.py:72
  56.3 8.8 %collective-permute-start.7 = (bf16[4,8,128]{2,0,1:T(4,128)(2,1)S(1)}, bf16[4,8,128]{2,0,1:T(4,128)(2,1)S(1)}, u32[]{:S(2)}, u32[]{:S(2)}) collective-permute-start(bf16[4,8,128]{2,0,1:T(4,128)(2,1)S(1)} %get-tuple-element.67), channel_id=1, source_target_pairs={{0,8},{1,9},{2,10},{3,11},{4,12},{5,13},{6,14},{7,15},{8,0},{9,1},... | collective-permute-start | bytes 24584 | tf_op jit(solution)/shard_map/ppermute | solution.py:72
  57.7 10.7 %collective-permute-start.8 = (bf16[4,8,128]{2,0,1:T(4,128)(2,1)S(1)}, bf16[4,8,128]{2,0,1:T(4,128)(2,1)S(1)}, u32[]{:S(2)}, u32[]{:S(2)}) collective-permute-start(bf16[4,8,128]{2,0,1:T(4,128)(2,1)S(1)} %get-tuple-element.67), channel_id=1, source_target_pairs={{0,7},{1,8},{2,9},{3,10},{4,11},{5,12},{6,13},{7,14},{8,15},{9,0},... | collective-permute-start | bytes 24584 | tf_op jit(solution)/shard_map/ppermute | solution.py:72
  61.0 8.9 %collective-permute-start.9 = (bf16[4,8,128]{2,0,1:T(4,128)(2,1)S(1)}, bf16[4,8,128]{2,0,1:T(4,128)(2,1)S(1)}, u32[]{:S(2)}, u32[]{:S(2)}) collective-permute-start(bf16[4,8,128]{2,0,1:T(4,128)(2,1)S(1)} %get-tuple-element.67), channel_id=1, source_target_pairs={{0,6},{1,7},{2,8},{3,9},{4,10},{5,11},{6,12},{7,13},{8,14},{9,15},... | collective-permute-start | bytes 24584 | tf_op jit(solution)/shard_map/ppermute | solution.py:72
  62.9 7.1 %collective-permute-start.10 = (bf16[4,8,128]{2,0,1:T(4,128)(2,1)S(1)}, bf16[4,8,128]{2,0,1:T(4,128)(2,1)S(1)}, u32[]{:S(2)}, u32[]{:S(2)}) collective-permute-start(bf16[4,8,128]{2,0,1:T(4,128)(2,1)S(1)} %get-tuple-element.67), channel_id=1, source_target_pairs={{0,5},{1,6},{2,7},{3,8},{4,9},{5,10},{6,11},{7,12},{8,13},{9,14},{... | collective-permute-start | bytes 24584 | tf_op jit(solution)/shard_map/ppermute | solution.py:72
  63.5 6.5 %collective-permute-start.11 = (bf16[4,8,128]{2,0,1:T(4,128)(2,1)S(1)}, bf16[4,8,128]{2,0,1:T(4,128)(2,1)S(1)}, u32[]{:S(2)}, u32[]{:S(2)}) collective-permute-start(bf16[4,8,128]{2,0,1:T(4,128)(2,1)S(1)} %get-tuple-element.67), channel_id=1, source_target_pairs={{0,4},{1,5},{2,6},{3,7},{4,8},{5,9},{6,10},{7,11},{8,12},{9,13},{1... | collective-permute-start | bytes 24584 | tf_op jit(solution)/shard_map/ppermute | solution.py:72
  65.1 6.7 %collective-permute-start.12 = (bf16[4,8,128]{2,0,1:T(4,128)(2,1)S(1)}, bf16[4,8,128]{2,0,1:T(4,128)(2,1)S(1)}, u32[]{:S(2)}, u32[]{:S(2)}) collective-permute-start(bf16[4,8,128]{2,0,1:T(4,128)(2,1)S(1)} %get-tuple-element.67), channel_id=1, source_target_pairs={{0,3},{1,4},{2,5},{3,6},{4,7},{5,8},{6,9},{7,10},{8,11},{9,12},{10... | collective-permute-start | bytes 24584 | tf_op jit(solution)/shard_map/ppermute | solution.py:72
  68.4 6.4 %collective-permute-start.13 = (bf16[4,8,128]{2,0,1:T(4,128)(2,1)S(1)}, bf16[4,8,128]{2,0,1:T(4,128)(2,1)S(1)}, u32[]{:S(2)}, u32[]{:S(2)}) collective-permute-start(bf16[4,8,128]{2,0,1:T(4,128)(2,1)S(1)} %get-tuple-element.67), channel_id=1, source_target_pairs={{0,2},{1,3},{2,4},{3,5},{4,6},{5,7},{6,8},{7,9},{8,10},{9,11},{10,... | collective-permute-start | bytes 24584 | tf_op jit(solution)/shard_map/ppermute | solution.py:72
  69.9 7.3 %collective-permute-start.14 = (bf16[4,8,128]{2,0,1:T(4,128)(2,1)S(1)}, bf16[4,8,128]{2,0,1:T(4,128)(2,1)S(1)}, u32[]{:S(2)}, u32[]{:S(2)}) collective-permute-start(bf16[4,8,128]{2,0,1:T(4,128)(2,1)S(1)} %get-tuple-element.67), channel_id=1, source_target_pairs={{0,1},{1,2},{2,3},{3,4},{4,5},{5,6},{6,7},{7,8},{8,9},{9,10},{10,1... | collective-permute-start | bytes 24584 | tf_op jit(solution)/shard_map/ppermute | solution.py:72
  77.7 4.7 %copy-start.10 = (bf16[128,128]{1,0:T(8,128)(2,1)S(1)}, bf16[128,128]{1,0:T(8,128)(2,1)}, u32[]{:S(2)}) copy-start(bf16[128,128]{1,0:T(8,128)(2,1)} %param.27) | copy-start | bytes 98308
  77.7 4.7 %copy-start.11 = (bf16[128,128]{1,0:T(8,128)(2,1)S(1)}, bf16[128,128]{1,0:T(8,128)(2,1)}, u32[]{:S(2)}) copy-start(bf16[128,128]{1,0:T(8,128)(2,1)} %param.26) | copy-start | bytes 98308

commit v3 on v0

v3 whole, which is shorter than its diff:
```python
import functools

import jax
import jax.numpy as jnp
from jax import lax
from jax.experimental import pallas as pl
from jax.experimental.pallas import tpu as pltpu
from jax.sharding import PartitionSpec as P

HEADS = 4
HEAD_DIM = 32
LANES = 128
LOG2_E = 1.4426950408889634
F32 = jnp.float32
BF16 = jnp.bfloat16
NN = (((1,), (0,)), ((), ()))
NT = (((1,), (1,)), ((), ()))
TN = (((0,), (0,)), ((), ()))


def dot(left, right, dims=NN):
    return lax.dot_general(left, right, dims, preferred_element_type=F32)


def sigmoid(values):
    return 0.5 * jnp.tanh(0.5 * values) + 0.5


def flipped(weight):
    return weight.astype(F32).T.astype(BF16)


def lane_tiles(values):
    lanes = values.shape[1]
    return [(t, slice(t * LANES, (t + 1) * LANES)) for t in range(lanes // LANES)]


def lane_norm(values):
    centered = values - jnp.mean(values, axis=-1, keepdims=True)
    variance = jnp.mean(centered * centered, axis=-1, keepdims=True)
    return (centered * lax.rsqrt(variance + 1e-05)).astype(BF16)


def edges_kernel(pair, w_left, w_left_gate, w_right, w_right_gate, out, held):
    rows = pair.shape[0]
    channels = w_left.shape[1]
    weights = jnp.concatenate(
        [flipped(w[...]) for w in (w_left, w_left_gate, w_right, w_right_gate)], axis=0
    )
    for i in range(rows):
        normed = lane_norm(pair[i].astype(F32))
        both = dot(weights, normed, NT)
        for side in range(2):
            base = 2 * side * channels
            act = sigmoid(both[base + channels : base + 2 * channels]) * both[base : base + channels]
            for tile, lanes in lane_tiles(act):
                held[tile, pl.ds(side * rows + i, channels, stride=2 * rows), :] = act[:, lanes]
    block = out.shape[1]
    for owner in range(out.shape[0]):
        for tile, lanes in lane_tiles(pair):
            out[owner, :, lanes] = held[tile, owner * block : (owner + 1) * block, :].astype(BF16)


def gate_kernel(pair, w_tri_gate, out):
    for i in range(pair.shape[0]):
        out[i] = sigmoid(dot(lane_norm(pair[i].astype(F32)), w_tri_gate[...]))


def triangle_sides(edges, rows, channel):
    sides = [[], []]
    for source in range(edges.shape[0]):
        block = edges[source, channel * 2 * rows : (channel + 1) * 2 * rows, :].astype(F32)
        sides[0].append(block[:rows])
        sides[1].append(block[rows:])
    return [jnp.concatenate(side, axis=0).astype(BF16) for side in sides]


def triangle_kernel(rows, edges, out):
    for pair_of in range(0, out.shape[1] // rows, 2):
        products = [dot(*triangle_sides(edges, rows, pair_of + o), NT) for o in range(2)]
        for owner in range(out.shape[0]):
            mine = slice(owner * rows, (owner + 1) * rows)
            out[owner, pair_of * rows : (pair_of + 2) * rows, :] = jnp.concatenate(
                [p[mine] for p in products], axis=0
            ).astype(BF16)


def partial_kernel(rows, edges, out):
    for channel in range(out.shape[0]):
        out[channel] = dot(*triangle_sides(edges, rows, channel), NT)


def update_kernel(returned, gate, pair, w_tri_out, w_bias_t, first_pass, att_norm, bias, held, bias_held):
    rows, cols = pair.shape[0], pair.shape[1]
    owners, block = returned.shape[0], returned.shape[1]
    channels = owners * block // rows
    total = jnp.zeros((rows, cols), F32)
    for owner in range(owners):
        total += jnp.sum(returned[owner].astype(F32).reshape(block // rows, rows, cols), axis=0)
    average = total / channels
    square = jnp.zeros((rows, cols), F32)
    for owner in range(owners):
        centered = returned[owner].astype(F32).reshape(block // rows, rows, cols) - average
        square += jnp.sum(centered * centered, axis=0)
        for tile, lanes in lane_tiles(pair):
            held[tile, owner * block : (owner + 1) * block, :] = centered.reshape(block, cols)[:, lanes]
    scale = lax.rsqrt(square / channels + 1e-05)
    for i in range(rows):
        tri_norm = jnp.concatenate(
            [held[tile, pl.ds(i, channels, stride=rows), :] for tile, _ in lane_tiles(pair)], axis=1
        )
        tri_norm = tri_norm * scale[i : i + 1]
        update = dot(tri_norm.T.astype(BF16), w_tri_out[...])
        passed = pair[i].astype(F32) + gate[i] * update
        first_pass[i] = passed
        normed = lane_norm(passed)
        att_norm[i] = normed
        row_bias = dot(w_bias_t[...], normed, NT)
        for head in range(HEADS):
            bias_held[head * rows + i : head * rows + i + 1, :] = row_bias[head : head + 1]
    rounded = bias_held[...].astype(BF16)
    for owner in range(bias.shape[0]):
        bias[owner] = rounded


def project_kernel(att_norm, w_query, w_key, w_value, w_att_gate, query, key, value_t, gate_t):
    w_direct = jnp.concatenate([w_query[...], w_key[...]], axis=1)
    w_flipped = jnp.concatenate([flipped(w_value[...]), flipped(w_att_gate[...])], axis=0)
    split = query.shape[2]
    for i in range(att_norm.shape[0]):
        normed = att_norm[i]
        direct = dot(normed, w_direct).astype(BF16)
        query[i] = direct[:, :split]
        key[i] = direct[:, split:]
        turned = dot(w_flipped, normed, NT)
        value_t[i] = turned[:split].astype(BF16)
        gate_t[i] = sigmoid(turned[split:])


def attend_kernel(query, key, value_t, gate_t, first_pass, bias, w_att_out, out, bias_t):
    rows, cols, width = query.shape
    head_rows = bias.shape[1] // HEADS
    for head in range(HEADS):
        parts = [
            bias[owner].astype(F32)[head * head_rows : (head + 1) * head_rows]
            for owner in range(bias.shape[0])
        ]
        bias_t[head] = jnp.concatenate(parts, axis=0).T * LOG2_E
    lane = lax.broadcasted_iota(jnp.int32, (1, width), 1)
    score_scale = LOG2_E / HEAD_DIM**0.5
    ones = jnp.ones((16, key.shape[1]), BF16)
    for i in range(rows):
        keys = key[i]
        queries = query[i]
        gated = []
        for head in range(HEADS):
            inside = (lane >= head * HEAD_DIM) & (lane < (head + 1) * HEAD_DIM)
            chosen = jnp.where(inside, queries, jnp.zeros_like(queries))
            scores = dot(keys, chosen, NT) * score_scale + bias_t[head]
            peak = jnp.max(scores, axis=0, keepdims=True)
            weights = jnp.exp2(scores - peak).astype(BF16)
            mine = slice(head * HEAD_DIM, (head + 1) * HEAD_DIM)
            summed = dot(jnp.concatenate([value_t[i, mine, :], ones], axis=0), weights)
            total = summed[HEAD_DIM : HEAD_DIM + 1]
            gated.append(summed[:HEAD_DIM] * (1.0 / total) * gate_t[i, mine, :])
        gated_t = jnp.concatenate(gated, axis=0)
        result = first_pass[i] + dot(gated_t.T.astype(BF16), w_att_out[...])
        out[i] = result.astype(BF16)


def call(kernel, outs, scratch, flops, *operands):
    vmem = pl.BlockSpec(memory_space=pltpu.VMEM)
    shapes = [jax.ShapeDtypeStruct(shape, dtype) for shape, dtype in outs]
    moved = sum(o.size * o.dtype.itemsize for o in operands)
    got = pl.pallas_call(
        kernel,
        out_shape=shapes,
        in_specs=[vmem] * len(operands),
        out_specs=[vmem] * len(shapes),
        scratch_shapes=[pltpu.VMEM(shape, dtype) for shape, dtype in scratch],
        compiler_params=pltpu.CompilerParams(vmem_limit_bytes=48 * 2**20),
        cost_estimate=pl.CostEstimate(flops=flops, bytes_accessed=moved, transcendentals=0),
    )(*operands)
    return got if len(got) > 1 else got[0]


def body(
    pair_rep,
    w_left,
    w_left_gate,
    w_right,
    w_right_gate,
    w_tri_gate,
    w_tri_out,
    w_query,
    w_key,
    w_value,
    w_bias,
    w_att_gate,
    w_att_out,
):
    rows, cols, width = pair_rep.shape
    channels = w_left.shape[1]
    owners, col_parts = lax.axis_size("row"), lax.axis_size("col")
    own = channels // owners
    residues = owners * rows
    cells = rows * cols

    edges = call(
        edges_kernel,
        [((owners, own * 2 * rows, cols), BF16)],
        [((cols // LANES, channels * 2 * rows, LANES), F32)],
        8 * cells * width * channels,
        pair_rep,
        w_left,
        w_left_gate,
        w_right,
        w_right_gate,
    )
    spread = lax.all_to_all(edges, "row", split_axis=0, concat_axis=0, tiled=True)
    gate = call(
        gate_kernel, [((rows, cols, width), F32)], [], 2 * cells * width * width, pair_rep, w_tri_gate
    )
    flops = 2 * own * residues * residues * cols
    if col_parts == 1:
        summed = call(
            functools.partial(triangle_kernel, rows),
            [((owners, own * rows, residues), BF16)],
            [],
            flops,
            spread,
        )
    else:
        partial_sums = call(
            functools.partial(partial_kernel, rows),
            [((own, residues, residues), F32)],
            [],
            flops,
            spread,
        )
        summed = lax.psum_scatter(partial_sums, "col", scatter_dimension=2, tiled=True).astype(BF16)
        summed = summed.reshape(own, owners, rows, cols).swapaxes(0, 1)
        summed = summed.reshape(owners, own * rows, cols)
    returned = lax.all_to_all(summed, "row", split_axis=0, concat_axis=0, tiled=True)
    first_pass, att_norm, bias_copies = call(
        update_kernel,
        [
            ((rows, cols, width), F32),
            ((rows, cols, width), BF16),
            ((owners, HEADS * rows, cols), BF16),
        ],
        [((cols // LANES, channels * rows, LANES), F32), ((HEADS * rows, cols), F32)],
        2 * cells * channels * width,
        returned,
        gate,
        pair_rep,
        w_tri_out,
        w_bias.T,
    )
    bias = lax.all_to_all(bias_copies, "row", split_axis=0, concat_axis=0, tiled=True)
    query, key, value_t, gate_t = call(
        project_kernel,
        [
            ((rows, cols, width), BF16),
            ((rows, cols, width), BF16),
            ((rows, width, cols), BF16),
            ((rows, width, cols), F32),
        ],
        [],
        8 * cells * width * width,
        att_norm,
        w_query,
        w_key,
        w_value,
        w_att_gate,
    )
    if col_parts > 1:
        bias = lax.all_to_all(bias, "col", split_axis=0, concat_axis=2, tiled=True)
        key = lax.all_gather(key, "col", axis=1, tiled=True)
        value_t = lax.all_gather(value_t, "col", axis=2, tiled=True)
    return call(
        attend_kernel,
        [((rows, cols, width), BF16)],
        [((HEADS, key.shape[1], cols), F32)],
        4 * cells * key.shape[1] * width,
        query,
        key,
        value_t,
        gate_t,
        first_pass,
        bias,
        w_att_out,
    )


def solution(mesh):
    in_specs = (P(("grp", "row"), "col", None),) + (P(),) * 12
    out_specs = P(("grp", "row"), "col", None)
    return jax.shard_map(body, mesh=mesh, in_specs=in_specs, out_specs=out_specs, check_vma=False)
```

time: 91.8 us -> 64.7 us (0.70)
  blocking collectives: 61.5 us -> 23.3 us
  Pallas kernels: 0 us -> 13.1 us
  waiting for transfers between devices: 8.73 us -> 15.8 us
  matrix products: 7.03 us -> 0 us
  local copies, waits for them, and re-layouts: 7.84 us -> 4.02 us
  starting transfers between devices: 4.02 us -> 7.71 us
  other arithmetic: 1.17 us -> 0 us
    all_gather x1 -> x0, blocking collectives: 38.3 us -> none  [body(): every_row = lax.all_gather(bias_local, 'row', axis=1, tiled=True)]
    pallas_call x0 -> x6, Pallas kernels: none -> 13.1 us  [call(): pl.pallas_call(kernel, out_shape=shapes, in_specs=[vmem] * len(operands),...]
    all_to_all x1 -> x2, waiting for transfers between devices: 8.73 us -> 15.8 us  [the longest x1 8.57 us: body(): lax.all_to_all(summed, 'row', split_axis=0, concat_axis=0, tiled=True)]
    dot_general x28 -> x0, matrix products: 7.03 us -> none  [the longest x8 1.9 us: attend_row(): jnp.einsum('jhd,khd->hjk', query_row, key_row, preferred_element_type=jnp...]
    all_to_all x1 -> x2, starting transfers between devices: 4.02 us -> 7.71 us  [the longest x1 4.02 us: body(): lax.all_to_all(summed, 'row', split_axis=0, concat_axis=0, tiled=True)]
    convert_element_type x2 -> x0, local copies, waits for them, and re-layouts: 1.73 us -> none  [the longest x1 0.88 us: body(): lax.psum_scatter(partial_sums, 'col', scatter_dimension=2, tiled=True)]
    unnamed x25 -> x28, local copies, waits for them, and re-layouts: 5.31 us -> 4.02 us
  transfers between devices with their start and end apart: 1 -> 2, of which waited for: 1 -> 2; matrix products, arithmetic and copies ran while one was open for 0% -> 0% of each run, Pallas kernels for 0% -> 1%
where the time goes in v3:
time: 64.7 us; the launch traced here: 64.1 us
  blocking collectives  23.3 us (36%)
  waiting for transfers between devices  15.8 us (24%)
  Pallas kernels  13.1 us (20%)
  starting transfers between devices  7.71 us (12%)
  local copies, waits for them, and re-layouts  4.02 us (6%)
    all_to_all x1, blocking collectives, body(): lax.all_to_all(edges, 'row', split_axis=0, concat_axis=0, tiled=True)  23.3 us
    pallas_call x6, Pallas kernels, call(): pl.pallas_call(kernel, out_shape=shapes, in_specs=[vmem] * len(operands),...  13.1 us
    all_to_all x1, waiting for transfers between devices, body(): lax.all_to_all(summed, 'row', split_axis=0, concat_axis=0, tiled=True)  8.57 us
    all_to_all x1, waiting for transfers between devices, body(): lax.all_to_all(bias_copies, 'row', split_axis=0, concat_axis=0, tiled=True)  7.26 us
    all_to_all x1, starting transfers between devices, body(): lax.all_to_all(summed, 'row', split_axis=0, concat_axis=0, tiled=True)  4.02 us
    unnamed x28, local copies, waits for them, and re-layouts  4.02 us
    all_to_all x1, starting transfers between devices, body(): lax.all_to_all(bias_copies, 'row', split_axis=0, concat_axis=0, tiled=True)  3.68 us
  transfers between devices with their start and end apart: 2, of which 2 were waited for; matrix products, arithmetic and copies ran while one was open for 0% of the time, Pallas kernels for 1%

profile of v3, /device:TPU:0, one launch (start us, length us, event | category | flops | bytes accessed | tf_op | source)
XLA Modules:
  0.0 64.1 jit_solution(14333021837525730296)
XLA Ops:
  0.0 0.0 copy-start
  0.0 0.9 %copy-done = bf16[8,128,128]{2,1,0:T(8,128)(2,1)S(1)} copy-done((bf16[8,128,128]{2,1,0:T(8,128)(2,1)S(1)}, bf16[8,128,128]{2,1,0:T(8,128)(2,1)}, u32[]{:S(2)}) %copy-start) | copy-done | bytes 262168
  1.0 0.8 %copy-done.3 = bf16[128,128]{1,0:T(8,128)(2,1)S(1)} copy-done((bf16[128,128]{1,0:T(8,128)(2,1)S(1)}, bf16[128,128]{1,0:T(8,128)(2,1)}, u32[]{:S(2)}) %copy-start.3) | copy-done | bytes 32792
  1.7 0.0 copy-start.4
  1.7 0.8 %copy-done.4 = bf16[128,128]{1,0:T(8,128)(2,1)S(1)} copy-done((bf16[128,128]{1,0:T(8,128)(2,1)S(1)}, bf16[128,128]{1,0:T(8,128)(2,1)}, u32[]{:S(2)}) %copy-start.4) | copy-done | bytes 32792
  2.5 0.0 copy-start.5
  2.5 0.8 %copy-done.5 = bf16[128,128]{1,0:T(8,128)(2,1)S(1)} copy-done((bf16[128,128]{1,0:T(8,128)(2,1)S(1)}, bf16[128,128]{1,0:T(8,128)(2,1)}, u32[]{:S(2)}) %copy-start.5) | copy-done | bytes 32792
  3.2 0.0 copy-start.6
  3.2 0.8 %copy-done.6 = bf16[128,128]{1,0:T(8,128)(2,1)S(1)} copy-done((bf16[128,128]{1,0:T(8,128)(2,1)S(1)}, bf16[128,128]{1,0:T(8,128)(2,1)}, u32[]{:S(2)}) %copy-start.6) | copy-done | bytes 32792
  4.0 1.2 %shard_map.127 = bf16[16,128,128]{2,1,0:T(8,128)(2,1)S(1)} custom-call(bf16[8,128,128]{2,1,0:T(8,128)(2,1)S(1)} %copy-done, bf16[128,128]{1,0:T(8,128)(2,1)S(1)} %copy-done.3, bf16[128,128]{1,0:T(8,128)(2,1)S(1)} %copy-done.4, bf16[128,128]{1,0:T(8,128)(2,1)S(1)} %copy-done.5, bf16[128,128]{1,0:T(8,128)(2,1)S(1)} %copy-done.6), custom_call_target="tpu_custom_call" | custom-call | flops 134217728 | bytes 393216 | tf_op jit(solution)/shard_map/pallas_call | solution.py:175
  5.2 23.3 %all_to_all.15.edges = bf16[16,128,128]{2,1,0:T(8,128)(2,1)S(1)} all-to-all(bf16[16,128,128]{2,1,0:T(8,128)(2,1)S(1)} %shard_map.127), channel_id=1, replica_groups=mesh['grp'=2,'row'=16,'col'=1] {'row'}, dimensions={0} | all-to-all | bytes 1048576 | tf_op jit(solution)/shard_map/all_to_all | solution.py:220
  28.5 1.0 %shard_map.128 = bf16[16,64,128]{2,1,0:T(8,128)(2,1)} custom-call(bf16[16,128,128]{2,1,0:T(8,128)(2,1)S(1)} %all_to_all.15.edges), custom_call_target="tpu_custom_call" | custom-call | flops 33554432 | bytes 524288 | tf_op jit(solution)/shard_map/pallas_call | solution.py:175
  29.5 4.0 %all-to-all-start.1 = ((bf16[16,64,128]{2,1,0:T(8,128)(2,1)}), bf16[16,64,128]{2,1,0:T(8,128)(2,1)S(1)}, u32[]{:S(2)}, u32[]{:S(2)}) async-start(bf16[16,64,128]{2,1,0:T(8,128)(2,1)} %shard_map.128), calls=%async_computation.1 | async-start | bytes 524288 | tf_op jit(solution)/shard_map/all_to_all | solution.py:244
  33.5 0.0 copy-done.1
  33.5 0.0 copy-done.7
  33.5 0.0 copy-start.8
  33.6 0.5 shard_map.129.gate
  34.0 0.0 copy-start.9
  34.1 8.6 %all-to-all-done.1.returned = bf16[16,64,128]{2,1,0:T(8,128)(2,1)S(1)} async-done(((bf16[16,64,128]{2,1,0:T(8,128)(2,1)}), bf16[16,64,128]{2,1,0:T(8,128)(2,1)S(1)}, u32[]{:S(2)}, u32[]{:S(2)}) %all-to-all-start.1) | async-done | bytes 262176 | tf_op jit(solution)/shard_map/all_to_all | solution.py:244
  42.6 0.0 copy-done.8
  42.6 0.0 copy-done.9
  42.6 2.4 %shard_map.130 = (f32[8,128,128]{2,1,0:T(8,128)S(1)}, bf16[8,128,128]{2,1,0:T(8,128)(2,1)S(1)}, bf16[16,32,128]{2,1,0:T(8,128)(2,1)}) custom-call(bf16[16,64,128]{2,1,0:T(8,128)(2,1)S(1)} %all-to-all-done.1.returned, f32[8,128,128]{2,1,0:T(8,128)S(1)} %shard_map.129.gate, bf16[8,128,128]{2,1,0:T(8,128)(2,1)S(1)} %copy-done.1, ...), custom_call_target="tpu_custom_call" | custom-call | flops 33554432 | bytes 1082368 | tf_op jit(solution)/shard_map/pallas_call | solution.py:175
  45.1 3.7 %all-to-all-start.2 = ((bf16[16,32,128]{2,1,0:T(8,128)(2,1)}), bf16[16,32,128]{2,1,0:T(8,128)(2,1)S(1)}, u32[]{:S(2)}, u32[]{:S(2)}) async-start(bf16[16,32,128]{2,1,0:T(8,128)(2,1)} %get-tuple-element.18), calls=%async_computation.2 | async-start | bytes 262144 | tf_op jit(solution)/shard_map/all_to_all | solution.py:260
  48.8 0.0 copy-done.10
  48.8 0.0 copy-done.11
  48.8 0.0 copy-done.12
  48.8 0.0 copy-done.13
  48.8 0.0 copy-start.2
  48.8 0.5 shard_map.131
  49.3 7.3 %all-to-all-done.2.bias = bf16[16,32,128]{2,1,0:T(8,128)(2,1)S(1)} async-done(((bf16[16,32,128]{2,1,0:T(8,128)(2,1)}), bf16[16,32,128]{2,1,0:T(8,128)(2,1)S(1)}, u32[]{:S(2)}, u32[]{:S(2)}) %all-to-all-start.2) | async-done | bytes 131104 | tf_op jit(solution)/shard_map/all_to_all | solution.py:260
  56.6 0.0 copy-done.2
  56.6 7.5 %shard_map.132 = bf16[8,128,128]{2,1,0:T(8,128)(2,1)} custom-call(bf16[8,128,128]{2,1,0:T(8,128)(2,1)S(1)} %get-tuple-element.13.query, bf16[8,128,128]{2,1,0:T(8,128)(2,1)S(1)} %get-tuple-element.14.key, bf16[8,128,128]{2,1,0:T(8,128)(2,1)S(1)} %get-tuple-element.15.value_t, f32[8,128,128]{2,1,0:T(8,128)S(1)} %get-tuple-element.16.gate_t, ...), custom_call_target="tpu_custom_call" | custom-call | flops 67108864 | bytes 1998848 | tf_op jit(solution)/shard_map/pallas_call | solution.py:175
  (7 shorter events, 0.0 us)
Async XLA Ops:
  0.0 0.9 %copy-start = (bf16[8,128,128]{2,1,0:T(8,128)(2,1)S(1)}, bf16[8,128,128]{2,1,0:T(8,128)(2,1)}, u32[]{:S(2)}) copy-start(bf16[8,128,128]{2,1,0:T(8,128)(2,1)} %pair.5) | copy-start | bytes 786436
  1.0 0.8 %copy-start.3 = (bf16[128,128]{1,0:T(8,128)(2,1)S(1)}, bf16[128,128]{1,0:T(8,128)(2,1)}, u32[]{:S(2)}) copy-start(bf16[128,128]{1,0:T(8,128)(2,1)} %w_left.1) | copy-start | bytes 98308
  1.7 0.8 %copy-start.4 = (bf16[128,128]{1,0:T(8,128)(2,1)S(1)}, bf16[128,128]{1,0:T(8,128)(2,1)}, u32[]{:S(2)}) copy-start(bf16[128,128]{1,0:T(8,128)(2,1)} %w_left_gate.1) | copy-start | bytes 98308
  2.5 0.8 %copy-start.5 = (bf16[128,128]{1,0:T(8,128)(2,1)S(1)}, bf16[128,128]{1,0:T(8,128)(2,1)}, u32[]{:S(2)}) copy-start(bf16[128,128]{1,0:T(8,128)(2,1)} %w_right.1) | copy-start | bytes 98308
  3.2 0.8 %copy-start.6 = (bf16[128,128]{1,0:T(8,128)(2,1)S(1)}, bf16[128,128]{1,0:T(8,128)(2,1)}, u32[]{:S(2)}) copy-start(bf16[128,128]{1,0:T(8,128)(2,1)} %w_right_gate.1) | copy-start | bytes 98308
  29.5 4.0 %copy-start.1 = (bf16[8,128,128]{2,1,0:T(8,128)(2,1)S(1)}, bf16[8,128,128]{2,1,0:T(8,128)(2,1)}, u32[]{:S(2)}) copy-start(bf16[8,128,128]{2,1,0:T(8,128)(2,1)} %pair.5) | copy-start | bytes 786436
  29.5 4.0 %copy-start.7 = (bf16[128,128]{1,0:T(8,128)(2,1)S(1)}, bf16[128,128]{1,0:T(8,128)(2,1)}, u32[]{:S(2)}) copy-start(bf16[128,128]{1,0:T(8,128)(2,1)} %w_tri_gate.1) | copy-start | bytes 98308
  29.5 13.1 %all-to-all-start.1 = ((bf16[16,64,128]{2,1,0:T(8,128)(2,1)}), bf16[16,64,128]{2,1,0:T(8,128)(2,1)S(1)}, u32[]{:S(2)}, u32[]{:S(2)}) async-start(bf16[16,64,128]{2,1,0:T(8,128)(2,1)} %shard_map.128), calls=%async_computation.1 | async-start | bytes 524288 | tf_op jit(solution)/shard_map/all_to_all | solution.py:244
  33.5 9.1 %copy-start.8 = (bf16[128,128]{1,0:T(8,128)(2,1)S(1)}, bf16[128,128]{1,0:T(8,128)(2,1)}, u32[]{:S(2)}) copy-start(bf16[128,128]{1,0:T(8,128)(2,1)} %w_tri_out.1) | copy-start | bytes 98308
  34.0 8.6 %copy-start.9 = (bf16[128,4]{0,1:T(4,128)(2,1)S(1)}, bf16[128,4]{0,1:T(4,128)(2,1)}, u32[]{:S(2)}) copy-start(bf16[128,4]{0,1:T(4,128)(2,1)} %param.23) | copy-start | bytes 3076
  45.1 3.7 %copy-start.10 = (bf16[128,128]{1,0:T(8,128)(2,1)S(1)}, bf16[128,128]{1,0:T(8,128)(2,1)}, u32[]{:S(2)}) copy-start(bf16[128,128]{1,0:T(8,128)(2,1)} %w_query.1) | copy-start | bytes 98308
  45.1 3.7 %copy-start.11 = (bf16[128,128]{1,0:T(8,128)(2,1)S(1)}, bf16[128,128]{1,0:T(8,128)(2,1)}, u32[]{:S(2)}) copy-start(bf16[128,128]{1,0:T(8,128)(2,1)} %w_key.1) | copy-start | bytes 98308
  45.1 3.7 %copy-start.12 = (bf16[128,128]{1,0:T(8,128)(2,1)S(1)}, bf16[128,128]{1,0:T(8,128)(2,1)}, u32[]{:S(2)}) copy-start(bf16[128,128]{1,0:T(8,128)(2,1)} %w_value.1) | copy-start | bytes 98308
  45.1 3.7 %copy-start.13 = (bf16[128,128]{1,0:T(8,128)(2,1)S(1)}, bf16[128,128]{1,0:T(8,128)(2,1)}, u32[]{:S(2)}) copy-start(bf16[128,128]{1,0:T(8,128)(2,1)} %w_att_gate.1) | copy-start | bytes 98308
  45.1 11.5 %all-to-all-start.2 = ((bf16[16,32,128]{2,1,0:T(8,128)(2,1)}), bf16[16,32,128]{2,1,0:T(8,128)(2,1)S(1)}, u32[]{:S(2)}, u32[]{:S(2)}) async-start(bf16[16,32,128]{2,1,0:T(8,128)(2,1)} %get-tuple-element.18), calls=%async_computation.2 | async-start | bytes 262144 | tf_op jit(solution)/shard_map/all_to_all | solution.py:260
  48.8 7.8 %copy-start.2 = (bf16[128,128]{1,0:T(8,128)(2,1)S(1)}, bf16[128,128]{1,0:T(8,128)(2,1)}, u32[]{:S(2)}) copy-start(bf16[128,128]{1,0:T(8,128)(2,1)} %w_att_out.1) | copy-start | bytes 98308

commit v4 on v3

--- a/solution.py
+++ b/solution.py
@@ -184,6 +184,33 @@
     return got if len(got) > 1 else got[0]
 
 
+def stages(owners):
+    near = 1 << (owners.bit_length() // 2)
+    far = owners // near
+    lines = [[f * near + c for f in range(far)] for c in range(near)]
+    planes = [[f * near + c for c in range(near)] for f in range(far)]
+    return far, near, lines, planes
+
+
+def swap(blocks, groups, axis):
+    return lax.all_to_all(
+        blocks, "row", split_axis=axis, concat_axis=axis, axis_index_groups=groups, tiled=True
+    )
+
+
+def exchange(blocks):
+    far, near, lines, planes = stages(blocks.shape[0])
+    split = blocks.reshape(far, near, *blocks.shape[1:])
+    return swap(swap(split, lines, 0), planes, 1).reshape(blocks.shape)
+
+
+def gather(copies, owners):
+    far, near, lines, planes = stages(owners)
+    plane = swap(copies, planes, 0)
+    plane = jnp.broadcast_to(plane[None], (far, *plane.shape))
+    return swap(plane, lines, 0).reshape(owners, *copies.shape[1:])
+
+
 def body(
     pair_rep,
     w_left,
@@ -217,7 +244,7 @@
         w_right,
         w_right_gate,
     )
-    spread = lax.all_to_all(edges, "row", split_axis=0, concat_axis=0, tiled=True)
+    spread = exchange(edges)
     gate = call(
         gate_kernel, [((rows, cols, width), F32)], [], 2 * cells * width * width, pair_rep, w_tri_gate
     )
@@ -241,13 +268,13 @@
         summed = lax.psum_scatter(partial_sums, "col", scatter_dimension=2, tiled=True).astype(BF16)
         summed = summed.reshape(own, owners, rows, cols).swapaxes(0, 1)
         summed = summed.reshape(owners, own * rows, cols)
-    returned = lax.all_to_all(summed, "row", split_axis=0, concat_axis=0, tiled=True)
+    returned = exchange(summed)
     first_pass, att_norm, bias_copies = call(
         update_kernel,
         [
             ((rows, cols, width), F32),
             ((rows, cols, width), BF16),
-            ((owners, HEADS * rows, cols), BF16),
+            ((stages(owners)[1], HEADS * rows, cols), BF16),
         ],
         [((cols // LANES, channels * rows, LANES), F32), ((HEADS * rows, cols), F32)],
         2 * cells * channels * width,
@@ -257,7 +284,7 @@
         w_tri_out,
         w_bias.T,
     )
-    bias = lax.all_to_all(bias_copies, "row", split_axis=0, concat_axis=0, tiled=True)
+    bias = gather(bias_copies, owners)
     query, key, value_t, gate_t = call(
         project_kernel,
         [

time: 64.7 us -> 85 us (1.31)
  blocking collectives: 23.3 us -> 48.9 us
  waiting for transfers between devices: 15.8 us -> 10.2 us
  local copies, waits for them, and re-layouts: 4.02 us -> 6.16 us
  Pallas kernels: 13.1 us -> 11.7 us
    all_to_all x1 -> x4, blocking collectives: 23.3 us -> 48.9 us  [swap(): lax.all_to_all(blocks, 'row', split_axis=axis, concat_axis=axis, axis_ind...]
    all_to_all x2, waiting for transfers between devices: 15.8 us -> 10.2 us  [swap(): lax.all_to_all(blocks, 'row', split_axis=axis, concat_axis=axis, axis_ind...]
    pallas_call x6, Pallas kernels: 13.1 us -> 11.7 us  [call(): pl.pallas_call(kernel, out_shape=shapes, in_specs=[vmem] * len(operands),...]
where the time goes in v4:
time: 85 us; the launch traced here: 84.2 us
  blocking collectives  48.9 us (58%)
  Pallas kernels  11.7 us (14%)
  waiting for transfers between devices  10.2 us (12%)
  starting transfers between devices  7.01 us (8%)
  local copies, waits for them, and re-layouts  6.16 us (7%)
    all_to_all x4, blocking collectives, swap(): lax.all_to_all(blocks, 'row', split_axis=axis, concat_axis=axis, axis_ind...  48.9 us
    pallas_call x6, Pallas kernels, call(): pl.pallas_call(kernel, out_shape=shapes, in_specs=[vmem] * len(operands),...  11.7 us
    all_to_all x2, waiting for transfers between devices, swap(): lax.all_to_all(blocks, 'row', split_axis=axis, concat_axis=axis, axis_ind...  10.2 us
    all_to_all x2, starting transfers between devices, swap(): lax.all_to_all(blocks, 'row', split_axis=axis, concat_axis=axis, axis_ind...  7.01 us
    unnamed x28, local copies, waits for them, and re-layouts  4.68 us
  transfers between devices with their start and end apart: 2, of which 2 were waited for; matrix products, arithmetic and copies ran while one was open for 0% of the time, Pallas kernels for 1%

profile of v4, /device:TPU:0, one launch (start us, length us, event | category | flops | bytes accessed | tf_op | source)
XLA Modules:
  0.0 84.2 jit_solution(10292914610990715146)
XLA Ops:
  0.0 0.9 %copy-done = bf16[8,128,128]{2,1,0:T(8,128)(2,1)S(1)} copy-done((bf16[8,128,128]{2,1,0:T(8,128)(2,1)S(1)}, bf16[8,128,128]{2,1,0:T(8,128)(2,1)}, u32[]{:S(2)}) %copy-start) | copy-done | bytes 262168
  1.0 0.8 copy-done.3
  1.7 0.8 copy-done.4
  2.5 0.8 copy-done.5
  3.2 0.8 copy-done.6
  4.0 1.2 %shard_map.127 = bf16[16,128,128]{2,1,0:T(8,128)(2,1)S(1)} custom-call(bf16[8,128,128]{2,1,0:T(8,128)(2,1)S(1)} %copy-done, bf16[128,128]{1,0:T(8,128)(2,1)S(1)} %copy-done.3, bf16[128,128]{1,0:T(8,128)(2,1)S(1)} %copy-done.4, bf16[128,128]{1,0:T(8,128)(2,1)S(1)} %copy-done.5, bf16[128,128]{1,0:T(8,128)(2,1)S(1)} %copy-done.6), custom_call_target="tpu_custom_call" | custom-call | flops 134217728 | bytes 393216 | tf_op jit(solution)/shard_map/pallas_call | solution.py:175
  5.2 20.6 %all_to_all.30 = bf16[4,4,128,128]{3,2,1,0:T(8,128)(2,1)S(1)} all-to-all(bf16[4,4,128,128]{3,2,1,0:T(8,128)(2,1)S(1)} %bitcast.6), channel_id=1, replica_groups={{0,4,8,12},{1,5,9,13},{2,6,10,14},{3,7,11,15},{16,20,24,28},{17,21,25,2..., dimensions={0} | all-to-all | bytes 1048576 | tf_op jit(solution)/shard_map/all_to_all | solution.py:196
  25.9 10.9 %all_to_all.31 = bf16[4,4,128,128]{3,2,0,1:T(8,128)(2,1)S(1)} all-to-all(bf16[4,4,128,128]{3,2,0,1:T(8,128)(2,1)S(1)} %copy.18), channel_id=1, replica_groups={{0,1,2,3},{4,5,6,7},{8,9,10,11},{12,13,14,15},{16,17,18,19},{20,21,22,2..., dimensions={1} | all-to-all | bytes 1048576 | tf_op jit(solution)/shard_map/all_to_all | solution.py:196
  36.8 0.3 shard_map.128
  37.1 10.3 %all_to_all.32 = bf16[4,4,64,128]{3,2,1,0:T(8,128)(2,1)S(1)} all-to-all(bf16[4,4,64,128]{3,2,1,0:T(8,128)(2,1)S(1)} %bitcast.9), channel_id=1, replica_groups={{0,4,8,12},{1,5,9,13},{2,6,10,14},{3,7,11,15},{16,20,24,28},{17,21,25,2..., dimensions={0} | all-to-all | bytes 524288 | tf_op jit(solution)/shard_map/all_to_all | solution.py:196
  47.5 0.7 copy.20
  48.2 3.5 %all-to-all-start.3 = ((bf16[4,4,64,128]{3,2,0,1:T(8,128)(2,1)}), bf16[4,4,64,128]{3,2,0,1:T(8,128)(2,1)S(1)}, u32[]{:S(2)}, u32[]{:S(2)}) async-start(bf16[4,4,64,128]{3,2,0,1:T(8,128)(2,1)} %copy.20), calls=%async_computation.3 | async-start | bytes 524288 | tf_op jit(solution)/shard_map/all_to_all | solution.py:196
  51.7 0.0 copy-done.1
  51.7 0.0 copy-done.7
  51.8 0.5 shard_map.129.gate
  52.2 0.0 copy-start.8
  52.3 4.8 %all-to-all-done.3 = bf16[4,4,64,128]{3,2,0,1:T(8,128)(2,1)S(1)} async-done(((bf16[4,4,64,128]{3,2,0,1:T(8,128)(2,1)}), bf16[4,4,64,128]{3,2,0,1:T(8,128)(2,1)S(1)}, u32[]{:S(2)}, u32[]{:S(2)}) %all-to-all-start.3) | async-done | bytes 262176 | tf_op jit(solution)/shard_map/all_to_all | solution.py:196
  57.1 0.0 copy-start.9
  57.1 0.0 copy-done.8
  57.1 0.7 copy-done.9
  57.8 1.8 %shard_map.130 = (f32[8,128,128]{2,1,0:T(8,128)S(1)}, bf16[8,128,128]{2,1,0:T(8,128)(2,1)S(1)}, bf16[4,32,128]{2,1,0:T(8,128)(2,1)S(1)}) custom-call(bf16[16,64,128]{2,1,0:T(8,128)(2,1)S(1)} %bitcast.8, f32[8,128,128]{2,1,0:T(8,128)S(1)} %shard_map.129.gate, bf16[8,128,128]{2,1,0:T(8,128)(2,1)S(1)} %copy-done.1, bf16[128,128]{1,0:T(8,128)(2,1)S(1)} %copy-done.8, ...), custom_call_target="tpu_custom_call" | custom-call | flops 33554432 | bytes 1082368 | tf_op jit(solution)/shard_map/pallas_call | solution.py:175
  59.5 7.1 %all_to_all.33 = bf16[4,32,128]{2,1,0:T(8,128)(2,1)S(1)} all-to-all(bf16[4,32,128]{2,1,0:T(8,128)(2,1)S(1)} %get-tuple-element.18), channel_id=1, replica_groups={{0,1,2,3},{4,5,6,7},{8,9,10,11},{12,13,14,15},{16,17,18,19},{20,21,22,2..., dimensions={0} | all-to-all | bytes 65536 | tf_op jit(solution)/shard_map/all_to_all | solution.py:196
  66.6 0.7 broadcast_in_dim.2
  67.3 3.5 %all-to-all-start.5 = ((bf16[4,4,32,128]{3,2,1,0:T(8,128)(2,1)}), bf16[4,4,32,128]{3,2,1,0:T(8,128)(2,1)S(1)}, u32[]{:S(2)}, u32[]{:S(2)}) async-start(bf16[4,4,32,128]{3,2,1,0:T(8,128)(2,1)} %broadcast_in_dim.2), calls=%async_computation.5 | async-start | bytes 262144 | tf_op jit(solution)/shard_map/all_to_all | solution.py:196
  70.8 0.0 copy-done.10
  70.8 0.0 copy-done.11
  70.8 0.0 copy-done.12
  70.8 0.0 copy-done.13
  70.8 0.0 copy-start.2
  70.9 0.5 shard_map.131
  71.3 5.4 %all-to-all-done.5 = bf16[4,4,32,128]{3,2,1,0:T(8,128)(2,1)S(1)} async-done(((bf16[4,4,32,128]{3,2,1,0:T(8,128)(2,1)}), bf16[4,4,32,128]{3,2,1,0:T(8,128)(2,1)S(1)}, u32[]{:S(2)}, u32[]{:S(2)}) %all-to-all-start.5) | async-done | bytes 131104 | tf_op jit(solution)/shard_map/all_to_all | solution.py:196
  76.7 7.5 %shard_map.132 = bf16[8,128,128]{2,1,0:T(8,128)(2,1)} custom-call(bf16[8,128,128]{2,1,0:T(8,128)(2,1)S(1)} %get-tuple-element.13.query, bf16[8,128,128]{2,1,0:T(8,128)(2,1)S(1)} %get-tuple-element.14.key, bf16[8,128,128]{2,1,0:T(8,128)(2,1)S(1)} %get-tuple-element.15.value_t, f32[8,128,128]{2,1,0:T(8,128)S(1)} %get-tuple-element.16.gate_t, ...), custom_call_target="tpu_custom_call" | custom-call | flops 67108864 | bytes 1998848 | tf_op jit(solution)/shard_map/pallas_call | solution.py:175
  (15 shorter events, 0.1 us)
Async XLA Ops:
  0.0 0.9 %copy-start = (bf16[8,128,128]{2,1,0:T(8,128)(2,1)S(1)}, bf16[8,128,128]{2,1,0:T(8,128)(2,1)}, u32[]{:S(2)}) copy-start(bf16[8,128,128]{2,1,0:T(8,128)(2,1)} %pair.5) | copy-start | bytes 786436
  1.0 0.8 copy-start.3
  1.7 0.8 copy-start.4
  2.5 0.8 copy-start.5
  3.2 0.8 copy-start.6
  48.2 3.6 %copy-start.1 = (bf16[8,128,128]{2,1,0:T(8,128)(2,1)S(1)}, bf16[8,128,128]{2,1,0:T(8,128)(2,1)}, u32[]{:S(2)}) copy-start(bf16[8,128,128]{2,1,0:T(8,128)(2,1)} %pair.5) | copy-start | bytes 786436
  48.2 3.6 %copy-start.7 = (bf16[128,128]{1,0:T(8,128)(2,1)S(1)}, bf16[128,128]{1,0:T(8,128)(2,1)}, u32[]{:S(2)}) copy-start(bf16[128,128]{1,0:T(8,128)(2,1)} %w_tri_gate.1) | copy-start | bytes 98308
  48.2 8.9 %all-to-all-start.3 = ((bf16[4,4,64,128]{3,2,0,1:T(8,128)(2,1)}), bf16[4,4,64,128]{3,2,0,1:T(8,128)(2,1)S(1)}, u32[]{:S(2)}, u32[]{:S(2)}) async-start(bf16[4,4,64,128]{3,2,0,1:T(8,128)(2,1)} %copy.20), calls=%async_computation.3 | async-start | bytes 524288 | tf_op jit(solution)/shard_map/all_to_all | solution.py:196
  52.2 4.9 %copy-start.8 = (bf16[128,128]{1,0:T(8,128)(2,1)S(1)}, bf16[128,128]{1,0:T(8,128)(2,1)}, u32[]{:S(2)}) copy-start(bf16[128,128]{1,0:T(8,128)(2,1)} %w_tri_out.1) | copy-start | bytes 98308
  57.1 0.7 copy-start.9
  67.3 3.5 %copy-start.10 = (bf16[128,128]{1,0:T(8,128)(2,1)S(1)}, bf16[128,128]{1,0:T(8,128)(2,1)}, u32[]{:S(2)}) copy-start(bf16[128,128]{1,0:T(8,128)(2,1)} %w_query.1) | copy-start | bytes 98308
  67.3 3.5 %copy-start.11 = (bf16[128,128]{1,0:T(8,128)(2,1)S(1)}, bf16[128,128]{1,0:T(8,128)(2,1)}, u32[]{:S(2)}) copy-start(bf16[128,128]{1,0:T(8,128)(2,1)} %w_key.1) | copy-start | bytes 98308
  67.3 3.5 %copy-start.12 = (bf16[128,128]{1,0:T(8,128)(2,1)S(1)}, bf16[128,128]{1,0:T(8,128)(2,1)}, u32[]{:S(2)}) copy-start(bf16[128,128]{1,0:T(8,128)(2,1)} %w_value.1) | copy-start | bytes 98308
  67.3 3.5 %copy-start.13 = (bf16[128,128]{1,0:T(8,128)(2,1)S(1)}, bf16[128,128]{1,0:T(8,128)(2,1)}, u32[]{:S(2)}) copy-start(bf16[128,128]{1,0:T(8,128)(2,1)} %w_att_gate.1) | copy-start | bytes 98308
  67.3 9.4 %all-to-all-start.5 = ((bf16[4,4,32,128]{3,2,1,0:T(8,128)(2,1)}), bf16[4,4,32,128]{3,2,1,0:T(8,128)(2,1)S(1)}, u32[]{:S(2)}, u32[]{:S(2)}) async-start(bf16[4,4,32,128]{3,2,1,0:T(8,128)(2,1)} %broadcast_in_dim.2), calls=%async_computation.5 | async-start | bytes 262144 | tf_op jit(solution)/shard_map/all_to_all | solution.py:196
  70.8 5.8 %copy-start.2 = (bf16[128,128]{1,0:T(8,128)(2,1)S(1)}, bf16[128,128]{1,0:T(8,128)(2,1)}, u32[]{:S(2)}) copy-start(bf16[128,128]{1,0:T(8,128)(2,1)} %w_att_out.1) | copy-start | bytes 98308

commit v5 on v3

v5 whole, which is shorter than its diff:
```python
import functools

import jax
import jax.numpy as jnp
from jax import lax
from jax.experimental import pallas as pl
from jax.experimental.pallas import tpu as pltpu
from jax.sharding import PartitionSpec as P

HEADS = 4
HEAD_DIM = 32
LANES = 128
LOG2_E = 1.4426950408889634
F32 = jnp.float32
BF16 = jnp.bfloat16
NN = (((1,), (0,)), ((), ()))
NT = (((1,), (1,)), ((), ()))
TN = (((0,), (0,)), ((), ()))


def dot(left, right, dims=NN):
    return lax.dot_general(left, right, dims, preferred_element_type=F32)


def sigmoid(values):
    return 0.5 * jnp.tanh(0.5 * values) + 0.5


def flipped(weight):
    return weight.astype(F32).T.astype(BF16)


def lane_tiles(values):
    lanes = values.shape[1]
    return [(t, slice(t * LANES, (t + 1) * LANES)) for t in range(lanes // LANES)]


def lane_norm(values):
    centered = values - jnp.mean(values, axis=-1, keepdims=True)
    variance = jnp.mean(centered * centered, axis=-1, keepdims=True)
    return (centered * lax.rsqrt(variance + 1e-05)).astype(BF16)


def pipeline(rows, *steps):
    for tick in range(rows + len(steps) - 1):
        for late, step in enumerate(steps):
            if 0 <= tick - late < rows:
                step(tick - late)


def edges_kernel(*refs):
    given, (out, gate), (pair, weights, normed, held, sems) = refs[:6], refs[6:8], refs[8:]
    copies = [
        pltpu.make_async_copy(source, target, sems.at[n])
        for n, (source, target) in enumerate(zip(given, [weights.at[n] for n in range(5)] + [pair]))
    ]
    for copy in copies:
        copy.start()
    for copy in copies:
        copy.wait()
    rows = pair.shape[0]
    channels = weights.shape[2]
    turned = jnp.concatenate([flipped(weights[n]) for n in range(4)], axis=0)
    for i in range(rows):
        normed[i] = lane_norm(pair[i].astype(F32))
    for i in range(rows):
        both = dot(turned, normed[i], NT)
        for side in range(2):
            base = 2 * side * channels
            act = sigmoid(both[base + channels : base + 2 * channels]) * both[base : base + channels]
            for tile, lanes in lane_tiles(act):
                held[tile, pl.ds(side * rows + i, channels, stride=2 * rows), :] = act[:, lanes]
        gate[i] = sigmoid(dot(normed[i], weights[4]))
    block = out.shape[1]
    for owner in range(out.shape[0]):
        for tile, lanes in lane_tiles(pair):
            out[owner, :, lanes] = held[tile, owner * block : (owner + 1) * block, :].astype(BF16)


def triangle_sides(edges, rows, channel):
    sides = [[], []]
    for source in range(edges.shape[0]):
        block = edges[source, channel * 2 * rows : (channel + 1) * 2 * rows, :].astype(F32)
        sides[0].append(block[:rows])
        sides[1].append(block[rows:])
    return [jnp.concatenate(side, axis=0).astype(BF16) for side in sides]


def triangle_kernel(rows, edges, out):
    for pair_of in range(0, out.shape[1] // rows, 2):
        products = [dot(*triangle_sides(edges, rows, pair_of + o), NT) for o in range(2)]
        for owner in range(out.shape[0]):
            mine = slice(owner * rows, (owner + 1) * rows)
            out[owner, pair_of * rows : (pair_of + 2) * rows, :] = jnp.concatenate(
                [p[mine] for p in products], axis=0
            ).astype(BF16)


def partial_kernel(rows, edges, out):
    for channel in range(out.shape[0]):
        out[channel] = dot(*triangle_sides(edges, rows, channel), NT)


def update_kernel(
    returned, gate, pair, w_tri_out, w_bias_t, first_pass, att_norm, bias, held, bias_held, turned
):
    rows, cols = pair.shape[0], pair.shape[1]
    owners, block = returned.shape[0], returned.shape[1]
    channels = owners * block // rows
    total = jnp.zeros((rows, cols), F32)
    for owner in range(owners):
        total += jnp.sum(returned[owner].astype(F32).reshape(block // rows, rows, cols), axis=0)
    average = total / channels
    square = jnp.zeros((rows, cols), F32)
    for owner in range(owners):
        centered = returned[owner].astype(F32).reshape(block // rows, rows, cols) - average
        square += jnp.sum(centered * centered, axis=0)
        for tile, lanes in lane_tiles(pair):
            held[tile, owner * block : (owner + 1) * block, :] = centered.reshape(block, cols)[:, lanes]
    scale = lax.rsqrt(square / channels + 1e-05)

    def turn(i):
        tri_norm = jnp.concatenate(
            [held[tile, pl.ds(i, channels, stride=rows), :] for tile, _ in lane_tiles(pair)], axis=1
        )
        turned[i % 2] = (tri_norm * scale[i : i + 1]).T.astype(BF16)

    def update(i):
        first_pass[i] = pair[i].astype(F32) + gate[i] * dot(turned[i % 2], w_tri_out[...])

    def norm(i):
        att_norm[i] = lane_norm(first_pass[i])

    def project_bias(i):
        row_bias = dot(w_bias_t[...], att_norm[i], NT)
        for head in range(HEADS):
            bias_held[head * rows + i : head * rows + i + 1, :] = row_bias[head : head + 1]

    pipeline(rows, turn, update, norm, project_bias)
    rounded = bias_held[...].astype(BF16)
    for owner in range(bias.shape[0]):
        bias[owner] = rounded


def project_kernel(att_norm, w_query, w_key, w_value, w_att_gate, query_t, key, value_t, gate_t):
    w_turned = jnp.concatenate([flipped(w[...]) for w in (w_query, w_value, w_att_gate)], axis=0)
    width = w_query.shape[1]
    for i in range(att_norm.shape[0]):
        normed = att_norm[i]
        key[i] = dot(normed, w_key[...]).astype(BF16)
        turned = dot(w_turned, normed, NT)
        query_t[i] = turned[:width].astype(BF16)
        value_t[i] = turned[width : 2 * width].astype(BF16)
        gate_t[i] = sigmoid(turned[2 * width :])


def attend_kernel(
    query_t, key, value_t, gate_t, first_pass, bias, w_att_out, out, bias_t, scores, weights, gated
):
    rows, width, cols = query_t.shape
    head_rows = bias.shape[1] // HEADS
    score_scale = LOG2_E / HEAD_DIM**0.5
    ones = jnp.ones((16, key.shape[1]), BF16)
    heads = [
        (slice(h * HEAD_DIM, (h + 1) * HEAD_DIM), slice(h * cols, (h + 1) * cols)) for h in range(HEADS)
    ]

    def score(i):
        blocks = []
        for mine, _ in heads:
            above = jnp.zeros((mine.start, cols), BF16)
            below = jnp.zeros((width - mine.stop, cols), BF16)
            parts = [p for p in (above, query_t[i, mine, :], below) if p.shape[0]]
            blocks.append(jnp.concatenate(parts, axis=0))
        scores[i % 2] = dot(key[i], jnp.concatenate(blocks, axis=1)) * score_scale

    def soften(i):
        for _, span in heads:
            biased = scores[i % 2, :, span] + bias_t[:, span]
            peak = jnp.max(biased, axis=0, keepdims=True)
            weights[i % 2, :, span] = jnp.exp2(biased - peak).astype(BF16)

    def collect(i):
        for mine, span in heads:
            values = jnp.concatenate([value_t[i, mine, :], ones], axis=0)
            summed = dot(values, weights[i % 2, :, span])
            share = 1.0 / summed[HEAD_DIM : HEAD_DIM + 1]
            gated[i % 2, mine, :] = summed[:HEAD_DIM] * share * gate_t[i, mine, :]

    def finish(i):
        turned = gated[i % 2].T.astype(BF16)
        out[i] = (first_pass[i] + dot(turned, w_att_out[...])).astype(BF16)

    for head, (_, span) in enumerate(heads):
        parts = [
            bias[owner].astype(F32)[head * head_rows : (head + 1) * head_rows]
            for owner in range(bias.shape[0])
        ]
        bias_t[:, span] = jnp.concatenate(parts, axis=0).T * LOG2_E
    pipeline(rows, score, soften, collect, finish)


def call(kernel, outs, scratch, flops, *operands, copied=False):
    vmem = pl.BlockSpec(memory_space=pltpu.VMEM)
    given = pl.BlockSpec(memory_space=pltpu.HBM) if copied else vmem
    shapes = [jax.ShapeDtypeStruct(shape, dtype) for shape, dtype in outs]
    moved = sum(o.size * o.dtype.itemsize for o in operands)
    got = pl.pallas_call(
        kernel,
        out_shape=shapes,
        in_specs=[given] * len(operands),
        out_specs=[vmem] * len(shapes),
        scratch_shapes=[pltpu.VMEM(*s) if isinstance(s, tuple) else s for s in scratch],
        compiler_params=pltpu.CompilerParams(vmem_limit_bytes=48 * 2**20),
        cost_estimate=pl.CostEstimate(flops=flops, bytes_accessed=moved, transcendentals=0),
    )(*operands)
    return got if len(got) > 1 else got[0]


def body(
    pair_rep,
    w_left,
    w_left_gate,
    w_right,
    w_right_gate,
    w_tri_gate,
    w_tri_out,
    w_query,
    w_key,
    w_value,
    w_bias,
    w_att_gate,
    w_att_out,
):
    rows, cols, width = pair_rep.shape
    channels = w_left.shape[1]
    owners, col_parts = lax.axis_size("row"), lax.axis_size("col")
    own = channels // owners
    residues = owners * rows
    cells = rows * cols

    edges, gate = call(
        edges_kernel,
        [((owners, own * 2 * rows, cols), BF16), ((rows, cols, width), F32)],
        [
            (pair_rep.shape, BF16),
            ((5, width, channels), BF16),
            (pair_rep.shape, BF16),
            ((cols // LANES, channels * 2 * rows, LANES), F32),
            pltpu.SemaphoreType.DMA((6,)),
        ],
        10 * cells * width * channels,
        w_left,
        w_left_gate,
        w_right,
        w_right_gate,
        w_tri_gate,
        pair_rep,
        copied=True,
    )
    spread = lax.all_to_all(edges, "row", split_axis=0, concat_axis=0, tiled=True)
    flops = 2 * own * residues * residues * cols
    if col_parts == 1:
        summed = call(
            functools.partial(triangle_kernel, rows),
            [((owners, own * rows, residues), BF16)],
            [],
            flops,
            spread,
        )
    else:
        partial_sums = call(
            functools.partial(partial_kernel, rows),
            [((own, residues, residues), F32)],
            [],
            flops,
            spread,
        )
        summed = lax.psum_scatter(partial_sums, "col", scatter_dimension=2, tiled=True).astype(BF16)
        summed = summed.reshape(own, owners, rows, cols).swapaxes(0, 1)
        summed = summed.reshape(owners, own * rows, cols)
    returned = lax.all_to_all(summed, "row", split_axis=0, concat_axis=0, tiled=True)
    first_pass, att_norm, bias_copies = call(
        update_kernel,
        [
            ((rows, cols, width), F32),
            ((rows, cols, width), BF16),
            ((owners, HEADS * rows, cols), BF16),
        ],
        [
            ((cols // LANES, channels * rows, LANES), F32),
            ((HEADS * rows, cols), F32),
            ((2, cols, channels), BF16),
        ],
        2 * cells * channels * width,
        returned,
        gate,
        pair_rep,
        w_tri_out,
        w_bias.T,
    )
    bias = lax.all_to_all(bias_copies, "row", split_axis=0, concat_axis=0, tiled=True)
    att_norm, bias = lax.optimization_barrier((att_norm, bias))
    query_t, key, value_t, gate_t = call(
        project_kernel,
        [
            ((rows, width, cols), BF16),
            ((rows, cols, width), BF16),
            ((rows, width, cols), BF16),
            ((rows, width, cols), F32),
        ],
        [],
        8 * cells * width * width,
        att_norm,
        w_query,
        w_key,
        w_value,
        w_att_gate,
    )
    if col_parts > 1:
        bias = lax.all_to_all(bias, "col", split_axis=0, concat_axis=2, tiled=True)
        key = lax.all_gather(key, "col", axis=1, tiled=True)
        value_t = lax.all_gather(value_t, "col", axis=2, tiled=True)
    keys = key.shape[1]
    return call(
        attend_kernel,
        [((rows, cols, width), BF16)],
        [
            ((keys, HEADS * cols), F32),
            ((2, keys, HEADS * cols), F32),
            ((2, keys, HEADS * cols), BF16),
            ((2, width, cols), F32),
        ],
        4 * cells * keys * width,
        query_t,
        key,
        value_t,
        gate_t,
        first_pass,
        bias,
        w_att_out,
    )


def solution(mesh):
    in_specs = (P(("grp", "row"), "col", None),) + (P(),) * 12
    out_specs = P(("grp", "row"), "col", None)
    return jax.shard_map(body, mesh=mesh, in_specs=in_specs, out_specs=out_specs, check_vma=False)
```

time: 64.7 us -> 59.8 us (0.924)
  blocking collectives: 23.3 us -> 47.4 us
  waiting for transfers between devices: 15.8 us -> 0 us
  starting transfers between devices: 7.71 us -> 0 us
  Pallas kernels: 13.1 us -> 5.87 us
  local copies, waits for them, and re-layouts: 4.02 us -> 5.63 us
    all_to_all x0 -> x2, blocking collectives: none -> 24.2 us  [the longest x1 12.9 us: body(): lax.all_to_all(summed, 'row', split_axis=0, concat_axis=0, tiled=True)]
    all_to_all x2 -> x0, waiting for transfers between devices: 15.8 us -> none  [the longest x1 8.57 us: body(): lax.all_to_all(summed, 'row', split_axis=0, concat_axis=0, tiled=True)]
    all_to_all x2 -> x0, starting transfers between devices: 7.71 us -> none  [the longest x1 4.02 us: body(): lax.all_to_all(summed, 'row', split_axis=0, concat_axis=0, tiled=True)]
    pallas_call x6 -> x5, Pallas kernels: 13.1 us -> 5.87 us  [call(): pl.pallas_call(kernel, out_shape=shapes, in_specs=[given] * len(operands)...]
    unnamed x28, local copies, waits for them, and re-layouts: 4.02 us -> 5.63 us
  transfers between devices with their start and end apart: 2 -> 0, of which waited for: 2 -> 0; matrix products, arithmetic and copies ran while one was open for 0% -> 0% of each run, Pallas kernels for 1% -> 0%
where the time goes in v5:
time: 59.8 us; the launch traced here: 59.1 us
  blocking collectives  47.4 us (79%)
  Pallas kernels  5.87 us (10%)
  local copies, waits for them, and re-layouts  5.63 us (9%)
    all_to_all x1, blocking collectives, body(): lax.all_to_all(edges, 'row', split_axis=0, concat_axis=0, tiled=True)  23.2 us
    all_to_all x1, blocking collectives, body(): lax.all_to_all(summed, 'row', split_axis=0, concat_axis=0, tiled=True)  12.9 us
    all_to_all x1, blocking collectives, body(): lax.all_to_all(bias_copies, 'row', split_axis=0, concat_axis=0, tiled=True)  11.3 us
    pallas_call x5, Pallas kernels, call(): pl.pallas_call(kernel, out_shape=shapes, in_specs=[given] * len(operands)...  5.87 us
    unnamed x28, local copies, waits for them, and re-layouts  5.63 us

profile of v5, /device:TPU:0, one launch (start us, length us, event | category | flops | bytes accessed | tf_op | source)
XLA Modules:
  0.0 59.1 jit_solution(13606005062830919047)
XLA Ops:
  0.0 0.0 copy-start
  0.0 0.9 %copy-done = bf16[8,128,128]{2,1,0:T(8,128)(2,1)S(1)} copy-done((bf16[8,128,128]{2,1,0:T(8,128)(2,1)S(1)}, bf16[8,128,128]{2,1,0:T(8,128)(2,1)}, u32[]{:S(2)}) %copy-start) | copy-done | bytes 262168
  1.0 0.0 copy-start.5
  1.0 0.8 %copy-done.5 = bf16[128,128]{1,0:T(8,128)(2,1)S(1)} copy-done((bf16[128,128]{1,0:T(8,128)(2,1)S(1)}, bf16[128,128]{1,0:T(8,128)(2,1)}, u32[]{:S(2)}) %copy-start.5) | copy-done | bytes 32792
  1.7 0.0 copy-start.6
  1.7 0.8 %copy-done.6 = bf16[128,128]{1,0:T(8,128)(2,1)S(1)} copy-done((bf16[128,128]{1,0:T(8,128)(2,1)S(1)}, bf16[128,128]{1,0:T(8,128)(2,1)}, u32[]{:S(2)}) %copy-start.6) | copy-done | bytes 32792
  2.5 0.8 %copy-done.7 = bf16[128,128]{1,0:T(8,128)(2,1)S(1)} copy-done((bf16[128,128]{1,0:T(8,128)(2,1)S(1)}, bf16[128,128]{1,0:T(8,128)(2,1)}, u32[]{:S(2)}) %copy-start.7) | copy-done | bytes 32792
  3.2 0.8 %copy-done.8 = bf16[128,128]{1,0:T(8,128)(2,1)S(1)} copy-done((bf16[128,128]{1,0:T(8,128)(2,1)S(1)}, bf16[128,128]{1,0:T(8,128)(2,1)}, u32[]{:S(2)}) %copy-start.8) | copy-done | bytes 32792
  4.0 0.8 %copy-done.9 = bf16[128,128]{1,0:T(8,128)(2,1)S(1)} copy-done((bf16[128,128]{1,0:T(8,128)(2,1)S(1)}, bf16[128,128]{1,0:T(8,128)(2,1)}, u32[]{:S(2)}) %copy-start.9) | copy-done | bytes 32792
  4.7 1.5 %shard_map.127 = (bf16[16,128,128]{2,1,0:T(8,128)(2,1)S(1)}, f32[8,128,128]{2,1,0:T(8,128)S(1)}) custom-call(bf16[128,128]{1,0:T(8,128)(2,1)S(1)} %copy-done.5, bf16[128,128]{1,0:T(8,128)(2,1)S(1)} %copy-done.6, bf16[128,128]{1,0:T(8,128)(2,1)S(1)} %copy-done.7, bf16[128,128]{1,0:T(8,128)(2,1)S(1)} %copy-done.8, bf16[128,128]{1,0:T(8,128)(2,1)S(1)} %copy-done.9, ...), custom_call_target="tpu_custom_call" | custom-call | flops 167772160 | bytes 425984 | tf_op jit(solution)/shard_map/pallas_call | solution.py:208
  6.3 23.2 %all_to_all.15.edges = bf16[16,128,128]{2,1,0:T(8,128)(2,1)S(1)} all-to-all(bf16[16,128,128]{2,1,0:T(8,128)(2,1)S(1)} %get-tuple-element.16), channel_id=1, replica_groups=mesh['grp'=2,'row'=16,'col'=1] {'row'}, dimensions={0} | all-to-all | bytes 1048576 | tf_op jit(solution)/shard_map/all_to_all | solution.py:261
  29.5 0.3 shard_map.128
  29.8 0.0 copy-start.1
  29.8 0.0 copy-start.3
  29.8 12.9 %all_to_all.16.returned = bf16[16,64,128]{2,1,0:T(8,128)(2,1)S(1)} all-to-all(bf16[16,64,128]{2,1,0:T(8,128)(2,1)S(1)} %shard_map.128), channel_id=1, replica_groups=mesh['grp'=2,'row'=16,'col'=1] {'row'}, dimensions={0} | all-to-all | bytes 524288 | tf_op jit(solution)/shard_map/all_to_all | solution.py:282
  42.8 0.0 copy-done.1
  42.8 0.0 copy-done.3
  42.8 0.7 %copy-done.4 = bf16[128,4]{0,1:T(4,128)(2,1)S(1)} copy-done((bf16[128,4]{0,1:T(4,128)(2,1)S(1)}, bf16[128,4]{0,1:T(4,128)(2,1)}, u32[]{:S(2)}) %copy-start.4) | copy-done | bytes 1048
  43.5 1.3 %shard_map.129 = (f32[8,128,128]{2,1,0:T(8,128)S(1)}, bf16[8,128,128]{2,1,0:T(8,128)(2,1)S(1)}, bf16[16,32,128]{2,1,0:T(8,128)(2,1)S(1)}) custom-call(bf16[16,64,128]{2,1,0:T(8,128)(2,1)S(1)} %all_to_all.16.returned, f32[8,128,128]{2,1,0:T(8,128)S(1)} %get-tuple-element.17.gate, bf16[8,128,128]{2,1,0:T(8,128)(2,1)S(1)} %copy-done.1, ...), custom_call_target="tpu_custom_call" | custom-call | flops 33554432 | bytes 1082368 | tf_op jit(solution)/shard_map/pallas_call | solution.py:208
  44.7 0.0 copy-start.10
  44.8 0.0 copy-start.11
  44.8 0.0 copy-start.12
  44.8 0.0 copy-start.13
  44.8 11.3 %all_to_all.17.bias = bf16[16,32,128]{2,1,0:T(8,128)(2,1)S(1)} all-to-all(bf16[16,32,128]{2,1,0:T(8,128)(2,1)S(1)} %get-tuple-element.19), channel_id=1, replica_groups=mesh['grp'=2,'row'=16,'col'=1] {'row'}, dimensions={0} | all-to-all | bytes 262144 | tf_op jit(solution)/shard_map/all_to_all | solution.py:302
  56.1 0.0 copy-done.10
  56.1 0.0 copy-done.11
  56.1 0.0 copy-done.12
  56.1 0.0 copy-done.13
  56.1 0.0 copy-start.2
  56.1 0.6 shard_map.130
  56.7 0.2 copy-done.2
  56.8 2.2 %shard_map.131 = bf16[8,128,128]{2,1,0:T(8,128)(2,1)} custom-call(bf16[8,128,128]{2,1,0:T(8,128)(2,1)S(1)} %get-tuple-element.21.query_t, bf16[8,128,128]{2,1,0:T(8,128)(2,1)S(1)} %get-tuple-element.22.key, bf16[8,128,128]{2,1,0:T(8,128)(2,1)S(1)} %get-tuple-element.23.value_t, f32[8,128,128]{2,1,0:T(8,128)S(1)} %get-tuple-element.24.gate_t, ...), custom_call_target="tpu_custom_call" | custom-call | flops 67108864 | bytes 1998848 | tf_op jit(solution)/shard_map/pallas_call | solution.py:208
  (4 shorter events, 0.0 us)
Async XLA Ops:
  0.0 0.9 %copy-start = (bf16[8,128,128]{2,1,0:T(8,128)(2,1)S(1)}, bf16[8,128,128]{2,1,0:T(8,128)(2,1)}, u32[]{:S(2)}) copy-start(bf16[8,128,128]{2,1,0:T(8,128)(2,1)} %pair.1) | copy-start | bytes 786436
  1.0 0.8 %copy-start.5 = (bf16[128,128]{1,0:T(8,128)(2,1)S(1)}, bf16[128,128]{1,0:T(8,128)(2,1)}, u32[]{:S(2)}) copy-start(bf16[128,128]{1,0:T(8,128)(2,1)} %refs_0_.1) | copy-start | bytes 98308
  1.7 0.8 %copy-start.6 = (bf16[128,128]{1,0:T(8,128)(2,1)S(1)}, bf16[128,128]{1,0:T(8,128)(2,1)}, u32[]{:S(2)}) copy-start(bf16[128,128]{1,0:T(8,128)(2,1)} %refs_1_.1) | copy-start | bytes 98308
  2.5 0.8 %copy-start.7 = (bf16[128,128]{1,0:T(8,128)(2,1)S(1)}, bf16[128,128]{1,0:T(8,128)(2,1)}, u32[]{:S(2)}) copy-start(bf16[128,128]{1,0:T(8,128)(2,1)} %refs_2_.1) | copy-start | bytes 98308
  3.2 0.8 %copy-start.8 = (bf16[128,128]{1,0:T(8,128)(2,1)S(1)}, bf16[128,128]{1,0:T(8,128)(2,1)}, u32[]{:S(2)}) copy-start(bf16[128,128]{1,0:T(8,128)(2,1)} %refs_3_.1) | copy-start | bytes 98308
  4.0 0.8 %copy-start.9 = (bf16[128,128]{1,0:T(8,128)(2,1)S(1)}, bf16[128,128]{1,0:T(8,128)(2,1)}, u32[]{:S(2)}) copy-start(bf16[128,128]{1,0:T(8,128)(2,1)} %refs_4_.1) | copy-start | bytes 98308
  29.8 13.0 %copy-start.1 = (bf16[8,128,128]{2,1,0:T(8,128)(2,1)S(1)}, bf16[8,128,128]{2,1,0:T(8,128)(2,1)}, u32[]{:S(2)}) copy-start(bf16[8,128,128]{2,1,0:T(8,128)(2,1)} %pair.1) | copy-start | bytes 786436
  29.8 12.9 %copy-start.3 = (bf16[128,128]{1,0:T(8,128)(2,1)S(1)}, bf16[128,128]{1,0:T(8,128)(2,1)}, u32[]{:S(2)}) copy-start(bf16[128,128]{1,0:T(8,128)(2,1)} %w_tri_out.1) | copy-start | bytes 98308
  42.8 0.7 %copy-start.4 = (bf16[128,4]{0,1:T(4,128)(2,1)S(1)}, bf16[128,4]{0,1:T(4,128)(2,1)}, u32[]{:S(2)}) copy-start(bf16[128,4]{0,1:T(4,128)(2,1)} %param.23) | copy-start | bytes 3076
  44.7 11.3 %copy-start.10 = (bf16[128,128]{1,0:T(8,128)(2,1)S(1)}, bf16[128,128]{1,0:T(8,128)(2,1)}, u32[]{:S(2)}) copy-start(bf16[128,128]{1,0:T(8,128)(2,1)} %w_query.1) | copy-start | bytes 98308
  44.8 11.3 %copy-start.11 = (bf16[128,128]{1,0:T(8,128)(2,1)S(1)}, bf16[128,128]{1,0:T(8,128)(2,1)}, u32[]{:S(2)}) copy-start(bf16[128,128]{1,0:T(8,128)(2,1)} %w_key.1) | copy-start | bytes 98308
  44.8 11.3 %copy-start.12 = (bf16[128,128]{1,0:T(8,128)(2,1)S(1)}, bf16[128,128]{1,0:T(8,128)(2,1)}, u32[]{:S(2)}) copy-start(bf16[128,128]{1,0:T(8,128)(2,1)} %w_value.1) | copy-start | bytes 98308
  44.8 11.3 %copy-start.13 = (bf16[128,128]{1,0:T(8,128)(2,1)S(1)}, bf16[128,128]{1,0:T(8,128)(2,1)}, u32[]{:S(2)}) copy-start(bf16[128,128]{1,0:T(8,128)(2,1)} %w_att_gate.1) | copy-start | bytes 98308
  56.1 0.8 %copy-start.2 = (bf16[128,128]{1,0:T(8,128)(2,1)S(1)}, bf16[128,128]{1,0:T(8,128)(2,1)}, u32[]{:S(2)}) copy-start(bf16[128,128]{1,0:T(8,128)(2,1)} %w_att_out.1) | copy-start | bytes 98308

commit v6 on v5

--- a/solution.py
+++ b/solution.py
@@ -28,6 +28,18 @@
 
 def flipped(weight):
     return weight.astype(F32).T.astype(BF16)
+
+
+def slot(rank, ranks):
+    return ranks - 1 - rank
+
+
+def swap(blocks):
+    ranks = blocks.shape[0]
+    order = [slot(rank, ranks) for rank in range(ranks)]
+    return lax.all_to_all(
+        blocks, "row", split_axis=0, concat_axis=0, axis_index_groups=[order], tiled=True
+    )
 
 
 def lane_tiles(values):
@@ -71,16 +83,17 @@
             for tile, lanes in lane_tiles(act):
                 held[tile, pl.ds(side * rows + i, channels, stride=2 * rows), :] = act[:, lanes]
         gate[i] = sigmoid(dot(normed[i], weights[4]))
-    block = out.shape[1]
-    for owner in range(out.shape[0]):
+    owners, block = out.shape[0], out.shape[1]
+    for owner in range(owners):
         for tile, lanes in lane_tiles(pair):
-            out[owner, :, lanes] = held[tile, owner * block : (owner + 1) * block, :].astype(BF16)
+            out[slot(owner, owners), :, lanes] = held[tile, owner * block : (owner + 1) * block, :].astype(BF16)
 
 
 def triangle_sides(edges, rows, channel):
     sides = [[], []]
-    for source in range(edges.shape[0]):
-        block = edges[source, channel * 2 * rows : (channel + 1) * 2 * rows, :].astype(F32)
+    sources = edges.shape[0]
+    for source in range(sources):
+        block = edges[slot(source, sources), channel * 2 * rows : (channel + 1) * 2 * rows, :].astype(F32)
         sides[0].append(block[:rows])
         sides[1].append(block[rows:])
     return [jnp.concatenate(side, axis=0).astype(BF16) for side in sides]
@@ -89,9 +102,10 @@
 def triangle_kernel(rows, edges, out):
     for pair_of in range(0, out.shape[1] // rows, 2):
         products = [dot(*triangle_sides(edges, rows, pair_of + o), NT) for o in range(2)]
-        for owner in range(out.shape[0]):
+        owners = out.shape[0]
+        for owner in range(owners):
             mine = slice(owner * rows, (owner + 1) * rows)
-            out[owner, pair_of * rows : (pair_of + 2) * rows, :] = jnp.concatenate(
+            out[slot(owner, owners), pair_of * rows : (pair_of + 2) * rows, :] = jnp.concatenate(
                 [p[mine] for p in products], axis=0
             ).astype(BF16)
 
@@ -102,8 +116,27 @@
 
 
 def update_kernel(
-    returned, gate, pair, w_tri_out, w_bias_t, first_pass, att_norm, bias, held, bias_held, turned
+    w_tri_out_given,
+    w_bias_given,
+    returned,
+    gate,
+    pair,
+    first_pass,
+    att_norm,
+    bias,
+    held,
+    bias_held,
+    turned,
+    w_tri_out,
+    w_bias_t,
+    sems,
 ):
+    copies = [
+        pltpu.make_async_copy(w_tri_out_given, w_tri_out, sems.at[0]),
+        pltpu.make_async_copy(w_bias_given, w_bias_t, sems.at[1]),
+    ]
+    for copy in copies:
+        copy.start()
     rows, cols = pair.shape[0], pair.shape[1]
     owners, block = returned.shape[0], returned.shape[1]
     channels = owners * block // rows
@@ -113,11 +146,13 @@
     average = total / channels
     square = jnp.zeros((rows, cols), F32)
     for owner in range(owners):
-        centered = returned[owner].astype(F32).reshape(block // rows, rows, cols) - average
+        centered = returned[slot(owner, owners)].astype(F32).reshape(block // rows, rows, cols) - average
         square += jnp.sum(centered * centered, axis=0)
         for tile, lanes in lane_tiles(pair):
             held[tile, owner * block : (owner + 1) * block, :] = centered.reshape(block, cols)[:, lanes]
     scale = lax.rsqrt(square / channels + 1e-05)
+    for copy in copies:
+        copy.wait()
 
     def turn(i):
         tri_norm = jnp.concatenate(
@@ -193,22 +228,26 @@
 
     for head, (_, span) in enumerate(heads):
         parts = [
-            bias[owner].astype(F32)[head * head_rows : (head + 1) * head_rows]
+            bias[slot(owner, bias.shape[0])].astype(F32)[head * head_rows : (head + 1) * head_rows]
             for owner in range(bias.shape[0])
         ]
         bias_t[:, span] = jnp.concatenate(parts, axis=0).T * LOG2_E
     pipeline(rows, score, soften, collect, finish)
 
 
-def call(kernel, outs, scratch, flops, *operands, copied=False):
+def call(kernel, outs, scratch, flops, *operands, fetched=0):
     vmem = pl.BlockSpec(memory_space=pltpu.VMEM)
-    given = pl.BlockSpec(memory_space=pltpu.HBM) if copied else vmem
+    far = pl.BlockSpec(memory_space=pltpu.HBM)
     shapes = [jax.ShapeDtypeStruct(shape, dtype) for shape, dtype in outs]
     moved = sum(o.size * o.dtype.itemsize for o in operands)
+    operands = [
+        pltpu.with_memory_space_constraint(o, pltpu.HBM) if n < fetched else o
+        for n, o in enumerate(operands)
+    ]
     got = pl.pallas_call(
         kernel,
         out_shape=shapes,
-        in_specs=[given] * len(operands),
+        in_specs=[far] * fetched + [vmem] * (len(operands) - fetched),
         out_specs=[vmem] * len(shapes),
         scratch_shapes=[pltpu.VMEM(*s) if isinstance(s, tuple) else s for s in scratch],
         compiler_params=pltpu.CompilerParams(vmem_limit_bytes=48 * 2**20),
@@ -256,9 +295,9 @@
         w_right_gate,
         w_tri_gate,
         pair_rep,
-        copied=True,
-    )
-    spread = lax.all_to_all(edges, "row", split_axis=0, concat_axis=0, tiled=True)
+        fetched=6,
+    )
+    spread = swap(edges)
     flops = 2 * own * residues * residues * cols
     if col_parts == 1:
         summed = call(
@@ -277,9 +316,9 @@
             spread,
         )
         summed = lax.psum_scatter(partial_sums, "col", scatter_dimension=2, tiled=True).astype(BF16)
-        summed = summed.reshape(own, owners, rows, cols).swapaxes(0, 1)
+        summed = summed.reshape(own, owners, rows, cols).swapaxes(0, 1)[::-1]
         summed = summed.reshape(owners, own * rows, cols)
-    returned = lax.all_to_all(summed, "row", split_axis=0, concat_axis=0, tiled=True)
+    returned = swap(summed)
     first_pass, att_norm, bias_copies = call(
         update_kernel,
         [
@@ -291,15 +330,19 @@
             ((cols // LANES, channels * rows, LANES), F32),
             ((HEADS * rows, cols), F32),
             ((2, cols, channels), BF16),
+            (w_tri_out.shape, BF16),
+            (w_bias.shape[::-1], BF16),
+            pltpu.SemaphoreType.DMA((2,)),
         ],
         2 * cells * channels * width,
+        w_tri_out,
+        w_bias.T,
         returned,
         gate,
         pair_rep,
-        w_tri_out,
-        w_bias.T,
-    )
-    bias = lax.all_to_all(bias_copies, "row", split_axis=0, concat_axis=0, tiled=True)
+        fetched=2,
+    )
+    bias = swap(bias_copies)
     att_norm, bias = lax.optimization_barrier((att_norm, bias))
     query_t, key, value_t, gate_t = call(
         project_kernel,
@@ -318,7 +361,7 @@
         w_att_gate,
     )
     if col_parts > 1:
-        bias = lax.all_to_all(bias, "col", split_axis=0, concat_axis=2, tiled=True)
+        bias = lax.all_to_all(bias[::-1], "col", split_axis=0, concat_axis=2, tiled=True)[::-1]
         key = lax.all_gather(key, "col", axis=1, tiled=True)
         value_t = lax.all_gather(value_t, "col", axis=2, tiled=True)
     keys = key.shape[1]

time: 59.8 us -> 52.9 us (0.88)
  local copies, waits for them, and re-layouts: 5.63 us -> 0.22 us
  blocking collectives: 47.4 us -> 44.8 us
  Pallas kernels: 5.87 us -> 7.36 us
    unnamed x28 -> x12, local copies, waits for them, and re-layouts: 5.63 us -> 0.22 us
    all_to_all x3, blocking collectives: 47.4 us -> 44.8 us  [swap(): lax.all_to_all(blocks, 'row', split_axis=0, concat_axis=0, axis_index_gro...]
    pallas_call x5, Pallas kernels: 5.87 us -> 7.36 us  [call(): pl.pallas_call(kernel, out_shape=shapes, in_specs=[far] * fetched + [vmem...]
where the time goes in v6:
time: 52.9 us; the launch traced here: 52.5 us
  blocking collectives  44.8 us (85%)
  Pallas kernels  7.36 us (14%)
    all_to_all x3, blocking collectives, swap(): lax.all_to_all(blocks, 'row', split_axis=0, concat_axis=0, axis_index_gro...  44.8 us
    pallas_call x5, Pallas kernels, call(): pl.pallas_call(kernel, out_shape=shapes, in_specs=[far] * fetched + [vmem...  7.36 us

profile of v6, /device:TPU:0, one launch (start us, length us, event | category | flops | bytes accessed | tf_op | source)
XLA Modules:
  0.0 52.5 jit_solution(16932610364720965475)
XLA Ops:
  0.0 2.4 %shard_map.127 = (bf16[16,128,128]{2,1,0:T(8,128)(2,1)S(1)}, f32[8,128,128]{2,1,0:T(8,128)S(1)}) custom-call(bf16[128,128]{1,0:T(8,128)(2,1)} %refs_0_.1, bf16[128,128]{1,0:T(8,128)(2,1)} %refs_1_.1, bf16[128,128]{1,0:T(8,128)(2,1)} %refs_2_.1, bf16[128,128]{1,0:T(8,128)(2,1)} %refs_3_.1, bf16[128,128]{1,0:T(8,128)(2,1)} %refs_4_.1, bf16[8,128,128]{2,1,0:T(8,128)(2,1)} %pair.1), custom_call_target="tpu_custom_call" | custom-call | flops 167772160 | bytes 425984 | tf_op jit(solution)/shard_map/pallas_call | solution.py:247
  2.4 21.8 %all_to_all.15.edges = bf16[16,128,128]{2,1,0:T(8,128)(2,1)S(1)} all-to-all(bf16[16,128,128]{2,1,0:T(8,128)(2,1)S(1)} %get-tuple-element.16), channel_id=1, replica_groups={{15,14,13,12,11,10,9,8,7,6,5,4,3,2,1,0},{31,30,29,28,27,26,25,24,23,22,..., dimensions={0} | all-to-all | bytes 1048576 | tf_op jit(solution)/shard_map/all_to_all | solution.py:40
  24.2 0.3 shard_map.128
  24.5 0.0 copy-start
  24.5 12.5 %all_to_all.16.returned = bf16[16,64,128]{2,1,0:T(8,128)(2,1)S(1)} all-to-all(bf16[16,64,128]{2,1,0:T(8,128)(2,1)S(1)} %shard_map.128), channel_id=1, replica_groups={{15,14,13,12,11,10,9,8,7,6,5,4,3,2,1,0},{31,30,29,28,27,26,25,24,23,22,..., dimensions={0} | all-to-all | bytes 524288 | tf_op jit(solution)/shard_map/all_to_all | solution.py:40
  37.0 0.0 copy-done
  37.0 1.9 %shard_map.129 = (f32[8,128,128]{2,1,0:T(8,128)S(1)}, bf16[8,128,128]{2,1,0:T(8,128)(2,1)S(1)}, bf16[16,32,128]{2,1,0:T(8,128)(2,1)S(1)}) custom-call(bf16[128,128]{1,0:T(8,128)(2,1)} %w_tri_out_given.1, bf16[4,128]{1,0:T(4,128)(2,1)} %bitcast.1, bf16[16,64,128]{2,1,0:T(8,128)(2,1)S(1)} %all_to_all.16.returned, f32[8,128,128]{2,1,0:T(8,128)S(1)} %get-tuple-element.17.gate, ...), custom_call_target="tpu_custom_call" | custom-call | flops 33554432 | bytes 1082368 | tf_op jit(solution)/shard_map/pallas_call | solution.py:247
  39.0 0.0 copy-start.2
  39.0 0.0 copy-start.3
  39.0 0.0 copy-start.4
  39.0 0.0 copy-start.5
  39.0 10.5 %all_to_all.17.bias = bf16[16,32,128]{2,1,0:T(8,128)(2,1)S(1)} all-to-all(bf16[16,32,128]{2,1,0:T(8,128)(2,1)S(1)} %get-tuple-element.19), channel_id=1, replica_groups={{15,14,13,12,11,10,9,8,7,6,5,4,3,2,1,0},{31,30,29,28,27,26,25,24,23,22,..., dimensions={0} | all-to-all | bytes 262144 | tf_op jit(solution)/shard_map/all_to_all | solution.py:40
  49.5 0.0 copy-done.2
  49.5 0.0 copy-done.3
  49.5 0.0 copy-done.4
  49.5 0.0 copy-done.5
  49.5 0.0 copy-start.1
  49.5 0.6 %shard_map.130 = (bf16[8,128,128]{2,1,0:T(8,128)(2,1)S(1)}, bf16[8,128,128]{2,1,0:T(8,128)(2,1)S(1)}, bf16[8,128,128]{2,1,0:T(8,128)(2,1)S(1)}, f32[8,128,128]{2,1,0:T(8,128)S(1)}) custom-call(bf16[8,128,128]{2,1,0:T(8,128)(2,1)S(1)} %get-tuple-element.20.att_norm, bf16[128,128]{1,0:T(8,128)(2,1)S(1)} %copy-done.2, bf16[128,128]{1,0:T(8,128)(2,1)S(1)} %copy-done.3, ...), custom_call_target="tpu_custom_call" | custom-call | flops 134217728 | bytes 393216 | tf_op jit(solution)/shard_map/pallas_call | solution.py:247
  50.1 0.2 copy-done.1
  50.3 2.2 %shard_map.131 = bf16[8,128,128]{2,1,0:T(8,128)(2,1)} custom-call(bf16[8,128,128]{2,1,0:T(8,128)(2,1)S(1)} %get-tuple-element.21.query_t, bf16[8,128,128]{2,1,0:T(8,128)(2,1)S(1)} %get-tuple-element.22.key, bf16[8,128,128]{2,1,0:T(8,128)(2,1)S(1)} %get-tuple-element.23.value_t, f32[8,128,128]{2,1,0:T(8,128)S(1)} %get-tuple-element.24.gate_t, ...), custom_call_target="tpu_custom_call" | custom-call | flops 67108864 | bytes 1998848 | tf_op jit(solution)/shard_map/pallas_call | solution.py:247
Async XLA Ops:
  24.5 12.6 %copy-start = (bf16[8,128,128]{2,1,0:T(8,128)(2,1)S(1)}, bf16[8,128,128]{2,1,0:T(8,128)(2,1)}, u32[]{:S(2)}) copy-start(bf16[8,128,128]{2,1,0:T(8,128)(2,1)} %pair.1) | copy-start | bytes 786436
  39.0 10.5 %copy-start.2 = (bf16[128,128]{1,0:T(8,128)(2,1)S(1)}, bf16[128,128]{1,0:T(8,128)(2,1)}, u32[]{:S(2)}) copy-start(bf16[128,128]{1,0:T(8,128)(2,1)} %w_query.1) | copy-start | bytes 98308
  39.0 10.5 %copy-start.3 = (bf16[128,128]{1,0:T(8,128)(2,1)S(1)}, bf16[128,128]{1,0:T(8,128)(2,1)}, u32[]{:S(2)}) copy-start(bf16[128,128]{1,0:T(8,128)(2,1)} %w_key.1) | copy-start | bytes 98308
  39.0 10.5 %copy-start.4 = (bf16[128,128]{1,0:T(8,128)(2,1)S(1)}, bf16[128,128]{1,0:T(8,128)(2,1)}, u32[]{:S(2)}) copy-start(bf16[128,128]{1,0:T(8,128)(2,1)} %w_value.1) | copy-start | bytes 98308
  39.0 10.5 %copy-start.5 = (bf16[128,128]{1,0:T(8,128)(2,1)S(1)}, bf16[128,128]{1,0:T(8,128)(2,1)}, u32[]{:S(2)}) copy-start(bf16[128,128]{1,0:T(8,128)(2,1)} %w_att_gate.1) | copy-start | bytes 98308
  49.5 0.8 %copy-start.1 = (bf16[128,128]{1,0:T(8,128)(2,1)S(1)}, bf16[128,128]{1,0:T(8,128)(2,1)}, u32[]{:S(2)}) copy-start(bf16[128,128]{1,0:T(8,128)(2,1)} %w_att_out.1) | copy-start | bytes 98308

commit v7 on v6

--- a/solution.py
+++ b/solution.py
@@ -2,6 +2,7 @@
 
 import jax
 import jax.numpy as jnp
+import numpy as np
 from jax import lax
 from jax.experimental import pallas as pl
 from jax.experimental.pallas import tpu as pltpu
@@ -30,16 +31,32 @@
     return weight.astype(F32).T.astype(BF16)
 
 
+def listing(ranks):
+    first = ranks - 1 - ranks // 4
+    return [first] + [rank for rank in range(ranks - 1, -1, -1) if rank != first]
+
+
 def slot(rank, ranks):
-    return ranks - 1 - rank
+    return listing(ranks).index(rank)
 
 
 def swap(blocks):
-    ranks = blocks.shape[0]
-    order = [slot(rank, ranks) for rank in range(ranks)]
     return lax.all_to_all(
-        blocks, "row", split_axis=0, concat_axis=0, axis_index_groups=[order], tiled=True
+        blocks,
+        "row",
+        split_axis=0,
+        concat_axis=0,
+        axis_index_groups=[listing(blocks.shape[0])],
+        tiled=True,
     )
+
+
+def by_rank(blocks):
+    return blocks[np.array([slot(r, blocks.shape[0]) for r in range(blocks.shape[0])])]
+
+
+def by_slot(blocks):
+    return blocks[np.array(listing(blocks.shape[0]))]
 
 
 def lane_tiles(values):
@@ -61,14 +78,15 @@
 
 
 def edges_kernel(*refs):
-    given, (out, gate), (pair, weights, normed, held, sems) = refs[:6], refs[6:8], refs[8:]
+    given, (out, gate, *staged), (pair, weights, normed, held, sems) = refs[:13], refs[13:22], refs[22:]
+    targets = [pair, *(weights.at[n] for n in range(5)), *staged]
     copies = [
         pltpu.make_async_copy(source, target, sems.at[n])
-        for n, (source, target) in enumerate(zip(given, [weights.at[n] for n in range(5)] + [pair]))
+        for n, (source, target) in enumerate(zip(given, targets))
     ]
     for copy in copies:
         copy.start()
-    for copy in copies:
+    for copy in copies[:6]:
         copy.wait()
     rows = pair.shape[0]
     channels = weights.shape[2]
@@ -87,6 +105,8 @@
     for owner in range(owners):
         for tile, lanes in lane_tiles(pair):
             out[slot(owner, owners), :, lanes] = held[tile, owner * block : (owner + 1) * block, :].astype(BF16)
+    for copy in copies[6:]:
+        copy.wait()
 
 
 def triangle_sides(edges, rows, channel):
@@ -116,27 +136,8 @@
 
 
 def update_kernel(
-    w_tri_out_given,
-    w_bias_given,
-    returned,
-    gate,
-    pair,
-    first_pass,
-    att_norm,
-    bias,
-    held,
-    bias_held,
-    turned,
-    w_tri_out,
-    w_bias_t,
-    sems,
+    returned, gate, pair, w_tri_out, w_bias_t, first_pass, att_norm, bias, held, bias_held, turned
 ):
-    copies = [
-        pltpu.make_async_copy(w_tri_out_given, w_tri_out, sems.at[0]),
-        pltpu.make_async_copy(w_bias_given, w_bias_t, sems.at[1]),
-    ]
-    for copy in copies:
-        copy.start()
     rows, cols = pair.shape[0], pair.shape[1]
     owners, block = returned.shape[0], returned.shape[1]
     channels = owners * block // rows
@@ -151,8 +152,6 @@
         for tile, lanes in lane_tiles(pair):
             held[tile, owner * block : (owner + 1) * block, :] = centered.reshape(block, cols)[:, lanes]
     scale = lax.rsqrt(square / channels + 1e-05)
-    for copy in copies:
-        copy.wait()
 
     def turn(i):
         tri_norm = jnp.concatenate(
@@ -177,10 +176,11 @@
         bias[owner] = rounded
 
 
-def project_kernel(att_norm, w_query, w_key, w_value, w_att_gate, query_t, key, value_t, gate_t):
+def projector(att_norm, w_query, w_key, w_value, w_att_gate, query_t, key, value_t, gate_t):
     w_turned = jnp.concatenate([flipped(w[...]) for w in (w_query, w_value, w_att_gate)], axis=0)
     width = w_query.shape[1]
-    for i in range(att_norm.shape[0]):
+
+    def project(i):
         normed = att_norm[i]
         key[i] = dot(normed, w_key[...]).astype(BF16)
         turned = dot(w_turned, normed, NT)
@@ -188,9 +188,33 @@
         value_t[i] = turned[width : 2 * width].astype(BF16)
         gate_t[i] = sigmoid(turned[2 * width :])
 
+    return project
+
+
+def project_kernel(*refs):
+    pipeline(refs[0].shape[0], projector(*refs))
+
+
+def whole_kernel(att_norm, w_query, w_key, w_value, w_att_gate, *refs):
+    given, projected, held = refs[:4], refs[4:8], refs[8:]
+    project = projector(att_norm, w_query, w_key, w_value, w_att_gate, *projected)
+    attend_kernel(*projected, *given, *held, before=(project,))
+
 
 def attend_kernel(
-    query_t, key, value_t, gate_t, first_pass, bias, w_att_out, out, bias_t, scores, weights, gated
+    query_t,
+    key,
+    value_t,
+    gate_t,
+    first_pass,
+    bias,
+    w_att_out,
+    out,
+    bias_t,
+    scores,
+    weights,
+    gated,
+    before=(),
 ):
     rows, width, cols = query_t.shape
     head_rows = bias.shape[1] // HEADS
@@ -232,7 +256,7 @@
             for owner in range(bias.shape[0])
         ]
         bias_t[:, span] = jnp.concatenate(parts, axis=0).T * LOG2_E
-    pipeline(rows, score, soften, collect, finish)
+    pipeline(rows, *before, score, soften, collect, finish)
 
 
 def call(kernel, outs, scratch, flops, *operands, fetched=0):
@@ -278,24 +302,36 @@
     residues = owners * rows
     cells = rows * cols
 
-    edges, gate = call(
+    edges, gate, w_tri_out, w_query, w_key, w_value, w_att_gate, w_att_out, w_bias_t = call(
         edges_kernel,
-        [((owners, own * 2 * rows, cols), BF16), ((rows, cols, width), F32)],
+        [
+            ((owners, own * 2 * rows, cols), BF16),
+            ((rows, cols, width), F32),
+            *[(w.shape, BF16) for w in (w_tri_out, w_query, w_key, w_value, w_att_gate, w_att_out)],
+            (w_bias.shape[::-1], BF16),
+        ],
         [
             (pair_rep.shape, BF16),
             ((5, width, channels), BF16),
             (pair_rep.shape, BF16),
             ((cols // LANES, channels * 2 * rows, LANES), F32),
-            pltpu.SemaphoreType.DMA((6,)),
+            pltpu.SemaphoreType.DMA((13,)),
         ],
         10 * cells * width * channels,
+        pair_rep,
         w_left,
         w_left_gate,
         w_right,
         w_right_gate,
         w_tri_gate,
-        pair_rep,
-        fetched=6,
+        w_tri_out,
+        w_query,
+        w_key,
+        w_value,
+        w_att_gate,
+        w_att_out,
+        w_bias.T,
+        fetched=13,
     )
     spread = swap(edges)
     flops = 2 * own * residues * residues * cols
@@ -316,7 +352,7 @@
             spread,
         )
         summed = lax.psum_scatter(partial_sums, "col", scatter_dimension=2, tiled=True).astype(BF16)
-        summed = summed.reshape(own, owners, rows, cols).swapaxes(0, 1)[::-1]
+        summed = by_slot(summed.reshape(own, owners, rows, cols).swapaxes(0, 1))
         summed = summed.reshape(owners, own * rows, cols)
     returned = swap(summed)
     first_pass, att_norm, bias_copies = call(
@@ -330,59 +366,41 @@
             ((cols // LANES, channels * rows, LANES), F32),
             ((HEADS * rows, cols), F32),
             ((2, cols, channels), BF16),
-            (w_tri_out.shape, BF16),
-            (w_bias.shape[::-1], BF16),
-            pltpu.SemaphoreType.DMA((2,)),
         ],
         2 * cells * channels * width,
-        w_tri_out,
-        w_bias.T,
         returned,
         gate,
         pair_rep,
-        fetched=2,
+        w_tri_out,
+        w_bias_t,
     )
     bias = swap(bias_copies)
-    att_norm, bias = lax.optimization_barrier((att_norm, bias))
-    query_t, key, value_t, gate_t = call(
-        project_kernel,
-        [
-            ((rows, width, cols), BF16),
-            ((rows, cols, width), BF16),
-            ((rows, width, cols), BF16),
-            ((rows, width, cols), F32),
-        ],
-        [],
-        8 * cells * width * width,
-        att_norm,
-        w_query,
-        w_key,
-        w_value,
-        w_att_gate,
-    )
-    if col_parts > 1:
-        bias = lax.all_to_all(bias[::-1], "col", split_axis=0, concat_axis=2, tiled=True)[::-1]
-        key = lax.all_gather(key, "col", axis=1, tiled=True)
-        value_t = lax.all_gather(value_t, "col", axis=2, tiled=True)
-    keys = key.shape[1]
-    return call(
-        attend_kernel,
-        [((rows, cols, width), BF16)],
-        [
-            ((keys, HEADS * cols), F32),
-            ((2, keys, HEADS * cols), F32),
-            ((2, keys, HEADS * cols), BF16),
-            ((2, width, cols), F32),
-        ],
-        4 * cells * keys * width,
-        query_t,
-        key,
-        value_t,
-        gate_t,
-        first_pass,
-        bias,
-        w_att_out,
-    )
+    projected = [
+        ((rows, width, cols), BF16),
+        ((rows, cols, width), BF16),
+        ((rows, width, cols), BF16),
+        ((rows, width, cols), F32),
+    ]
+    projecting = (att_norm, w_query, w_key, w_value, w_att_gate)
+    residues = cols * col_parts
+    out = [((rows, cols, width), BF16)]
+    held = [
+        ((residues, HEADS * cols), F32),
+        ((2, residues, HEADS * cols), F32),
+        ((2, residues, HEADS * cols), BF16),
+        ((2, width, cols), F32),
+    ]
+    project_flops, attend_flops = 8 * cells * width * width, 4 * cells * residues * width
+    if col_parts == 1:
+        flops = project_flops + attend_flops
+        given = (first_pass, bias, w_att_out)
+        return call(whole_kernel, out, projected + held, flops, *projecting, *given)
+    query_t, key, value_t, gate_t = call(project_kernel, projected, [], project_flops, *projecting)
+    bias = by_slot(lax.all_to_all(by_rank(bias), "col", split_axis=0, concat_axis=2, tiled=True))
+    key = lax.all_gather(key, "col", axis=1, tiled=True)
+    value_t = lax.all_gather(value_t, "col", axis=2, tiled=True)
+    given = (query_t, key, value_t, gate_t, first_pass, bias, w_att_out)
+    return call(attend_kernel, out, held, attend_flops, *given)
 
 
 def solution(mesh):

time: 52.9 us -> 49.1 us (0.928)
  blocking collectives: 44.8 us -> 42.3 us
  Pallas kernels: 7.36 us -> 6.49 us
    all_to_all x3, blocking collectives: 44.8 us -> 42.3 us  [swap(): lax.all_to_all(blocks, 'row', split_axis=0, concat_axis=0, axis_index_gro...]
    pallas_call x5 -> x4, Pallas kernels: 7.36 us -> 6.49 us  [call(): pl.pallas_call(kernel, out_shape=shapes, in_specs=[far] * fetched + [vmem...]
where the time goes in v7:
time: 49.1 us; the launch traced here: 48.9 us
  blocking collectives  42.3 us (86%)
  Pallas kernels  6.49 us (13%)
    all_to_all x3, blocking collectives, swap(): lax.all_to_all(blocks, 'row', split_axis=0, concat_axis=0, axis_index_gro...  42.3 us
    pallas_call x4, Pallas kernels, call(): pl.pallas_call(kernel, out_shape=shapes, in_specs=[far] * fetched + [vmem...  6.49 us

profile of v7, /device:TPU:0, one launch (start us, length us, event | category | flops | bytes accessed | tf_op | source)
XLA Modules:
  0.0 48.9 jit_solution(17315215508333955547)
XLA Ops:
  0.0 2.3 %shard_map.127 = (bf16[16,128,128]{2,1,0:T(8,128)(2,1)S(1)}, f32[8,128,128]{2,1,0:T(8,128)S(1)}, bf16[128,128]{1,0:T(8,128)(2,1)S(1)}, bf16[128,128]{1,0:T(8,128...) custom-call(bf16[8,128,128]{2,1,0:T(8,128)(2,1)} %pair.1, ...), custom_call_target="tpu_custom_call" | custom-call | flops 167772160 | bytes 623616 | tf_op jit(solution)/shard_map/pallas_call | solution.py:271
  2.4 20.6 %all_to_all.15.edges = bf16[16,128,128]{2,1,0:T(8,128)(2,1)S(1)} all-to-all(bf16[16,128,128]{2,1,0:T(8,128)(2,1)S(1)} %get-tuple-element.17), channel_id=1, replica_groups={{11,15,14,13,12,10,9,8,7,6,5,4,3,2,1,0},{27,31,30,29,28,26,25,24,23,22,..., dimensions={0} | all-to-all | bytes 1048576 | tf_op jit(solution)/shard_map/all_to_all | solution.py:44
  23.0 0.3 shard_map.128
  23.3 0.0 copy-start
  23.3 11.6 %all_to_all.16.returned = bf16[16,64,128]{2,1,0:T(8,128)(2,1)S(1)} all-to-all(bf16[16,64,128]{2,1,0:T(8,128)(2,1)S(1)} %shard_map.128), channel_id=1, replica_groups={{11,15,14,13,12,10,9,8,7,6,5,4,3,2,1,0},{27,31,30,29,28,26,25,24,23,22,..., dimensions={0} | all-to-all | bytes 524288 | tf_op jit(solution)/shard_map/all_to_all | solution.py:44
  34.8 0.0 copy-done
  34.8 1.3 %shard_map.129 = (f32[8,128,128]{2,1,0:T(8,128)S(1)}, bf16[8,128,128]{2,1,0:T(8,128)(2,1)S(1)}, bf16[16,32,128]{2,1,0:T(8,128)(2,1)S(1)}) custom-call(bf16[16,64,128]{2,1,0:T(8,128)(2,1)S(1)} %all_to_all.16.returned, f32[8,128,128]{2,1,0:T(8,128)S(1)} %get-tuple-element.18.gate, bf16[8,128,128]{2,1,0:T(8,128)(2,1)S(1)} %copy-done, ...), custom_call_target="tpu_custom_call" | custom-call | flops 33554432 | bytes 1082368 | tf_op jit(solution)/shard_map/pallas_call | solution.py:271
  36.1 10.2 %all_to_all.17.refs_1_ = bf16[16,32,128]{2,1,0:T(8,128)(2,1)S(1)} all-to-all(bf16[16,32,128]{2,1,0:T(8,128)(2,1)S(1)} %get-tuple-element.27), channel_id=1, replica_groups={{11,15,14,13,12,10,9,8,7,6,5,4,3,2,1,0},{27,31,30,29,28,26,25,24,23,22,..., dimensions={0} | all-to-all | bytes 262144 | tf_op jit(solution)/shard_map/all_to_all | solution.py:44
  46.3 2.5 %shard_map.130 = bf16[8,128,128]{2,1,0:T(8,128)(2,1)} custom-call(bf16[8,128,128]{2,1,0:T(8,128)(2,1)S(1)} %get-tuple-element.21.att_norm, bf16[128,128]{1,0:T(8,128)(2,1)S(1)} %get-tuple-element.22.w_query, bf16[128,128]{1,0:T(8,128)(2,1)S(1)} %get-tuple-element.23.w_key, bf16[128,128]{1,0:T(8,128)(2,1)S(1)} %get-tuple-element.24.w_value, ...), custom_call_target="tpu_custom_call" | custom-call | flops 201326592 | bytes 1081344 | tf_op jit(solution)/shard_map/pallas_call | solution.py:271
Async XLA Ops:
  23.3 11.6 %copy-start = (bf16[8,128,128]{2,1,0:T(8,128)(2,1)S(1)}, bf16[8,128,128]{2,1,0:T(8,128)(2,1)}, u32[]{:S(2)}) copy-start(bf16[8,128,128]{2,1,0:T(8,128)(2,1)} %pair.1) | copy-start | bytes 786436

commit v8 on v7

--- a/solution.py
+++ b/solution.py
@@ -31,32 +31,36 @@
     return weight.astype(F32).T.astype(BF16)
 
 
-def listing(ranks):
-    first = ranks - 1 - ranks // 4
-    return [first] + [rank for rank in range(ranks - 1, -1, -1) if rank != first]
-
-
-def slot(rank, ranks):
-    return listing(ranks).index(rank)
-
-
-def swap(blocks):
+def listing(step, ranks):
+    first, order = {
+        "edges": (5 * ranks // 8, -1),
+        "triangle": (ranks - 1 - ranks // 4, 1),
+        "bias": (ranks // 2 - 1, -1),
+    }[step]
+    return [first] + [rank for rank in range(ranks)[::order] if rank != first]
+
+
+def slot(step, rank, ranks):
+    return listing(step, ranks).index(rank)
+
+
+def swap(step, blocks):
     return lax.all_to_all(
         blocks,
         "row",
         split_axis=0,
         concat_axis=0,
-        axis_index_groups=[listing(blocks.shape[0])],
+        axis_index_groups=[listing(step, blocks.shape[0])],
         tiled=True,
     )
 
 
-def by_rank(blocks):
-    return blocks[np.array([slot(r, blocks.shape[0]) for r in range(blocks.shape[0])])]
-
-
-def by_slot(blocks):
-    return blocks[np.array(listing(blocks.shape[0]))]
+def by_rank(step, blocks):
+    return blocks[np.array([slot(step, r, blocks.shape[0]) for r in range(blocks.shape[0])])]
+
+
+def by_slot(step, blocks):
+    return blocks[np.array(listing(step, blocks.shape[0]))]
 
 
 def lane_tiles(values):
@@ -104,7 +108,7 @@
     owners, block = out.shape[0], out.shape[1]
     for owner in range(owners):
         for tile, lanes in lane_tiles(pair):
-            out[slot(owner, owners), :, lanes] = held[tile, owner * block : (owner + 1) * block, :].astype(BF16)
+            out[slot("edges", owner, owners), :, lanes] = held[tile, owner * block : (owner + 1) * block, :].astype(BF16)
     for copy in copies[6:]:
         copy.wait()
 
@@ -113,7 +117,7 @@
     sides = [[], []]
     sources = edges.shape[0]
     for source in range(sources):
-        block = edges[slot(source, sources), channel * 2 * rows : (channel + 1) * 2 * rows, :].astype(F32)
+        block = edges[slot("edges", source, sources), channel * 2 * rows : (channel + 1) * 2 * rows, :].astype(F32)
         sides[0].append(block[:rows])
         sides[1].append(block[rows:])
     return [jnp.concatenate(side, axis=0).astype(BF16) for side in sides]
@@ -125,7 +129,7 @@
         owners = out.shape[0]
         for owner in range(owners):
             mine = slice(owner * rows, (owner + 1) * rows)
-            out[slot(owner, owners), pair_of * rows : (pair_of + 2) * rows, :] = jnp.concatenate(
+            out[slot("triangle", owner, owners), pair_of * rows : (pair_of + 2) * rows, :] = jnp.concatenate(
                 [p[mine] for p in products], axis=0
             ).astype(BF16)
 
@@ -147,7 +151,8 @@
     average = total / channels
     square = jnp.zeros((rows, cols), F32)
     for owner in range(owners):
-        centered = returned[slot(owner, owners)].astype(F32).reshape(block // rows, rows, cols) - average
+        block_now = returned[slot("triangle", owner, owners)].astype(F32)
+        centered = block_now.reshape(block // rows, rows, cols) - average
         square += jnp.sum(centered * centered, axis=0)
         for tile, lanes in lane_tiles(pair):
             held[tile, owner * block : (owner + 1) * block, :] = centered.reshape(block, cols)[:, lanes]
@@ -252,7 +257,7 @@
 
     for head, (_, span) in enumerate(heads):
         parts = [
-            bias[slot(owner, bias.shape[0])].astype(F32)[head * head_rows : (head + 1) * head_rows]
+            bias[slot("bias", owner, bias.shape[0])].astype(F32)[head * head_rows : (head + 1) * head_rows]
             for owner in range(bias.shape[0])
         ]
         bias_t[:, span] = jnp.concatenate(parts, axis=0).T * LOG2_E
@@ -333,7 +338,7 @@
         w_bias.T,
         fetched=13,
     )
-    spread = swap(edges)
+    spread = swap("edges", edges)
     flops = 2 * own * residues * residues * cols
     if col_parts == 1:
         summed = call(
@@ -352,9 +357,9 @@
             spread,
         )
         summed = lax.psum_scatter(partial_sums, "col", scatter_dimension=2, tiled=True).astype(BF16)
-        summed = by_slot(summed.reshape(own, owners, rows, cols).swapaxes(0, 1))
+        summed = by_slot("triangle", summed.reshape(own, owners, rows, cols).swapaxes(0, 1))
         summed = summed.reshape(owners, own * rows, cols)
-    returned = swap(summed)
+    returned = swap("triangle", summed)
     first_pass, att_norm, bias_copies = call(
         update_kernel,
         [
@@ -374,7 +379,7 @@
         w_tri_out,
         w_bias_t,
     )
-    bias = swap(bias_copies)
+    bias = swap("bias", bias_copies)
     projected = [
         ((rows, width, cols), BF16),
         ((rows, cols, width), BF16),
@@ -396,7 +401,9 @@
         given = (first_pass, bias, w_att_out)
         return call(whole_kernel, out, projected + held, flops, *projecting, *given)
     query_t, key, value_t, gate_t = call(project_kernel, projected, [], project_flops, *projecting)
-    bias = by_slot(lax.all_to_all(by_rank(bias), "col", split_axis=0, concat_axis=2, tiled=True))
+    bias = by_slot(
+        "bias", lax.all_to_all(by_rank("bias", bias), "col", split_axis=0, concat_axis=2, tiled=True)
+    )
     key = lax.all_gather(key, "col", axis=1, tiled=True)
     value_t = lax.all_gather(value_t, "col", axis=2, tiled=True)
     given = (query_t, key, value_t, gate_t, first_pass, bias, w_att_out)

time: 49.1 us -> 50 us (1.018)
  blocking collectives: 42.3 us -> 43.3 us
    all_to_all x3, blocking collectives: 42.3 us -> 43.3 us  [swap(): lax.all_to_all(blocks, 'row', split_axis=0, concat_axis=0, axis_index_gro...]
where the time goes in v8:
time: 50 us; the launch traced here: 49.8 us
  blocking collectives  43.3 us (87%)
  Pallas kernels  6.48 us (13%)
    all_to_all x3, blocking collectives, swap(): lax.all_to_all(blocks, 'row', split_axis=0, concat_axis=0, axis_index_gro...  43.3 us
    pallas_call x4, Pallas kernels, call(): pl.pallas_call(kernel, out_shape=shapes, in_specs=[far] * fetched + [vmem...  6.48 us

profile of v8, /device:TPU:0, one launch (start us, length us, event | category | flops | bytes accessed | tf_op | source)
XLA Modules:
  0.0 49.8 jit_solution(6328549079844797787)
XLA Ops:
  0.0 2.3 %shard_map.127 = (bf16[16,128,128]{2,1,0:T(8,128)(2,1)S(1)}, f32[8,128,128]{2,1,0:T(8,128)S(1)}, bf16[128,128]{1,0:T(8,128)(2,1)S(1)}, bf16[128,128]{1,0:T(8,128...) custom-call(bf16[8,128,128]{2,1,0:T(8,128)(2,1)} %pair.1, ...), custom_call_target="tpu_custom_call" | custom-call | flops 167772160 | bytes 623616 | tf_op jit(solution)/shard_map/pallas_call | solution.py:276
  2.4 21.3 %all_to_all.15.edges = bf16[16,128,128]{2,1,0:T(8,128)(2,1)S(1)} all-to-all(bf16[16,128,128]{2,1,0:T(8,128)(2,1)S(1)} %get-tuple-element.17), channel_id=1, replica_groups={{10,15,14,13,12,11,9,8,7,6,5,4,3,2,1,0},{26,31,30,29,28,27,25,24,23,22,..., dimensions={0} | all-to-all | bytes 1048576 | tf_op jit(solution)/shard_map/all_to_all | solution.py:48
  23.6 0.3 shard_map.128
  23.9 0.0 copy-start
  23.9 11.3 %all_to_all.16.returned = bf16[16,64,128]{2,1,0:T(8,128)(2,1)S(1)} all-to-all(bf16[16,64,128]{2,1,0:T(8,128)(2,1)S(1)} %shard_map.128), channel_id=1, replica_groups={{11,0,1,2,3,4,5,6,7,8,9,10,12,13,14,15},{27,16,17,18,19,20,21,22,23,24,..., dimensions={0} | all-to-all | bytes 524288 | tf_op jit(solution)/shard_map/all_to_all | solution.py:48
  35.2 0.0 copy-done
  35.2 1.3 %shard_map.129 = (f32[8,128,128]{2,1,0:T(8,128)S(1)}, bf16[8,128,128]{2,1,0:T(8,128)(2,1)S(1)}, bf16[16,32,128]{2,1,0:T(8,128)(2,1)S(1)}) custom-call(bf16[16,64,128]{2,1,0:T(8,128)(2,1)S(1)} %all_to_all.16.returned, f32[8,128,128]{2,1,0:T(8,128)S(1)} %get-tuple-element.18.gate, bf16[8,128,128]{2,1,0:T(8,128)(2,1)S(1)} %copy-done, ...), custom_call_target="tpu_custom_call" | custom-call | flops 33554432 | bytes 1082368 | tf_op jit(solution)/shard_map/pallas_call | solution.py:276
  36.5 10.8 %all_to_all.17.refs_1_ = bf16[16,32,128]{2,1,0:T(8,128)(2,1)S(1)} all-to-all(bf16[16,32,128]{2,1,0:T(8,128)(2,1)S(1)} %get-tuple-element.27), channel_id=1, replica_groups={{7,15,14,13,12,11,10,9,8,6,5,4,3,2,1,0},{23,31,30,29,28,27,26,25,24,22,..., dimensions={0} | all-to-all | bytes 262144 | tf_op jit(solution)/shard_map/all_to_all | solution.py:48
  47.3 2.5 %shard_map.130 = bf16[8,128,128]{2,1,0:T(8,128)(2,1)} custom-call(bf16[8,128,128]{2,1,0:T(8,128)(2,1)S(1)} %get-tuple-element.21.att_norm, bf16[128,128]{1,0:T(8,128)(2,1)S(1)} %get-tuple-element.22.w_query, bf16[128,128]{1,0:T(8,128)(2,1)S(1)} %get-tuple-element.23.w_key, bf16[128,128]{1,0:T(8,128)(2,1)S(1)} %get-tuple-element.24.w_value, ...), custom_call_target="tpu_custom_call" | custom-call | flops 201326592 | bytes 1081344 | tf_op jit(solution)/shard_map/pallas_call | solution.py:276
Async XLA Ops:
  23.9 11.3 %copy-start = (bf16[8,128,128]{2,1,0:T(8,128)(2,1)S(1)}, bf16[8,128,128]{2,1,0:T(8,128)(2,1)}, u32[]{:S(2)}) copy-start(bf16[8,128,128]{2,1,0:T(8,128)(2,1)} %pair.1) | copy-start | bytes 786436

commit v9 on v7

--- a/solution.py
+++ b/solution.py
@@ -27,8 +27,11 @@
     return 0.5 * jnp.tanh(0.5 * values) + 0.5
 
 
-def flipped(weight):
-    return weight.astype(F32).T.astype(BF16)
+def twice(weight):
+    zeros = jnp.zeros_like(weight)
+    return jnp.concatenate(
+        [jnp.concatenate([weight, zeros], axis=1), jnp.concatenate([zeros, weight], axis=1)], axis=0
+    )
 
 
 def listing(ranks):
@@ -70,11 +73,15 @@
     return (centered * lax.rsqrt(variance + 1e-05)).astype(BF16)
 
 
+def side_by_side(held, i):
+    return jnp.concatenate([held[i], held[i + 1]], axis=1)
+
+
 def pipeline(rows, *steps):
-    for tick in range(rows + len(steps) - 1):
+    for tick in range(len(rows) + len(steps) - 1):
         for late, step in enumerate(steps):
-            if 0 <= tick - late < rows:
-                step(tick - late)
+            if 0 <= tick - late < len(rows):
+                step(rows[tick - late])
 
 
 def edges_kernel(*refs):
@@ -88,19 +95,30 @@
         copy.start()
     for copy in copies[:6]:
         copy.wait()
-    rows = pair.shape[0]
+    rows, width = pair.shape[0], pair.shape[2]
     channels = weights.shape[2]
-    turned = jnp.concatenate([flipped(weights[n]) for n in range(4)], axis=0)
-    for i in range(rows):
+    cols = pair.shape[1]
+    turned = jnp.concatenate([weights[n].T for n in range(4)], axis=0)
+    gate_weight = twice(weights[4])
+
+    def norm(i):
         normed[i] = lane_norm(pair[i].astype(F32))
-    for i in range(rows):
-        both = dot(turned, normed[i], NT)
+        normed[i + 1] = lane_norm(pair[i + 1].astype(F32))
+
+    def project(i):
+        both = dot(turned, jnp.concatenate([normed[i], normed[i + 1]], axis=0), NT)
         for side in range(2):
             base = 2 * side * channels
             act = sigmoid(both[base + channels : base + 2 * channels]) * both[base : base + channels]
             for tile, lanes in lane_tiles(act):
-                held[tile, pl.ds(side * rows + i, channels, stride=2 * rows), :] = act[:, lanes]
-        gate[i] = sigmoid(dot(normed[i], weights[4]))
+                row, part = divmod(tile, cols // LANES)
+                place = pl.ds(side * rows + i + row, channels, stride=2 * rows)
+                held[part, place, :] = act[:, lanes]
+        opened = sigmoid(dot(side_by_side(normed, i), gate_weight))
+        gate[i] = opened[:, :width]
+        gate[i + 1] = opened[:, width:]
+
+    pipeline(range(0, rows, 2), norm, project)
     owners, block = out.shape[0], out.shape[1]
     for owner in range(owners):
         for tile, lanes in lane_tiles(pair):
@@ -138,7 +156,7 @@
 def update_kernel(
     returned, gate, pair, w_tri_out, w_bias_t, first_pass, att_norm, bias, held, bias_held, turned
 ):
-    rows, cols = pair.shape[0], pair.shape[1]
+    rows, cols, width = pair.shape
     owners, block = returned.shape[0], returned.shape[1]
     channels = owners * block // rows
     total = jnp.zeros((rows, cols), F32)
@@ -153,46 +171,59 @@
             held[tile, owner * block : (owner + 1) * block, :] = centered.reshape(block, cols)[:, lanes]
     scale = lax.rsqrt(square / channels + 1e-05)
 
+    weight = twice(w_tri_out[...])
+
     def turn(i):
-        tri_norm = jnp.concatenate(
-            [held[tile, pl.ds(i, channels, stride=rows), :] for tile, _ in lane_tiles(pair)], axis=1
-        )
-        turned[i % 2] = (tri_norm * scale[i : i + 1]).T.astype(BF16)
+        for row in (i, i + 1):
+            tri_norm = jnp.concatenate(
+                [held[tile, pl.ds(row, channels, stride=rows), :] for tile, _ in lane_tiles(pair)], axis=1
+            )
+            turned[row % 4] = (tri_norm * scale[row : row + 1]).astype(BF16).T
 
     def update(i):
-        first_pass[i] = pair[i].astype(F32) + gate[i] * dot(turned[i % 2], w_tri_out[...])
+        both = dot(side_by_side(turned, i % 4), weight)
+        first_pass[i] = pair[i].astype(F32) + gate[i] * both[:, :width]
+        first_pass[i + 1] = pair[i + 1].astype(F32) + gate[i + 1] * both[:, width:]
 
     def norm(i):
-        att_norm[i] = lane_norm(first_pass[i])
+        for row in (i, i + 1):
+            att_norm[row] = lane_norm(first_pass[row])
 
     def project_bias(i):
-        row_bias = dot(w_bias_t[...], att_norm[i], NT)
-        for head in range(HEADS):
-            bias_held[head * rows + i : head * rows + i + 1, :] = row_bias[head : head + 1]
-
-    pipeline(rows, turn, update, norm, project_bias)
+        both = dot(w_bias_t[...], jnp.concatenate([att_norm[i], att_norm[i + 1]], axis=0), NT)
+        for row in range(2):
+            for head in range(HEADS):
+                place = head * rows + i + row
+                bias_held[place : place + 1, :] = both[head : head + 1, row * cols : (row + 1) * cols]
+
+    pipeline(range(0, rows, 2), turn, update, norm, project_bias)
     rounded = bias_held[...].astype(BF16)
     for owner in range(bias.shape[0]):
         bias[owner] = rounded
 
 
 def projector(att_norm, w_query, w_key, w_value, w_att_gate, query_t, key, value_t, gate_t):
-    w_turned = jnp.concatenate([flipped(w[...]) for w in (w_query, w_value, w_att_gate)], axis=0)
-    width = w_query.shape[1]
+    w_turned = jnp.concatenate([w[...].T for w in (w_query, w_value, w_att_gate)], axis=0)
+    w_direct = twice(w_key[...])
+    cols, width = att_norm.shape[1], w_query.shape[1]
 
     def project(i):
-        normed = att_norm[i]
-        key[i] = dot(normed, w_key[...]).astype(BF16)
-        turned = dot(w_turned, normed, NT)
-        query_t[i] = turned[:width].astype(BF16)
-        value_t[i] = turned[width : 2 * width].astype(BF16)
-        gate_t[i] = sigmoid(turned[2 * width :])
+        if i % 2:
+            return
+        keys = dot(side_by_side(att_norm, i), w_direct).astype(BF16)
+        turned = dot(w_turned, jnp.concatenate([att_norm[i], att_norm[i + 1]], axis=0), NT)
+        for row in range(2):
+            key[i + row] = keys[:, row * width : (row + 1) * width]
+            mine = turned[:, row * cols : (row + 1) * cols]
+            query_t[i + row] = mine[:width].astype(BF16)
+            value_t[i + row] = mine[width : 2 * width].astype(BF16)
+            gate_t[i + row] = sigmoid(mine[2 * width :])
 
     return project
 
 
 def project_kernel(*refs):
-    pipeline(refs[0].shape[0], projector(*refs))
+    pipeline(range(refs[0].shape[0]), projector(*refs))
 
 
 def whole_kernel(att_norm, w_query, w_key, w_value, w_att_gate, *refs):
@@ -233,30 +264,45 @@
             blocks.append(jnp.concatenate(parts, axis=0))
         scores[i % 2] = dot(key[i], jnp.concatenate(blocks, axis=1)) * score_scale
 
+    def turn_bias():
+        for head, (_, span) in enumerate(heads):
+            parts = [
+                bias[slot(owner, bias.shape[0])].astype(F32)[head * head_rows : (head + 1) * head_rows]
+                for owner in range(bias.shape[0])
+            ]
+            bias_t[:, span] = jnp.concatenate(parts, axis=0).T * LOG2_E
+
     def soften(i):
+        if i == 0:
+            turn_bias()
         for _, span in heads:
             biased = scores[i % 2, :, span] + bias_t[:, span]
             peak = jnp.max(biased, axis=0, keepdims=True)
             weights[i % 2, :, span] = jnp.exp2(biased - peak).astype(BF16)
 
     def collect(i):
-        for mine, span in heads:
-            values = jnp.concatenate([value_t[i, mine, :], ones], axis=0)
-            summed = dot(values, weights[i % 2, :, span])
-            share = 1.0 / summed[HEAD_DIM : HEAD_DIM + 1]
-            gated[i % 2, mine, :] = summed[:HEAD_DIM] * share * gate_t[i, mine, :]
+        for head in range(0, HEADS, 2):
+            (first, left), (second, right) = heads[head : head + 2]
+            values = jnp.concatenate([value_t[i, first.start : second.stop, :], ones], axis=0)
+            summed = dot(values, weights[i % 2, :, left.start : right.stop])
+            share = 1.0 / summed[2 * HEAD_DIM : 2 * HEAD_DIM + 1]
+            for mine, there, lanes in (
+                (first, slice(0, HEAD_DIM), slice(0, cols)),
+                (second, slice(HEAD_DIM, 2 * HEAD_DIM), slice(cols, 2 * cols)),
+            ):
+                attended = summed[there, lanes] * share[:, lanes] * gate_t[i, mine, :]
+                gated[i % 4, mine, :] = attended.astype(BF16)
 
     def finish(i):
-        turned = gated[i % 2].T.astype(BF16)
-        out[i] = (first_pass[i] + dot(turned, w_att_out[...])).astype(BF16)
-
-    for head, (_, span) in enumerate(heads):
-        parts = [
-            bias[slot(owner, bias.shape[0])].astype(F32)[head * head_rows : (head + 1) * head_rows]
-            for owner in range(bias.shape[0])
-        ]
-        bias_t[:, span] = jnp.concatenate(parts, axis=0).T * LOG2_E
-    pipeline(rows, *before, score, soften, collect, finish)
+        if i % 2 == 0:
+            return
+        turned = jnp.concatenate([gated[(i - 1) % 4].T, gated[i % 4].T], axis=1)
+        both = dot(turned, w_last)
+        out[i - 1] = (first_pass[i - 1] + both[:, :width]).astype(BF16)
+        out[i] = (first_pass[i] + both[:, width:]).astype(BF16)
+
+    w_last = twice(w_att_out[...])
+    pipeline(range(rows), *before, score, soften, collect, finish)
 
 
 def call(kernel, outs, scratch, flops, *operands, fetched=0):
@@ -365,7 +411,7 @@
         [
             ((cols // LANES, channels * rows, LANES), F32),
             ((HEADS * rows, cols), F32),
-            ((2, cols, channels), BF16),
+            ((4, cols, channels), BF16),
         ],
         2 * cells * channels * width,
         returned,
@@ -388,7 +434,7 @@
         ((residues, HEADS * cols), F32),
         ((2, residues, HEADS * cols), F32),
         ((2, residues, HEADS * cols), BF16),
-        ((2, width, cols), F32),
+        ((4, width, cols), BF16),
     ]
     project_flops, attend_flops = 8 * cells * width * width, 4 * cells * residues * width
     if col_parts == 1:

time: 49.1 us -> 48.4 us (0.986)
  Pallas kernels: 6.49 us -> 5.78 us
    pallas_call x4, Pallas kernels: 6.49 us -> 5.78 us  [call(): pl.pallas_call(kernel, out_shape=shapes, in_specs=[far] * fetched + [vmem...]
where the time goes in v9:
time: 48.4 us; the launch traced here: 48.2 us
  blocking collectives  42.3 us (87%)
  Pallas kernels  5.78 us (12%)
    all_to_all x3, blocking collectives, swap(): lax.all_to_all(blocks, 'row', split_axis=0, concat_axis=0, axis_index_gro...  42.3 us
    pallas_call x4, Pallas kernels, call(): pl.pallas_call(kernel, out_shape=shapes, in_specs=[far] * fetched + [vmem...  5.78 us

profile of v9, /device:TPU:0, one launch (start us, length us, event | category | flops | bytes accessed | tf_op | source)
XLA Modules:
  0.0 48.2 jit_solution(1843220703000619826)
XLA Ops:
  0.0 2.1 %shard_map.127 = (bf16[16,128,128]{2,1,0:T(8,128)(2,1)S(1)}, f32[8,128,128]{2,1,0:T(8,128)S(1)}, bf16[128,128]{1,0:T(8,128)(2,1)S(1)}, bf16[128,128]{1,0:T(8,128...) custom-call(bf16[8,128,128]{2,1,0:T(8,128)(2,1)} %pair.1, ...), custom_call_target="tpu_custom_call" | custom-call | flops 167772160 | bytes 623616 | tf_op jit(solution)/shard_map/pallas_call | solution.py:317
  2.1 20.6 %all_to_all.15.edges = bf16[16,128,128]{2,1,0:T(8,128)(2,1)S(1)} all-to-all(bf16[16,128,128]{2,1,0:T(8,128)(2,1)S(1)} %get-tuple-element.17), channel_id=1, replica_groups={{11,15,14,13,12,10,9,8,7,6,5,4,3,2,1,0},{27,31,30,29,28,26,25,24,23,22,..., dimensions={0} | all-to-all | bytes 1048576 | tf_op jit(solution)/shard_map/all_to_all | solution.py:47
  22.8 0.3 shard_map.128
  23.1 0.0 copy-start
  23.1 11.6 %all_to_all.16.returned = bf16[16,64,128]{2,1,0:T(8,128)(2,1)S(1)} all-to-all(bf16[16,64,128]{2,1,0:T(8,128)(2,1)S(1)} %shard_map.128), channel_id=1, replica_groups={{11,15,14,13,12,10,9,8,7,6,5,4,3,2,1,0},{27,31,30,29,28,26,25,24,23,22,..., dimensions={0} | all-to-all | bytes 524288 | tf_op jit(solution)/shard_map/all_to_all | solution.py:47
  34.6 0.0 copy-done
  34.6 0.9 %shard_map.129 = (f32[8,128,128]{2,1,0:T(8,128)S(1)}, bf16[8,128,128]{2,1,0:T(8,128)(2,1)S(1)}, bf16[16,32,128]{2,1,0:T(8,128)(2,1)S(1)}) custom-call(bf16[16,64,128]{2,1,0:T(8,128)(2,1)S(1)} %all_to_all.16.returned, f32[8,128,128]{2,1,0:T(8,128)S(1)} %get-tuple-element.18.gate, bf16[8,128,128]{2,1,0:T(8,128)(2,1)S(1)} %copy-done, ...), custom_call_target="tpu_custom_call" | custom-call | flops 33554432 | bytes 1082368 | tf_op jit(solution)/shard_map/pallas_call | solution.py:317
  35.5 10.2 %all_to_all.17.refs_1_ = bf16[16,32,128]{2,1,0:T(8,128)(2,1)S(1)} all-to-all(bf16[16,32,128]{2,1,0:T(8,128)(2,1)S(1)} %get-tuple-element.27), channel_id=1, replica_groups={{11,15,14,13,12,10,9,8,7,6,5,4,3,2,1,0},{27,31,30,29,28,26,25,24,23,22,..., dimensions={0} | all-to-all | bytes 262144 | tf_op jit(solution)/shard_map/all_to_all | solution.py:47
  45.7 2.4 %shard_map.130 = bf16[8,128,128]{2,1,0:T(8,128)(2,1)} custom-call(bf16[8,128,128]{2,1,0:T(8,128)(2,1)S(1)} %get-tuple-element.21.att_norm, bf16[128,128]{1,0:T(8,128)(2,1)S(1)} %get-tuple-element.22.w_query, bf16[128,128]{1,0:T(8,128)(2,1)S(1)} %get-tuple-element.23.w_key, bf16[128,128]{1,0:T(8,128)(2,1)S(1)} %get-tuple-element.24.w_value, ...), custom_call_target="tpu_custom_call" | custom-call | flops 201326592 | bytes 1081344 | tf_op jit(solution)/shard_map/pallas_call | solution.py:317
Async XLA Ops:
  23.1 11.6 %copy-start = (bf16[8,128,128]{2,1,0:T(8,128)(2,1)S(1)}, bf16[8,128,128]{2,1,0:T(8,128)(2,1)}, u32[]{:S(2)}) copy-start(bf16[8,128,128]{2,1,0:T(8,128)(2,1)} %pair.1) | copy-start | bytes 786436

commit v10 on v9

--- a/solution.py
+++ b/solution.py
@@ -43,14 +43,12 @@
     return listing(ranks).index(rank)
 
 
-def swap(blocks):
+def swap(blocks, ranks):
+    members = blocks.shape[0]
+    order = listing(members)
+    groups = [[first + member for member in order] for first in range(0, ranks, members)]
     return lax.all_to_all(
-        blocks,
-        "row",
-        split_axis=0,
-        concat_axis=0,
-        axis_index_groups=[listing(blocks.shape[0])],
-        tiled=True,
+        blocks, "row", split_axis=0, concat_axis=0, axis_index_groups=groups, tiled=True
     )
 
 
@@ -85,7 +83,8 @@
 
 
 def edges_kernel(*refs):
-    given, (out, gate, *staged), (pair, weights, normed, held, sems) = refs[:13], refs[13:22], refs[22:]
+    given, (left, right, gate, *staged) = refs[:13], refs[13:23]
+    pair, weights, normed, held, sems = refs[23:]
     targets = [pair, *(weights.at[n] for n in range(5)), *staged]
     copies = [
         pltpu.make_async_copy(source, target, sems.at[n])
@@ -112,45 +111,51 @@
             act = sigmoid(both[base + channels : base + 2 * channels]) * both[base : base + channels]
             for tile, lanes in lane_tiles(act):
                 row, part = divmod(tile, cols // LANES)
-                place = pl.ds(side * rows + i + row, channels, stride=2 * rows)
-                held[part, place, :] = act[:, lanes]
+                held[part, side, pl.ds(i + row, channels, stride=rows), :] = act[:, lanes]
         opened = sigmoid(dot(side_by_side(normed, i), gate_weight))
         gate[i] = opened[:, :width]
         gate[i + 1] = opened[:, width:]
 
     pipeline(range(0, rows, 2), norm, project)
-    owners, block = out.shape[0], out.shape[1]
-    for owner in range(owners):
+    half, block = left.shape[0], left.shape[1]
+    for member in range(half):
+        mine = slice(member * block, (member + 1) * block)
         for tile, lanes in lane_tiles(pair):
-            out[slot(owner, owners), :, lanes] = held[tile, owner * block : (owner + 1) * block, :].astype(BF16)
+            left[slot(member, half), :, lanes] = held[tile, 0, mine, :].astype(BF16)
+            sent = held[tile, 1, mine, :].astype(BF16)
+            for owner in range(member, right.shape[0], half):
+                right[slot(owner, right.shape[0]), :, lanes] = sent
     for copy in copies[6:]:
         copy.wait()
 
 
-def triangle_sides(edges, rows, channel):
-    sides = [[], []]
+def channel_rows(edges, rows, channel):
     sources = edges.shape[0]
-    for source in range(sources):
-        block = edges[slot(source, sources), channel * 2 * rows : (channel + 1) * 2 * rows, :].astype(F32)
-        sides[0].append(block[:rows])
-        sides[1].append(block[rows:])
-    return [jnp.concatenate(side, axis=0).astype(BF16) for side in sides]
-
-
-def triangle_kernel(rows, edges, out):
-    for pair_of in range(0, out.shape[1] // rows, 2):
-        products = [dot(*triangle_sides(edges, rows, pair_of + o), NT) for o in range(2)]
-        owners = out.shape[0]
+    mine = slice(channel * rows, (channel + 1) * rows)
+    both = slice(channel // 2 * 2 * rows, (channel // 2 + 1) * 2 * rows)
+    inner = slice(mine.start - both.start, mine.stop - both.start)
+    parts = [edges[slot(r, sources), both, :].astype(F32)[inner] for r in range(sources)]
+    return jnp.concatenate(parts, axis=0).astype(BF16)
+
+
+def triangle_product(left, right, rows, channel):
+    return dot(channel_rows(left, rows, channel), channel_rows(right, rows, channel), NT)
+
+
+def triangle_kernel(rows, left, right, out):
+    owners = out.shape[0]
+    for channel in range(0, out.shape[1] // rows, 2):
+        products = [triangle_product(left, right, rows, channel + o) for o in range(2)]
         for owner in range(owners):
             mine = slice(owner * rows, (owner + 1) * rows)
-            out[slot(owner, owners), pair_of * rows : (pair_of + 2) * rows, :] = jnp.concatenate(
+            out[slot(owner, owners), channel * rows : (channel + 2) * rows, :] = jnp.concatenate(
                 [p[mine] for p in products], axis=0
             ).astype(BF16)
 
 
-def partial_kernel(rows, edges, out):
+def partial_kernel(rows, left, right, out):
     for channel in range(out.shape[0]):
-        out[channel] = dot(*triangle_sides(edges, rows, channel), NT)
+        out[channel] = triangle_product(left, right, rows, channel)
 
 
 def update_kernel(
@@ -344,14 +349,16 @@
     rows, cols, width = pair_rep.shape
     channels = w_left.shape[1]
     owners, col_parts = lax.axis_size("row"), lax.axis_size("col")
-    own = channels // owners
+    half = owners // 2
+    own = channels // half
     residues = owners * rows
     cells = rows * cols
 
-    edges, gate, w_tri_out, w_query, w_key, w_value, w_att_gate, w_att_out, w_bias_t = call(
+    left, right, gate, w_tri_out, w_query, w_key, w_value, w_att_gate, w_att_out, w_bias_t = call(
         edges_kernel,
         [
-            ((owners, own * 2 * rows, cols), BF16),
+            ((half, own * rows, cols), BF16),
+            ((owners, own * rows, cols), BF16),
             ((rows, cols, width), F32),
             *[(w.shape, BF16) for w in (w_tri_out, w_query, w_key, w_value, w_att_gate, w_att_out)],
             (w_bias.shape[::-1], BF16),
@@ -360,7 +367,7 @@
             (pair_rep.shape, BF16),
             ((5, width, channels), BF16),
             (pair_rep.shape, BF16),
-            ((cols // LANES, channels * 2 * rows, LANES), F32),
+            ((cols // LANES, 2, channels * rows, LANES), F32),
             pltpu.SemaphoreType.DMA((13,)),
         ],
         10 * cells * width * channels,
@@ -379,28 +386,31 @@
         w_bias.T,
         fetched=13,
     )
-    spread = swap(edges)
-    flops = 2 * own * residues * residues * cols
+    right = swap(right, owners)
+    left = swap(left, owners)
+    flops = 2 * own * half * rows * residues * cols
     if col_parts == 1:
         summed = call(
             functools.partial(triangle_kernel, rows),
-            [((owners, own * rows, residues), BF16)],
+            [((half, own * rows, residues), BF16)],
             [],
             flops,
-            spread,
+            left,
+            right,
         )
     else:
         partial_sums = call(
             functools.partial(partial_kernel, rows),
-            [((own, residues, residues), F32)],
+            [((own, half * rows, residues), F32)],
             [],
             flops,
-            spread,
+            left,
+            right,
         )
         summed = lax.psum_scatter(partial_sums, "col", scatter_dimension=2, tiled=True).astype(BF16)
-        summed = by_slot(summed.reshape(own, owners, rows, cols).swapaxes(0, 1))
-        summed = summed.reshape(owners, own * rows, cols)
-    returned = swap(summed)
+        summed = by_slot(summed.reshape(own, half, rows, cols).swapaxes(0, 1))
+        summed = summed.reshape(half, own * rows, cols)
+    returned = swap(summed, owners)
     first_pass, att_norm, bias_copies = call(
         update_kernel,
         [
@@ -420,7 +430,7 @@
         w_tri_out,
         w_bias_t,
     )
-    bias = swap(bias_copies)
+    bias = swap(bias_copies, owners)
     projected = [
         ((rows, width, cols), BF16),
         ((rows, cols, width), BF16),

time: 48.4 us -> 54.5 us (1.13)
  blocking collectives: 42.3 us -> 48.4 us
    all_to_all x3 -> x4, blocking collectives: 42.3 us -> 48.4 us  [swap(): lax.all_to_all(blocks, 'row', split_axis=0, concat_axis=0, axis_index_gro...]
where the time goes in v10:
time: 54.5 us; the launch traced here: 54.3 us
  blocking collectives  48.4 us (89%)
  Pallas kernels  5.84 us (11%)
    all_to_all x4, blocking collectives, swap(): lax.all_to_all(blocks, 'row', split_axis=0, concat_axis=0, axis_index_gro...  48.4 us
    pallas_call x4, Pallas kernels, call(): pl.pallas_call(kernel, out_shape=shapes, in_specs=[far] * fetched + [vmem...  5.84 us

profile of v10, /device:TPU:0, one launch (start us, length us, event | category | flops | bytes accessed | tf_op | source)
XLA Modules:
  0.0 54.3 jit_solution(13803038583844313166)
XLA Ops:
  0.0 2.0 %shard_map.127 = (bf16[8,128,128]{2,1,0:T(8,128)(2,1)S(1)}, bf16[16,128,128]{2,1,0:T(8,128)(2,1)S(1)}, f32[8,128,128]{2,1,0:T(8,128)S(1)}, bf16[128,128]{1,0:T(8...) custom-call(bf16[8,128,128]{2,1,0:T(8,128)(2,1)} %pair.1, ...), custom_call_target="tpu_custom_call" | custom-call | flops 167772160 | bytes 623616 | tf_op jit(solution)/shard_map/pallas_call | solution.py:322
  2.0 11.2 %all_to_all.20.left = bf16[8,128,128]{2,1,0:T(8,128)(2,1)S(1)} all-to-all(bf16[8,128,128]{2,1,0:T(8,128)(2,1)S(1)} %get-tuple-element.18), channel_id=1, replica_groups={{5,7,6,4,3,2,1,0},{13,15,14,12,11,10,9,8},{21,23,22,20,19,18,17,16},{29..., dimensions={0} | all-to-all | bytes 524288 | tf_op jit(solution)/shard_map/all_to_all | solution.py:50
  13.3 17.9 %all_to_all.21.right = bf16[16,128,128]{2,1,0:T(8,128)(2,1)S(1)} all-to-all(bf16[16,128,128]{2,1,0:T(8,128)(2,1)S(1)} %get-tuple-element.19), channel_id=1, replica_groups={{11,15,14,13,12,10,9,8,7,6,5,4,3,2,1,0},{27,31,30,29,28,26,25,24,23,22,..., dimensions={0} | all-to-all | bytes 1048576 | tf_op jit(solution)/shard_map/all_to_all | solution.py:50
  31.2 0.4 shard_map.128
  31.6 0.0 copy-start
  31.6 9.2 %all_to_all.22.returned = bf16[8,128,128]{2,1,0:T(8,128)(2,1)S(1)} all-to-all(bf16[8,128,128]{2,1,0:T(8,128)(2,1)S(1)} %shard_map.128), channel_id=1, replica_groups={{5,7,6,4,3,2,1,0},{13,15,14,12,11,10,9,8},{21,23,22,20,19,18,17,16},{29..., dimensions={0} | all-to-all | bytes 524288 | tf_op jit(solution)/shard_map/all_to_all | solution.py:50
  40.8 0.0 copy-done
  40.8 0.9 %shard_map.129 = (f32[8,128,128]{2,1,0:T(8,128)S(1)}, bf16[8,128,128]{2,1,0:T(8,128)(2,1)S(1)}, bf16[16,32,128]{2,1,0:T(8,128)(2,1)S(1)}) custom-call(bf16[8,128,128]{2,1,0:T(8,128)(2,1)S(1)} %all_to_all.22.returned, f32[8,128,128]{2,1,0:T(8,128)S(1)} %get-tuple-element.20.gate, bf16[8,128,128]{2,1,0:T(8,128)(2,1)S(1)} %copy-done, ...), custom_call_target="tpu_custom_call" | custom-call | flops 33554432 | bytes 1082368 | tf_op jit(solution)/shard_map/pallas_call | solution.py:322
  41.8 10.1 %all_to_all.23.refs_1_ = bf16[16,32,128]{2,1,0:T(8,128)(2,1)S(1)} all-to-all(bf16[16,32,128]{2,1,0:T(8,128)(2,1)S(1)} %get-tuple-element.29), channel_id=1, replica_groups={{11,15,14,13,12,10,9,8,7,6,5,4,3,2,1,0},{27,31,30,29,28,26,25,24,23,22,..., dimensions={0} | all-to-all | bytes 262144 | tf_op jit(solution)/shard_map/all_to_all | solution.py:50
  51.8 2.5 %shard_map.130 = bf16[8,128,128]{2,1,0:T(8,128)(2,1)} custom-call(bf16[8,128,128]{2,1,0:T(8,128)(2,1)S(1)} %get-tuple-element.23.att_norm, bf16[128,128]{1,0:T(8,128)(2,1)S(1)} %get-tuple-element.24.w_query, bf16[128,128]{1,0:T(8,128)(2,1)S(1)} %get-tuple-element.25.w_key, bf16[128,128]{1,0:T(8,128)(2,1)S(1)} %get-tuple-element.26.w_value, ...), custom_call_target="tpu_custom_call" | custom-call | flops 201326592 | bytes 1081344 | tf_op jit(solution)/shard_map/pallas_call | solution.py:322
Async XLA Ops:
  31.6 9.2 %copy-start = (bf16[8,128,128]{2,1,0:T(8,128)(2,1)S(1)}, bf16[8,128,128]{2,1,0:T(8,128)(2,1)}, u32[]{:S(2)}) copy-start(bf16[8,128,128]{2,1,0:T(8,128)(2,1)} %pair.1) | copy-start | bytes 786436

commit v11 on v10

--- a/solution.py
+++ b/solution.py
@@ -82,51 +82,64 @@
                 step(rows[tick - late])
 
 
-def edges_kernel(*refs):
-    given, (left, right, gate, *staged) = refs[:13], refs[13:23]
-    pair, weights, normed, held, sems = refs[23:]
-    targets = [pair, *(weights.at[n] for n in range(5)), *staged]
+def gated_edges(normed, weight, weight_gate, held):
+    rows, cols = normed.shape[0], normed.shape[1]
+    channels = weight.shape[1]
+    turned = jnp.concatenate([weight[...].T, weight_gate[...].T], axis=0)
+
+    def project(i):
+        both = dot(turned, jnp.concatenate([normed[i], normed[i + 1]], axis=0), NT)
+        act = sigmoid(both[channels:]) * both[:channels]
+        for tile, lanes in lane_tiles(act):
+            row, part = divmod(tile, cols // LANES)
+            held[part, pl.ds(i + row, channels, stride=rows), :] = act[:, lanes]
+
+    return project
+
+
+def deal(held, out, members):
+    owners, block = out.shape[0], out.shape[1]
+    for member in range(members):
+        for part in range(held.shape[0]):
+            sent = held[part, member * block : (member + 1) * block, :].astype(BF16)
+            for owner in range(member, owners, members):
+                out[slot(owner, owners), :, part * LANES : (part + 1) * LANES] = sent
+
+
+def right_kernel(members, *refs):
+    given, (right, normed, *staged), (pair, w_right, w_right_gate, held, sems) = refs[:13], refs[13:25], refs[25:]
+    targets = [pair, w_right, w_right_gate, *staged]
     copies = [
         pltpu.make_async_copy(source, target, sems.at[n])
         for n, (source, target) in enumerate(zip(given, targets))
     ]
     for copy in copies:
         copy.start()
-    for copy in copies[:6]:
+    for copy in copies[:3]:
         copy.wait()
-    rows, width = pair.shape[0], pair.shape[2]
-    channels = weights.shape[2]
-    cols = pair.shape[1]
-    turned = jnp.concatenate([weights[n].T for n in range(4)], axis=0)
-    gate_weight = twice(weights[4])
 
     def norm(i):
         normed[i] = lane_norm(pair[i].astype(F32))
         normed[i + 1] = lane_norm(pair[i + 1].astype(F32))
 
-    def project(i):
-        both = dot(turned, jnp.concatenate([normed[i], normed[i + 1]], axis=0), NT)
-        for side in range(2):
-            base = 2 * side * channels
-            act = sigmoid(both[base + channels : base + 2 * channels]) * both[base : base + channels]
-            for tile, lanes in lane_tiles(act):
-                row, part = divmod(tile, cols // LANES)
-                held[part, side, pl.ds(i + row, channels, stride=rows), :] = act[:, lanes]
+    pipeline(range(0, pair.shape[0], 2), norm, gated_edges(normed, w_right, w_right_gate, held))
+    deal(held, right, members)
+    for copy in copies[3:]:
+        copy.wait()
+
+
+def left_kernel(normed, w_left, w_left_gate, w_tri_gate, left, gate, held):
+    width = w_tri_gate.shape[1]
+    gate_weight = twice(w_tri_gate[...])
+
+    def open_gate(i):
         opened = sigmoid(dot(side_by_side(normed, i), gate_weight))
         gate[i] = opened[:, :width]
         gate[i + 1] = opened[:, width:]
 
-    pipeline(range(0, rows, 2), norm, project)
-    half, block = left.shape[0], left.shape[1]
-    for member in range(half):
-        mine = slice(member * block, (member + 1) * block)
-        for tile, lanes in lane_tiles(pair):
-            left[slot(member, half), :, lanes] = held[tile, 0, mine, :].astype(BF16)
-            sent = held[tile, 1, mine, :].astype(BF16)
-            for owner in range(member, right.shape[0], half):
-                right[slot(owner, right.shape[0]), :, lanes] = sent
-    for copy in copies[6:]:
-        copy.wait()
+    step = gated_edges(normed, w_left, w_left_gate, held)
+    pipeline(range(0, normed.shape[0], 2), step, open_gate)
+    deal(held, left, left.shape[0])
 
 
 def channel_rows(edges, rows, channel):
@@ -354,39 +367,42 @@
     residues = owners * rows
     cells = rows * cols
 
-    left, right, gate, w_tri_out, w_query, w_key, w_value, w_att_gate, w_att_out, w_bias_t = call(
-        edges_kernel,
+    later = (w_left, w_left_gate, w_tri_gate, w_tri_out, w_query, w_key, w_value, w_att_gate, w_att_out)
+    right, normed, *later, w_bias_t = call(
+        functools.partial(right_kernel, half),
         [
-            ((half, own * rows, cols), BF16),
             ((owners, own * rows, cols), BF16),
-            ((rows, cols, width), F32),
-            *[(w.shape, BF16) for w in (w_tri_out, w_query, w_key, w_value, w_att_gate, w_att_out)],
+            (pair_rep.shape, BF16),
+            *[(w.shape, BF16) for w in later],
             (w_bias.shape[::-1], BF16),
         ],
         [
             (pair_rep.shape, BF16),
-            ((5, width, channels), BF16),
-            (pair_rep.shape, BF16),
-            ((cols // LANES, 2, channels * rows, LANES), F32),
+            (w_right.shape, BF16),
+            (w_right_gate.shape, BF16),
+            ((cols // LANES, channels * rows, LANES), F32),
             pltpu.SemaphoreType.DMA((13,)),
         ],
-        10 * cells * width * channels,
+        4 * cells * width * channels,
         pair_rep,
-        w_left,
-        w_left_gate,
         w_right,
         w_right_gate,
-        w_tri_gate,
-        w_tri_out,
-        w_query,
-        w_key,
-        w_value,
-        w_att_gate,
-        w_att_out,
+        *later,
         w_bias.T,
         fetched=13,
     )
+    w_left, w_left_gate, w_tri_gate, w_tri_out, w_query, w_key, w_value, w_att_gate, w_att_out = later
     right = swap(right, owners)
+    left, gate = call(
+        left_kernel,
+        [((half, own * rows, cols), BF16), ((rows, cols, width), F32)],
+        [((cols // LANES, channels * rows, LANES), F32)],
+        6 * cells * width * channels,
+        normed,
+        w_left,
+        w_left_gate,
+        w_tri_gate,
+    )
     left = swap(left, owners)
     flops = 2 * own * half * rows * residues * cols
     if col_parts == 1:

time: 54.5 us -> 54.8 us (level)
    pallas_call x4 -> x5, Pallas kernels: 5.84 us -> 6.14 us  [call(): pl.pallas_call(kernel, out_shape=shapes, in_specs=[far] * fetched + [vmem...]
where the time goes in v11:
time: 54.8 us; the launch traced here: 54.6 us
  blocking collectives  48.4 us (88%)
  Pallas kernels  6.14 us (11%)
    all_to_all x4, blocking collectives, swap(): lax.all_to_all(blocks, 'row', split_axis=0, concat_axis=0, axis_index_gro...  48.4 us
    pallas_call x5, Pallas kernels, call(): pl.pallas_call(kernel, out_shape=shapes, in_specs=[far] * fetched + [vmem...  6.14 us

profile of v11, /device:TPU:0, one launch (start us, length us, event | category | flops | bytes accessed | tf_op | source)
XLA Modules:
  0.0 54.6 jit_solution(8503812378907631530)
XLA Ops:
  0.0 1.9 %shard_map.127 = (bf16[16,128,128]{2,1,0:T(8,128)(2,1)S(1)}, bf16[8,128,128]{2,1,0:T(8,128)(2,1)S(1)}, bf16[128,128]{1,0:T(8,128)(2,1)S(1)}, bf16[128,128]{1,0:T...) custom-call(bf16[8,128,128]{2,1,0:T(8,128)(2,1)} %pair.1, ...), custom_call_target="tpu_custom_call" | custom-call | flops 67108864 | bytes 623616 | tf_op jit(solution)/shard_map/pallas_call | solution.py:335
  1.9 0.5 shard_map.128
  2.4 11.2 %all_to_all.20.left = bf16[8,128,128]{2,1,0:T(8,128)(2,1)S(1)} all-to-all(bf16[8,128,128]{2,1,0:T(8,128)(2,1)S(1)} %get-tuple-element.26), channel_id=1, replica_groups={{5,7,6,4,3,2,1,0},{13,15,14,12,11,10,9,8},{21,23,22,20,19,18,17,16},{29..., dimensions={0} | all-to-all | bytes 524288 | tf_op jit(solution)/shard_map/all_to_all | solution.py:50
  13.6 17.9 %all_to_all.21.right = bf16[16,128,128]{2,1,0:T(8,128)(2,1)S(1)} all-to-all(bf16[16,128,128]{2,1,0:T(8,128)(2,1)S(1)} %get-tuple-element.27), channel_id=1, replica_groups={{11,15,14,13,12,10,9,8,7,6,5,4,3,2,1,0},{27,31,30,29,28,26,25,24,23,22,..., dimensions={0} | all-to-all | bytes 1048576 | tf_op jit(solution)/shard_map/all_to_all | solution.py:50
  31.5 0.4 shard_map.129
  31.9 0.0 copy-start
  31.9 9.2 %all_to_all.22.returned = bf16[8,128,128]{2,1,0:T(8,128)(2,1)S(1)} all-to-all(bf16[8,128,128]{2,1,0:T(8,128)(2,1)S(1)} %shard_map.129), channel_id=1, replica_groups={{5,7,6,4,3,2,1,0},{13,15,14,12,11,10,9,8},{21,23,22,20,19,18,17,16},{29..., dimensions={0} | all-to-all | bytes 524288 | tf_op jit(solution)/shard_map/all_to_all | solution.py:50
  41.1 0.0 copy-done
  41.1 0.9 %shard_map.130 = (f32[8,128,128]{2,1,0:T(8,128)S(1)}, bf16[8,128,128]{2,1,0:T(8,128)(2,1)S(1)}, bf16[16,32,128]{2,1,0:T(8,128)(2,1)S(1)}) custom-call(bf16[8,128,128]{2,1,0:T(8,128)(2,1)S(1)} %all_to_all.22.returned, f32[8,128,128]{2,1,0:T(8,128)S(1)} %get-tuple-element.28.gate, bf16[8,128,128]{2,1,0:T(8,128)(2,1)S(1)} %copy-done, ...), custom_call_target="tpu_custom_call" | custom-call | flops 33554432 | bytes 1082368 | tf_op jit(solution)/shard_map/pallas_call | solution.py:335
  42.0 10.1 %all_to_all.23.refs_1_ = bf16[16,32,128]{2,1,0:T(8,128)(2,1)S(1)} all-to-all(bf16[16,32,128]{2,1,0:T(8,128)(2,1)S(1)} %get-tuple-element.37), channel_id=1, replica_groups={{11,15,14,13,12,10,9,8,7,6,5,4,3,2,1,0},{27,31,30,29,28,26,25,24,23,22,..., dimensions={0} | all-to-all | bytes 262144 | tf_op jit(solution)/shard_map/all_to_all | solution.py:50
  52.1 2.5 %shard_map.131 = bf16[8,128,128]{2,1,0:T(8,128)(2,1)} custom-call(bf16[8,128,128]{2,1,0:T(8,128)(2,1)S(1)} %get-tuple-element.31.att_norm, bf16[128,128]{1,0:T(8,128)(2,1)S(1)} %get-tuple-element.32.w_query, bf16[128,128]{1,0:T(8,128)(2,1)S(1)} %get-tuple-element.33.w_key, bf16[128,128]{1,0:T(8,128)(2,1)S(1)} %get-tuple-element.34.w_value, ...), custom_call_target="tpu_custom_call" | custom-call | flops 201326592 | bytes 1081344 | tf_op jit(solution)/shard_map/pallas_call | solution.py:335
Async XLA Ops:
  31.9 9.2 %copy-start = (bf16[8,128,128]{2,1,0:T(8,128)(2,1)S(1)}, bf16[8,128,128]{2,1,0:T(8,128)(2,1)}, u32[]{:S(2)}) copy-start(bf16[8,128,128]{2,1,0:T(8,128)(2,1)} %pair.1) | copy-start | bytes 786436

commit v12 on v11

--- a/solution.py
+++ b/solution.py
@@ -43,6 +43,11 @@
     return listing(ranks).index(rank)
 
 
+def slot_of(rank, ranks):
+    first = listing(ranks)[0]
+    return jnp.where(rank == first, 0, ranks - 1 - rank + (rank > first).astype(jnp.int32))
+
+
 def swap(blocks, ranks):
     members = blocks.shape[0]
     order = listing(members)
@@ -95,15 +100,6 @@
             held[part, pl.ds(i + row, channels, stride=rows), :] = act[:, lanes]
 
     return project
-
-
-def deal(held, out, members):
-    owners, block = out.shape[0], out.shape[1]
-    for member in range(members):
-        for part in range(held.shape[0]):
-            sent = held[part, member * block : (member + 1) * block, :].astype(BF16)
-            for owner in range(member, owners, members):
-                out[slot(owner, owners), :, part * LANES : (part + 1) * LANES] = sent
 
 
 def right_kernel(members, *refs):
@@ -123,12 +119,19 @@
         normed[i + 1] = lane_norm(pair[i + 1].astype(F32))
 
     pipeline(range(0, pair.shape[0], 2), norm, gated_edges(normed, w_right, w_right_gate, held))
-    deal(held, right, members)
+    owners, block = right.shape[0], right.shape[1]
+    for member in range(members):
+        for part in range(held.shape[0]):
+            sent = held[part, member * block : (member + 1) * block, :].astype(BF16)
+            for owner in range(member, owners, members):
+                right[slot(owner, owners), :, part * LANES : (part + 1) * LANES] = sent
     for copy in copies[3:]:
         copy.wait()
 
 
-def left_kernel(normed, w_left, w_left_gate, w_tri_gate, left, gate, held):
+def left_kernel(normed, w_left, w_left_gate, w_tri_gate, gate, *refs):
+    left, held = refs[:-1], refs[-1]
+    me = lax.rem(lax.axis_index("row"), len(left))
     width = w_tri_gate.shape[1]
     gate_weight = twice(w_tri_gate[...])
 
@@ -139,36 +142,49 @@
 
     step = gated_edges(normed, w_left, w_left_gate, held)
     pipeline(range(0, normed.shape[0], 2), step, open_gate)
-    deal(held, left, left.shape[0])
-
-
-def channel_rows(edges, rows, channel):
-    sources = edges.shape[0]
+    for turn, out in enumerate(left):
+        block = out.shape[0]
+        mine = pl.ds(pl.multiple_of((me ^ turn) * block, block), block)
+        for part in range(held.shape[0]):
+            out[:, part * LANES : (part + 1) * LANES] = held[part, mine, :].astype(BF16)
+
+
+def channel_rows(blocks, rows, channel):
     mine = slice(channel * rows, (channel + 1) * rows)
     both = slice(channel // 2 * 2 * rows, (channel // 2 + 1) * 2 * rows)
     inner = slice(mine.start - both.start, mine.stop - both.start)
-    parts = [edges[slot(r, sources), both, :].astype(F32)[inner] for r in range(sources)]
+    parts = [block[both, :].astype(F32)[inner] for block in blocks]
     return jnp.concatenate(parts, axis=0).astype(BF16)
 
 
 def triangle_product(left, right, rows, channel):
-    return dot(channel_rows(left, rows, channel), channel_rows(right, rows, channel), NT)
-
-
-def triangle_kernel(rows, left, right, out):
-    owners = out.shape[0]
+    ranks = right.shape[0]
+    by_owner = [right.at[slot(r, ranks)] for r in range(ranks)]
+    return dot(channel_rows(left, rows, channel), channel_rows(by_owner, rows, channel), NT)
+
+
+def triangle_kernel(rows, right, *refs):
+    left, out = refs[:-1], refs[-1]
+    members = len(left)
+    me = lax.rem(lax.axis_index("row"), members)
     for channel in range(0, out.shape[1] // rows, 2):
         products = [triangle_product(left, right, rows, channel + o) for o in range(2)]
-        for owner in range(owners):
-            mine = slice(owner * rows, (owner + 1) * rows)
-            out[slot(owner, owners), channel * rows : (channel + 2) * rows, :] = jnp.concatenate(
+        for turn in range(members):
+            mine = slice(turn * rows, (turn + 1) * rows)
+            out[slot_of(me ^ turn, members), channel * rows : (channel + 2) * rows, :] = jnp.concatenate(
                 [p[mine] for p in products], axis=0
             ).astype(BF16)
 
 
-def partial_kernel(rows, left, right, out):
+def partial_kernel(rows, right, *refs):
+    left, out = refs[:-1], refs[-1]
+    members = len(left)
+    me = lax.rem(lax.axis_index("row"), members)
     for channel in range(out.shape[0]):
-        out[channel] = triangle_product(left, right, rows, channel)
+        product = triangle_product(left, right, rows, channel)
+        for turn in range(members):
+            place = pl.ds(pl.multiple_of((me ^ turn) * rows, rows), rows)
+            out[channel, place, :] = product[turn * rows : (turn + 1) * rows]
 
 
 def update_kernel(
@@ -393,9 +409,9 @@
     )
     w_left, w_left_gate, w_tri_gate, w_tri_out, w_query, w_key, w_value, w_att_gate, w_att_out = later
     right = swap(right, owners)
-    left, gate = call(
+    gate, *left = call(
         left_kernel,
-        [((half, own * rows, cols), BF16), ((rows, cols, width), F32)],
+        [((rows, cols, width), F32)] + [((own * rows, cols), BF16)] * half,
         [((cols // LANES, channels * rows, LANES), F32)],
         6 * cells * width * channels,
         normed,
@@ -403,7 +419,8 @@
         w_left_gate,
         w_tri_gate,
     )
-    left = swap(left, owners)
+    for turn in range(1, half):
+        left[turn] = lax.ppermute(left[turn], "row", [(r, r ^ turn) for r in range(owners)])
     flops = 2 * own * half * rows * residues * cols
     if col_parts == 1:
         summed = call(
@@ -411,8 +428,8 @@
             [((half, own * rows, residues), BF16)],
             [],
             flops,
-            left,
             right,
+            *left,
         )
     else:
         partial_sums = call(
@@ -420,8 +437,8 @@
             [((own, half * rows, residues), F32)],
             [],
             flops,
-            left,
             right,
+            *left,
         )
         summed = lax.psum_scatter(partial_sums, "col", scatter_dimension=2, tiled=True).astype(BF16)
         summed = by_slot(summed.reshape(own, half, rows, cols).swapaxes(0, 1))

time: 54.8 us -> 49 us (0.89)
  blocking collectives: 48.4 us -> 19.9 us
  starting transfers between devices: 0 us -> 18.4 us
  waiting for transfers between devices: 0 us -> 3.39 us
  Pallas kernels: 6.14 us -> 6.95 us
    all_to_all x4 -> x2, blocking collectives: 48.4 us -> 19.9 us  [swap(): lax.all_to_all(blocks, 'row', split_axis=0, concat_axis=0, axis_index_gro...]
    all_to_all x0 -> x1, starting transfers between devices: none -> 9.39 us  [swap(): lax.all_to_all(blocks, 'row', split_axis=0, concat_axis=0, axis_index_gro...]
    ppermute x0 -> x7, starting transfers between devices: none -> 9.04 us  [body(): lax.ppermute(left[turn], 'row', [(r, r ^ turn) for r in range(owners)])]
    ppermute x0 -> x7, waiting for transfers between devices: none -> 3.38 us  [body(): lax.ppermute(left[turn], 'row', [(r, r ^ turn) for r in range(owners)])]
    pallas_call x5, Pallas kernels: 6.14 us -> 6.95 us  [call(): pl.pallas_call(kernel, out_shape=shapes, in_specs=[far] * fetched + [vmem...]
  transfers between devices with their start and end apart: 0 -> 8, of which waited for: 0 -> 5; matrix products, arithmetic and copies ran while one was open for 0% -> 0% of each run, Pallas kernels for 0% -> 1%
where the time goes in v12:
time: 49 us; the launch traced here: 48.7 us
  blocking collectives  19.9 us (41%)
  starting transfers between devices  18.4 us (38%)
  Pallas kernels  6.95 us (14%)
  waiting for transfers between devices  3.39 us (7%)
    all_to_all x2, blocking collectives, swap(): lax.all_to_all(blocks, 'row', split_axis=0, concat_axis=0, axis_index_gro...  19.9 us
    all_to_all x1, starting transfers between devices, swap(): lax.all_to_all(blocks, 'row', split_axis=0, concat_axis=0, axis_index_gro...  9.39 us
    ppermute x7, starting transfers between devices, body(): lax.ppermute(left[turn], 'row', [(r, r ^ turn) for r in range(owners)])  9.04 us
    pallas_call x5, Pallas kernels, call(): pl.pallas_call(kernel, out_shape=shapes, in_specs=[far] * fetched + [vmem...  6.95 us
    ppermute x7, waiting for transfers between devices, body(): lax.ppermute(left[turn], 'row', [(r, r ^ turn) for r in range(owners)])  3.38 us
  transfers between devices with their start and end apart: 8, of which 5 were waited for; matrix products, arithmetic and copies ran while one was open for 0% of the time, Pallas kernels for 1%

profile of v12, /device:TPU:0, one launch (start us, length us, event | category | flops | bytes accessed | tf_op | source)
XLA Modules:
  0.0 48.7 jit_solution(11190177672161678645)
XLA Ops:
  0.0 2.7 %shard_map.127 = (bf16[16,128,128]{2,1,0:T(8,128)(2,1)}, bf16[8,128,128]{2,1,0:T(8,128)(2,1)S(1)}, bf16[128,128]{1,0:T(8,128)(2,1)S(1)}, bf16[128,128]{1,0:T(8,1...) custom-call(bf16[8,128,128]{2,1,0:T(8,128)(2,1)} %pair.1, ...), custom_call_target="tpu_custom_call" | custom-call | flops 67108864 | bytes 623616 | tf_op jit(solution)/shard_map/pallas_call | solution.py:351
  2.7 9.4 %all-to-all-start = ((bf16[16,128,128]{2,1,0:T(8,128)(2,1)}), bf16[16,128,128]{2,1,0:T(8,128)(2,1)S(1)}, u32[]{:S(2)}, u32[]{:S(2)}) async-start(bf16[16,128,128]{2,1,0:T(8,128)(2,1)} %get-tuple-element.29), calls=%async_computation | async-start | bytes 1048576 | tf_op jit(solution)/shard_map/all_to_all | solution.py:55
  12.1 0.5 shard_map.128
  12.5 0.6 %collective-permute-start = (bf16[128,128]{1,0:T(8,128)(2,1)S(1)}, bf16[128,128]{1,0:T(8,128)(2,1)S(1)}, u32[]{:S(2)}, u32[]{:S(2)}) collective-permute-start(bf16[128,128]{1,0:T(8,128)(2,1)S(1)} %get-tuple-element.35), channel_id=1, source_target_pairs={{0,1},{1,0},{2,3},{3,2},{4,5},{5,4},{6,7},{7,6},{8,9},{9,8},{10,11... | collective-permute-start | bytes 98312 | tf_op jit(solution)/shard_map/ppermute | solution.py:423
  13.2 0.6 %collective-permute-start.1 = (bf16[128,128]{1,0:T(8,128)(2,1)S(1)}, bf16[128,128]{1,0:T(8,128)(2,1)S(1)}, u32[]{:S(2)}, u32[]{:S(2)}) collective-permute-start(bf16[128,128]{1,0:T(8,128)(2,1)S(1)} %get-tuple-element.36), channel_id=1, source_target_pairs={{0,2},{1,3},{2,0},{3,1},{4,6},{5,7},{6,4},{7,5},{8,10},{9,11},{10,... | collective-permute-start | bytes 98312 | tf_op jit(solution)/shard_map/ppermute | solution.py:423
  13.7 2.4 %collective-permute-start.2 = (bf16[128,128]{1,0:T(8,128)(2,1)S(1)}, bf16[128,128]{1,0:T(8,128)(2,1)S(1)}, u32[]{:S(2)}, u32[]{:S(2)}) collective-permute-start(bf16[128,128]{1,0:T(8,128)(2,1)S(1)} %get-tuple-element.37), channel_id=1, source_target_pairs={{0,3},{1,2},{2,1},{3,0},{4,7},{5,6},{6,5},{7,4},{8,11},{9,10},{10,... | collective-permute-start | bytes 98312 | tf_op jit(solution)/shard_map/ppermute | solution.py:423
  16.1 0.5 %collective-permute-start.3 = (bf16[128,128]{1,0:T(8,128)(2,1)S(1)}, bf16[128,128]{1,0:T(8,128)(2,1)S(1)}, u32[]{:S(2)}, u32[]{:S(2)}) collective-permute-start(bf16[128,128]{1,0:T(8,128)(2,1)S(1)} %get-tuple-element.38), channel_id=1, source_target_pairs={{0,4},{1,5},{2,6},{3,7},{4,0},{5,1},{6,2},{7,3},{8,12},{9,13},{10,... | collective-permute-start | bytes 98312 | tf_op jit(solution)/shard_map/ppermute | solution.py:423
  16.6 1.5 %collective-permute-start.4 = (bf16[128,128]{1,0:T(8,128)(2,1)S(1)}, bf16[128,128]{1,0:T(8,128)(2,1)S(1)}, u32[]{:S(2)}, u32[]{:S(2)}) collective-permute-start(bf16[128,128]{1,0:T(8,128)(2,1)S(1)} %get-tuple-element.39), channel_id=1, source_target_pairs={{0,5},{1,4},{2,7},{3,6},{4,1},{5,0},{6,3},{7,2},{8,13},{9,12},{10,... | collective-permute-start | bytes 98312 | tf_op jit(solution)/shard_map/ppermute | solution.py:423
  18.1 0.8 %collective-permute-done.refs_1_ = bf16[128,128]{1,0:T(8,128)(2,1)S(1)} collective-permute-done((bf16[128,128]{1,0:T(8,128)(2,1)S(1)}, bf16[128,128]{1,0:T(8,128)(2,1)S(1)}, u32[]{:S(2)}, u32[]{:S(2)}) %collective-permute-start) | collective-permute-done | bytes 32800 | tf_op jit(solution)/shard_map/ppermute | solution.py:423
  18.9 0.0 collective-permute-start.5
  18.9 0.0 collective-permute-done.1.refs_2_
  18.9 3.5 %collective-permute-start.6 = (bf16[128,128]{1,0:T(8,128)(2,1)S(1)}, bf16[128,128]{1,0:T(8,128)(2,1)S(1)}, u32[]{:S(2)}, u32[]{:S(2)}) collective-permute-start(bf16[128,128]{1,0:T(8,128)(2,1)S(1)} %get-tuple-element.41), channel_id=1, source_target_pairs={{0,7},{1,6},{2,5},{3,4},{4,3},{5,2},{6,1},{7,0},{8,15},{9,14},{10,... | collective-permute-start | bytes 98312 | tf_op jit(solution)/shard_map/ppermute | solution.py:423
  22.4 0.0 collective-permute-done.2.refs_3_
  22.4 0.1 collective-permute-done.3.refs_4_
  22.5 0.6 %collective-permute-done.4.refs_5_ = bf16[128,128]{1,0:T(8,128)(2,1)S(1)} collective-permute-done((bf16[128,128]{1,0:T(8,128)(2,1)S(1)}, bf16[128,128]{1,0:T(8,128)(2,1)S(1)}, u32[]{:S(2)}, u32[]{:S(2)}) %collective-permute-start.4) | collective-permute-done | bytes 32800 | tf_op jit(solution)/shard_map/ppermute | solution.py:423
  23.1 1.6 %collective-permute-done.5.refs_6_ = bf16[128,128]{1,0:T(8,128)(2,1)S(1)} collective-permute-done((bf16[128,128]{1,0:T(8,128)(2,1)S(1)}, bf16[128,128]{1,0:T(8,128)(2,1)S(1)}, u32[]{:S(2)}, u32[]{:S(2)}) %collective-permute-start.5) | collective-permute-done | bytes 32800 | tf_op jit(solution)/shard_map/ppermute | solution.py:423
  24.7 0.3 collective-permute-done.6.refs_7_
  25.0 0.0 all-to-all-done.right
  25.0 0.5 shard_map.129
  25.4 0.0 copy-start
  25.4 9.8 %all_to_all.15.returned = bf16[8,128,128]{2,1,0:T(8,128)(2,1)S(1)} all-to-all(bf16[8,128,128]{2,1,0:T(8,128)(2,1)S(1)} %shard_map.129), channel_id=1, replica_groups={{5,7,6,4,3,2,1,0},{13,15,14,12,11,10,9,8},{21,23,22,20,19,18,17,16},{29..., dimensions={0} | all-to-all | bytes 524288 | tf_op jit(solution)/shard_map/all_to_all | solution.py:55
  35.3 0.0 copy-done
  35.3 0.9 %shard_map.130 = (f32[8,128,128]{2,1,0:T(8,128)S(1)}, bf16[8,128,128]{2,1,0:T(8,128)(2,1)S(1)}, bf16[16,32,128]{2,1,0:T(8,128)(2,1)S(1)}) custom-call(bf16[8,128,128]{2,1,0:T(8,128)(2,1)S(1)} %all_to_all.15.returned, f32[8,128,128]{2,1,0:T(8,128)S(1)} %get-tuple-element.42.gate, bf16[8,128,128]{2,1,0:T(8,128)(2,1)S(1)} %copy-done, ...), custom_call_target="tpu_custom_call" | custom-call | flops 33554432 | bytes 1082368 | tf_op jit(solution)/shard_map/pallas_call | solution.py:351
  36.2 10.1 %all_to_all.16.refs_1_ = bf16[16,32,128]{2,1,0:T(8,128)(2,1)S(1)} all-to-all(bf16[16,32,128]{2,1,0:T(8,128)(2,1)S(1)} %get-tuple-element.51), channel_id=1, replica_groups={{11,15,14,13,12,10,9,8,7,6,5,4,3,2,1,0},{27,31,30,29,28,26,25,24,23,22,..., dimensions={0} | all-to-all | bytes 262144 | tf_op jit(solution)/shard_map/all_to_all | solution.py:55
  46.2 2.5 %shard_map.131 = bf16[8,128,128]{2,1,0:T(8,128)(2,1)} custom-call(bf16[8,128,128]{2,1,0:T(8,128)(2,1)S(1)} %get-tuple-element.45.att_norm, bf16[128,128]{1,0:T(8,128)(2,1)S(1)} %get-tuple-element.46.w_query, bf16[128,128]{1,0:T(8,128)(2,1)S(1)} %get-tuple-element.47.w_key, bf16[128,128]{1,0:T(8,128)(2,1)S(1)} %get-tuple-element.48.w_value, ...), custom_call_target="tpu_custom_call" | custom-call | flops 201326592 | bytes 1081344 | tf_op jit(solution)/shard_map/pallas_call | solution.py:351
Async XLA Ops:
  2.7 22.3 %all-to-all-start = ((bf16[16,128,128]{2,1,0:T(8,128)(2,1)}), bf16[16,128,128]{2,1,0:T(8,128)(2,1)S(1)}, u32[]{:S(2)}, u32[]{:S(2)}) async-start(bf16[16,128,128]{2,1,0:T(8,128)(2,1)} %get-tuple-element.29), calls=%async_computation | async-start | bytes 1048576 | tf_op jit(solution)/shard_map/all_to_all | solution.py:55
  12.5 6.3 %collective-permute-start = (bf16[128,128]{1,0:T(8,128)(2,1)S(1)}, bf16[128,128]{1,0:T(8,128)(2,1)S(1)}, u32[]{:S(2)}, u32[]{:S(2)}) collective-permute-start(bf16[128,128]{1,0:T(8,128)(2,1)S(1)} %get-tuple-element.35), channel_id=1, source_target_pairs={{0,1},{1,0},{2,3},{3,2},{4,5},{5,4},{6,7},{7,6},{8,9},{9,8},{10,11... | collective-permute-start | bytes 98312 | tf_op jit(solution)/shard_map/ppermute | solution.py:423
  13.2 5.7 %collective-permute-start.1 = (bf16[128,128]{1,0:T(8,128)(2,1)S(1)}, bf16[128,128]{1,0:T(8,128)(2,1)S(1)}, u32[]{:S(2)}, u32[]{:S(2)}) collective-permute-start(bf16[128,128]{1,0:T(8,128)(2,1)S(1)} %get-tuple-element.36), channel_id=1, source_target_pairs={{0,2},{1,3},{2,0},{3,1},{4,6},{5,7},{6,4},{7,5},{8,10},{9,11},{10,... | collective-permute-start | bytes 98312 | tf_op jit(solution)/shard_map/ppermute | solution.py:423
  13.7 8.6 %collective-permute-start.2 = (bf16[128,128]{1,0:T(8,128)(2,1)S(1)}, bf16[128,128]{1,0:T(8,128)(2,1)S(1)}, u32[]{:S(2)}, u32[]{:S(2)}) collective-permute-start(bf16[128,128]{1,0:T(8,128)(2,1)S(1)} %get-tuple-element.37), channel_id=1, source_target_pairs={{0,3},{1,2},{2,1},{3,0},{4,7},{5,6},{6,5},{7,4},{8,11},{9,10},{10,... | collective-permute-start | bytes 98312 | tf_op jit(solution)/shard_map/ppermute | solution.py:423
  16.1 6.4 %collective-permute-start.3 = (bf16[128,128]{1,0:T(8,128)(2,1)S(1)}, bf16[128,128]{1,0:T(8,128)(2,1)S(1)}, u32[]{:S(2)}, u32[]{:S(2)}) collective-permute-start(bf16[128,128]{1,0:T(8,128)(2,1)S(1)} %get-tuple-element.38), channel_id=1, source_target_pairs={{0,4},{1,5},{2,6},{3,7},{4,0},{5,1},{6,2},{7,3},{8,12},{9,13},{10,... | collective-permute-start | bytes 98312 | tf_op jit(solution)/shard_map/ppermute | solution.py:423
  16.6 6.5 %collective-permute-start.4 = (bf16[128,128]{1,0:T(8,128)(2,1)S(1)}, bf16[128,128]{1,0:T(8,128)(2,1)S(1)}, u32[]{:S(2)}, u32[]{:S(2)}) collective-permute-start(bf16[128,128]{1,0:T(8,128)(2,1)S(1)} %get-tuple-element.39), channel_id=1, source_target_pairs={{0,5},{1,4},{2,7},{3,6},{4,1},{5,0},{6,3},{7,2},{8,13},{9,12},{10,... | collective-permute-start | bytes 98312 | tf_op jit(solution)/shard_map/ppermute | solution.py:423
  18.9 5.8 %collective-permute-start.5 = (bf16[128,128]{1,0:T(8,128)(2,1)S(1)}, bf16[128,128]{1,0:T(8,128)(2,1)S(1)}, u32[]{:S(2)}, u32[]{:S(2)}) collective-permute-start(bf16[128,128]{1,0:T(8,128)(2,1)S(1)} %get-tuple-element.40), channel_id=1, source_target_pairs={{0,6},{1,7},{2,4},{3,5},{4,2},{5,3},{6,0},{7,1},{8,14},{9,15},{10,... | collective-permute-start | bytes 98312 | tf_op jit(solution)/shard_map/ppermute | solution.py:423
  18.9 6.1 %collective-permute-start.6 = (bf16[128,128]{1,0:T(8,128)(2,1)S(1)}, bf16[128,128]{1,0:T(8,128)(2,1)S(1)}, u32[]{:S(2)}, u32[]{:S(2)}) collective-permute-start(bf16[128,128]{1,0:T(8,128)(2,1)S(1)} %get-tuple-element.41), channel_id=1, source_target_pairs={{0,7},{1,6},{2,5},{3,4},{4,3},{5,2},{6,1},{7,0},{8,15},{9,14},{10,... | collective-permute-start | bytes 98312 | tf_op jit(solution)/shard_map/ppermute | solution.py:423
  25.4 9.8 %copy-start = (bf16[8,128,128]{2,1,0:T(8,128)(2,1)S(1)}, bf16[8,128,128]{2,1,0:T(8,128)(2,1)}, u32[]{:S(2)}) copy-start(bf16[8,128,128]{2,1,0:T(8,128)(2,1)} %pair.1) | copy-start | bytes 786436

commit v13 on v12

--- a/solution.py
+++ b/solution.py
@@ -131,7 +131,8 @@
 
 def left_kernel(normed, w_left, w_left_gate, w_tri_gate, gate, *refs):
     left, held = refs[:-1], refs[-1]
-    me = lax.rem(lax.axis_index("row"), len(left))
+    near = len(left)
+    me = lax.rem(lax.axis_index("row"), 2 * near)
     width = w_tri_gate.shape[1]
     gate_weight = twice(w_tri_gate[...])
 
@@ -142,11 +143,12 @@
 
     step = gated_edges(normed, w_left, w_left_gate, held)
     pipeline(range(0, normed.shape[0], 2), step, open_gate)
-    for turn, out in enumerate(left):
-        block = out.shape[0]
+    for turn in range(2 * near):
+        block = left[0].shape[1]
         mine = pl.ds(pl.multiple_of((me ^ turn) * block, block), block)
         for part in range(held.shape[0]):
-            out[:, part * LANES : (part + 1) * LANES] = held[part, mine, :].astype(BF16)
+            lanes = slice(part * LANES, (part + 1) * LANES)
+            left[turn % near][turn // near, :, lanes] = held[part, mine, :].astype(BF16)
 
 
 def channel_rows(blocks, rows, channel):
@@ -163,8 +165,13 @@
     return dot(channel_rows(left, rows, channel), channel_rows(by_owner, rows, channel), NT)
 
 
+def left_blocks(refs):
+    *near, far = refs
+    return [block.at[0] for block in near] + [far.at[s] for s in range(len(near))]
+
+
 def triangle_kernel(rows, right, *refs):
-    left, out = refs[:-1], refs[-1]
+    left, out = left_blocks(refs[:-1]), refs[-1]
     members = len(left)
     me = lax.rem(lax.axis_index("row"), members)
     for channel in range(0, out.shape[1] // rows, 2):
@@ -177,7 +184,7 @@
 
 
 def partial_kernel(rows, right, *refs):
-    left, out = refs[:-1], refs[-1]
+    left, out = left_blocks(refs[:-1]), refs[-1]
     members = len(left)
     me = lax.rem(lax.axis_index("row"), members)
     for channel in range(out.shape[0]):
@@ -379,6 +386,7 @@
     channels = w_left.shape[1]
     owners, col_parts = lax.axis_size("row"), lax.axis_size("col")
     half = owners // 2
+    near = half // 2
     own = channels // half
     residues = owners * rows
     cells = rows * cols
@@ -411,7 +419,7 @@
     right = swap(right, owners)
     gate, *left = call(
         left_kernel,
-        [((rows, cols, width), F32)] + [((own * rows, cols), BF16)] * half,
+        [((rows, cols, width), F32)] + [((2, own * rows, cols), BF16)] * near,
         [((cols // LANES, channels * rows, LANES), F32)],
         6 * cells * width * channels,
         normed,
@@ -419,8 +427,10 @@
         w_left_gate,
         w_tri_gate,
     )
-    for turn in range(1, half):
+    for turn in range(1, near):
         left[turn] = lax.ppermute(left[turn], "row", [(r, r ^ turn) for r in range(owners)])
+    passed_on = jnp.stack([block[1] for block in left])
+    left.append(lax.ppermute(passed_on, "row", [(r, r ^ near) for r in range(owners)]))
     flops = 2 * own * half * rows * residues * cols
     if col_parts == 1:
         summed = call(

time: 49 us -> 50.7 us (1.035)
  starting transfers between devices: 18.4 us -> 14 us
  waiting for transfers between devices: 3.39 us -> 7.66 us
  local copies, waits for them, and re-layouts: 0.01 us -> 2.04 us
    ppermute x7 -> x3, starting transfers between devices: 9.04 us -> 3.55 us  [body(): lax.ppermute(left[turn], 'row', [(r, r ^ turn) for r in range(owners)])]
    ppermute x0 -> x1, waiting for transfers between devices: none -> 4.05 us  [body(): lax.ppermute(passed_on, 'row', [(r, r ^ near) for r in range(owners)])]
    unnamed x2 -> x10, local copies, waits for them, and re-layouts: 0.01 us -> 1.27 us
    ppermute x0 -> x1, starting transfers between devices: none -> 1.08 us  [body(): lax.ppermute(passed_on, 'row', [(r, r ^ near) for r in range(owners)])]
    slice x0 -> x6, local copies, waits for them, and re-layouts: none -> 0.77 us  [body(): passed_on = jnp.stack([block[1] for block in left])]
    ppermute x7 -> x3, waiting for transfers between devices: 3.38 us -> 3.6 us  [body(): lax.ppermute(left[turn], 'row', [(r, r ^ turn) for r in range(owners)])]
  transfers between devices with their start and end apart: 8 -> 5, of which waited for: 5 -> 2; matrix products, arithmetic and copies ran while one was open for 0% -> 0% of each run, Pallas kernels for 1% -> 1%
where the time goes in v13:
time: 50.7 us; the launch traced here: 50.3 us
  blocking collectives  19.6 us (39%)
  starting transfers between devices  14 us (28%)
  waiting for transfers between devices  7.66 us (15%)
  Pallas kernels  6.93 us (14%)
  local copies, waits for them, and re-layouts  2.04 us (4%)
    all_to_all x2, blocking collectives, swap(): lax.all_to_all(blocks, 'row', split_axis=0, concat_axis=0, axis_index_gro...  19.6 us
    all_to_all x1, starting transfers between devices, swap(): lax.all_to_all(blocks, 'row', split_axis=0, concat_axis=0, axis_index_gro...  9.39 us
    pallas_call x5, Pallas kernels, call(): pl.pallas_call(kernel, out_shape=shapes, in_specs=[far] * fetched + [vmem...  6.93 us
    ppermute x1, waiting for transfers between devices, body(): lax.ppermute(passed_on, 'row', [(r, r ^ near) for r in range(owners)])  4.05 us
    ppermute x3, waiting for transfers between devices, body(): lax.ppermute(left[turn], 'row', [(r, r ^ turn) for r in range(owners)])  3.6 us
    ppermute x3, starting transfers between devices, body(): lax.ppermute(left[turn], 'row', [(r, r ^ turn) for r in range(owners)])  3.55 us
    unnamed x10, local copies, waits for them, and re-layouts  1.27 us
    ppermute x1, starting transfers between devices, body(): lax.ppermute(passed_on, 'row', [(r, r ^ near) for r in range(owners)])  1.08 us
  transfers between devices with their start and end apart: 5, of which 2 were waited for; matrix products, arithmetic and copies ran while one was open for 0% of the time, Pallas kernels for 1%

profile of v13, /device:TPU:0, one launch (start us, length us, event | category | flops | bytes accessed | tf_op | source)
XLA Modules:
  0.0 50.3 jit_solution(5879257924761747272)
XLA Ops:
  0.0 2.7 %shard_map.127 = (bf16[16,128,128]{2,1,0:T(8,128)(2,1)}, bf16[8,128,128]{2,1,0:T(8,128)(2,1)S(1)}, bf16[128,128]{1,0:T(8,128)(2,1)S(1)}, bf16[128,128]{1,0:T(8,1...) custom-call(bf16[8,128,128]{2,1,0:T(8,128)(2,1)} %pair.1, ...), custom_call_target="tpu_custom_call" | custom-call | flops 67108864 | bytes 623616 | tf_op jit(solution)/shard_map/pallas_call | solution.py:358
  2.7 9.4 %all-to-all-start = ((bf16[16,128,128]{2,1,0:T(8,128)(2,1)}), bf16[16,128,128]{2,1,0:T(8,128)(2,1)S(1)}, u32[]{:S(2)}, u32[]{:S(2)}) async-start(bf16[16,128,128]{2,1,0:T(8,128)(2,1)} %get-tuple-element.25), calls=%async_computation | async-start | bytes 1048576 | tf_op jit(solution)/shard_map/all_to_all | solution.py:55
  12.1 0.5 shard_map.128
  12.5 0.6 %collective-permute-start = (bf16[2,128,128]{2,1,0:T(8,128)(2,1)S(1)}, bf16[2,128,128]{2,1,0:T(8,128)(2,1)S(1)}, u32[]{:S(2)}, u32[]{:S(2)}) collective-permute-start(bf16[2,128,128]{2,1,0:T(8,128)(2,1)S(1)} %get-tuple-element.31), channel_id=1, source_target_pairs={{0,1},{1,0},{2,3},{3,2},{4,5},{5,4},{6,7},{7,6},{8,9},{9,8},{10,11... | collective-permute-start | bytes 196616 | tf_op jit(solution)/shard_map/ppermute | solution.py:431
  13.2 0.6 %collective-permute-start.1 = (bf16[2,128,128]{2,1,0:T(8,128)(2,1)S(1)}, bf16[2,128,128]{2,1,0:T(8,128)(2,1)S(1)}, u32[]{:S(2)}, u32[]{:S(2)}) collective-permute-start(bf16[2,128,128]{2,1,0:T(8,128)(2,1)S(1)} %get-tuple-element.32), channel_id=1, source_target_pairs={{0,2},{1,3},{2,0},{3,1},{4,6},{5,7},{6,4},{7,5},{8,10},{9,11},{10,... | collective-permute-start | bytes 196616 | tf_op jit(solution)/shard_map/ppermute | solution.py:431
  13.7 2.4 %collective-permute-start.2 = (bf16[2,128,128]{2,1,0:T(8,128)(2,1)S(1)}, bf16[2,128,128]{2,1,0:T(8,128)(2,1)S(1)}, u32[]{:S(2)}, u32[]{:S(2)}) collective-permute-start(bf16[2,128,128]{2,1,0:T(8,128)(2,1)S(1)} %get-tuple-element.33), channel_id=1, source_target_pairs={{0,3},{1,2},{2,1},{3,0},{4,7},{5,6},{6,5},{7,4},{8,11},{9,10},{10,... | collective-permute-start | bytes 196616 | tf_op jit(solution)/shard_map/ppermute | solution.py:431
  16.1 3.6 %collective-permute-done.refs_1_ = bf16[2,128,128]{2,1,0:T(8,128)(2,1)S(1)} collective-permute-done((bf16[2,128,128]{2,1,0:T(8,128)(2,1)S(1)}, bf16[2,128,128]{2,1,0:T(8,128)(2,1)S(1)}, u32[]{:S(2)}, u32[]{:S(2)}) %collective-permute-start) | collective-permute-done | bytes 65568 | tf_op jit(solution)/shard_map/ppermute | solution.py:431
  19.7 0.0 copy-start.1
  19.7 0.6 %copy-done.1 = bf16[2,128,128]{2,1,0:T(8,128)(2,1)} copy-done((bf16[2,128,128]{2,1,0:T(8,128)(2,1)}, bf16[2,128,128]{2,1,0:T(8,128)(2,1)S(1)}, u32[]{:S(2)}) %copy-start.1) | copy-done | bytes 65560
  20.3 0.0 collective-permute-done.1.refs_2_
  20.3 0.0 copy-start.3
  20.3 0.6 %copy-done.3 = bf16[2,128,128]{2,1,0:T(8,128)(2,1)} copy-done((bf16[2,128,128]{2,1,0:T(8,128)(2,1)}, bf16[2,128,128]{2,1,0:T(8,128)(2,1)S(1)}, u32[]{:S(2)}) %copy-start.3) | copy-done | bytes 65560
  20.9 0.0 slice-start
  20.9 0.0 collective-permute-done.2.refs_3_
  20.9 0.0 slice-start.1
  21.0 0.7 %slice-done = bf16[1,128,128]{2,1,0:T(8,128)(2,1)S(1)} async-done(((bf16[2,128,128]{2,1,0:T(8,128)(2,1)}), bf16[1,128,128]{2,1,0:T(8,128)(2,1)S(1)}, s32[]{:S(2)}) %slice-start) | async-done | bytes 32792 | tf_op jit(solution)/shard_map/slice | solution.py:432
  21.7 0.0 slice-done.1
  21.7 0.0 copy-start.2
  21.7 0.0 copy-start.4
  21.7 1.1 %collective-permute-start.3 = (bf16[4,128,128]{2,1,0:T(8,128)(2,1)S(1)}, bf16[4,128,128]{2,1,0:T(8,128)(2,1)S(1)}, u32[]{:S(2)}, u32[]{:S(2)}) collective-permute-start(bf16[4,128,128]{2,1,0:T(8,128)(2,1)S(1)} %pad_maximum_fusion), channel_id=1, source_target_pairs={{0,4},{1,5},{2,6},{3,7},{4,0},{5,1},{6,2},{7,3},{8,12},{9,13},{10,... | collective-permute-start | bytes 393224 | tf_op jit(solution)/shard_map/ppermute | solution.py:433
  22.8 4.1 %collective-permute-done.3.refs_4_ = bf16[4,128,128]{2,1,0:T(8,128)(2,1)S(1)} collective-permute-done((bf16[4,128,128]{2,1,0:T(8,128)(2,1)S(1)}, bf16[4,128,128]{2,1,0:T(8,128)(2,1)S(1)}, u32[]{:S(2)}, u32[]{:S(2)}) %collective-permute-start.3) | collective-permute-done | bytes 131104 | tf_op jit(solution)/shard_map/ppermute | solution.py:433
  26.9 0.0 all-to-all-done.right
  26.9 0.0 copy-done.2
  26.9 0.0 copy-done.4
  26.9 0.4 shard_map.129
  27.3 0.0 copy-start
  27.4 9.5 %all_to_all.15.returned = bf16[8,128,128]{2,1,0:T(8,128)(2,1)S(1)} all-to-all(bf16[8,128,128]{2,1,0:T(8,128)(2,1)S(1)} %shard_map.129), channel_id=1, replica_groups={{5,7,6,4,3,2,1,0},{13,15,14,12,11,10,9,8},{21,23,22,20,19,18,17,16},{29..., dimensions={0} | all-to-all | bytes 524288 | tf_op jit(solution)/shard_map/all_to_all | solution.py:55
  36.9 0.0 copy-done
  36.9 0.9 %shard_map.130 = (f32[8,128,128]{2,1,0:T(8,128)S(1)}, bf16[8,128,128]{2,1,0:T(8,128)(2,1)S(1)}, bf16[16,32,128]{2,1,0:T(8,128)(2,1)S(1)}) custom-call(bf16[8,128,128]{2,1,0:T(8,128)(2,1)S(1)} %all_to_all.15.returned, f32[8,128,128]{2,1,0:T(8,128)S(1)} %get-tuple-element.34.gate, bf16[8,128,128]{2,1,0:T(8,128)(2,1)S(1)} %copy-done, ...), custom_call_target="tpu_custom_call" | custom-call | flops 33554432 | bytes 1082368 | tf_op jit(solution)/shard_map/pallas_call | solution.py:358
  37.8 10.1 %all_to_all.16.refs_1_ = bf16[16,32,128]{2,1,0:T(8,128)(2,1)S(1)} all-to-all(bf16[16,32,128]{2,1,0:T(8,128)(2,1)S(1)} %get-tuple-element.43), channel_id=1, replica_groups={{11,15,14,13,12,10,9,8,7,6,5,4,3,2,1,0},{27,31,30,29,28,26,25,24,23,22,..., dimensions={0} | all-to-all | bytes 262144 | tf_op jit(solution)/shard_map/all_to_all | solution.py:55
  47.8 2.5 %shard_map.131 = bf16[8,128,128]{2,1,0:T(8,128)(2,1)} custom-call(bf16[8,128,128]{2,1,0:T(8,128)(2,1)S(1)} %get-tuple-element.37.att_norm, bf16[128,128]{1,0:T(8,128)(2,1)S(1)} %get-tuple-element.38.w_query, bf16[128,128]{1,0:T(8,128)(2,1)S(1)} %get-tuple-element.39.w_key, bf16[128,128]{1,0:T(8,128)(2,1)S(1)} %get-tuple-element.40.w_value, ...), custom_call_target="tpu_custom_call" | custom-call | flops 201326592 | bytes 1081344 | tf_op jit(solution)/shard_map/pallas_call | solution.py:358
  (3 shorter events, 0.0 us)
Async XLA Ops:
  2.7 24.2 %all-to-all-start = ((bf16[16,128,128]{2,1,0:T(8,128)(2,1)}), bf16[16,128,128]{2,1,0:T(8,128)(2,1)S(1)}, u32[]{:S(2)}, u32[]{:S(2)}) async-start(bf16[16,128,128]{2,1,0:T(8,128)(2,1)} %get-tuple-element.25), calls=%async_computation | async-start | bytes 1048576 | tf_op jit(solution)/shard_map/all_to_all | solution.py:55
  12.5 7.2 %collective-permute-start = (bf16[2,128,128]{2,1,0:T(8,128)(2,1)S(1)}, bf16[2,128,128]{2,1,0:T(8,128)(2,1)S(1)}, u32[]{:S(2)}, u32[]{:S(2)}) collective-permute-start(bf16[2,128,128]{2,1,0:T(8,128)(2,1)S(1)} %get-tuple-element.31), channel_id=1, source_target_pairs={{0,1},{1,0},{2,3},{3,2},{4,5},{5,4},{6,7},{7,6},{8,9},{9,8},{10,11... | collective-permute-start | bytes 196616 | tf_op jit(solution)/shard_map/ppermute | solution.py:431
  13.2 7.2 %collective-permute-start.1 = (bf16[2,128,128]{2,1,0:T(8,128)(2,1)S(1)}, bf16[2,128,128]{2,1,0:T(8,128)(2,1)S(1)}, u32[]{:S(2)}, u32[]{:S(2)}) collective-permute-start(bf16[2,128,128]{2,1,0:T(8,128)(2,1)S(1)} %get-tuple-element.32), channel_id=1, source_target_pairs={{0,2},{1,3},{2,0},{3,1},{4,6},{5,7},{6,4},{7,5},{8,10},{9,11},{10,... | collective-permute-start | bytes 196616 | tf_op jit(solution)/shard_map/ppermute | solution.py:431
  13.7 7.2 %collective-permute-start.2 = (bf16[2,128,128]{2,1,0:T(8,128)(2,1)S(1)}, bf16[2,128,128]{2,1,0:T(8,128)(2,1)S(1)}, u32[]{:S(2)}, u32[]{:S(2)}) collective-permute-start(bf16[2,128,128]{2,1,0:T(8,128)(2,1)S(1)} %get-tuple-element.33), channel_id=1, source_target_pairs={{0,3},{1,2},{2,1},{3,0},{4,7},{5,6},{6,5},{7,4},{8,11},{9,10},{10,... | collective-permute-start | bytes 196616 | tf_op jit(solution)/shard_map/ppermute | solution.py:431
  19.7 0.6 %copy-start.1 = (bf16[2,128,128]{2,1,0:T(8,128)(2,1)}, bf16[2,128,128]{2,1,0:T(8,128)(2,1)S(1)}, u32[]{:S(2)}) copy-start(bf16[2,128,128]{2,1,0:T(8,128)(2,1)S(1)} %collective-permute-done.refs_1_) | copy-start | bytes 196612
  20.3 0.6 %copy-start.3 = (bf16[2,128,128]{2,1,0:T(8,128)(2,1)}, bf16[2,128,128]{2,1,0:T(8,128)(2,1)S(1)}, u32[]{:S(2)}) copy-start(bf16[2,128,128]{2,1,0:T(8,128)(2,1)S(1)} %collective-permute-done.1.refs_2_) | copy-start | bytes 196612
  20.9 0.8 %slice-start = ((bf16[2,128,128]{2,1,0:T(8,128)(2,1)}), bf16[1,128,128]{2,1,0:T(8,128)(2,1)S(1)}, s32[]{:S(2)}) async-start(bf16[2,128,128]{2,1,0:T(8,128)(2,1)} %copy-done.1), calls=%async_computation.3 | async-start | bytes 65536 | tf_op jit(solution)/shard_map/slice | solution.py:432
  20.9 0.8 %slice-start.1 = ((bf16[2,128,128]{2,1,0:T(8,128)(2,1)}), bf16[1,128,128]{2,1,0:T(8,128)(2,1)S(1)}, s32[]{:S(2)}) async-start(bf16[2,128,128]{2,1,0:T(8,128)(2,1)} %copy-done.3), calls=%async_computation.4 | async-start | bytes 65536 | tf_op jit(solution)/shard_map/slice | solution.py:432
  21.7 5.2 %copy-start.2 = (bf16[2,128,128]{2,1,0:T(8,128)(2,1)S(1)}, bf16[2,128,128]{2,1,0:T(8,128)(2,1)}, u32[]{:S(2)}) copy-start(bf16[2,128,128]{2,1,0:T(8,128)(2,1)} %copy-done.1) | copy-start | bytes 196612
  21.7 5.2 %copy-start.4 = (bf16[2,128,128]{2,1,0:T(8,128)(2,1)S(1)}, bf16[2,128,128]{2,1,0:T(8,128)(2,1)}, u32[]{:S(2)}) copy-start(bf16[2,128,128]{2,1,0:T(8,128)(2,1)} %copy-done.3) | copy-start | bytes 196612
  21.7 5.1 %collective-permute-start.3 = (bf16[4,128,128]{2,1,0:T(8,128)(2,1)S(1)}, bf16[4,128,128]{2,1,0:T(8,128)(2,1)S(1)}, u32[]{:S(2)}, u32[]{:S(2)}) collective-permute-start(bf16[4,128,128]{2,1,0:T(8,128)(2,1)S(1)} %pad_maximum_fusion), channel_id=1, source_target_pairs={{0,4},{1,5},{2,6},{3,7},{4,0},{5,1},{6,2},{7,3},{8,12},{9,13},{10,... | collective-permute-start | bytes 393224 | tf_op jit(solution)/shard_map/ppermute | solution.py:433
  27.3 9.5 %copy-start = (bf16[8,128,128]{2,1,0:T(8,128)(2,1)S(1)}, bf16[8,128,128]{2,1,0:T(8,128)(2,1)}, u32[]{:S(2)}) copy-start(bf16[8,128,128]{2,1,0:T(8,128)(2,1)} %pair.1) | copy-start | bytes 786436

commit v14 on v9

--- a/solution.py
+++ b/solution.py
@@ -82,6 +82,15 @@
         for late, step in enumerate(steps):
             if 0 <= tick - late < len(rows):
                 step(rows[tick - late])
+
+
+def looped(rows, *steps):
+    def tick(now, carry):
+        for late, step in reversed(list(enumerate(steps))):
+            step(jnp.clip(now - late, 0, rows - 1))
+        return carry
+
+    lax.fori_loop(0, rows + len(steps) - 1, tick, 0)
 
 
 def edges_kernel(*refs):
@@ -204,26 +213,21 @@
 
 def projector(att_norm, w_query, w_key, w_value, w_att_gate, query_t, key, value_t, gate_t):
     w_turned = jnp.concatenate([w[...].T for w in (w_query, w_value, w_att_gate)], axis=0)
-    w_direct = twice(w_key[...])
-    cols, width = att_norm.shape[1], w_query.shape[1]
+    width = w_query.shape[1]
 
     def project(i):
-        if i % 2:
-            return
-        keys = dot(side_by_side(att_norm, i), w_direct).astype(BF16)
-        turned = dot(w_turned, jnp.concatenate([att_norm[i], att_norm[i + 1]], axis=0), NT)
-        for row in range(2):
-            key[i + row] = keys[:, row * width : (row + 1) * width]
-            mine = turned[:, row * cols : (row + 1) * cols]
-            query_t[i + row] = mine[:width].astype(BF16)
-            value_t[i + row] = mine[width : 2 * width].astype(BF16)
-            gate_t[i + row] = sigmoid(mine[2 * width :])
+        normed = att_norm[i]
+        key[i] = dot(normed, w_key[...]).astype(BF16)
+        turned = dot(w_turned, normed, NT)
+        query_t[i] = turned[:width].astype(BF16)
+        value_t[i] = turned[width : 2 * width].astype(BF16)
+        gate_t[i] = sigmoid(turned[2 * width :])
 
     return project
 
 
 def project_kernel(*refs):
-    pipeline(range(refs[0].shape[0]), projector(*refs))
+    looped(refs[0].shape[0], projector(*refs))
 
 
 def whole_kernel(att_norm, w_query, w_key, w_value, w_att_gate, *refs):
@@ -262,47 +266,38 @@
             below = jnp.zeros((width - mine.stop, cols), BF16)
             parts = [p for p in (above, query_t[i, mine, :], below) if p.shape[0]]
             blocks.append(jnp.concatenate(parts, axis=0))
-        scores[i % 2] = dot(key[i], jnp.concatenate(blocks, axis=1)) * score_scale
-
-    def turn_bias():
-        for head, (_, span) in enumerate(heads):
-            parts = [
-                bias[slot(owner, bias.shape[0])].astype(F32)[head * head_rows : (head + 1) * head_rows]
-                for owner in range(bias.shape[0])
-            ]
-            bias_t[:, span] = jnp.concatenate(parts, axis=0).T * LOG2_E
+        scores[lax.rem(i, 2)] = dot(key[i], jnp.concatenate(blocks, axis=1)) * score_scale
 
     def soften(i):
-        if i == 0:
-            turn_bias()
         for _, span in heads:
-            biased = scores[i % 2, :, span] + bias_t[:, span]
+            biased = scores[lax.rem(i, 2), :, span] + bias_t[:, span]
             peak = jnp.max(biased, axis=0, keepdims=True)
-            weights[i % 2, :, span] = jnp.exp2(biased - peak).astype(BF16)
+            weights[lax.rem(i, 2), :, span] = jnp.exp2(biased - peak).astype(BF16)
 
     def collect(i):
         for head in range(0, HEADS, 2):
             (first, left), (second, right) = heads[head : head + 2]
             values = jnp.concatenate([value_t[i, first.start : second.stop, :], ones], axis=0)
-            summed = dot(values, weights[i % 2, :, left.start : right.stop])
+            summed = dot(values, weights[lax.rem(i, 2), :, left.start : right.stop])
             share = 1.0 / summed[2 * HEAD_DIM : 2 * HEAD_DIM + 1]
             for mine, there, lanes in (
                 (first, slice(0, HEAD_DIM), slice(0, cols)),
                 (second, slice(HEAD_DIM, 2 * HEAD_DIM), slice(cols, 2 * cols)),
             ):
                 attended = summed[there, lanes] * share[:, lanes] * gate_t[i, mine, :]
-                gated[i % 4, mine, :] = attended.astype(BF16)
+                gated[lax.rem(i, 2), mine, :] = attended.astype(BF16)
 
     def finish(i):
-        if i % 2 == 0:
-            return
-        turned = jnp.concatenate([gated[(i - 1) % 4].T, gated[i % 4].T], axis=1)
-        both = dot(turned, w_last)
-        out[i - 1] = (first_pass[i - 1] + both[:, :width]).astype(BF16)
-        out[i] = (first_pass[i] + both[:, width:]).astype(BF16)
-
-    w_last = twice(w_att_out[...])
-    pipeline(range(rows), *before, score, soften, collect, finish)
+        turned = gated[lax.rem(i, 2)].T
+        out[i] = (first_pass[i] + dot(turned, w_att_out[...])).astype(BF16)
+
+    for head, (_, span) in enumerate(heads):
+        parts = [
+            bias[slot(owner, bias.shape[0])].astype(F32)[head * head_rows : (head + 1) * head_rows]
+            for owner in range(bias.shape[0])
+        ]
+        bias_t[:, span] = jnp.concatenate(parts, axis=0).T * LOG2_E
+    looped(rows, *before, score, soften, collect, finish)
 
 
 def call(kernel, outs, scratch, flops, *operands, fetched=0):
@@ -434,7 +429,7 @@
         ((residues, HEADS * cols), F32),
         ((2, residues, HEADS * cols), F32),
         ((2, residues, HEADS * cols), BF16),
-        ((4, width, cols), BF16),
+        ((2, width, cols), BF16),
     ]
     project_flops, attend_flops = 8 * cells * width * width, 4 * cells * residues * width
     if col_parts == 1:

time: 48.4 us -> 50.3 us (1.039)
  Pallas kernels: 5.78 us -> 7.64 us
    pallas_call x4, Pallas kernels: 5.78 us -> 7.64 us  [call(): pl.pallas_call(kernel, out_shape=shapes, in_specs=[far] * fetched + [vmem...]
where the time goes in v14:
time: 50.3 us; the launch traced here: 50 us
  blocking collectives  42.3 us (84%)
  Pallas kernels  7.64 us (15%)
    all_to_all x3, blocking collectives, swap(): lax.all_to_all(blocks, 'row', split_axis=0, concat_axis=0, axis_index_gro...  42.3 us
    pallas_call x4, Pallas kernels, call(): pl.pallas_call(kernel, out_shape=shapes, in_specs=[far] * fetched + [vmem...  7.64 us

profile of v14, /device:TPU:0, one launch (start us, length us, event | category | flops | bytes accessed | tf_op | source)
XLA Modules:
  0.0 50.0 jit_solution(16198546969605291584)
XLA Ops:
  0.0 2.1 %shard_map.127 = (bf16[16,128,128]{2,1,0:T(8,128)(2,1)S(1)}, f32[8,128,128]{2,1,0:T(8,128)S(1)}, bf16[128,128]{1,0:T(8,128)(2,1)S(1)}, bf16[128,128]{1,0:T(8,128...) custom-call(bf16[8,128,128]{2,1,0:T(8,128)(2,1)} %pair.1, ...), custom_call_target="tpu_custom_call" | custom-call | flops 167772160 | bytes 623616 | tf_op jit(solution)/shard_map/pallas_call | solution.py:312
  2.1 20.6 %all_to_all.15.edges = bf16[16,128,128]{2,1,0:T(8,128)(2,1)S(1)} all-to-all(bf16[16,128,128]{2,1,0:T(8,128)(2,1)S(1)} %get-tuple-element.17), channel_id=1, replica_groups={{11,15,14,13,12,10,9,8,7,6,5,4,3,2,1,0},{27,31,30,29,28,26,25,24,23,22,..., dimensions={0} | all-to-all | bytes 1048576 | tf_op jit(solution)/shard_map/all_to_all | solution.py:47
  22.8 0.3 shard_map.128
  23.1 0.0 copy-start
  23.1 11.6 %all_to_all.16.returned = bf16[16,64,128]{2,1,0:T(8,128)(2,1)S(1)} all-to-all(bf16[16,64,128]{2,1,0:T(8,128)(2,1)S(1)} %shard_map.128), channel_id=1, replica_groups={{11,15,14,13,12,10,9,8,7,6,5,4,3,2,1,0},{27,31,30,29,28,26,25,24,23,22,..., dimensions={0} | all-to-all | bytes 524288 | tf_op jit(solution)/shard_map/all_to_all | solution.py:47
  34.6 0.0 copy-done
  34.6 0.9 %shard_map.129 = (f32[8,128,128]{2,1,0:T(8,128)S(1)}, bf16[8,128,128]{2,1,0:T(8,128)(2,1)S(1)}, bf16[16,32,128]{2,1,0:T(8,128)(2,1)S(1)}) custom-call(bf16[16,64,128]{2,1,0:T(8,128)(2,1)S(1)} %all_to_all.16.returned, f32[8,128,128]{2,1,0:T(8,128)S(1)} %get-tuple-element.18.gate, bf16[8,128,128]{2,1,0:T(8,128)(2,1)S(1)} %copy-done, ...), custom_call_target="tpu_custom_call" | custom-call | flops 33554432 | bytes 1082368 | tf_op jit(solution)/shard_map/pallas_call | solution.py:312
  35.5 10.2 %all_to_all.17.refs_1_ = bf16[16,32,128]{2,1,0:T(8,128)(2,1)S(1)} all-to-all(bf16[16,32,128]{2,1,0:T(8,128)(2,1)S(1)} %get-tuple-element.27), channel_id=1, replica_groups={{11,15,14,13,12,10,9,8,7,6,5,4,3,2,1,0},{27,31,30,29,28,26,25,24,23,22,..., dimensions={0} | all-to-all | bytes 262144 | tf_op jit(solution)/shard_map/all_to_all | solution.py:47
  45.7 4.3 %shard_map.130 = bf16[8,128,128]{2,1,0:T(8,128)(2,1)} custom-call(bf16[8,128,128]{2,1,0:T(8,128)(2,1)S(1)} %get-tuple-element.21.att_norm, bf16[128,128]{1,0:T(8,128)(2,1)S(1)} %get-tuple-element.22.w_query, bf16[128,128]{1,0:T(8,128)(2,1)S(1)} %get-tuple-element.23.w_key, bf16[128,128]{1,0:T(8,128)(2,1)S(1)} %get-tuple-element.24.w_value, ...), custom_call_target="tpu_custom_call" | custom-call | flops 201326592 | bytes 1081344 | tf_op jit(solution)/shard_map/pallas_call | solution.py:312
Async XLA Ops:
  23.1 11.6 %copy-start = (bf16[8,128,128]{2,1,0:T(8,128)(2,1)S(1)}, bf16[8,128,128]{2,1,0:T(8,128)(2,1)}, u32[]{:S(2)}) copy-start(bf16[8,128,128]{2,1,0:T(8,128)(2,1)} %pair.1) | copy-start | bytes 786436

commit v15 on v9

--- a/solution.py
+++ b/solution.py
@@ -208,8 +208,6 @@
     cols, width = att_norm.shape[1], w_query.shape[1]
 
     def project(i):
-        if i % 2:
-            return
         keys = dot(side_by_side(att_norm, i), w_direct).astype(BF16)
         turned = dot(w_turned, jnp.concatenate([att_norm[i], att_norm[i + 1]], axis=0), NT)
         for row in range(2):
@@ -223,7 +221,7 @@
 
 
 def project_kernel(*refs):
-    pipeline(range(refs[0].shape[0]), projector(*refs))
+    pipeline(range(0, refs[0].shape[0], 2), projector(*refs))
 
 
 def whole_kernel(att_norm, w_query, w_key, w_value, w_att_gate, *refs):
@@ -243,8 +241,11 @@
     out,
     bias_t,
     scores,
+    peaks,
     weights,
     gated,
+    done,
+    sems,
     before=(),
 ):
     rows, width, cols = query_t.shape
@@ -256,56 +257,62 @@
     ]
 
     def score(i):
-        blocks = []
-        for mine, _ in heads:
-            above = jnp.zeros((mine.start, cols), BF16)
-            below = jnp.zeros((width - mine.stop, cols), BF16)
-            parts = [p for p in (above, query_t[i, mine, :], below) if p.shape[0]]
-            blocks.append(jnp.concatenate(parts, axis=0))
-        scores[i % 2] = dot(key[i], jnp.concatenate(blocks, axis=1)) * score_scale
-
-    def turn_bias():
-        for head, (_, span) in enumerate(heads):
-            parts = [
-                bias[slot(owner, bias.shape[0])].astype(F32)[head * head_rows : (head + 1) * head_rows]
-                for owner in range(bias.shape[0])
-            ]
-            bias_t[:, span] = jnp.concatenate(parts, axis=0).T * LOG2_E
+        for row in (i, i + 1):
+            blocks = []
+            for mine, _ in heads:
+                above = jnp.zeros((mine.start, cols), BF16)
+                below = jnp.zeros((width - mine.stop, cols), BF16)
+                parts = [p for p in (above, query_t[row, mine, :], below) if p.shape[0]]
+                blocks.append(jnp.concatenate(parts, axis=0))
+            raw = dot(key[row], jnp.concatenate(blocks, axis=1))
+            for _, span in heads:
+                biased = raw[:, span] * score_scale + bias_t[:, span]
+                scores[row % 4, :, span] = biased
+                peaks[row % 4, :, span] = jnp.max(biased, axis=0, keepdims=True)
 
     def soften(i):
-        if i == 0:
-            turn_bias()
-        for _, span in heads:
-            biased = scores[i % 2, :, span] + bias_t[:, span]
-            peak = jnp.max(biased, axis=0, keepdims=True)
-            weights[i % 2, :, span] = jnp.exp2(biased - peak).astype(BF16)
+        for row in (i, i + 1):
+            for _, span in heads:
+                lowered = scores[row % 4, :, span] - peaks[row % 4, :, span]
+                weights[row % 4, :, span] = jnp.exp2(lowered).astype(BF16)
 
     def collect(i):
-        for head in range(0, HEADS, 2):
-            (first, left), (second, right) = heads[head : head + 2]
-            values = jnp.concatenate([value_t[i, first.start : second.stop, :], ones], axis=0)
-            summed = dot(values, weights[i % 2, :, left.start : right.stop])
-            share = 1.0 / summed[2 * HEAD_DIM : 2 * HEAD_DIM + 1]
-            for mine, there, lanes in (
-                (first, slice(0, HEAD_DIM), slice(0, cols)),
-                (second, slice(HEAD_DIM, 2 * HEAD_DIM), slice(cols, 2 * cols)),
-            ):
-                attended = summed[there, lanes] * share[:, lanes] * gate_t[i, mine, :]
-                gated[i % 4, mine, :] = attended.astype(BF16)
+        for row in (i, i + 1):
+            for head in range(0, HEADS, 2):
+                (first, left), (second, right) = heads[head : head + 2]
+                values = jnp.concatenate([value_t[row, first.start : second.stop, :], ones], axis=0)
+                summed = dot(values, weights[row % 4, :, left.start : right.stop])
+                share = 1.0 / summed[2 * HEAD_DIM : 2 * HEAD_DIM + 1]
+                for mine, there, lanes in (
+                    (first, slice(0, HEAD_DIM), slice(0, cols)),
+                    (second, slice(HEAD_DIM, 2 * HEAD_DIM), slice(cols, 2 * cols)),
+                ):
+                    attended = summed[there, lanes] * share[:, lanes] * gate_t[row, mine, :]
+                    gated[row % 4, mine, :] = attended.astype(BF16)
 
     def finish(i):
-        if i % 2 == 0:
-            return
-        turned = jnp.concatenate([gated[(i - 1) % 4].T, gated[i % 4].T], axis=1)
+        turned = jnp.concatenate([gated[i % 4].T, gated[(i + 1) % 4].T], axis=1)
         both = dot(turned, w_last)
-        out[i - 1] = (first_pass[i - 1] + both[:, :width]).astype(BF16)
-        out[i] = (first_pass[i] + both[:, width:]).astype(BF16)
-
+        done[i] = (first_pass[i] + both[:, :width]).astype(BF16)
+        done[i + 1] = (first_pass[i + 1] + both[:, width:]).astype(BF16)
+        copy = pltpu.make_async_copy(done.at[pl.ds(i, 2)], out.at[pl.ds(i, 2)], sems.at[i // 2])
+        copy.start()
+        copies.append(copy)
+
+    copies = []
     w_last = twice(w_att_out[...])
-    pipeline(range(rows), *before, score, soften, collect, finish)
-
-
-def call(kernel, outs, scratch, flops, *operands, fetched=0):
+    for head, (_, span) in enumerate(heads):
+        parts = [
+            bias[slot(owner, bias.shape[0])].astype(F32)[head * head_rows : (head + 1) * head_rows]
+            for owner in range(bias.shape[0])
+        ]
+        bias_t[:, span] = jnp.concatenate(parts, axis=0).T * LOG2_E
+    pipeline(range(0, rows, 2), *before, score, soften, collect, finish)
+    for copy in copies:
+        copy.wait()
+
+
+def call(kernel, outs, scratch, flops, *operands, fetched=0, sent=False):
     vmem = pl.BlockSpec(memory_space=pltpu.VMEM)
     far = pl.BlockSpec(memory_space=pltpu.HBM)
     shapes = [jax.ShapeDtypeStruct(shape, dtype) for shape, dtype in outs]
@@ -318,7 +325,7 @@
         kernel,
         out_shape=shapes,
         in_specs=[far] * fetched + [vmem] * (len(operands) - fetched),
-        out_specs=[vmem] * len(shapes),
+        out_specs=[far if sent else vmem] * len(shapes),
         scratch_shapes=[pltpu.VMEM(*s) if isinstance(s, tuple) else s for s in scratch],
         compiler_params=pltpu.CompilerParams(vmem_limit_bytes=48 * 2**20),
         cost_estimate=pl.CostEstimate(flops=flops, bytes_accessed=moved, transcendentals=0),
@@ -432,21 +439,24 @@
     out = [((rows, cols, width), BF16)]
     held = [
         ((residues, HEADS * cols), F32),
-        ((2, residues, HEADS * cols), F32),
-        ((2, residues, HEADS * cols), BF16),
+        ((4, residues, HEADS * cols), F32),
+        ((4, 1, HEADS * cols), F32),
+        ((4, residues, HEADS * cols), BF16),
         ((4, width, cols), BF16),
+        ((rows, cols, width), BF16),
+        pltpu.SemaphoreType.DMA((rows // 2,)),
     ]
     project_flops, attend_flops = 8 * cells * width * width, 4 * cells * residues * width
     if col_parts == 1:
         flops = project_flops + attend_flops
         given = (first_pass, bias, w_att_out)
-        return call(whole_kernel, out, projected + held, flops, *projecting, *given)
+        return call(whole_kernel, out, projected + held, flops, *projecting, *given, sent=True)
     query_t, key, value_t, gate_t = call(project_kernel, projected, [], project_flops, *projecting)
     bias = by_slot(lax.all_to_all(by_rank(bias), "col", split_axis=0, concat_axis=2, tiled=True))
     key = lax.all_gather(key, "col", axis=1, tiled=True)
     value_t = lax.all_gather(value_t, "col", axis=2, tiled=True)
     given = (query_t, key, value_t, gate_t, first_pass, bias, w_att_out)
-    return call(attend_kernel, out, held, attend_flops, *given)
+    return call(attend_kernel, out, held, attend_flops, *given, sent=True)
 
 
 def solution(mesh):

time: 48.4 us -> 48 us (level)
  no operation moved by 1% of the time
where the time goes in v15:
time: 48 us; the launch traced here: 47.8 us
  blocking collectives  42.3 us (88%)
  Pallas kernels  5.39 us (11%)
    all_to_all x3, blocking collectives, swap(): lax.all_to_all(blocks, 'row', split_axis=0, concat_axis=0, axis_index_gro...  42.3 us
    pallas_call x4, Pallas kernels, call(): pl.pallas_call(kernel, out_shape=shapes, in_specs=[far] * fetched + [vmem...  5.39 us

profile of v15, /device:TPU:0, one launch (start us, length us, event | category | flops | bytes accessed | tf_op | source)
XLA Modules:
  0.0 47.8 jit_solution(11150610863683810010)
XLA Ops:
  0.0 2.1 %shard_map.127 = (bf16[16,128,128]{2,1,0:T(8,128)(2,1)S(1)}, f32[8,128,128]{2,1,0:T(8,128)S(1)}, bf16[128,128]{1,0:T(8,128)(2,1)S(1)}, bf16[128,128]{1,0:T(8,128...) custom-call(bf16[8,128,128]{2,1,0:T(8,128)(2,1)} %pair.1, ...), custom_call_target="tpu_custom_call" | custom-call | flops 167772160 | bytes 623616 | tf_op jit(solution)/shard_map/pallas_call | solution.py:324
  2.1 20.6 %all_to_all.15.edges = bf16[16,128,128]{2,1,0:T(8,128)(2,1)S(1)} all-to-all(bf16[16,128,128]{2,1,0:T(8,128)(2,1)S(1)} %get-tuple-element.17), channel_id=1, replica_groups={{11,15,14,13,12,10,9,8,7,6,5,4,3,2,1,0},{27,31,30,29,28,26,25,24,23,22,..., dimensions={0} | all-to-all | bytes 1048576 | tf_op jit(solution)/shard_map/all_to_all | solution.py:47
  22.8 0.3 shard_map.128
  23.1 0.0 copy-start
  23.1 11.6 %all_to_all.16.returned = bf16[16,64,128]{2,1,0:T(8,128)(2,1)S(1)} all-to-all(bf16[16,64,128]{2,1,0:T(8,128)(2,1)S(1)} %shard_map.128), channel_id=1, replica_groups={{11,15,14,13,12,10,9,8,7,6,5,4,3,2,1,0},{27,31,30,29,28,26,25,24,23,22,..., dimensions={0} | all-to-all | bytes 524288 | tf_op jit(solution)/shard_map/all_to_all | solution.py:47
  34.6 0.0 copy-done
  34.6 0.9 %shard_map.129 = (f32[8,128,128]{2,1,0:T(8,128)S(1)}, bf16[8,128,128]{2,1,0:T(8,128)(2,1)S(1)}, bf16[16,32,128]{2,1,0:T(8,128)(2,1)S(1)}) custom-call(bf16[16,64,128]{2,1,0:T(8,128)(2,1)S(1)} %all_to_all.16.returned, f32[8,128,128]{2,1,0:T(8,128)S(1)} %get-tuple-element.18.gate, bf16[8,128,128]{2,1,0:T(8,128)(2,1)S(1)} %copy-done, ...), custom_call_target="tpu_custom_call" | custom-call | flops 33554432 | bytes 1082368 | tf_op jit(solution)/shard_map/pallas_call | solution.py:324
  35.5 10.2 %all_to_all.17.refs_1_ = bf16[16,32,128]{2,1,0:T(8,128)(2,1)S(1)} all-to-all(bf16[16,32,128]{2,1,0:T(8,128)(2,1)S(1)} %get-tuple-element.27), channel_id=1, replica_groups={{11,15,14,13,12,10,9,8,7,6,5,4,3,2,1,0},{27,31,30,29,28,26,25,24,23,22,..., dimensions={0} | all-to-all | bytes 262144 | tf_op jit(solution)/shard_map/all_to_all | solution.py:47
  45.7 2.1 %shard_map.130 = bf16[8,128,128]{2,1,0:T(8,128)(2,1)} custom-call(bf16[8,128,128]{2,1,0:T(8,128)(2,1)S(1)} %get-tuple-element.21.att_norm, bf16[128,128]{1,0:T(8,128)(2,1)S(1)} %get-tuple-element.22.w_query, bf16[128,128]{1,0:T(8,128)(2,1)S(1)} %get-tuple-element.23.w_key, bf16[128,128]{1,0:T(8,128)(2,1)S(1)} %get-tuple-element.24.w_value, ...), custom_call_target="tpu_custom_call" | custom-call | flops 201326592 | bytes 1081344 | tf_op jit(solution)/shard_map/pallas_call | solution.py:324
Async XLA Ops:
  23.1 11.6 %copy-start = (bf16[8,128,128]{2,1,0:T(8,128)(2,1)S(1)}, bf16[8,128,128]{2,1,0:T(8,128)(2,1)}, u32[]{:S(2)}) copy-start(bf16[8,128,128]{2,1,0:T(8,128)(2,1)} %pair.1) | copy-start | bytes 786436

commit v16 on v13

--- a/solution.py
+++ b/solution.py
@@ -102,53 +102,54 @@
     return project
 
 
-def right_kernel(members, *refs):
-    given, (right, normed, *staged), (pair, w_right, w_right_gate, held, sems) = refs[:13], refs[13:25], refs[25:]
-    targets = [pair, w_right, w_right_gate, *staged]
+def edges_kernel(*refs):
+    given, (right, far, near, normed, *staged) = refs[:13], refs[13:25]
+    pair, weights, held, sems = refs[25:]
+    targets = [pair, *(weights.at[n] for n in range(4)), *staged]
     copies = [
         pltpu.make_async_copy(source, target, sems.at[n])
         for n, (source, target) in enumerate(zip(given, targets))
     ]
     for copy in copies:
         copy.start()
-    for copy in copies[:3]:
+    for copy in copies[:5]:
         copy.wait()
 
     def norm(i):
         normed[i] = lane_norm(pair[i].astype(F32))
         normed[i + 1] = lane_norm(pair[i + 1].astype(F32))
 
-    pipeline(range(0, pair.shape[0], 2), norm, gated_edges(normed, w_right, w_right_gate, held))
-    owners, block = right.shape[0], right.shape[1]
+    steps = [gated_edges(normed, weights.at[2 * n], weights.at[2 * n + 1], held.at[n]) for n in range(2)]
+    pipeline(range(0, pair.shape[0], 2), norm, *steps)
+    owners, block, parts = right.shape[0], right.shape[1], held.shape[1]
+    members, turns = owners // 2, near.shape[0]
+    me = lax.rem(lax.axis_index("row"), members)
     for member in range(members):
-        for part in range(held.shape[0]):
-            sent = held[part, member * block : (member + 1) * block, :].astype(BF16)
+        mine = pl.ds(pl.multiple_of((me ^ member) * block, block), block)
+        out = (near, far)[member // turns]
+        for part in range(parts):
+            lanes = slice(part * LANES, (part + 1) * LANES)
+            out[member % turns, :, lanes] = held[0, part, mine, :].astype(BF16)
+    for member in range(members):
+        for part in range(parts):
+            lanes = slice(part * LANES, (part + 1) * LANES)
+            sent = held[1, part, member * block : (member + 1) * block, :].astype(BF16)
             for owner in range(member, owners, members):
-                right[slot(owner, owners), :, part * LANES : (part + 1) * LANES] = sent
-    for copy in copies[3:]:
+                right[slot(owner, owners), :, lanes] = sent
+    for copy in copies[5:]:
         copy.wait()
 
 
-def left_kernel(normed, w_left, w_left_gate, w_tri_gate, gate, *refs):
-    left, held = refs[:-1], refs[-1]
-    near = len(left)
-    me = lax.rem(lax.axis_index("row"), 2 * near)
+def merge_kernel(normed, w_tri_gate, near, passed, gate, *left):
+    for turn, out in enumerate(left):
+        out[0] = near[turn]
+        out[1] = passed[turn]
     width = w_tri_gate.shape[1]
     gate_weight = twice(w_tri_gate[...])
-
-    def open_gate(i):
+    for i in range(0, normed.shape[0], 2):
         opened = sigmoid(dot(side_by_side(normed, i), gate_weight))
         gate[i] = opened[:, :width]
         gate[i + 1] = opened[:, width:]
-
-    step = gated_edges(normed, w_left, w_left_gate, held)
-    pipeline(range(0, normed.shape[0], 2), step, open_gate)
-    for turn in range(2 * near):
-        block = left[0].shape[1]
-        mine = pl.ds(pl.multiple_of((me ^ turn) * block, block), block)
-        for part in range(held.shape[0]):
-            lanes = slice(part * LANES, (part + 1) * LANES)
-            left[turn % near][turn // near, :, lanes] = held[part, mine, :].astype(BF16)
 
 
 def channel_rows(blocks, rows, channel):
@@ -166,8 +167,7 @@
 
 
 def left_blocks(refs):
-    *near, far = refs
-    return [block.at[0] for block in near] + [far.at[s] for s in range(len(near))]
+    return [block.at[0] for block in refs] + [block.at[1] for block in refs]
 
 
 def triangle_kernel(rows, right, *refs):
@@ -249,8 +249,6 @@
     cols, width = att_norm.shape[1], w_query.shape[1]
 
     def project(i):
-        if i % 2:
-            return
         keys = dot(side_by_side(att_norm, i), w_direct).astype(BF16)
         turned = dot(w_turned, jnp.concatenate([att_norm[i], att_norm[i + 1]], axis=0), NT)
         for row in range(2):
@@ -264,7 +262,7 @@
 
 
 def project_kernel(*refs):
-    pipeline(range(refs[0].shape[0]), projector(*refs))
+    pipeline(range(0, refs[0].shape[0], 2), projector(*refs))
 
 
 def whole_kernel(att_norm, w_query, w_key, w_value, w_att_gate, *refs):
@@ -284,8 +282,11 @@
     out,
     bias_t,
     scores,
+    peaks,
     weights,
     gated,
+    done,
+    sems,
     before=(),
 ):
     rows, width, cols = query_t.shape
@@ -297,56 +298,62 @@
     ]
 
     def score(i):
-        blocks = []
-        for mine, _ in heads:
-            above = jnp.zeros((mine.start, cols), BF16)
-            below = jnp.zeros((width - mine.stop, cols), BF16)
-            parts = [p for p in (above, query_t[i, mine, :], below) if p.shape[0]]
-            blocks.append(jnp.concatenate(parts, axis=0))
-        scores[i % 2] = dot(key[i], jnp.concatenate(blocks, axis=1)) * score_scale
-
-    def turn_bias():
-        for head, (_, span) in enumerate(heads):
-            parts = [
-                bias[slot(owner, bias.shape[0])].astype(F32)[head * head_rows : (head + 1) * head_rows]
-                for owner in range(bias.shape[0])
-            ]
-            bias_t[:, span] = jnp.concatenate(parts, axis=0).T * LOG2_E
+        for row in (i, i + 1):
+            blocks = []
+            for mine, _ in heads:
+                above = jnp.zeros((mine.start, cols), BF16)
+                below = jnp.zeros((width - mine.stop, cols), BF16)
+                parts = [p for p in (above, query_t[row, mine, :], below) if p.shape[0]]
+                blocks.append(jnp.concatenate(parts, axis=0))
+            raw = dot(key[row], jnp.concatenate(blocks, axis=1))
+            for _, span in heads:
+                biased = raw[:, span] * score_scale + bias_t[:, span]
+                scores[row % 4, :, span] = biased
+                peaks[row % 4, :, span] = jnp.max(biased, axis=0, keepdims=True)
 
     def soften(i):
-        if i == 0:
-            turn_bias()
-        for _, span in heads:
-            biased = scores[i % 2, :, span] + bias_t[:, span]
-            peak = jnp.max(biased, axis=0, keepdims=True)
-            weights[i % 2, :, span] = jnp.exp2(biased - peak).astype(BF16)
+        for row in (i, i + 1):
+            for _, span in heads:
+                lowered = scores[row % 4, :, span] - peaks[row % 4, :, span]
+                weights[row % 4, :, span] = jnp.exp2(lowered).astype(BF16)
 
     def collect(i):
-        for head in range(0, HEADS, 2):
-            (first, left), (second, right) = heads[head : head + 2]
-            values = jnp.concatenate([value_t[i, first.start : second.stop, :], ones], axis=0)
-            summed = dot(values, weights[i % 2, :, left.start : right.stop])
-            share = 1.0 / summed[2 * HEAD_DIM : 2 * HEAD_DIM + 1]
-            for mine, there, lanes in (
-                (first, slice(0, HEAD_DIM), slice(0, cols)),
-                (second, slice(HEAD_DIM, 2 * HEAD_DIM), slice(cols, 2 * cols)),
-            ):
-                attended = summed[there, lanes] * share[:, lanes] * gate_t[i, mine, :]
-                gated[i % 4, mine, :] = attended.astype(BF16)
+        for row in (i, i + 1):
+            for head in range(0, HEADS, 2):
+                (first, left), (second, right) = heads[head : head + 2]
+                values = jnp.concatenate([value_t[row, first.start : second.stop, :], ones], axis=0)
+                summed = dot(values, weights[row % 4, :, left.start : right.stop])
+                share = 1.0 / summed[2 * HEAD_DIM : 2 * HEAD_DIM + 1]
+                for mine, there, lanes in (
+                    (first, slice(0, HEAD_DIM), slice(0, cols)),
+                    (second, slice(HEAD_DIM, 2 * HEAD_DIM), slice(cols, 2 * cols)),
+                ):
+                    attended = summed[there, lanes] * share[:, lanes] * gate_t[row, mine, :]
+                    gated[row % 4, mine, :] = attended.astype(BF16)
 
     def finish(i):
-        if i % 2 == 0:
-            return
-        turned = jnp.concatenate([gated[(i - 1) % 4].T, gated[i % 4].T], axis=1)
+        turned = jnp.concatenate([gated[i % 4].T, gated[(i + 1) % 4].T], axis=1)
         both = dot(turned, w_last)
-        out[i - 1] = (first_pass[i - 1] + both[:, :width]).astype(BF16)
-        out[i] = (first_pass[i] + both[:, width:]).astype(BF16)
-
+        done[i] = (first_pass[i] + both[:, :width]).astype(BF16)
+        done[i + 1] = (first_pass[i + 1] + both[:, width:]).astype(BF16)
+        copy = pltpu.make_async_copy(done.at[pl.ds(i, 2)], out.at[pl.ds(i, 2)], sems.at[i // 2])
+        copy.start()
+        copies.append(copy)
+
+    copies = []
     w_last = twice(w_att_out[...])
-    pipeline(range(rows), *before, score, soften, collect, finish)
-
-
-def call(kernel, outs, scratch, flops, *operands, fetched=0):
+    for head, (_, span) in enumerate(heads):
+        parts = [
+            bias[slot(owner, bias.shape[0])].astype(F32)[head * head_rows : (head + 1) * head_rows]
+            for owner in range(bias.shape[0])
+        ]
+        bias_t[:, span] = jnp.concatenate(parts, axis=0).T * LOG2_E
+    pipeline(range(0, rows, 2), *before, score, soften, collect, finish)
+    for copy in copies:
+        copy.wait()
+
+
+def call(kernel, outs, scratch, flops, *operands, fetched=0, sent=False):
     vmem = pl.BlockSpec(memory_space=pltpu.VMEM)
     far = pl.BlockSpec(memory_space=pltpu.HBM)
     shapes = [jax.ShapeDtypeStruct(shape, dtype) for shape, dtype in outs]
@@ -359,7 +366,7 @@
         kernel,
         out_shape=shapes,
         in_specs=[far] * fetched + [vmem] * (len(operands) - fetched),
-        out_specs=[vmem] * len(shapes),
+        out_specs=[far if sent else vmem] * len(shapes),
         scratch_shapes=[pltpu.VMEM(*s) if isinstance(s, tuple) else s for s in scratch],
         compiler_params=pltpu.CompilerParams(vmem_limit_bytes=48 * 2**20),
         cost_estimate=pl.CostEstimate(flops=flops, bytes_accessed=moved, transcendentals=0),
@@ -391,46 +398,48 @@
     residues = owners * rows
     cells = rows * cols
 
-    later = (w_left, w_left_gate, w_tri_gate, w_tri_out, w_query, w_key, w_value, w_att_gate, w_att_out)
-    right, normed, *later, w_bias_t = call(
-        functools.partial(right_kernel, half),
+    later = (w_tri_gate, w_tri_out, w_query, w_key, w_value, w_att_gate, w_att_out)
+    right, far, left, normed, *later, w_bias_t = call(
+        edges_kernel,
         [
             ((owners, own * rows, cols), BF16),
+            ((near, own * rows, cols), BF16),
+            ((near, own * rows, cols), BF16),
             (pair_rep.shape, BF16),
             *[(w.shape, BF16) for w in later],
             (w_bias.shape[::-1], BF16),
         ],
         [
             (pair_rep.shape, BF16),
-            (w_right.shape, BF16),
-            (w_right_gate.shape, BF16),
-            ((cols // LANES, channels * rows, LANES), F32),
+            ((4, width, channels), BF16),
+            ((2, cols // LANES, channels * rows, LANES), F32),
             pltpu.SemaphoreType.DMA((13,)),
         ],
-        4 * cells * width * channels,
+        8 * cells * width * channels,
         pair_rep,
+        w_left,
+        w_left_gate,
         w_right,
         w_right_gate,
         *later,
         w_bias.T,
         fetched=13,
     )
-    w_left, w_left_gate, w_tri_gate, w_tri_out, w_query, w_key, w_value, w_att_gate, w_att_out = later
+    w_tri_gate, w_tri_out, w_query, w_key, w_value, w_att_gate, w_att_out = later
+    passed = lax.ppermute(far, "row", [(r, r ^ near) for r in range(owners)])
     right = swap(right, owners)
     gate, *left = call(
-        left_kernel,
+        merge_kernel,
         [((rows, cols, width), F32)] + [((2, own * rows, cols), BF16)] * near,
-        [((cols // LANES, channels * rows, LANES), F32)],
-        6 * cells * width * channels,
+        [],
+        2 * cells * width * channels,
         normed,
-        w_left,
-        w_left_gate,
         w_tri_gate,
+        left,
+        passed,
     )
     for turn in range(1, near):
         left[turn] = lax.ppermute(left[turn], "row", [(r, r ^ turn) for r in range(owners)])
-    passed_on = jnp.stack([block[1] for block in left])
-    left.append(lax.ppermute(passed_on, "row", [(r, r ^ near) for r in range(owners)]))
     flops = 2 * own * half * rows * residues * cols
     if col_parts == 1:
         summed = call(
@@ -485,21 +494,24 @@
     out = [((rows, cols, width), BF16)]
     held = [
         ((residues, HEADS * cols), F32),
-        ((2, residues, HEADS * cols), F32),
-        ((2, residues, HEADS * cols), BF16),
+        ((4, residues, HEADS * cols), F32),
+        ((4, 1, HEADS * cols), F32),
+        ((4, residues, HEADS * cols), BF16),
         ((4, width, cols), BF16),
+        ((rows, cols, width), BF16),
+        pltpu.SemaphoreType.DMA((rows // 2,)),
     ]
     project_flops, attend_flops = 8 * cells * width * width, 4 * cells * residues * width
     if col_parts == 1:
         flops = project_flops + attend_flops
         given = (first_pass, bias, w_att_out)
-        return call(whole_kernel, out, projected + held, flops, *projecting, *given)
+        return call(whole_kernel, out, projected + held, flops, *projecting, *given, sent=True)
     query_t, key, value_t, gate_t = call(project_kernel, projected, [], project_flops, *projecting)
     bias = by_slot(lax.all_to_all(by_rank(bias), "col", split_axis=0, concat_axis=2, tiled=True))
     key = lax.all_gather(key, "col", axis=1, tiled=True)
     value_t = lax.all_gather(value_t, "col", axis=2, tiled=True)
     given = (query_t, key, value_t, gate_t, first_pass, bias, w_att_out)
-    return call(attend_kernel, out, held, attend_flops, *given)
+    return call(attend_kernel, out, held, attend_flops, *given, sent=True)
 
 
 def solution(mesh):

time: 50.7 us -> 54.8 us (1.081)
  waiting for transfers between devices: 7.66 us -> 14.6 us
  local copies, waits for them, and re-layouts: 2.04 us -> 0.01 us
    ppermute x1, waiting for transfers between devices: 4.05 us -> 11.8 us  [body(): passed = lax.ppermute(far, 'row', [(r, r ^ near) for r in range(owners)])]
    unnamed x10 -> x2, local copies, waits for them, and re-layouts: 1.27 us -> 0.01 us
    ppermute x3, waiting for transfers between devices: 3.6 us -> 2.78 us  [body(): lax.ppermute(left[turn], 'row', [(r, r ^ turn) for r in range(owners)])]
    slice x6 -> x0, local copies, waits for them, and re-layouts: 0.77 us -> none  [body(): passed_on = jnp.stack([block[1] for block in left])]
  transfers between devices with their start and end apart: 5 -> 5, of which waited for: 2 -> 4; matrix products, arithmetic and copies ran while one was open for 0% -> 0% of each run, Pallas kernels for 1% -> 0%
where the time goes in v16:
time: 54.8 us; the launch traced here: 54.5 us
  blocking collectives  19.8 us (36%)
  waiting for transfers between devices  14.6 us (27%)
  starting transfers between devices  13.5 us (25%)
  Pallas kernels  6.57 us (12%)
    all_to_all x2, blocking collectives, swap(): lax.all_to_all(blocks, 'row', split_axis=0, concat_axis=0, axis_index_gro...  19.8 us
    ppermute x1, waiting for transfers between devices, body(): passed = lax.ppermute(far, 'row', [(r, r ^ near) for r in range(owners)])  11.8 us
    all_to_all x1, starting transfers between devices, swap(): lax.all_to_all(blocks, 'row', split_axis=0, concat_axis=0, axis_index_gro...  9.39 us
    pallas_call x5, Pallas kernels, call(): pl.pallas_call(kernel, out_shape=shapes, in_specs=[far] * fetched + [vmem...  6.57 us
    ppermute x3, starting transfers between devices, body(): lax.ppermute(left[turn], 'row', [(r, r ^ turn) for r in range(owners)])  3.55 us
    ppermute x3, waiting for transfers between devices, body(): lax.ppermute(left[turn], 'row', [(r, r ^ turn) for r in range(owners)])  2.78 us
  transfers between devices with their start and end apart: 5, of which 4 were waited for; matrix products, arithmetic and copies ran while one was open for 0% of the time, Pallas kernels for 0%

profile of v16, /device:TPU:0, one launch (start us, length us, event | category | flops | bytes accessed | tf_op | source)
XLA Modules:
  0.0 54.5 jit_solution(8961055913811214001)
XLA Ops:
  0.0 2.9 %shard_map.127 = (bf16[16,128,128]{2,1,0:T(8,128)(2,1)}, bf16[4,128,128]{2,1,0:T(8,128)(2,1)S(1)}, bf16[4,128,128]{2,1,0:T(8,128)(2,1)S(1)}, bf16[8,128,128]{2,1...) custom-call(bf16[8,128,128]{2,1,0:T(8,128)(2,1)} %pair.1, ...), custom_call_target="tpu_custom_call" | custom-call | flops 134217728 | bytes 623616 | tf_op jit(solution)/shard_map/pallas_call | solution.py:365
  2.9 9.4 %all-to-all-start = ((bf16[16,128,128]{2,1,0:T(8,128)(2,1)}), bf16[16,128,128]{2,1,0:T(8,128)(2,1)S(1)}, u32[]{:S(2)}, u32[]{:S(2)}) async-start(bf16[16,128,128]{2,1,0:T(8,128)(2,1)} %get-tuple-element.25), calls=%async_computation | async-start | bytes 1048576 | tf_op jit(solution)/shard_map/all_to_all | solution.py:55
  12.3 0.5 collective-permute-start
  12.8 11.8 %collective-permute-done.passed = bf16[4,128,128]{2,1,0:T(8,128)(2,1)S(1)} collective-permute-done((bf16[4,128,128]{2,1,0:T(8,128)(2,1)S(1)}, bf16[4,128,128]{2,1,0:T(8,128)(2,1)S(1)}, u32[]{:S(2)}, u32[]{:S(2)}) %collective-permute-start) | collective-permute-done | bytes 131104 | tf_op jit(solution)/shard_map/ppermute | solution.py:429
  24.7 0.3 shard_map.128
  24.9 0.7 %collective-permute-start.1 = (bf16[2,128,128]{2,1,0:T(8,128)(2,1)S(1)}, bf16[2,128,128]{2,1,0:T(8,128)(2,1)S(1)}, u32[]{:S(2)}, u32[]{:S(2)}) collective-permute-start(bf16[2,128,128]{2,1,0:T(8,128)(2,1)S(1)} %get-tuple-element.31), channel_id=1, source_target_pairs={{0,1},{1,0},{2,3},{3,2},{4,5},{5,4},{6,7},{7,6},{8,9},{9,8},{10,11... | collective-permute-start | bytes 196616 | tf_op jit(solution)/shard_map/ppermute | solution.py:442
  25.6 0.5 collective-permute-start.2
  26.1 2.4 %collective-permute-start.3 = (bf16[2,128,128]{2,1,0:T(8,128)(2,1)S(1)}, bf16[2,128,128]{2,1,0:T(8,128)(2,1)S(1)}, u32[]{:S(2)}, u32[]{:S(2)}) collective-permute-start(bf16[2,128,128]{2,1,0:T(8,128)(2,1)S(1)} %get-tuple-element.33), channel_id=1, source_target_pairs={{0,3},{1,2},{2,1},{3,0},{4,7},{5,6},{6,5},{7,4},{8,11},{9,10},{10,... | collective-permute-start | bytes 196616 | tf_op jit(solution)/shard_map/ppermute | solution.py:442
  28.5 1.0 %collective-permute-done.1.refs_1_ = bf16[2,128,128]{2,1,0:T(8,128)(2,1)S(1)} collective-permute-done((bf16[2,128,128]{2,1,0:T(8,128)(2,1)S(1)}, bf16[2,128,128]{2,1,0:T(8,128)(2,1)S(1)}, u32[]{:S(2)}, u32[]{:S(2)}) %collective-permute-start.1) | collective-permute-done | bytes 65568 | tf_op jit(solution)/shard_map/ppermute | solution.py:442
  29.5 0.4 collective-permute-done.2.refs_2_
  29.9 1.4 %collective-permute-done.3.refs_3_ = bf16[2,128,128]{2,1,0:T(8,128)(2,1)S(1)} collective-permute-done((bf16[2,128,128]{2,1,0:T(8,128)(2,1)S(1)}, bf16[2,128,128]{2,1,0:T(8,128)(2,1)S(1)}, u32[]{:S(2)}, u32[]{:S(2)}) %collective-permute-start.3) | collective-permute-done | bytes 65568 | tf_op jit(solution)/shard_map/ppermute | solution.py:442
  31.3 0.0 all-to-all-done.right
  31.3 0.5 shard_map.129
  31.7 0.0 copy-start
  31.7 9.7 %all_to_all.15.returned = bf16[8,128,128]{2,1,0:T(8,128)(2,1)S(1)} all-to-all(bf16[8,128,128]{2,1,0:T(8,128)(2,1)S(1)} %shard_map.129), channel_id=1, replica_groups={{5,7,6,4,3,2,1,0},{13,15,14,12,11,10,9,8},{21,23,22,20,19,18,17,16},{29..., dimensions={0} | all-to-all | bytes 524288 | tf_op jit(solution)/shard_map/all_to_all | solution.py:55
  41.5 0.0 copy-done
  41.5 0.9 %shard_map.130 = (f32[8,128,128]{2,1,0:T(8,128)S(1)}, bf16[8,128,128]{2,1,0:T(8,128)(2,1)S(1)}, bf16[16,32,128]{2,1,0:T(8,128)(2,1)S(1)}) custom-call(bf16[8,128,128]{2,1,0:T(8,128)(2,1)S(1)} %all_to_all.15.returned, f32[8,128,128]{2,1,0:T(8,128)S(1)} %get-tuple-element.34.gate, bf16[8,128,128]{2,1,0:T(8,128)(2,1)S(1)} %copy-done, ...), custom_call_target="tpu_custom_call" | custom-call | flops 33554432 | bytes 1082368 | tf_op jit(solution)/shard_map/pallas_call | solution.py:365
  42.4 10.1 %all_to_all.16.refs_1_ = bf16[16,32,128]{2,1,0:T(8,128)(2,1)S(1)} all-to-all(bf16[16,32,128]{2,1,0:T(8,128)(2,1)S(1)} %get-tuple-element.43), channel_id=1, replica_groups={{11,15,14,13,12,10,9,8,7,6,5,4,3,2,1,0},{27,31,30,29,28,26,25,24,23,22,..., dimensions={0} | all-to-all | bytes 262144 | tf_op jit(solution)/shard_map/all_to_all | solution.py:55
  52.4 2.1 %shard_map.131 = bf16[8,128,128]{2,1,0:T(8,128)(2,1)} custom-call(bf16[8,128,128]{2,1,0:T(8,128)(2,1)S(1)} %get-tuple-element.37.att_norm, bf16[128,128]{1,0:T(8,128)(2,1)S(1)} %get-tuple-element.38.w_query, bf16[128,128]{1,0:T(8,128)(2,1)S(1)} %get-tuple-element.39.w_key, bf16[128,128]{1,0:T(8,128)(2,1)S(1)} %get-tuple-element.40.w_value, ...), custom_call_target="tpu_custom_call" | custom-call | flops 201326592 | bytes 1081344 | tf_op jit(solution)/shard_map/pallas_call | solution.py:365
Async XLA Ops:
  2.9 28.4 %all-to-all-start = ((bf16[16,128,128]{2,1,0:T(8,128)(2,1)}), bf16[16,128,128]{2,1,0:T(8,128)(2,1)S(1)}, u32[]{:S(2)}, u32[]{:S(2)}) async-start(bf16[16,128,128]{2,1,0:T(8,128)(2,1)} %get-tuple-element.25), calls=%async_computation | async-start | bytes 1048576 | tf_op jit(solution)/shard_map/all_to_all | solution.py:55
  12.3 12.4 %collective-permute-start = (bf16[4,128,128]{2,1,0:T(8,128)(2,1)S(1)}, bf16[4,128,128]{2,1,0:T(8,128)(2,1)S(1)}, u32[]{:S(2)}, u32[]{:S(2)}) collective-permute-start(bf16[4,128,128]{2,1,0:T(8,128)(2,1)S(1)} %get-tuple-element.29), channel_id=1, source_target_pairs={{0,4},{1,5},{2,6},{3,7},{4,0},{5,1},{6,2},{7,3},{8,12},{9,13},{10,... | collective-permute-start | bytes 393224 | tf_op jit(solution)/shard_map/ppermute | solution.py:429
  24.9 4.5 %collective-permute-start.1 = (bf16[2,128,128]{2,1,0:T(8,128)(2,1)S(1)}, bf16[2,128,128]{2,1,0:T(8,128)(2,1)S(1)}, u32[]{:S(2)}, u32[]{:S(2)}) collective-permute-start(bf16[2,128,128]{2,1,0:T(8,128)(2,1)S(1)} %get-tuple-element.31), channel_id=1, source_target_pairs={{0,1},{1,0},{2,3},{3,2},{4,5},{5,4},{6,7},{7,6},{8,9},{9,8},{10,11... | collective-permute-start | bytes 196616 | tf_op jit(solution)/shard_map/ppermute | solution.py:442
  25.6 4.3 %collective-permute-start.2 = (bf16[2,128,128]{2,1,0:T(8,128)(2,1)S(1)}, bf16[2,128,128]{2,1,0:T(8,128)(2,1)S(1)}, u32[]{:S(2)}, u32[]{:S(2)}) collective-permute-start(bf16[2,128,128]{2,1,0:T(8,128)(2,1)S(1)} %get-tuple-element.32), channel_id=1, source_target_pairs={{0,2},{1,3},{2,0},{3,1},{4,6},{5,7},{6,4},{7,5},{8,10},{9,11},{10,... | collective-permute-start | bytes 196616 | tf_op jit(solution)/shard_map/ppermute | solution.py:442
  26.1 5.2 %collective-permute-start.3 = (bf16[2,128,128]{2,1,0:T(8,128)(2,1)S(1)}, bf16[2,128,128]{2,1,0:T(8,128)(2,1)S(1)}, u32[]{:S(2)}, u32[]{:S(2)}) collective-permute-start(bf16[2,128,128]{2,1,0:T(8,128)(2,1)S(1)} %get-tuple-element.33), channel_id=1, source_target_pairs={{0,3},{1,2},{2,1},{3,0},{4,7},{5,6},{6,5},{7,4},{8,11},{9,10},{10,... | collective-permute-start | bytes 196616 | tf_op jit(solution)/shard_map/ppermute | solution.py:442
  31.7 9.7 %copy-start = (bf16[8,128,128]{2,1,0:T(8,128)(2,1)S(1)}, bf16[8,128,128]{2,1,0:T(8,128)(2,1)}, u32[]{:S(2)}) copy-start(bf16[8,128,128]{2,1,0:T(8,128)(2,1)} %pair.1) | copy-start | bytes 786436

commit v17 on v15

--- a/solution.py
+++ b/solution.py
@@ -52,6 +52,23 @@
         axis_index_groups=[listing(blocks.shape[0])],
         tiled=True,
     )
+
+
+def swap_apart(blocks):
+    ranks, groups = blocks.shape[0], lax.axis_size("grp")
+    orders = [listing(ranks), list(range(ranks))]
+    return lax.all_to_all(
+        blocks,
+        ("grp", "row"),
+        split_axis=0,
+        concat_axis=0,
+        axis_index_groups=[[g * ranks + r for r in orders[g % 2]] for g in range(groups)],
+        tiled=True,
+    )
+
+
+def slot_apart(rank, ranks):
+    return jnp.where(lax.rem(lax.axis_index("grp"), 2) == 0, slot(rank, ranks), rank)
 
 
 def by_rank(blocks):
@@ -121,8 +138,9 @@
     pipeline(range(0, rows, 2), norm, project)
     owners, block = out.shape[0], out.shape[1]
     for owner in range(owners):
+        place = slot_apart(owner, owners)
         for tile, lanes in lane_tiles(pair):
-            out[slot(owner, owners), :, lanes] = held[tile, owner * block : (owner + 1) * block, :].astype(BF16)
+            out[place, :, lanes] = held[tile, owner * block : (owner + 1) * block, :].astype(BF16)
     for copy in copies[6:]:
         copy.wait()
 
@@ -131,7 +149,7 @@
     sides = [[], []]
     sources = edges.shape[0]
     for source in range(sources):
-        block = edges[slot(source, sources), channel * 2 * rows : (channel + 1) * 2 * rows, :].astype(F32)
+        block = edges[slot_apart(source, sources), channel * 2 * rows : (channel + 1) * 2 * rows, :].astype(F32)
         sides[0].append(block[:rows])
         sides[1].append(block[rows:])
     return [jnp.concatenate(side, axis=0).astype(BF16) for side in sides]
@@ -386,7 +404,7 @@
         w_bias.T,
         fetched=13,
     )
-    spread = swap(edges)
+    spread = swap_apart(edges)
     flops = 2 * own * residues * residues * cols
     if col_parts == 1:
         summed = call(

time: 48 us -> 50.3 us (1.048)
  blocking collectives: 42.3 us -> 44.6 us
    all_to_all x0 -> x1, blocking collectives: none -> 20.2 us  [swap_apart(): lax.all_to_all(blocks, ('grp', 'row'), split_axis=0, concat_axis=0, axis_...]
    all_to_all x3 -> x2, blocking collectives: 42.3 us -> 24.4 us  [swap(): lax.all_to_all(blocks, 'row', split_axis=0, concat_axis=0, axis_index_gro...]
where the time goes in v17:
time: 50.3 us; the launch traced here: 50 us
  blocking collectives  44.6 us (89%)
  Pallas kernels  5.39 us (11%)
    all_to_all x2, blocking collectives, swap(): lax.all_to_all(blocks, 'row', split_axis=0, concat_axis=0, axis_index_gro...  24.4 us
    all_to_all x1, blocking collectives, swap_apart(): lax.all_to_all(blocks, ('grp', 'row'), split_axis=0, concat_axis=0, axis_...  20.2 us
    pallas_call x4, Pallas kernels, call(): pl.pallas_call(kernel, out_shape=shapes, in_specs=[far] * fetched + [vmem...  5.39 us

profile of v17, /device:TPU:0, one launch (start us, length us, event | category | flops | bytes accessed | tf_op | source)
XLA Modules:
  0.0 50.0 jit_solution(7368002500636823750)
XLA Ops:
  0.0 2.1 %shard_map.127 = (bf16[16,128,128]{2,1,0:T(8,128)(2,1)S(1)}, f32[8,128,128]{2,1,0:T(8,128)S(1)}, bf16[128,128]{1,0:T(8,128)(2,1)S(1)}, bf16[128,128]{1,0:T(8,128...) custom-call(bf16[8,128,128]{2,1,0:T(8,128)(2,1)} %pair.1, ...), custom_call_target="tpu_custom_call" | custom-call | flops 167772160 | bytes 623616 | tf_op jit(solution)/shard_map/pallas_call | solution.py:342
  2.1 20.2 %all_to_all.15.edges = bf16[16,128,128]{2,1,0:T(8,128)(2,1)S(1)} all-to-all(bf16[16,128,128]{2,1,0:T(8,128)(2,1)S(1)} %get-tuple-element.17), channel_id=1, replica_groups={{11,15,14,13,12,10,9,8,7,6,5,4,3,2,1,0},{16,17,18,19,20,21,22,23,24,25,..., dimensions={0} | all-to-all | bytes 1048576 | tf_op jit(solution)/shard_map/all_to_all | solution.py:60
  22.3 0.3 shard_map.128
  22.6 0.0 copy-start
  22.6 14.2 %all_to_all.16.returned = bf16[16,64,128]{2,1,0:T(8,128)(2,1)S(1)} all-to-all(bf16[16,64,128]{2,1,0:T(8,128)(2,1)S(1)} %shard_map.128), channel_id=1, replica_groups={{11,15,14,13,12,10,9,8,7,6,5,4,3,2,1,0},{27,31,30,29,28,26,25,24,23,22,..., dimensions={0} | all-to-all | bytes 524288 | tf_op jit(solution)/shard_map/all_to_all | solution.py:47
  36.8 0.0 copy-done
  36.8 0.9 %shard_map.129 = (f32[8,128,128]{2,1,0:T(8,128)S(1)}, bf16[8,128,128]{2,1,0:T(8,128)(2,1)S(1)}, bf16[16,32,128]{2,1,0:T(8,128)(2,1)S(1)}) custom-call(bf16[16,64,128]{2,1,0:T(8,128)(2,1)S(1)} %all_to_all.16.returned, f32[8,128,128]{2,1,0:T(8,128)S(1)} %get-tuple-element.18.gate, bf16[8,128,128]{2,1,0:T(8,128)(2,1)S(1)} %copy-done, ...), custom_call_target="tpu_custom_call" | custom-call | flops 33554432 | bytes 1082368 | tf_op jit(solution)/shard_map/pallas_call | solution.py:342
  37.7 10.2 %all_to_all.17.refs_1_ = bf16[16,32,128]{2,1,0:T(8,128)(2,1)S(1)} all-to-all(bf16[16,32,128]{2,1,0:T(8,128)(2,1)S(1)} %get-tuple-element.27), channel_id=1, replica_groups={{11,15,14,13,12,10,9,8,7,6,5,4,3,2,1,0},{27,31,30,29,28,26,25,24,23,22,..., dimensions={0} | all-to-all | bytes 262144 | tf_op jit(solution)/shard_map/all_to_all | solution.py:47
  48.0 2.1 %shard_map.130 = bf16[8,128,128]{2,1,0:T(8,128)(2,1)} custom-call(bf16[8,128,128]{2,1,0:T(8,128)(2,1)S(1)} %get-tuple-element.21.att_norm, bf16[128,128]{1,0:T(8,128)(2,1)S(1)} %get-tuple-element.22.w_query, bf16[128,128]{1,0:T(8,128)(2,1)S(1)} %get-tuple-element.23.w_key, bf16[128,128]{1,0:T(8,128)(2,1)S(1)} %get-tuple-element.24.w_value, ...), custom_call_target="tpu_custom_call" | custom-call | flops 201326592 | bytes 1081344 | tf_op jit(solution)/shard_map/pallas_call | solution.py:342
Async XLA Ops:
  22.6 14.2 %copy-start = (bf16[8,128,128]{2,1,0:T(8,128)(2,1)S(1)}, bf16[8,128,128]{2,1,0:T(8,128)(2,1)}, u32[]{:S(2)}) copy-start(bf16[8,128,128]{2,1,0:T(8,128)(2,1)} %pair.1) | copy-start | bytes 786436

commit v18 on v17

--- a/solution.py
+++ b/solution.py
@@ -67,8 +67,13 @@
     )
 
 
-def slot_apart(rank, ranks):
-    return jnp.where(lax.rem(lax.axis_index("grp"), 2) == 0, slot(rank, ranks), rank)
+def in_odd_group():
+    return lax.rem(lax.axis_index("grp"), 2) == 1
+
+
+def slots_apart(ranks):
+    odd = in_odd_group()
+    return [jnp.where(odd, rank, slot(rank, ranks)) for rank in range(ranks)]
 
 
 def by_rank(blocks):
@@ -138,9 +143,8 @@
     pipeline(range(0, rows, 2), norm, project)
     owners, block = out.shape[0], out.shape[1]
     for owner in range(owners):
-        place = slot_apart(owner, owners)
         for tile, lanes in lane_tiles(pair):
-            out[place, :, lanes] = held[tile, owner * block : (owner + 1) * block, :].astype(BF16)
+            out[slot(owner, owners), :, lanes] = held[tile, owner * block : (owner + 1) * block, :].astype(BF16)
     for copy in copies[6:]:
         copy.wait()
 
@@ -149,19 +153,19 @@
     sides = [[], []]
     sources = edges.shape[0]
     for source in range(sources):
-        block = edges[slot_apart(source, sources), channel * 2 * rows : (channel + 1) * 2 * rows, :].astype(F32)
+        block = edges[slot(source, sources), channel * 2 * rows : (channel + 1) * 2 * rows, :].astype(F32)
         sides[0].append(block[:rows])
         sides[1].append(block[rows:])
     return [jnp.concatenate(side, axis=0).astype(BF16) for side in sides]
 
 
 def triangle_kernel(rows, edges, out):
+    places = slots_apart(out.shape[0])
     for pair_of in range(0, out.shape[1] // rows, 2):
         products = [dot(*triangle_sides(edges, rows, pair_of + o), NT) for o in range(2)]
-        owners = out.shape[0]
-        for owner in range(owners):
+        for owner, place in enumerate(places):
             mine = slice(owner * rows, (owner + 1) * rows)
-            out[slot(owner, owners), pair_of * rows : (pair_of + 2) * rows, :] = jnp.concatenate(
+            out[place, pair_of * rows : (pair_of + 2) * rows, :] = jnp.concatenate(
                 [p[mine] for p in products], axis=0
             ).astype(BF16)
 
@@ -176,6 +180,7 @@
 ):
     rows, cols, width = pair.shape
     owners, block = returned.shape[0], returned.shape[1]
+    places = slots_apart(owners)
     channels = owners * block // rows
     total = jnp.zeros((rows, cols), F32)
     for owner in range(owners):
@@ -183,7 +188,7 @@
     average = total / channels
     square = jnp.zeros((rows, cols), F32)
     for owner in range(owners):
-        centered = returned[slot(owner, owners)].astype(F32).reshape(block // rows, rows, cols) - average
+        centered = returned[places[owner]].astype(F32).reshape(block // rows, rows, cols) - average
         square += jnp.sum(centered * centered, axis=0)
         for tile, lanes in lane_tiles(pair):
             held[tile, owner * block : (owner + 1) * block, :] = centered.reshape(block, cols)[:, lanes]
@@ -404,7 +409,7 @@
         w_bias.T,
         fetched=13,
     )
-    spread = swap_apart(edges)
+    spread = swap(edges)
     flops = 2 * own * residues * residues * cols
     if col_parts == 1:
         summed = call(
@@ -423,9 +428,10 @@
             spread,
         )
         summed = lax.psum_scatter(partial_sums, "col", scatter_dimension=2, tiled=True).astype(BF16)
-        summed = by_slot(summed.reshape(own, owners, rows, cols).swapaxes(0, 1))
+        summed = summed.reshape(own, owners, rows, cols).swapaxes(0, 1)
+        summed = jnp.where(in_odd_group(), summed, by_slot(summed))
         summed = summed.reshape(owners, own * rows, cols)
-    returned = swap(summed)
+    returned = swap_apart(summed)
     first_pass, att_norm, bias_copies = call(
         update_kernel,
         [

time: 50.3 us -> 49.7 us (0.988)
    all_to_all x1, blocking collectives: 20.2 us -> 13.4 us  [swap_apart(): lax.all_to_all(blocks, ('grp', 'row'), split_axis=0, concat_axis=0, axis_...]
    all_to_all x2, blocking collectives: 24.4 us -> 30.7 us  [swap(): lax.all_to_all(blocks, 'row', split_axis=0, concat_axis=0, axis_index_gro...]
where the time goes in v18:
time: 49.7 us; the launch traced here: 49.5 us
  blocking collectives  44.1 us (89%)
  Pallas kernels  5.38 us (11%)
    all_to_all x2, blocking collectives, swap(): lax.all_to_all(blocks, 'row', split_axis=0, concat_axis=0, axis_index_gro...  30.7 us
    all_to_all x1, blocking collectives, swap_apart(): lax.all_to_all(blocks, ('grp', 'row'), split_axis=0, concat_axis=0, axis_...  13.4 us
    pallas_call x4, Pallas kernels, call(): pl.pallas_call(kernel, out_shape=shapes, in_specs=[far] * fetched + [vmem...  5.38 us

profile of v18, /device:TPU:0, one launch (start us, length us, event | category | flops | bytes accessed | tf_op | source)
XLA Modules:
  0.0 49.5 jit_solution(1451917556122110991)
XLA Ops:
  0.0 2.1 %shard_map.127 = (bf16[16,128,128]{2,1,0:T(8,128)(2,1)S(1)}, f32[8,128,128]{2,1,0:T(8,128)S(1)}, bf16[128,128]{1,0:T(8,128)(2,1)S(1)}, bf16[128,128]{1,0:T(8,128...) custom-call(bf16[8,128,128]{2,1,0:T(8,128)(2,1)} %pair.1, ...), custom_call_target="tpu_custom_call" | custom-call | flops 167772160 | bytes 623616 | tf_op jit(solution)/shard_map/pallas_call | solution.py:347
  2.1 20.6 %all_to_all.15.edges = bf16[16,128,128]{2,1,0:T(8,128)(2,1)S(1)} all-to-all(bf16[16,128,128]{2,1,0:T(8,128)(2,1)S(1)} %get-tuple-element.17), channel_id=1, replica_groups={{11,15,14,13,12,10,9,8,7,6,5,4,3,2,1,0},{27,31,30,29,28,26,25,24,23,22,..., dimensions={0} | all-to-all | bytes 1048576 | tf_op jit(solution)/shard_map/all_to_all | solution.py:47
  22.8 0.3 shard_map.128
  23.1 0.0 copy-start
  23.1 13.4 %all_to_all.16.returned = bf16[16,64,128]{2,1,0:T(8,128)(2,1)S(1)} all-to-all(bf16[16,64,128]{2,1,0:T(8,128)(2,1)S(1)} %shard_map.128), channel_id=1, replica_groups={{11,15,14,13,12,10,9,8,7,6,5,4,3,2,1,0},{16,17,18,19,20,21,22,23,24,25,..., dimensions={0} | all-to-all | bytes 524288 | tf_op jit(solution)/shard_map/all_to_all | solution.py:60
  36.5 0.0 copy-done
  36.5 0.9 %shard_map.129 = (f32[8,128,128]{2,1,0:T(8,128)S(1)}, bf16[8,128,128]{2,1,0:T(8,128)(2,1)S(1)}, bf16[16,32,128]{2,1,0:T(8,128)(2,1)S(1)}) custom-call(bf16[16,64,128]{2,1,0:T(8,128)(2,1)S(1)} %all_to_all.16.returned, f32[8,128,128]{2,1,0:T(8,128)S(1)} %get-tuple-element.18.gate, bf16[8,128,128]{2,1,0:T(8,128)(2,1)S(1)} %copy-done, ...), custom_call_target="tpu_custom_call" | custom-call | flops 33554432 | bytes 1082368 | tf_op jit(solution)/shard_map/pallas_call | solution.py:347
  37.3 10.1 %all_to_all.17.refs_1_ = bf16[16,32,128]{2,1,0:T(8,128)(2,1)S(1)} all-to-all(bf16[16,32,128]{2,1,0:T(8,128)(2,1)S(1)} %get-tuple-element.27), channel_id=1, replica_groups={{11,15,14,13,12,10,9,8,7,6,5,4,3,2,1,0},{27,31,30,29,28,26,25,24,23,22,..., dimensions={0} | all-to-all | bytes 262144 | tf_op jit(solution)/shard_map/all_to_all | solution.py:47
  47.4 2.1 %shard_map.130 = bf16[8,128,128]{2,1,0:T(8,128)(2,1)} custom-call(bf16[8,128,128]{2,1,0:T(8,128)(2,1)S(1)} %get-tuple-element.21.att_norm, bf16[128,128]{1,0:T(8,128)(2,1)S(1)} %get-tuple-element.22.w_query, bf16[128,128]{1,0:T(8,128)(2,1)S(1)} %get-tuple-element.23.w_key, bf16[128,128]{1,0:T(8,128)(2,1)S(1)} %get-tuple-element.24.w_value, ...), custom_call_target="tpu_custom_call" | custom-call | flops 201326592 | bytes 1081344 | tf_op jit(solution)/shard_map/pallas_call | solution.py:347
Async XLA Ops:
  23.1 13.4 %copy-start = (bf16[8,128,128]{2,1,0:T(8,128)(2,1)S(1)}, bf16[8,128,128]{2,1,0:T(8,128)(2,1)}, u32[]{:S(2)}) copy-start(bf16[8,128,128]{2,1,0:T(8,128)(2,1)} %pair.1) | copy-start | bytes 786436

commit v19 on v15

--- a/solution.py
+++ b/solution.py
@@ -1,4 +1,5 @@
 import functools
+import math
 
 import jax
 import jax.numpy as jnp
@@ -35,8 +36,9 @@
 
 
 def listing(ranks):
-    first = ranks - 1 - ranks // 4
-    return [first] + [rank for rank in range(ranks - 1, -1, -1) if rank != first]
+    first, stride = ranks - 1 - ranks // 4, 5
+    assert math.gcd(stride, ranks) == 1
+    return [(first + stride * n) % ranks for n in range(ranks)]
 
 
 def slot(rank, ranks):

time: 48 us -> 47.9 us (level)
  no operation moved by 1% of the time
where the time goes in v19:
time: 47.9 us; the launch traced here: 47.7 us
  blocking collectives  42.3 us (88%)
  Pallas kernels  5.39 us (11%)
    all_to_all x3, blocking collectives, swap(): lax.all_to_all(blocks, 'row', split_axis=0, concat_axis=0, axis_index_gro...  42.3 us
    pallas_call x4, Pallas kernels, call(): pl.pallas_call(kernel, out_shape=shapes, in_specs=[far] * fetched + [vmem...  5.39 us

profile of v19, /device:TPU:0, one launch (start us, length us, event | category | flops | bytes accessed | tf_op | source)
XLA Modules:
  0.0 47.7 jit_solution(6622999930101883907)
XLA Ops:
  0.0 2.1 %shard_map.127 = (bf16[16,128,128]{2,1,0:T(8,128)(2,1)S(1)}, f32[8,128,128]{2,1,0:T(8,128)S(1)}, bf16[128,128]{1,0:T(8,128)(2,1)S(1)}, bf16[128,128]{1,0:T(8,128...) custom-call(bf16[8,128,128]{2,1,0:T(8,128)(2,1)} %pair.1, ...), custom_call_target="tpu_custom_call" | custom-call | flops 167772160 | bytes 623616 | tf_op jit(solution)/shard_map/pallas_call | solution.py:326
  2.1 20.1 %all_to_all.15.edges = bf16[16,128,128]{2,1,0:T(8,128)(2,1)S(1)} all-to-all(bf16[16,128,128]{2,1,0:T(8,128)(2,1)S(1)} %get-tuple-element.17), channel_id=1, replica_groups={{11,0,5,10,15,4,9,14,3,8,13,2,7,12,1,6},{27,16,21,26,31,20,25,30,19,24,..., dimensions={0} | all-to-all | bytes 1048576 | tf_op jit(solution)/shard_map/all_to_all | solution.py:49
  22.2 0.3 shard_map.128
  22.5 0.0 copy-start
  22.6 11.7 %all_to_all.16.returned = bf16[16,64,128]{2,1,0:T(8,128)(2,1)S(1)} all-to-all(bf16[16,64,128]{2,1,0:T(8,128)(2,1)S(1)} %shard_map.128), channel_id=1, replica_groups={{11,0,5,10,15,4,9,14,3,8,13,2,7,12,1,6},{27,16,21,26,31,20,25,30,19,24,..., dimensions={0} | all-to-all | bytes 524288 | tf_op jit(solution)/shard_map/all_to_all | solution.py:49
  34.2 0.0 copy-done
  34.2 0.9 %shard_map.129 = (f32[8,128,128]{2,1,0:T(8,128)S(1)}, bf16[8,128,128]{2,1,0:T(8,128)(2,1)S(1)}, bf16[16,32,128]{2,1,0:T(8,128)(2,1)S(1)}) custom-call(bf16[16,64,128]{2,1,0:T(8,128)(2,1)S(1)} %all_to_all.16.returned, f32[8,128,128]{2,1,0:T(8,128)S(1)} %get-tuple-element.18.gate, bf16[8,128,128]{2,1,0:T(8,128)(2,1)S(1)} %copy-done, ...), custom_call_target="tpu_custom_call" | custom-call | flops 33554432 | bytes 1082368 | tf_op jit(solution)/shard_map/pallas_call | solution.py:326
  35.1 10.5 %all_to_all.17.refs_1_ = bf16[16,32,128]{2,1,0:T(8,128)(2,1)S(1)} all-to-all(bf16[16,32,128]{2,1,0:T(8,128)(2,1)S(1)} %get-tuple-element.27), channel_id=1, replica_groups={{11,0,5,10,15,4,9,14,3,8,13,2,7,12,1,6},{27,16,21,26,31,20,25,30,19,24,..., dimensions={0} | all-to-all | bytes 262144 | tf_op jit(solution)/shard_map/all_to_all | solution.py:49
  45.6 2.1 %shard_map.130 = bf16[8,128,128]{2,1,0:T(8,128)(2,1)} custom-call(bf16[8,128,128]{2,1,0:T(8,128)(2,1)S(1)} %get-tuple-element.21.att_norm, bf16[128,128]{1,0:T(8,128)(2,1)S(1)} %get-tuple-element.22.w_query, bf16[128,128]{1,0:T(8,128)(2,1)S(1)} %get-tuple-element.23.w_key, bf16[128,128]{1,0:T(8,128)(2,1)S(1)} %get-tuple-element.24.w_value, ...), custom_call_target="tpu_custom_call" | custom-call | flops 201326592 | bytes 1081344 | tf_op jit(solution)/shard_map/pallas_call | solution.py:326
Async XLA Ops:
  22.5 11.7 %copy-start = (bf16[8,128,128]{2,1,0:T(8,128)(2,1)S(1)}, bf16[8,128,128]{2,1,0:T(8,128)(2,1)}, u32[]{:S(2)}) copy-start(bf16[8,128,128]{2,1,0:T(8,128)(2,1)} %pair.1) | copy-start | bytes 786436

commit v20 on v19

--- a/solution.py
+++ b/solution.py
@@ -88,27 +88,34 @@
 
 def edges_kernel(*refs):
     given, (out, gate, *staged), (pair, weights, normed, held, sems) = refs[:13], refs[13:22], refs[22:]
-    targets = [pair, *(weights.at[n] for n in range(5)), *staged]
+    targets = [*(weights.at[n] for n in range(5)), *staged]
     copies = [
         pltpu.make_async_copy(source, target, sems.at[n])
-        for n, (source, target) in enumerate(zip(given, targets))
+        for n, (source, target) in enumerate(zip(given[1:], targets))
     ]
-    for copy in copies:
+    arrivals = []
+    for n in range(pair.shape[0] // 2):
+        two = pl.ds(2 * n, 2)
+        arrivals.append(pltpu.make_async_copy(given[0].at[two], pair.at[two], sems.at[len(copies) + n]))
+    for copy in copies[:4] + arrivals + copies[4:]:
         copy.start()
-    for copy in copies[:6]:
+    for copy in copies[:4]:
         copy.wait()
     rows, width = pair.shape[0], pair.shape[2]
     channels = weights.shape[2]
     cols = pair.shape[1]
     turned = jnp.concatenate([weights[n].T for n in range(4)], axis=0)
+    copies[4].wait()
     gate_weight = twice(weights[4])
 
     def norm(i):
+        arrivals[i // 2].wait()
         normed[i] = lane_norm(pair[i].astype(F32))
         normed[i + 1] = lane_norm(pair[i + 1].astype(F32))
 
     def project(i):
         both = dot(turned, jnp.concatenate([normed[i], normed[i + 1]], axis=0), NT)
+        gates = dot(side_by_side(normed, i), gate_weight)
         for side in range(2):
             base = 2 * side * channels
             act = sigmoid(both[base + channels : base + 2 * channels]) * both[base : base + channels]
@@ -116,7 +123,7 @@
                 row, part = divmod(tile, cols // LANES)
                 place = pl.ds(side * rows + i + row, channels, stride=2 * rows)
                 held[part, place, :] = act[:, lanes]
-        opened = sigmoid(dot(side_by_side(normed, i), gate_weight))
+        opened = sigmoid(gates)
         gate[i] = opened[:, :width]
         gate[i + 1] = opened[:, width:]
 
@@ -125,7 +132,7 @@
     for owner in range(owners):
         for tile, lanes in lane_tiles(pair):
             out[slot(owner, owners), :, lanes] = held[tile, owner * block : (owner + 1) * block, :].astype(BF16)
-    for copy in copies[6:]:
+    for copy in copies[5:]:
         copy.wait()
 
 
@@ -210,8 +217,9 @@
     cols, width = att_norm.shape[1], w_query.shape[1]
 
     def project(i):
-        keys = dot(side_by_side(att_norm, i), w_direct).astype(BF16)
+        keys = dot(side_by_side(att_norm, i), w_direct)
         turned = dot(w_turned, jnp.concatenate([att_norm[i], att_norm[i + 1]], axis=0), NT)
+        keys = keys.astype(BF16)
         for row in range(2):
             key[i + row] = keys[:, row * width : (row + 1) * width]
             mine = turned[:, row * cols : (row + 1) * cols]
@@ -258,17 +266,20 @@
         (slice(h * HEAD_DIM, (h + 1) * HEAD_DIM), slice(h * cols, (h + 1) * cols)) for h in range(HEADS)
     ]
 
+    def raw_scores(row):
+        blocks = []
+        for mine, _ in heads:
+            above = jnp.zeros((mine.start, cols), BF16)
+            below = jnp.zeros((width - mine.stop, cols), BF16)
+            parts = [p for p in (above, query_t[row, mine, :], below) if p.shape[0]]
+            blocks.append(jnp.concatenate(parts, axis=0))
+        return dot(key[row], jnp.concatenate(blocks, axis=1))
+
     def score(i):
+        raw = [raw_scores(i), raw_scores(i + 1)]
         for row in (i, i + 1):
-            blocks = []
-            for mine, _ in heads:
-                above = jnp.zeros((mine.start, cols), BF16)
-                below = jnp.zeros((width - mine.stop, cols), BF16)
-                parts = [p for p in (above, query_t[row, mine, :], below) if p.shape[0]]
-                blocks.append(jnp.concatenate(parts, axis=0))
-            raw = dot(key[row], jnp.concatenate(blocks, axis=1))
             for _, span in heads:
-                biased = raw[:, span] * score_scale + bias_t[:, span]
+                biased = raw[row - i][:, span] * score_scale + bias_t[:, span]
                 scores[row % 4, :, span] = biased
                 peaks[row % 4, :, span] = jnp.max(biased, axis=0, keepdims=True)
 
@@ -279,18 +290,19 @@
                 weights[row % 4, :, span] = jnp.exp2(lowered).astype(BF16)
 
     def collect(i):
-        for row in (i, i + 1):
-            for head in range(0, HEADS, 2):
-                (first, left), (second, right) = heads[head : head + 2]
-                values = jnp.concatenate([value_t[row, first.start : second.stop, :], ones], axis=0)
-                summed = dot(values, weights[row % 4, :, left.start : right.stop])
-                share = 1.0 / summed[2 * HEAD_DIM : 2 * HEAD_DIM + 1]
-                for mine, there, lanes in (
-                    (first, slice(0, HEAD_DIM), slice(0, cols)),
-                    (second, slice(HEAD_DIM, 2 * HEAD_DIM), slice(cols, 2 * cols)),
-                ):
-                    attended = summed[there, lanes] * share[:, lanes] * gate_t[row, mine, :]
-                    gated[row % 4, mine, :] = attended.astype(BF16)
+        pairs = [(row, heads[head], heads[head + 1]) for row in (i, i + 1) for head in range(0, HEADS, 2)]
+        sums = []
+        for row, (first, left), (second, right) in pairs:
+            values = jnp.concatenate([value_t[row, first.start : second.stop, :], ones], axis=0)
+            sums.append(dot(values, weights[row % 4, :, left.start : right.stop]))
+        for (row, (first, _), (second, _)), summed in zip(pairs, sums):
+            share = 1.0 / summed[2 * HEAD_DIM : 2 * HEAD_DIM + 1]
+            for mine, there, lanes in (
+                (first, slice(0, HEAD_DIM), slice(0, cols)),
+                (second, slice(HEAD_DIM, 2 * HEAD_DIM), slice(cols, 2 * cols)),
+            ):
+                attended = summed[there, lanes] * share[:, lanes] * gate_t[row, mine, :]
+                gated[row % 4, mine, :] = attended.astype(BF16)
 
     def finish(i):
         turned = jnp.concatenate([gated[i % 4].T, gated[(i + 1) % 4].T], axis=1)
@@ -370,7 +382,7 @@
             ((5, width, channels), BF16),
             (pair_rep.shape, BF16),
             ((cols // LANES, channels * 2 * rows, LANES), F32),
-            pltpu.SemaphoreType.DMA((13,)),
+            pltpu.SemaphoreType.DMA((12 + rows // 2,)),
         ],
         10 * cells * width * channels,
         pair_rep,

time: 47.9 us -> 48.4 us (1.010)
  no operation moved by 1% of the time
where the time goes in v20:
time: 48.4 us; the launch traced here: 48.1 us
  blocking collectives  42.3 us (87%)
  Pallas kernels  5.79 us (12%)
    all_to_all x3, blocking collectives, swap(): lax.all_to_all(blocks, 'row', split_axis=0, concat_axis=0, axis_index_gro...  42.3 us
    pallas_call x4, Pallas kernels, call(): pl.pallas_call(kernel, out_shape=shapes, in_specs=[far] * fetched + [vmem...  5.79 us

profile of v20, /device:TPU:0, one launch (start us, length us, event | category | flops | bytes accessed | tf_op | source)
XLA Modules:
  0.0 48.1 jit_solution(8620533804395243027)
XLA Ops:
  0.0 2.5 %shard_map.127 = (bf16[16,128,128]{2,1,0:T(8,128)(2,1)S(1)}, f32[8,128,128]{2,1,0:T(8,128)S(1)}, bf16[128,128]{1,0:T(8,128)(2,1)S(1)}, bf16[128,128]{1,0:T(8,128...) custom-call(bf16[8,128,128]{2,1,0:T(8,128)(2,1)} %pair.1, ...), custom_call_target="tpu_custom_call" | custom-call | flops 167772160 | bytes 623616 | tf_op jit(solution)/shard_map/pallas_call | solution.py:338
  2.5 20.1 %all_to_all.15.edges = bf16[16,128,128]{2,1,0:T(8,128)(2,1)S(1)} all-to-all(bf16[16,128,128]{2,1,0:T(8,128)(2,1)S(1)} %get-tuple-element.17), channel_id=1, replica_groups={{11,0,5,10,15,4,9,14,3,8,13,2,7,12,1,6},{27,16,21,26,31,20,25,30,19,24,..., dimensions={0} | all-to-all | bytes 1048576 | tf_op jit(solution)/shard_map/all_to_all | solution.py:49
  22.6 0.3 shard_map.128
  22.9 0.0 copy-start
  23.0 11.7 %all_to_all.16.returned = bf16[16,64,128]{2,1,0:T(8,128)(2,1)S(1)} all-to-all(bf16[16,64,128]{2,1,0:T(8,128)(2,1)S(1)} %shard_map.128), channel_id=1, replica_groups={{11,0,5,10,15,4,9,14,3,8,13,2,7,12,1,6},{27,16,21,26,31,20,25,30,19,24,..., dimensions={0} | all-to-all | bytes 524288 | tf_op jit(solution)/shard_map/all_to_all | solution.py:49
  34.6 0.0 copy-done
  34.6 0.9 %shard_map.129 = (f32[8,128,128]{2,1,0:T(8,128)S(1)}, bf16[8,128,128]{2,1,0:T(8,128)(2,1)S(1)}, bf16[16,32,128]{2,1,0:T(8,128)(2,1)S(1)}) custom-call(bf16[16,64,128]{2,1,0:T(8,128)(2,1)S(1)} %all_to_all.16.returned, f32[8,128,128]{2,1,0:T(8,128)S(1)} %get-tuple-element.18.gate, bf16[8,128,128]{2,1,0:T(8,128)(2,1)S(1)} %copy-done, ...), custom_call_target="tpu_custom_call" | custom-call | flops 33554432 | bytes 1082368 | tf_op jit(solution)/shard_map/pallas_call | solution.py:338
  35.5 10.5 %all_to_all.17.refs_1_ = bf16[16,32,128]{2,1,0:T(8,128)(2,1)S(1)} all-to-all(bf16[16,32,128]{2,1,0:T(8,128)(2,1)S(1)} %get-tuple-element.27), channel_id=1, replica_groups={{11,0,5,10,15,4,9,14,3,8,13,2,7,12,1,6},{27,16,21,26,31,20,25,30,19,24,..., dimensions={0} | all-to-all | bytes 262144 | tf_op jit(solution)/shard_map/all_to_all | solution.py:49
  46.0 2.1 %shard_map.130 = bf16[8,128,128]{2,1,0:T(8,128)(2,1)} custom-call(bf16[8,128,128]{2,1,0:T(8,128)(2,1)S(1)} %get-tuple-element.21.att_norm, bf16[128,128]{1,0:T(8,128)(2,1)S(1)} %get-tuple-element.22.w_query, bf16[128,128]{1,0:T(8,128)(2,1)S(1)} %get-tuple-element.23.w_key, bf16[128,128]{1,0:T(8,128)(2,1)S(1)} %get-tuple-element.24.w_value, ...), custom_call_target="tpu_custom_call" | custom-call | flops 201326592 | bytes 1081344 | tf_op jit(solution)/shard_map/pallas_call | solution.py:338
Async XLA Ops:
  22.9 11.7 %copy-start = (bf16[8,128,128]{2,1,0:T(8,128)(2,1)S(1)}, bf16[8,128,128]{2,1,0:T(8,128)(2,1)}, u32[]{:S(2)}) copy-start(bf16[8,128,128]{2,1,0:T(8,128)(2,1)} %pair.1) | copy-start | bytes 786436

commit v21 on v19

--- a/solution.py
+++ b/solution.py
@@ -35,33 +35,33 @@
     )
 
 
-def listing(ranks):
-    first, stride = ranks - 1 - ranks // 4, 5
+def listing(step, ranks):
+    first, stride = {"edges": ranks - 1, "triangle": ranks // 2, "bias": ranks // 4}[step], 5
     assert math.gcd(stride, ranks) == 1
     return [(first + stride * n) % ranks for n in range(ranks)]
 
 
-def slot(rank, ranks):
-    return listing(ranks).index(rank)
-
-
-def swap(blocks):
+def slot(step, rank, ranks):
+    return listing(step, ranks).index(rank)
+
+
+def swap(step, blocks):
     return lax.all_to_all(
         blocks,
         "row",
         split_axis=0,
         concat_axis=0,
-        axis_index_groups=[listing(blocks.shape[0])],
+        axis_index_groups=[listing(step, blocks.shape[0])],
         tiled=True,
     )
 
 
-def by_rank(blocks):
-    return blocks[np.array([slot(r, blocks.shape[0]) for r in range(blocks.shape[0])])]
-
-
-def by_slot(blocks):
-    return blocks[np.array(listing(blocks.shape[0]))]
+def by_rank(step, blocks):
+    return blocks[np.array([slot(step, r, blocks.shape[0]) for r in range(blocks.shape[0])])]
+
+
+def by_slot(step, blocks):
+    return blocks[np.array(listing(step, blocks.shape[0]))]
 
 
 def lane_tiles(values):
@@ -124,7 +124,7 @@
     owners, block = out.shape[0], out.shape[1]
     for owner in range(owners):
         for tile, lanes in lane_tiles(pair):
-            out[slot(owner, owners), :, lanes] = held[tile, owner * block : (owner + 1) * block, :].astype(BF16)
+            out[slot("edges", owner, owners), :, lanes] = held[tile, owner * block : (owner + 1) * block, :].astype(BF16)
     for copy in copies[6:]:
         copy.wait()
 
@@ -133,7 +133,7 @@
     sides = [[], []]
     sources = edges.shape[0]
     for source in range(sources):
-        block = edges[slot(source, sources), channel * 2 * rows : (channel + 1) * 2 * rows, :].astype(F32)
+        block = edges[slot("edges", source, sources), channel * 2 * rows : (channel + 1) * 2 * rows, :].astype(F32)
         sides[0].append(block[:rows])
         sides[1].append(block[rows:])
     return [jnp.concatenate(side, axis=0).astype(BF16) for side in sides]
@@ -145,7 +145,7 @@
         owners = out.shape[0]
         for owner in range(owners):
             mine = slice(owner * rows, (owner + 1) * rows)
-            out[slot(owner, owners), pair_of * rows : (pair_of + 2) * rows, :] = jnp.concatenate(
+            out[slot("triangle", owner, owners), pair_of * rows : (pair_of + 2) * rows, :] = jnp.concatenate(
                 [p[mine] for p in products], axis=0
             ).astype(BF16)
 
@@ -167,7 +167,7 @@
     average = total / channels
     square = jnp.zeros((rows, cols), F32)
     for owner in range(owners):
-        centered = returned[slot(owner, owners)].astype(F32).reshape(block // rows, rows, cols) - average
+        centered = returned[slot("triangle", owner, owners)].astype(F32).reshape(block // rows, rows, cols) - average
         square += jnp.sum(centered * centered, axis=0)
         for tile, lanes in lane_tiles(pair):
             held[tile, owner * block : (owner + 1) * block, :] = centered.reshape(block, cols)[:, lanes]
@@ -259,6 +259,8 @@
     ]
 
     def score(i):
+        if i == 0:
+            turn_bias()
         for row in (i, i + 1):
             blocks = []
             for mine, _ in heads:
@@ -301,14 +303,16 @@
         copy.start()
         copies.append(copy)
 
+    def turn_bias():
+        for head, (_, span) in enumerate(heads):
+            parts = [
+                bias[slot("bias", owner, bias.shape[0])].astype(F32)[head * head_rows : (head + 1) * head_rows]
+                for owner in range(bias.shape[0])
+            ]
+            bias_t[:, span] = jnp.concatenate(parts, axis=0).T * LOG2_E
+
     copies = []
     w_last = twice(w_att_out[...])
-    for head, (_, span) in enumerate(heads):
-        parts = [
-            bias[slot(owner, bias.shape[0])].astype(F32)[head * head_rows : (head + 1) * head_rows]
-            for owner in range(bias.shape[0])
-        ]
-        bias_t[:, span] = jnp.concatenate(parts, axis=0).T * LOG2_E
     pipeline(range(0, rows, 2), *before, score, soften, collect, finish)
     for copy in copies:
         copy.wait()
@@ -388,7 +392,7 @@
         w_bias.T,
         fetched=13,
     )
-    spread = swap(edges)
+    spread = swap("edges", edges)
     flops = 2 * own * residues * residues * cols
     if col_parts == 1:
         summed = call(
@@ -407,9 +411,9 @@
             spread,
         )
         summed = lax.psum_scatter(partial_sums, "col", scatter_dimension=2, tiled=True).astype(BF16)
-        summed = by_slot(summed.reshape(own, owners, rows, cols).swapaxes(0, 1))
+        summed = by_slot("triangle", summed.reshape(own, owners, rows, cols).swapaxes(0, 1))
         summed = summed.reshape(owners, own * rows, cols)
-    returned = swap(summed)
+    returned = swap("triangle", summed)
     first_pass, att_norm, bias_copies = call(
         update_kernel,
         [
@@ -429,7 +433,7 @@
         w_tri_out,
         w_bias_t,
     )
-    bias = swap(bias_copies)
+    bias = swap("bias", bias_copies)
     projected = [
         ((rows, width, cols), BF16),
         ((rows, cols, width), BF16),
@@ -454,7 +458,9 @@
         given = (first_pass, bias, w_att_out)
         return call(whole_kernel, out, projected + held, flops, *projecting, *given, sent=True)
     query_t, key, value_t, gate_t = call(project_kernel, projected, [], project_flops, *projecting)
-    bias = by_slot(lax.all_to_all(by_rank(bias), "col", split_axis=0, concat_axis=2, tiled=True))
+    bias = by_slot(
+        "bias", lax.all_to_all(by_rank("bias", bias), "col", split_axis=0, concat_axis=2, tiled=True)
+    )
     key = lax.all_gather(key, "col", axis=1, tiled=True)
     value_t = lax.all_gather(value_t, "col", axis=2, tiled=True)
     given = (query_t, key, value_t, gate_t, first_pass, bias, w_att_out)

time: 47.9 us -> 51.5 us (1.075)
  blocking collectives: 42.3 us -> 45.8 us
    all_to_all x3, blocking collectives: 42.3 us -> 45.8 us  [swap(): lax.all_to_all(blocks, 'row', split_axis=0, concat_axis=0, axis_index_gro...]
where the time goes in v21:
time: 51.5 us; the launch traced here: 51.2 us
  blocking collectives  45.8 us (89%)
  Pallas kernels  5.39 us (10%)
    all_to_all x3, blocking collectives, swap(): lax.all_to_all(blocks, 'row', split_axis=0, concat_axis=0, axis_index_gro...  45.8 us
    pallas_call x4, Pallas kernels, call(): pl.pallas_call(kernel, out_shape=shapes, in_specs=[far] * fetched + [vmem...  5.39 us

profile of v21, /device:TPU:0, one launch (start us, length us, event | category | flops | bytes accessed | tf_op | source)
XLA Modules:
  0.0 51.2 jit_solution(3941915654748618811)
XLA Ops:
  0.0 2.1 %shard_map.127 = (bf16[16,128,128]{2,1,0:T(8,128)(2,1)S(1)}, f32[8,128,128]{2,1,0:T(8,128)S(1)}, bf16[128,128]{1,0:T(8,128)(2,1)S(1)}, bf16[128,128]{1,0:T(8,128...) custom-call(bf16[8,128,128]{2,1,0:T(8,128)(2,1)} %pair.1, ...), custom_call_target="tpu_custom_call" | custom-call | flops 167772160 | bytes 623616 | tf_op jit(solution)/shard_map/pallas_call | solution.py:330
  2.1 20.8 %all_to_all.15.edges = bf16[16,128,128]{2,1,0:T(8,128)(2,1)S(1)} all-to-all(bf16[16,128,128]{2,1,0:T(8,128)(2,1)S(1)} %get-tuple-element.17), channel_id=1, replica_groups={{15,4,9,14,3,8,13,2,7,12,1,6,11,0,5,10},{31,20,25,30,19,24,29,18,23,28,..., dimensions={0} | all-to-all | bytes 1048576 | tf_op jit(solution)/shard_map/all_to_all | solution.py:49
  23.0 0.3 shard_map.128
  23.3 0.0 copy-start
  23.3 13.4 %all_to_all.16.returned = bf16[16,64,128]{2,1,0:T(8,128)(2,1)S(1)} all-to-all(bf16[16,64,128]{2,1,0:T(8,128)(2,1)S(1)} %shard_map.128), channel_id=1, replica_groups={{8,13,2,7,12,1,6,11,0,5,10,15,4,9,14,3},{24,29,18,23,28,17,22,27,16,21,..., dimensions={0} | all-to-all | bytes 524288 | tf_op jit(solution)/shard_map/all_to_all | solution.py:49
  36.7 0.0 copy-done
  36.7 0.9 %shard_map.129 = (f32[8,128,128]{2,1,0:T(8,128)S(1)}, bf16[8,128,128]{2,1,0:T(8,128)(2,1)S(1)}, bf16[16,32,128]{2,1,0:T(8,128)(2,1)S(1)}) custom-call(bf16[16,64,128]{2,1,0:T(8,128)(2,1)S(1)} %all_to_all.16.returned, f32[8,128,128]{2,1,0:T(8,128)S(1)} %get-tuple-element.18.gate, bf16[8,128,128]{2,1,0:T(8,128)(2,1)S(1)} %copy-done, ...), custom_call_target="tpu_custom_call" | custom-call | flops 33554432 | bytes 1082368 | tf_op jit(solution)/shard_map/pallas_call | solution.py:330
  37.6 11.6 %all_to_all.17.refs_1_ = bf16[16,32,128]{2,1,0:T(8,128)(2,1)S(1)} all-to-all(bf16[16,32,128]{2,1,0:T(8,128)(2,1)S(1)} %get-tuple-element.27), channel_id=1, replica_groups={{4,9,14,3,8,13,2,7,12,1,6,11,0,5,10,15},{20,25,30,19,24,29,18,23,28,17,..., dimensions={0} | all-to-all | bytes 262144 | tf_op jit(solution)/shard_map/all_to_all | solution.py:49
  49.2 2.1 %shard_map.130 = bf16[8,128,128]{2,1,0:T(8,128)(2,1)} custom-call(bf16[8,128,128]{2,1,0:T(8,128)(2,1)S(1)} %get-tuple-element.21.att_norm, bf16[128,128]{1,0:T(8,128)(2,1)S(1)} %get-tuple-element.22.w_query, bf16[128,128]{1,0:T(8,128)(2,1)S(1)} %get-tuple-element.23.w_key, bf16[128,128]{1,0:T(8,128)(2,1)S(1)} %get-tuple-element.24.w_value, ...), custom_call_target="tpu_custom_call" | custom-call | flops 201326592 | bytes 1081344 | tf_op jit(solution)/shard_map/pallas_call | solution.py:330
Async XLA Ops:
  23.3 13.4 %copy-start = (bf16[8,128,128]{2,1,0:T(8,128)(2,1)S(1)}, bf16[8,128,128]{2,1,0:T(8,128)(2,1)}, u32[]{:S(2)}) copy-start(bf16[8,128,128]{2,1,0:T(8,128)(2,1)} %pair.1) | copy-start | bytes 786436

commit v22 on v21

--- a/solution.py
+++ b/solution.py
@@ -36,7 +36,9 @@
 
 
 def listing(step, ranks):
-    first, stride = {"edges": ranks - 1, "triangle": ranks // 2, "bias": ranks // 4}[step], 5
+    first, stride = ranks - 1 - ranks // 4, 5
+    if step == "triangle":
+        return [first] + [rank for rank in range(ranks - 1, -1, -1) if rank != first]
     assert math.gcd(stride, ranks) == 1
     return [(first + stride * n) % ranks for n in range(ranks)]
 
@@ -259,8 +261,6 @@
     ]
 
     def score(i):
-        if i == 0:
-            turn_bias()
         for row in (i, i + 1):
             blocks = []
             for mine, _ in heads:
@@ -303,16 +303,14 @@
         copy.start()
         copies.append(copy)
 
-    def turn_bias():
-        for head, (_, span) in enumerate(heads):
-            parts = [
-                bias[slot("bias", owner, bias.shape[0])].astype(F32)[head * head_rows : (head + 1) * head_rows]
-                for owner in range(bias.shape[0])
-            ]
-            bias_t[:, span] = jnp.concatenate(parts, axis=0).T * LOG2_E
-
     copies = []
     w_last = twice(w_att_out[...])
+    for head, (_, span) in enumerate(heads):
+        parts = [
+            bias[slot("bias", owner, bias.shape[0])].astype(F32)[head * head_rows : (head + 1) * head_rows]
+            for owner in range(bias.shape[0])
+        ]
+        bias_t[:, span] = jnp.concatenate(parts, axis=0).T * LOG2_E
     pipeline(range(0, rows, 2), *before, score, soften, collect, finish)
     for copy in copies:
         copy.wait()
@@ -373,7 +371,7 @@
             (pair_rep.shape, BF16),
             ((5, width, channels), BF16),
             (pair_rep.shape, BF16),
-            ((cols // LANES, channels * 2 * rows, LANES), F32),
+            ((cols // LANES, (channels + 1) * 2 * rows, LANES), F32),
             pltpu.SemaphoreType.DMA((13,)),
         ],
         10 * cells * width * channels,
@@ -422,7 +420,7 @@
             ((owners, HEADS * rows, cols), BF16),
         ],
         [
-            ((cols // LANES, channels * rows, LANES), F32),
+            ((cols // LANES, (channels + 1) * rows, LANES), F32),
             ((HEADS * rows, cols), F32),
             ((4, cols, channels), BF16),
         ],

time: 51.5 us -> 47.9 us (0.930)
  blocking collectives: 45.8 us -> 42.3 us
    all_to_all x3, blocking collectives: 45.8 us -> 42.3 us  [swap(): lax.all_to_all(blocks, 'row', split_axis=0, concat_axis=0, axis_index_gro...]
where the time goes in v22:
time: 47.9 us; the launch traced here: 47.7 us
  blocking collectives  42.3 us (88%)
  Pallas kernels  5.39 us (11%)
    all_to_all x3, blocking collectives, swap(): lax.all_to_all(blocks, 'row', split_axis=0, concat_axis=0, axis_index_gro...  42.3 us
    pallas_call x4, Pallas kernels, call(): pl.pallas_call(kernel, out_shape=shapes, in_specs=[far] * fetched + [vmem...  5.39 us

profile of v22, /device:TPU:0, one launch (start us, length us, event | category | flops | bytes accessed | tf_op | source)
XLA Modules:
  0.0 47.7 jit_solution(7290743843054509063)
XLA Ops:
  0.0 2.1 %shard_map.127 = (bf16[16,128,128]{2,1,0:T(8,128)(2,1)S(1)}, f32[8,128,128]{2,1,0:T(8,128)S(1)}, bf16[128,128]{1,0:T(8,128)(2,1)S(1)}, bf16[128,128]{1,0:T(8,128...) custom-call(bf16[8,128,128]{2,1,0:T(8,128)(2,1)} %pair.1, ...), custom_call_target="tpu_custom_call" | custom-call | flops 167772160 | bytes 623616 | tf_op jit(solution)/shard_map/pallas_call | solution.py:328
  2.1 20.1 %all_to_all.15.edges = bf16[16,128,128]{2,1,0:T(8,128)(2,1)S(1)} all-to-all(bf16[16,128,128]{2,1,0:T(8,128)(2,1)S(1)} %get-tuple-element.17), channel_id=1, replica_groups={{11,0,5,10,15,4,9,14,3,8,13,2,7,12,1,6},{27,16,21,26,31,20,25,30,19,24,..., dimensions={0} | all-to-all | bytes 1048576 | tf_op jit(solution)/shard_map/all_to_all | solution.py:51
  22.2 0.3 shard_map.128
  22.5 0.0 copy-start
  22.6 12.1 %all_to_all.16.returned = bf16[16,64,128]{2,1,0:T(8,128)(2,1)S(1)} all-to-all(bf16[16,64,128]{2,1,0:T(8,128)(2,1)S(1)} %shard_map.128), channel_id=1, replica_groups={{11,15,14,13,12,10,9,8,7,6,5,4,3,2,1,0},{27,31,30,29,28,26,25,24,23,22,..., dimensions={0} | all-to-all | bytes 524288 | tf_op jit(solution)/shard_map/all_to_all | solution.py:51
  34.7 0.0 copy-done
  34.7 0.9 %shard_map.129 = (f32[8,128,128]{2,1,0:T(8,128)S(1)}, bf16[8,128,128]{2,1,0:T(8,128)(2,1)S(1)}, bf16[16,32,128]{2,1,0:T(8,128)(2,1)S(1)}) custom-call(bf16[16,64,128]{2,1,0:T(8,128)(2,1)S(1)} %all_to_all.16.returned, f32[8,128,128]{2,1,0:T(8,128)S(1)} %get-tuple-element.18.gate, bf16[8,128,128]{2,1,0:T(8,128)(2,1)S(1)} %copy-done, ...), custom_call_target="tpu_custom_call" | custom-call | flops 33554432 | bytes 1082368 | tf_op jit(solution)/shard_map/pallas_call | solution.py:328
  35.6 10.0 %all_to_all.17.refs_1_ = bf16[16,32,128]{2,1,0:T(8,128)(2,1)S(1)} all-to-all(bf16[16,32,128]{2,1,0:T(8,128)(2,1)S(1)} %get-tuple-element.27), channel_id=1, replica_groups={{11,0,5,10,15,4,9,14,3,8,13,2,7,12,1,6},{27,16,21,26,31,20,25,30,19,24,..., dimensions={0} | all-to-all | bytes 262144 | tf_op jit(solution)/shard_map/all_to_all | solution.py:51
  45.6 2.1 %shard_map.130 = bf16[8,128,128]{2,1,0:T(8,128)(2,1)} custom-call(bf16[8,128,128]{2,1,0:T(8,128)(2,1)S(1)} %get-tuple-element.21.att_norm, bf16[128,128]{1,0:T(8,128)(2,1)S(1)} %get-tuple-element.22.w_query, bf16[128,128]{1,0:T(8,128)(2,1)S(1)} %get-tuple-element.23.w_key, bf16[128,128]{1,0:T(8,128)(2,1)S(1)} %get-tuple-element.24.w_value, ...), custom_call_target="tpu_custom_call" | custom-call | flops 201326592 | bytes 1081344 | tf_op jit(solution)/shard_map/pallas_call | solution.py:328
Async XLA Ops:
  22.5 12.2 %copy-start = (bf16[8,128,128]{2,1,0:T(8,128)(2,1)S(1)}, bf16[8,128,128]{2,1,0:T(8,128)(2,1)}, u32[]{:S(2)}) copy-start(bf16[8,128,128]{2,1,0:T(8,128)(2,1)} %pair.1) | copy-start | bytes 786436

commit v23 on v16

--- a/solution.py
+++ b/solution.py
@@ -1,4 +1,5 @@
 import functools
+import math
 
 import jax
 import jax.numpy as jnp
@@ -34,13 +35,16 @@
     )
 
 
-def listing(ranks):
-    first = ranks - 1 - ranks // 4
-    return [first] + [rank for rank in range(ranks - 1, -1, -1) if rank != first]
-
-
-def slot(rank, ranks):
-    return listing(ranks).index(rank)
+def listing(ranks, mixed=False):
+    first, stride = ranks - 1 - ranks // 4, 5
+    if not mixed:
+        return [first] + [rank for rank in range(ranks - 1, -1, -1) if rank != first]
+    assert math.gcd(stride, ranks) == 1
+    return [(first + stride * n) % ranks for n in range(ranks)]
+
+
+def slot(rank, ranks, mixed=False):
+    return listing(ranks, mixed).index(rank)
 
 
 def slot_of(rank, ranks):
@@ -48,9 +52,9 @@
     return jnp.where(rank == first, 0, ranks - 1 - rank + (rank > first).astype(jnp.int32))
 
 
-def swap(blocks, ranks):
+def swap(blocks, ranks, mixed=False):
     members = blocks.shape[0]
-    order = listing(members)
+    order = listing(members, mixed)
     groups = [[first + member for member in order] for first in range(0, ranks, members)]
     return lax.all_to_all(
         blocks, "row", split_axis=0, concat_axis=0, axis_index_groups=groups, tiled=True
@@ -102,54 +106,51 @@
     return project
 
 
-def edges_kernel(*refs):
-    given, (right, far, near, normed, *staged) = refs[:13], refs[13:25]
-    pair, weights, held, sems = refs[25:]
-    targets = [pair, *(weights.at[n] for n in range(4)), *staged]
+def right_kernel(members, *refs):
+    given, (right, normed, *staged), (pair, w_right, w_right_gate, held, sems) = refs[:13], refs[13:25], refs[25:]
+    targets = [pair, w_right, w_right_gate, *staged]
     copies = [
         pltpu.make_async_copy(source, target, sems.at[n])
         for n, (source, target) in enumerate(zip(given, targets))
     ]
     for copy in copies:
         copy.start()
-    for copy in copies[:5]:
+    for copy in copies[:3]:
         copy.wait()
 
     def norm(i):
         normed[i] = lane_norm(pair[i].astype(F32))
         normed[i + 1] = lane_norm(pair[i + 1].astype(F32))
 
-    steps = [gated_edges(normed, weights.at[2 * n], weights.at[2 * n + 1], held.at[n]) for n in range(2)]
-    pipeline(range(0, pair.shape[0], 2), norm, *steps)
-    owners, block, parts = right.shape[0], right.shape[1], held.shape[1]
-    members, turns = owners // 2, near.shape[0]
-    me = lax.rem(lax.axis_index("row"), members)
+    pipeline(range(0, pair.shape[0], 2), norm, gated_edges(normed, w_right, w_right_gate, held))
+    owners, block = right.shape[0], right.shape[1]
     for member in range(members):
-        mine = pl.ds(pl.multiple_of((me ^ member) * block, block), block)
-        out = (near, far)[member // turns]
-        for part in range(parts):
-            lanes = slice(part * LANES, (part + 1) * LANES)
-            out[member % turns, :, lanes] = held[0, part, mine, :].astype(BF16)
-    for member in range(members):
-        for part in range(parts):
-            lanes = slice(part * LANES, (part + 1) * LANES)
-            sent = held[1, part, member * block : (member + 1) * block, :].astype(BF16)
+        for part in range(held.shape[0]):
+            sent = held[part, member * block : (member + 1) * block, :].astype(BF16)
             for owner in range(member, owners, members):
-                right[slot(owner, owners), :, lanes] = sent
-    for copy in copies[5:]:
+                right[slot(owner, owners, True), :, part * LANES : (part + 1) * LANES] = sent
+    for copy in copies[3:]:
         copy.wait()
 
 
-def merge_kernel(normed, w_tri_gate, near, passed, gate, *left):
-    for turn, out in enumerate(left):
-        out[0] = near[turn]
-        out[1] = passed[turn]
+def left_kernel(normed, w_left, w_left_gate, w_tri_gate, gate, *refs):
+    left, held = refs[:-1], refs[-1]
+    me = lax.rem(lax.axis_index("row"), len(left))
     width = w_tri_gate.shape[1]
     gate_weight = twice(w_tri_gate[...])
-    for i in range(0, normed.shape[0], 2):
+
+    def open_gate(i):
         opened = sigmoid(dot(side_by_side(normed, i), gate_weight))
         gate[i] = opened[:, :width]
         gate[i + 1] = opened[:, width:]
+
+    step = gated_edges(normed, w_left, w_left_gate, held)
+    pipeline(range(0, normed.shape[0], 2), step, open_gate)
+    for turn, out in enumerate(left):
+        block = out.shape[0]
+        mine = pl.ds(pl.multiple_of((me ^ turn) * block, block), block)
+        for part in range(held.shape[0]):
+            out[:, part * LANES : (part + 1) * LANES] = held[part, mine, :].astype(BF16)
 
 
 def channel_rows(blocks, rows, channel):
@@ -162,16 +163,12 @@
 
 def triangle_product(left, right, rows, channel):
     ranks = right.shape[0]
-    by_owner = [right.at[slot(r, ranks)] for r in range(ranks)]
+    by_owner = [right.at[slot(r, ranks, True)] for r in range(ranks)]
     return dot(channel_rows(left, rows, channel), channel_rows(by_owner, rows, channel), NT)
 
 
-def left_blocks(refs):
-    return [block.at[0] for block in refs] + [block.at[1] for block in refs]
-
-
 def triangle_kernel(rows, right, *refs):
-    left, out = left_blocks(refs[:-1]), refs[-1]
+    left, out = refs[:-1], refs[-1]
     members = len(left)
     me = lax.rem(lax.axis_index("row"), members)
     for channel in range(0, out.shape[1] // rows, 2):
@@ -184,7 +181,7 @@
 
 
 def partial_kernel(rows, right, *refs):
-    left, out = left_blocks(refs[:-1]), refs[-1]
+    left, out = refs[:-1], refs[-1]
     members = len(left)
     me = lax.rem(lax.axis_index("row"), members)
     for channel in range(out.shape[0]):
@@ -393,52 +390,47 @@
     channels = w_left.shape[1]
     owners, col_parts = lax.axis_size("row"), lax.axis_size("col")
     half = owners // 2
-    near = half // 2
     own = channels // half
     residues = owners * rows
     cells = rows * cols
 
-    later = (w_tri_gate, w_tri_out, w_query, w_key, w_value, w_att_gate, w_att_out)
-    right, far, left, normed, *later, w_bias_t = call(
-        edges_kernel,
+    later = (w_left, w_left_gate, w_tri_gate, w_tri_out, w_query, w_key, w_value, w_att_gate, w_att_out)
+    right, normed, *later, w_bias_t = call(
+        functools.partial(right_kernel, half),
         [
             ((owners, own * rows, cols), BF16),
-            ((near, own * rows, cols), BF16),
-            ((near, own * rows, cols), BF16),
             (pair_rep.shape, BF16),
             *[(w.shape, BF16) for w in later],
             (w_bias.shape[::-1], BF16),
         ],
         [
             (pair_rep.shape, BF16),
-            ((4, width, channels), BF16),
-            ((2, cols // LANES, channels * rows, LANES), F32),
+            (w_right.shape, BF16),
+            (w_right_gate.shape, BF16),
+            ((cols // LANES, (channels + 1) * rows, LANES), F32),
             pltpu.SemaphoreType.DMA((13,)),
         ],
-        8 * cells * width * channels,
+        4 * cells * width * channels,
         pair_rep,
-        w_left,
-        w_left_gate,
         w_right,
         w_right_gate,
         *later,
         w_bias.T,
         fetched=13,
     )
-    w_tri_gate, w_tri_out, w_query, w_key, w_value, w_att_gate, w_att_out = later
-    passed = lax.ppermute(far, "row", [(r, r ^ near) for r in range(owners)])
-    right = swap(right, owners)
+    w_left, w_left_gate, w_tri_gate, w_tri_out, w_query, w_key, w_value, w_att_gate, w_att_out = later
+    right = swap(right, owners, True)
     gate, *left = call(
-        merge_kernel,
-        [((rows, cols, width), F32)] + [((2, own * rows, cols), BF16)] * near,
-        [],
-        2 * cells * width * channels,
+        left_kernel,
+        [((rows, cols, width), F32)] + [((own * rows, cols), BF16)] * half,
+        [((cols // LANES, (channels + 1) * rows, LANES), F32)],
+        6 * cells * width * channels,
         normed,
+        w_left,
+        w_left_gate,
         w_tri_gate,
-        left,
-        passed,
     )
-    for turn in range(1, near):
+    for turn in range(half - 1, 0, -1):
         left[turn] = lax.ppermute(left[turn], "row", [(r, r ^ turn) for r in range(owners)])
     flops = 2 * own * half * rows * residues * cols
     if col_parts == 1:
@@ -471,7 +463,7 @@
             ((owners, HEADS * rows, cols), BF16),
         ],
         [
-            ((cols // LANES, channels * rows, LANES), F32),
+            ((cols // LANES, (channels + 1) * rows, LANES), F32),
             ((HEADS * rows, cols), F32),
             ((4, cols, channels), BF16),
         ],

time: 54.8 us -> 48.3 us (0.88)
  waiting for transfers between devices: 14.6 us -> 2.55 us
  starting transfers between devices: 13.5 us -> 18.7 us
    ppermute x1 -> x0, waiting for transfers between devices: 11.8 us -> none  [body(): passed = lax.ppermute(far, 'row', [(r, r ^ near) for r in range(owners)])]
    ppermute x3 -> x7, starting transfers between devices: 3.55 us -> 9.4 us  [body(): lax.ppermute(left[turn], 'row', [(r, r ^ turn) for r in range(owners)])]
    ppermute x3 -> x7, waiting for transfers between devices: 2.78 us -> 2.55 us  [body(): lax.ppermute(left[turn], 'row', [(r, r ^ turn) for r in range(owners)])]
  transfers between devices with their start and end apart: 5 -> 8, of which waited for: 4 -> 4; matrix products, arithmetic and copies ran while one was open for 0% -> 0% of each run, Pallas kernels for 0% -> 1%
where the time goes in v23:
time: 48.3 us; the launch traced here: 47.9 us
  blocking collectives  20.1 us (42%)
  starting transfers between devices  18.7 us (39%)
  Pallas kernels  6.56 us (14%)
  waiting for transfers between devices  2.55 us (5%)
    all_to_all x2, blocking collectives, swap(): lax.all_to_all(blocks, 'row', split_axis=0, concat_axis=0, axis_index_gro...  20.1 us
    ppermute x7, starting transfers between devices, body(): lax.ppermute(left[turn], 'row', [(r, r ^ turn) for r in range(owners)])  9.4 us
    all_to_all x1, starting transfers between devices, swap(): lax.all_to_all(blocks, 'row', split_axis=0, concat_axis=0, axis_index_gro...  9.29 us
    pallas_call x5, Pallas kernels, call(): pl.pallas_call(kernel, out_shape=shapes, in_specs=[far] * fetched + [vmem...  6.56 us
    ppermute x7, waiting for transfers between devices, body(): lax.ppermute(left[turn], 'row', [(r, r ^ turn) for r in range(owners)])  2.55 us
  transfers between devices with their start and end apart: 8, of which 4 were waited for; matrix products, arithmetic and copies ran while one was open for 0% of the time, Pallas kernels for 1%

profile of v23, /device:TPU:0, one launch (start us, length us, event | category | flops | bytes accessed | tf_op | source)
XLA Modules:
  0.0 47.9 jit_solution(5562823940456402780)
XLA Ops:
  0.0 2.7 %shard_map.127 = (bf16[16,128,128]{2,1,0:T(8,128)(2,1)}, bf16[8,128,128]{2,1,0:T(8,128)(2,1)S(1)}, bf16[128,128]{1,0:T(8,128)(2,1)S(1)}, bf16[128,128]{1,0:T(8,1...) custom-call(bf16[8,128,128]{2,1,0:T(8,128)(2,1)} %pair.1, ...), custom_call_target="tpu_custom_call" | custom-call | flops 67108864 | bytes 623616 | tf_op jit(solution)/shard_map/pallas_call | solution.py:362
  2.7 9.3 %all-to-all-start = ((bf16[16,128,128]{2,1,0:T(8,128)(2,1)}), bf16[16,128,128]{2,1,0:T(8,128)(2,1)S(1)}, u32[]{:S(2)}, u32[]{:S(2)}) async-start(bf16[16,128,128]{2,1,0:T(8,128)(2,1)} %get-tuple-element.29), calls=%async_computation | async-start | bytes 1048576 | tf_op jit(solution)/shard_map/all_to_all | solution.py:59
  12.0 0.5 shard_map.128
  12.5 0.7 %collective-permute-start = (bf16[128,128]{1,0:T(8,128)(2,1)S(1)}, bf16[128,128]{1,0:T(8,128)(2,1)S(1)}, u32[]{:S(2)}, u32[]{:S(2)}) collective-permute-start(bf16[128,128]{1,0:T(8,128)(2,1)S(1)} %get-tuple-element.35), channel_id=1, source_target_pairs={{0,1},{1,0},{2,3},{3,2},{4,5},{5,4},{6,7},{7,6},{8,9},{9,8},{10,11... | collective-permute-start | bytes 98312 | tf_op jit(solution)/shard_map/ppermute | solution.py:434
  13.2 0.5 %collective-permute-start.1 = (bf16[128,128]{1,0:T(8,128)(2,1)S(1)}, bf16[128,128]{1,0:T(8,128)(2,1)S(1)}, u32[]{:S(2)}, u32[]{:S(2)}) collective-permute-start(bf16[128,128]{1,0:T(8,128)(2,1)S(1)} %get-tuple-element.36), channel_id=1, source_target_pairs={{0,2},{1,3},{2,0},{3,1},{4,6},{5,7},{6,4},{7,5},{8,10},{9,11},{10,... | collective-permute-start | bytes 98312 | tf_op jit(solution)/shard_map/ppermute | solution.py:434
  13.7 2.3 %collective-permute-start.2 = (bf16[128,128]{1,0:T(8,128)(2,1)S(1)}, bf16[128,128]{1,0:T(8,128)(2,1)S(1)}, u32[]{:S(2)}, u32[]{:S(2)}) collective-permute-start(bf16[128,128]{1,0:T(8,128)(2,1)S(1)} %get-tuple-element.37), channel_id=1, source_target_pairs={{0,3},{1,2},{2,1},{3,0},{4,7},{5,6},{6,5},{7,4},{8,11},{9,10},{10,... | collective-permute-start | bytes 98312 | tf_op jit(solution)/shard_map/ppermute | solution.py:434
  16.0 0.6 %collective-permute-start.3 = (bf16[128,128]{1,0:T(8,128)(2,1)S(1)}, bf16[128,128]{1,0:T(8,128)(2,1)S(1)}, u32[]{:S(2)}, u32[]{:S(2)}) collective-permute-start(bf16[128,128]{1,0:T(8,128)(2,1)S(1)} %get-tuple-element.38), channel_id=1, source_target_pairs={{0,4},{1,5},{2,6},{3,7},{4,0},{5,1},{6,2},{7,3},{8,12},{9,13},{10,... | collective-permute-start | bytes 98312 | tf_op jit(solution)/shard_map/ppermute | solution.py:434
  16.6 1.5 %collective-permute-start.4 = (bf16[128,128]{1,0:T(8,128)(2,1)S(1)}, bf16[128,128]{1,0:T(8,128)(2,1)S(1)}, u32[]{:S(2)}, u32[]{:S(2)}) collective-permute-start(bf16[128,128]{1,0:T(8,128)(2,1)S(1)} %get-tuple-element.39), channel_id=1, source_target_pairs={{0,5},{1,4},{2,7},{3,6},{4,1},{5,0},{6,3},{7,2},{8,13},{9,12},{10,... | collective-permute-start | bytes 98312 | tf_op jit(solution)/shard_map/ppermute | solution.py:434
  18.1 0.0 collective-permute-done.refs_1_
  18.1 0.6 %collective-permute-start.5 = (bf16[128,128]{1,0:T(8,128)(2,1)S(1)}, bf16[128,128]{1,0:T(8,128)(2,1)S(1)}, u32[]{:S(2)}, u32[]{:S(2)}) collective-permute-start(bf16[128,128]{1,0:T(8,128)(2,1)S(1)} %get-tuple-element.40), channel_id=1, source_target_pairs={{0,6},{1,7},{2,4},{3,5},{4,2},{5,3},{6,0},{7,1},{8,14},{9,15},{10,... | collective-permute-start | bytes 98312 | tf_op jit(solution)/shard_map/ppermute | solution.py:434
  18.7 0.0 collective-permute-done.1.refs_2_
  18.7 3.2 %collective-permute-start.6 = (bf16[128,128]{1,0:T(8,128)(2,1)S(1)}, bf16[128,128]{1,0:T(8,128)(2,1)S(1)}, u32[]{:S(2)}, u32[]{:S(2)}) collective-permute-start(bf16[128,128]{1,0:T(8,128)(2,1)S(1)} %get-tuple-element.41), channel_id=1, source_target_pairs={{0,7},{1,6},{2,5},{3,4},{4,3},{5,2},{6,1},{7,0},{8,15},{9,14},{10,... | collective-permute-start | bytes 98312 | tf_op jit(solution)/shard_map/ppermute | solution.py:434
  21.9 0.0 collective-permute-done.2.refs_3_
  21.9 0.5 collective-permute-done.3.refs_4_
  22.3 0.6 %collective-permute-done.4.refs_5_ = bf16[128,128]{1,0:T(8,128)(2,1)S(1)} collective-permute-done((bf16[128,128]{1,0:T(8,128)(2,1)S(1)}, bf16[128,128]{1,0:T(8,128)(2,1)S(1)}, u32[]{:S(2)}, u32[]{:S(2)}) %collective-permute-start.4) | collective-permute-done | bytes 32800 | tf_op jit(solution)/shard_map/ppermute | solution.py:434
  23.0 1.1 %collective-permute-done.5.refs_6_ = bf16[128,128]{1,0:T(8,128)(2,1)S(1)} collective-permute-done((bf16[128,128]{1,0:T(8,128)(2,1)S(1)}, bf16[128,128]{1,0:T(8,128)(2,1)S(1)}, u32[]{:S(2)}, u32[]{:S(2)}) %collective-permute-start.5) | collective-permute-done | bytes 32800 | tf_op jit(solution)/shard_map/ppermute | solution.py:434
  24.1 0.3 collective-permute-done.6.refs_7_
  24.4 0.0 all-to-all-done.right
  24.4 0.5 shard_map.129
  24.9 0.0 copy-start
  24.9 10.0 %all_to_all.15.returned = bf16[8,128,128]{2,1,0:T(8,128)(2,1)S(1)} all-to-all(bf16[8,128,128]{2,1,0:T(8,128)(2,1)S(1)} %shard_map.129), channel_id=1, replica_groups={{5,7,6,4,3,2,1,0},{13,15,14,12,11,10,9,8},{21,23,22,20,19,18,17,16},{29..., dimensions={0} | all-to-all | bytes 524288 | tf_op jit(solution)/shard_map/all_to_all | solution.py:59
  34.9 0.0 copy-done
  34.9 0.9 %shard_map.130 = (f32[8,128,128]{2,1,0:T(8,128)S(1)}, bf16[8,128,128]{2,1,0:T(8,128)(2,1)S(1)}, bf16[16,32,128]{2,1,0:T(8,128)(2,1)S(1)}) custom-call(bf16[8,128,128]{2,1,0:T(8,128)(2,1)S(1)} %all_to_all.15.returned, f32[8,128,128]{2,1,0:T(8,128)S(1)} %get-tuple-element.42.gate, bf16[8,128,128]{2,1,0:T(8,128)(2,1)S(1)} %copy-done, ...), custom_call_target="tpu_custom_call" | custom-call | flops 33554432 | bytes 1082368 | tf_op jit(solution)/shard_map/pallas_call | solution.py:362
  35.8 10.1 %all_to_all.16.refs_1_ = bf16[16,32,128]{2,1,0:T(8,128)(2,1)S(1)} all-to-all(bf16[16,32,128]{2,1,0:T(8,128)(2,1)S(1)} %get-tuple-element.51), channel_id=1, replica_groups={{11,15,14,13,12,10,9,8,7,6,5,4,3,2,1,0},{27,31,30,29,28,26,25,24,23,22,..., dimensions={0} | all-to-all | bytes 262144 | tf_op jit(solution)/shard_map/all_to_all | solution.py:59
  45.9 2.1 %shard_map.131 = bf16[8,128,128]{2,1,0:T(8,128)(2,1)} custom-call(bf16[8,128,128]{2,1,0:T(8,128)(2,1)S(1)} %get-tuple-element.45.att_norm, bf16[128,128]{1,0:T(8,128)(2,1)S(1)} %get-tuple-element.46.w_query, bf16[128,128]{1,0:T(8,128)(2,1)S(1)} %get-tuple-element.47.w_key, bf16[128,128]{1,0:T(8,128)(2,1)S(1)} %get-tuple-element.48.w_value, ...), custom_call_target="tpu_custom_call" | custom-call | flops 201326592 | bytes 1081344 | tf_op jit(solution)/shard_map/pallas_call | solution.py:362
Async XLA Ops:
  2.7 21.7 %all-to-all-start = ((bf16[16,128,128]{2,1,0:T(8,128)(2,1)}), bf16[16,128,128]{2,1,0:T(8,128)(2,1)S(1)}, u32[]{:S(2)}, u32[]{:S(2)}) async-start(bf16[16,128,128]{2,1,0:T(8,128)(2,1)} %get-tuple-element.29), calls=%async_computation | async-start | bytes 1048576 | tf_op jit(solution)/shard_map/all_to_all | solution.py:59
  12.5 5.7 %collective-permute-start = (bf16[128,128]{1,0:T(8,128)(2,1)S(1)}, bf16[128,128]{1,0:T(8,128)(2,1)S(1)}, u32[]{:S(2)}, u32[]{:S(2)}) collective-permute-start(bf16[128,128]{1,0:T(8,128)(2,1)S(1)} %get-tuple-element.35), channel_id=1, source_target_pairs={{0,1},{1,0},{2,3},{3,2},{4,5},{5,4},{6,7},{7,6},{8,9},{9,8},{10,11... | collective-permute-start | bytes 98312 | tf_op jit(solution)/shard_map/ppermute | solution.py:434
  13.2 5.5 %collective-permute-start.1 = (bf16[128,128]{1,0:T(8,128)(2,1)S(1)}, bf16[128,128]{1,0:T(8,128)(2,1)S(1)}, u32[]{:S(2)}, u32[]{:S(2)}) collective-permute-start(bf16[128,128]{1,0:T(8,128)(2,1)S(1)} %get-tuple-element.36), channel_id=1, source_target_pairs={{0,2},{1,3},{2,0},{3,1},{4,6},{5,7},{6,4},{7,5},{8,10},{9,11},{10,... | collective-permute-start | bytes 98312 | tf_op jit(solution)/shard_map/ppermute | solution.py:434
  13.7 8.2 %collective-permute-start.2 = (bf16[128,128]{1,0:T(8,128)(2,1)S(1)}, bf16[128,128]{1,0:T(8,128)(2,1)S(1)}, u32[]{:S(2)}, u32[]{:S(2)}) collective-permute-start(bf16[128,128]{1,0:T(8,128)(2,1)S(1)} %get-tuple-element.37), channel_id=1, source_target_pairs={{0,3},{1,2},{2,1},{3,0},{4,7},{5,6},{6,5},{7,4},{8,11},{9,10},{10,... | collective-permute-start | bytes 98312 | tf_op jit(solution)/shard_map/ppermute | solution.py:434
  16.0 6.3 %collective-permute-start.3 = (bf16[128,128]{1,0:T(8,128)(2,1)S(1)}, bf16[128,128]{1,0:T(8,128)(2,1)S(1)}, u32[]{:S(2)}, u32[]{:S(2)}) collective-permute-start(bf16[128,128]{1,0:T(8,128)(2,1)S(1)} %get-tuple-element.38), channel_id=1, source_target_pairs={{0,4},{1,5},{2,6},{3,7},{4,0},{5,1},{6,2},{7,3},{8,12},{9,13},{10,... | collective-permute-start | bytes 98312 | tf_op jit(solution)/shard_map/ppermute | solution.py:434
  16.6 6.4 %collective-permute-start.4 = (bf16[128,128]{1,0:T(8,128)(2,1)S(1)}, bf16[128,128]{1,0:T(8,128)(2,1)S(1)}, u32[]{:S(2)}, u32[]{:S(2)}) collective-permute-start(bf16[128,128]{1,0:T(8,128)(2,1)S(1)} %get-tuple-element.39), channel_id=1, source_target_pairs={{0,5},{1,4},{2,7},{3,6},{4,1},{5,0},{6,3},{7,2},{8,13},{9,12},{10,... | collective-permute-start | bytes 98312 | tf_op jit(solution)/shard_map/ppermute | solution.py:434
  18.1 5.9 %collective-permute-start.5 = (bf16[128,128]{1,0:T(8,128)(2,1)S(1)}, bf16[128,128]{1,0:T(8,128)(2,1)S(1)}, u32[]{:S(2)}, u32[]{:S(2)}) collective-permute-start(bf16[128,128]{1,0:T(8,128)(2,1)S(1)} %get-tuple-element.40), channel_id=1, source_target_pairs={{0,6},{1,7},{2,4},{3,5},{4,2},{5,3},{6,0},{7,1},{8,14},{9,15},{10,... | collective-permute-start | bytes 98312 | tf_op jit(solution)/shard_map/ppermute | solution.py:434
  18.7 5.7 %collective-permute-start.6 = (bf16[128,128]{1,0:T(8,128)(2,1)S(1)}, bf16[128,128]{1,0:T(8,128)(2,1)S(1)}, u32[]{:S(2)}, u32[]{:S(2)}) collective-permute-start(bf16[128,128]{1,0:T(8,128)(2,1)S(1)} %get-tuple-element.41), channel_id=1, source_target_pairs={{0,7},{1,6},{2,5},{3,4},{4,3},{5,2},{6,1},{7,0},{8,15},{9,14},{10,... | collective-permute-start | bytes 98312 | tf_op jit(solution)/shard_map/ppermute | solution.py:434
  24.9 10.0 %copy-start = (bf16[8,128,128]{2,1,0:T(8,128)(2,1)S(1)}, bf16[8,128,128]{2,1,0:T(8,128)(2,1)}, u32[]{:S(2)}) copy-start(bf16[8,128,128]{2,1,0:T(8,128)(2,1)} %pair.1) | copy-start | bytes 786436

commit v24 on v23

--- a/solution.py
+++ b/solution.py
@@ -168,7 +168,7 @@
 
 
 def triangle_kernel(rows, right, *refs):
-    left, out = refs[:-1], refs[-1]
+    left, out = refs[-2::-1], refs[-1]
     members = len(left)
     me = lax.rem(lax.axis_index("row"), members)
     for channel in range(0, out.shape[1] // rows, 2):
@@ -181,7 +181,7 @@
 
 
 def partial_kernel(rows, right, *refs):
-    left, out = refs[:-1], refs[-1]
+    left, out = refs[-2::-1], refs[-1]
     members = len(left)
     me = lax.rem(lax.axis_index("row"), members)
     for channel in range(out.shape[0]):
@@ -440,7 +440,7 @@
             [],
             flops,
             right,
-            *left,
+            *left[::-1],
         )
     else:
         partial_sums = call(
@@ -449,7 +449,7 @@
             [],
             flops,
             right,
-            *left,
+            *left[::-1],
         )
         summed = lax.psum_scatter(partial_sums, "col", scatter_dimension=2, tiled=True).astype(BF16)
         summed = by_slot(summed.reshape(own, half, rows, cols).swapaxes(0, 1))

time: 48.3 us -> 52 us (1.077)
  waiting for transfers between devices: 2.55 us -> 6.56 us
  starting transfers between devices: 18.7 us -> 17.5 us
  blocking collectives: 20.1 us -> 21.1 us
    ppermute x7, waiting for transfers between devices: 2.55 us -> 6.55 us  [body(): lax.ppermute(left[turn], 'row', [(r, r ^ turn) for r in range(owners)])]
    ppermute x7, starting transfers between devices: 9.4 us -> 8.2 us  [body(): lax.ppermute(left[turn], 'row', [(r, r ^ turn) for r in range(owners)])]
    all_to_all x2, blocking collectives: 20.1 us -> 21.1 us  [swap(): lax.all_to_all(blocks, 'row', split_axis=0, concat_axis=0, axis_index_gro...]
  transfers between devices with their start and end apart: 8 -> 8, of which waited for: 4 -> 3; matrix products, arithmetic and copies ran while one was open for 0% -> 0% of each run, Pallas kernels for 1% -> 1%
where the time goes in v24:
time: 52 us; the launch traced here: 51.7 us
  blocking collectives  21.1 us (41%)
  starting transfers between devices  17.5 us (34%)
  Pallas kernels  6.56 us (13%)
  waiting for transfers between devices  6.56 us (13%)
    all_to_all x2, blocking collectives, swap(): lax.all_to_all(blocks, 'row', split_axis=0, concat_axis=0, axis_index_gro...  21.1 us
    all_to_all x1, starting transfers between devices, swap(): lax.all_to_all(blocks, 'row', split_axis=0, concat_axis=0, axis_index_gro...  9.29 us
    ppermute x7, starting transfers between devices, body(): lax.ppermute(left[turn], 'row', [(r, r ^ turn) for r in range(owners)])  8.2 us
    pallas_call x5, Pallas kernels, call(): pl.pallas_call(kernel, out_shape=shapes, in_specs=[far] * fetched + [vmem...  6.56 us
    ppermute x7, waiting for transfers between devices, body(): lax.ppermute(left[turn], 'row', [(r, r ^ turn) for r in range(owners)])  6.55 us
  transfers between devices with their start and end apart: 8, of which 3 were waited for; matrix products, arithmetic and copies ran while one was open for 0% of the time, Pallas kernels for 1%

profile of v24, /device:TPU:0, one launch (start us, length us, event | category | flops | bytes accessed | tf_op | source)
XLA Modules:
  0.0 51.7 jit_solution(18065956240978964277)
XLA Ops:
  0.0 2.7 %shard_map.127 = (bf16[16,128,128]{2,1,0:T(8,128)(2,1)}, bf16[8,128,128]{2,1,0:T(8,128)(2,1)S(1)}, bf16[128,128]{1,0:T(8,128)(2,1)S(1)}, bf16[128,128]{1,0:T(8,1...) custom-call(bf16[8,128,128]{2,1,0:T(8,128)(2,1)} %pair.1, ...), custom_call_target="tpu_custom_call" | custom-call | flops 67108864 | bytes 623616 | tf_op jit(solution)/shard_map/pallas_call | solution.py:362
  2.7 9.3 %all-to-all-start = ((bf16[16,128,128]{2,1,0:T(8,128)(2,1)}), bf16[16,128,128]{2,1,0:T(8,128)(2,1)S(1)}, u32[]{:S(2)}, u32[]{:S(2)}) async-start(bf16[16,128,128]{2,1,0:T(8,128)(2,1)} %get-tuple-element.29), calls=%async_computation | async-start | bytes 1048576 | tf_op jit(solution)/shard_map/all_to_all | solution.py:59
  12.0 0.5 shard_map.128
  12.5 0.7 %collective-permute-start = (bf16[128,128]{1,0:T(8,128)(2,1)S(1)}, bf16[128,128]{1,0:T(8,128)(2,1)S(1)}, u32[]{:S(2)}, u32[]{:S(2)}) collective-permute-start(bf16[128,128]{1,0:T(8,128)(2,1)S(1)} %get-tuple-element.34), channel_id=1, source_target_pairs={{0,7},{1,6},{2,5},{3,4},{4,3},{5,2},{6,1},{7,0},{8,15},{9,14},{10,... | collective-permute-start | bytes 98312 | tf_op jit(solution)/shard_map/ppermute | solution.py:434
  13.2 2.4 %collective-permute-start.1 = (bf16[128,128]{1,0:T(8,128)(2,1)S(1)}, bf16[128,128]{1,0:T(8,128)(2,1)S(1)}, u32[]{:S(2)}, u32[]{:S(2)}) collective-permute-start(bf16[128,128]{1,0:T(8,128)(2,1)S(1)} %get-tuple-element.35), channel_id=1, source_target_pairs={{0,6},{1,7},{2,4},{3,5},{4,2},{5,3},{6,0},{7,1},{8,14},{9,15},{10,... | collective-permute-start | bytes 98312 | tf_op jit(solution)/shard_map/ppermute | solution.py:434
  15.5 1.4 %collective-permute-start.2 = (bf16[128,128]{1,0:T(8,128)(2,1)S(1)}, bf16[128,128]{1,0:T(8,128)(2,1)S(1)}, u32[]{:S(2)}, u32[]{:S(2)}) collective-permute-start(bf16[128,128]{1,0:T(8,128)(2,1)S(1)} %get-tuple-element.36), channel_id=1, source_target_pairs={{0,5},{1,4},{2,7},{3,6},{4,1},{5,0},{6,3},{7,2},{8,13},{9,12},{10,... | collective-permute-start | bytes 98312 | tf_op jit(solution)/shard_map/ppermute | solution.py:434
  16.9 1.4 %collective-permute-start.3 = (bf16[128,128]{1,0:T(8,128)(2,1)S(1)}, bf16[128,128]{1,0:T(8,128)(2,1)S(1)}, u32[]{:S(2)}, u32[]{:S(2)}) collective-permute-start(bf16[128,128]{1,0:T(8,128)(2,1)S(1)} %get-tuple-element.37), channel_id=1, source_target_pairs={{0,4},{1,5},{2,6},{3,7},{4,0},{5,1},{6,2},{7,3},{8,12},{9,13},{10,... | collective-permute-start | bytes 98312 | tf_op jit(solution)/shard_map/ppermute | solution.py:434
  18.4 0.6 %collective-permute-start.4 = (bf16[128,128]{1,0:T(8,128)(2,1)S(1)}, bf16[128,128]{1,0:T(8,128)(2,1)S(1)}, u32[]{:S(2)}, u32[]{:S(2)}) collective-permute-start(bf16[128,128]{1,0:T(8,128)(2,1)S(1)} %get-tuple-element.38), channel_id=1, source_target_pairs={{0,3},{1,2},{2,1},{3,0},{4,7},{5,6},{6,5},{7,4},{8,11},{9,10},{10,... | collective-permute-start | bytes 98312 | tf_op jit(solution)/shard_map/ppermute | solution.py:434
  19.0 3.3 %collective-permute-done.refs_0_ = bf16[128,128]{1,0:T(8,128)(2,1)S(1)} collective-permute-done((bf16[128,128]{1,0:T(8,128)(2,1)S(1)}, bf16[128,128]{1,0:T(8,128)(2,1)S(1)}, u32[]{:S(2)}, u32[]{:S(2)}) %collective-permute-start) | collective-permute-done | bytes 32800 | tf_op jit(solution)/shard_map/ppermute | solution.py:434
  22.3 1.0 %collective-permute-start.5 = (bf16[128,128]{1,0:T(8,128)(2,1)S(1)}, bf16[128,128]{1,0:T(8,128)(2,1)S(1)}, u32[]{:S(2)}, u32[]{:S(2)}) collective-permute-start(bf16[128,128]{1,0:T(8,128)(2,1)S(1)} %get-tuple-element.39), channel_id=1, source_target_pairs={{0,2},{1,3},{2,0},{3,1},{4,6},{5,7},{6,4},{7,5},{8,10},{9,11},{10,... | collective-permute-start | bytes 98312 | tf_op jit(solution)/shard_map/ppermute | solution.py:434
  23.3 0.0 collective-permute-done.1.refs_1_
  23.3 0.7 %collective-permute-start.6 = (bf16[128,128]{1,0:T(8,128)(2,1)S(1)}, bf16[128,128]{1,0:T(8,128)(2,1)S(1)}, u32[]{:S(2)}, u32[]{:S(2)}) collective-permute-start(bf16[128,128]{1,0:T(8,128)(2,1)S(1)} %get-tuple-element.40), channel_id=1, source_target_pairs={{0,1},{1,0},{2,3},{3,2},{4,5},{5,4},{6,7},{7,6},{8,9},{9,8},{10,11... | collective-permute-start | bytes 98312 | tf_op jit(solution)/shard_map/ppermute | solution.py:434
  24.0 0.0 collective-permute-done.2.refs_2_
  24.0 0.0 collective-permute-done.3.refs_3_
  24.0 0.0 collective-permute-done.4.refs_4_
  24.0 2.2 %collective-permute-done.5.refs_5_ = bf16[128,128]{1,0:T(8,128)(2,1)S(1)} collective-permute-done((bf16[128,128]{1,0:T(8,128)(2,1)S(1)}, bf16[128,128]{1,0:T(8,128)(2,1)S(1)}, u32[]{:S(2)}, u32[]{:S(2)}) %collective-permute-start.5) | collective-permute-done | bytes 32800 | tf_op jit(solution)/shard_map/ppermute | solution.py:434
  26.2 1.0 %collective-permute-done.6.refs_6_ = bf16[128,128]{1,0:T(8,128)(2,1)S(1)} collective-permute-done((bf16[128,128]{1,0:T(8,128)(2,1)S(1)}, bf16[128,128]{1,0:T(8,128)(2,1)S(1)}, u32[]{:S(2)}, u32[]{:S(2)}) %collective-permute-start.6) | collective-permute-done | bytes 32800 | tf_op jit(solution)/shard_map/ppermute | solution.py:434
  27.2 0.0 all-to-all-done.right
  27.2 0.4 shard_map.129
  27.7 0.0 copy-start
  27.7 11.0 %all_to_all.15.returned = bf16[8,128,128]{2,1,0:T(8,128)(2,1)S(1)} all-to-all(bf16[8,128,128]{2,1,0:T(8,128)(2,1)S(1)} %shard_map.129), channel_id=1, replica_groups={{5,7,6,4,3,2,1,0},{13,15,14,12,11,10,9,8},{21,23,22,20,19,18,17,16},{29..., dimensions={0} | all-to-all | bytes 524288 | tf_op jit(solution)/shard_map/all_to_all | solution.py:59
  38.7 0.0 copy-done
  38.7 0.9 %shard_map.130 = (f32[8,128,128]{2,1,0:T(8,128)S(1)}, bf16[8,128,128]{2,1,0:T(8,128)(2,1)S(1)}, bf16[16,32,128]{2,1,0:T(8,128)(2,1)S(1)}) custom-call(bf16[8,128,128]{2,1,0:T(8,128)(2,1)S(1)} %all_to_all.15.returned, f32[8,128,128]{2,1,0:T(8,128)S(1)} %get-tuple-element.42.gate, bf16[8,128,128]{2,1,0:T(8,128)(2,1)S(1)} %copy-done, ...), custom_call_target="tpu_custom_call" | custom-call | flops 33554432 | bytes 1082368 | tf_op jit(solution)/shard_map/pallas_call | solution.py:362
  39.6 10.1 %all_to_all.16.refs_1_ = bf16[16,32,128]{2,1,0:T(8,128)(2,1)S(1)} all-to-all(bf16[16,32,128]{2,1,0:T(8,128)(2,1)S(1)} %get-tuple-element.51), channel_id=1, replica_groups={{11,15,14,13,12,10,9,8,7,6,5,4,3,2,1,0},{27,31,30,29,28,26,25,24,23,22,..., dimensions={0} | all-to-all | bytes 262144 | tf_op jit(solution)/shard_map/all_to_all | solution.py:59
  49.7 2.1 %shard_map.131 = bf16[8,128,128]{2,1,0:T(8,128)(2,1)} custom-call(bf16[8,128,128]{2,1,0:T(8,128)(2,1)S(1)} %get-tuple-element.45.att_norm, bf16[128,128]{1,0:T(8,128)(2,1)S(1)} %get-tuple-element.46.w_query, bf16[128,128]{1,0:T(8,128)(2,1)S(1)} %get-tuple-element.47.w_key, bf16[128,128]{1,0:T(8,128)(2,1)S(1)} %get-tuple-element.48.w_value, ...), custom_call_target="tpu_custom_call" | custom-call | flops 201326592 | bytes 1081344 | tf_op jit(solution)/shard_map/pallas_call | solution.py:362
Async XLA Ops:
  2.7 24.5 %all-to-all-start = ((bf16[16,128,128]{2,1,0:T(8,128)(2,1)}), bf16[16,128,128]{2,1,0:T(8,128)(2,1)S(1)}, u32[]{:S(2)}, u32[]{:S(2)}) async-start(bf16[16,128,128]{2,1,0:T(8,128)(2,1)} %get-tuple-element.29), calls=%async_computation | async-start | bytes 1048576 | tf_op jit(solution)/shard_map/all_to_all | solution.py:59
  12.5 9.9 %collective-permute-start = (bf16[128,128]{1,0:T(8,128)(2,1)S(1)}, bf16[128,128]{1,0:T(8,128)(2,1)S(1)}, u32[]{:S(2)}, u32[]{:S(2)}) collective-permute-start(bf16[128,128]{1,0:T(8,128)(2,1)S(1)} %get-tuple-element.34), channel_id=1, source_target_pairs={{0,7},{1,6},{2,5},{3,4},{4,3},{5,2},{6,1},{7,0},{8,15},{9,14},{10,... | collective-permute-start | bytes 98312 | tf_op jit(solution)/shard_map/ppermute | solution.py:434
  13.2 10.1 %collective-permute-start.1 = (bf16[128,128]{1,0:T(8,128)(2,1)S(1)}, bf16[128,128]{1,0:T(8,128)(2,1)S(1)}, u32[]{:S(2)}, u32[]{:S(2)}) collective-permute-start(bf16[128,128]{1,0:T(8,128)(2,1)S(1)} %get-tuple-element.35), channel_id=1, source_target_pairs={{0,6},{1,7},{2,4},{3,5},{4,2},{5,3},{6,0},{7,1},{8,14},{9,15},{10,... | collective-permute-start | bytes 98312 | tf_op jit(solution)/shard_map/ppermute | solution.py:434
  15.5 8.5 %collective-permute-start.2 = (bf16[128,128]{1,0:T(8,128)(2,1)S(1)}, bf16[128,128]{1,0:T(8,128)(2,1)S(1)}, u32[]{:S(2)}, u32[]{:S(2)}) collective-permute-start(bf16[128,128]{1,0:T(8,128)(2,1)S(1)} %get-tuple-element.36), channel_id=1, source_target_pairs={{0,5},{1,4},{2,7},{3,6},{4,1},{5,0},{6,3},{7,2},{8,13},{9,12},{10,... | collective-permute-start | bytes 98312 | tf_op jit(solution)/shard_map/ppermute | solution.py:434
  16.9 7.1 %collective-permute-start.3 = (bf16[128,128]{1,0:T(8,128)(2,1)S(1)}, bf16[128,128]{1,0:T(8,128)(2,1)S(1)}, u32[]{:S(2)}, u32[]{:S(2)}) collective-permute-start(bf16[128,128]{1,0:T(8,128)(2,1)S(1)} %get-tuple-element.37), channel_id=1, source_target_pairs={{0,4},{1,5},{2,6},{3,7},{4,0},{5,1},{6,2},{7,3},{8,12},{9,13},{10,... | collective-permute-start | bytes 98312 | tf_op jit(solution)/shard_map/ppermute | solution.py:434
  18.4 5.6 %collective-permute-start.4 = (bf16[128,128]{1,0:T(8,128)(2,1)S(1)}, bf16[128,128]{1,0:T(8,128)(2,1)S(1)}, u32[]{:S(2)}, u32[]{:S(2)}) collective-permute-start(bf16[128,128]{1,0:T(8,128)(2,1)S(1)} %get-tuple-element.38), channel_id=1, source_target_pairs={{0,3},{1,2},{2,1},{3,0},{4,7},{5,6},{6,5},{7,4},{8,11},{9,10},{10,... | collective-permute-start | bytes 98312 | tf_op jit(solution)/shard_map/ppermute | solution.py:434
  22.3 3.9 %collective-permute-start.5 = (bf16[128,128]{1,0:T(8,128)(2,1)S(1)}, bf16[128,128]{1,0:T(8,128)(2,1)S(1)}, u32[]{:S(2)}, u32[]{:S(2)}) collective-permute-start(bf16[128,128]{1,0:T(8,128)(2,1)S(1)} %get-tuple-element.39), channel_id=1, source_target_pairs={{0,2},{1,3},{2,0},{3,1},{4,6},{5,7},{6,4},{7,5},{8,10},{9,11},{10,... | collective-permute-start | bytes 98312 | tf_op jit(solution)/shard_map/ppermute | solution.py:434
  23.3 3.9 %collective-permute-start.6 = (bf16[128,128]{1,0:T(8,128)(2,1)S(1)}, bf16[128,128]{1,0:T(8,128)(2,1)S(1)}, u32[]{:S(2)}, u32[]{:S(2)}) collective-permute-start(bf16[128,128]{1,0:T(8,128)(2,1)S(1)} %get-tuple-element.40), channel_id=1, source_target_pairs={{0,1},{1,0},{2,3},{3,2},{4,5},{5,4},{6,7},{7,6},{8,9},{9,8},{10,11... | collective-permute-start | bytes 98312 | tf_op jit(solution)/shard_map/ppermute | solution.py:434
  27.7 11.0 %copy-start = (bf16[8,128,128]{2,1,0:T(8,128)(2,1)S(1)}, bf16[8,128,128]{2,1,0:T(8,128)(2,1)}, u32[]{:S(2)}) copy-start(bf16[8,128,128]{2,1,0:T(8,128)(2,1)} %pair.1) | copy-start | bytes 786436

commit v25 on v22

--- a/solution.py
+++ b/solution.py
@@ -12,6 +12,7 @@
 HEADS = 4
 HEAD_DIM = 32
 LANES = 128
+RING = 8
 LOG2_E = 1.4426950408889634
 F32 = jnp.float32
 BF16 = jnp.bfloat16
@@ -86,6 +87,14 @@
         for late, step in enumerate(steps):
             if 0 <= tick - late < len(rows):
                 step(rows[tick - late])
+
+
+def doubled(step):
+    def both(i):
+        step(i)
+        step(i + 2)
+
+    return both
 
 
 def edges_kernel(*refs):
@@ -271,31 +280,31 @@
             raw = dot(key[row], jnp.concatenate(blocks, axis=1))
             for _, span in heads:
                 biased = raw[:, span] * score_scale + bias_t[:, span]
-                scores[row % 4, :, span] = biased
-                peaks[row % 4, :, span] = jnp.max(biased, axis=0, keepdims=True)
+                scores[row % RING, :, span] = biased
+                peaks[row % RING, :, span] = jnp.max(biased, axis=0, keepdims=True)
 
     def soften(i):
         for row in (i, i + 1):
             for _, span in heads:
-                lowered = scores[row % 4, :, span] - peaks[row % 4, :, span]
-                weights[row % 4, :, span] = jnp.exp2(lowered).astype(BF16)
+                lowered = scores[row % RING, :, span] - peaks[row % RING, :, span]
+                weights[row % RING, :, span] = jnp.exp2(lowered).astype(BF16)
 
     def collect(i):
         for row in (i, i + 1):
             for head in range(0, HEADS, 2):
                 (first, left), (second, right) = heads[head : head + 2]
                 values = jnp.concatenate([value_t[row, first.start : second.stop, :], ones], axis=0)
-                summed = dot(values, weights[row % 4, :, left.start : right.stop])
+                summed = dot(values, weights[row % RING, :, left.start : right.stop])
                 share = 1.0 / summed[2 * HEAD_DIM : 2 * HEAD_DIM + 1]
                 for mine, there, lanes in (
                     (first, slice(0, HEAD_DIM), slice(0, cols)),
                     (second, slice(HEAD_DIM, 2 * HEAD_DIM), slice(cols, 2 * cols)),
                 ):
                     attended = summed[there, lanes] * share[:, lanes] * gate_t[row, mine, :]
-                    gated[row % 4, mine, :] = attended.astype(BF16)
+                    gated[row % RING, mine, :] = attended.astype(BF16)
 
     def finish(i):
-        turned = jnp.concatenate([gated[i % 4].T, gated[(i + 1) % 4].T], axis=1)
+        turned = jnp.concatenate([gated[i % RING].T, gated[(i + 1) % RING].T], axis=1)
         both = dot(turned, w_last)
         done[i] = (first_pass[i] + both[:, :width]).astype(BF16)
         done[i + 1] = (first_pass[i + 1] + both[:, width:]).astype(BF16)
@@ -311,7 +320,8 @@
             for owner in range(bias.shape[0])
         ]
         bias_t[:, span] = jnp.concatenate(parts, axis=0).T * LOG2_E
-    pipeline(range(0, rows, 2), *before, score, soften, collect, finish)
+    steps = [doubled(step) for step in (*before, score, soften, collect, finish)]
+    pipeline(range(0, rows, 4), *steps)
     for copy in copies:
         copy.wait()
 
@@ -443,10 +453,10 @@
     out = [((rows, cols, width), BF16)]
     held = [
         ((residues, HEADS * cols), F32),
-        ((4, residues, HEADS * cols), F32),
-        ((4, 1, HEADS * cols), F32),
-        ((4, residues, HEADS * cols), BF16),
-        ((4, width, cols), BF16),
+        ((RING, residues, HEADS * cols), F32),
+        ((RING, 1, HEADS * cols), F32),
+        ((RING, residues, HEADS * cols), BF16),
+        ((RING, width, cols), BF16),
         ((rows, cols, width), BF16),
         pltpu.SemaphoreType.DMA((rows // 2,)),
     ]

time: 47.9 us -> 48 us (level)
  no operation moved by 1% of the time
where the time goes in v25:
time: 48 us; the launch traced here: 47.8 us
  blocking collectives  42.3 us (88%)
  Pallas kernels  5.48 us (11%)
    all_to_all x3, blocking collectives, swap(): lax.all_to_all(blocks, 'row', split_axis=0, concat_axis=0, axis_index_gro...  42.3 us
    pallas_call x4, Pallas kernels, call(): pl.pallas_call(kernel, out_shape=shapes, in_specs=[far] * fetched + [vmem...  5.48 us

profile of v25, /device:TPU:0, one launch (start us, length us, event | category | flops | bytes accessed | tf_op | source)
XLA Modules:
  0.0 47.8 jit_solution(4503530113825605372)
XLA Ops:
  0.0 2.1 %shard_map.127 = (bf16[16,128,128]{2,1,0:T(8,128)(2,1)S(1)}, f32[8,128,128]{2,1,0:T(8,128)S(1)}, bf16[128,128]{1,0:T(8,128)(2,1)S(1)}, bf16[128,128]{1,0:T(8,128...) custom-call(bf16[8,128,128]{2,1,0:T(8,128)(2,1)} %pair.1, ...), custom_call_target="tpu_custom_call" | custom-call | flops 167772160 | bytes 623616 | tf_op jit(solution)/shard_map/pallas_call | solution.py:338
  2.1 20.1 %all_to_all.15.edges = bf16[16,128,128]{2,1,0:T(8,128)(2,1)S(1)} all-to-all(bf16[16,128,128]{2,1,0:T(8,128)(2,1)S(1)} %get-tuple-element.17), channel_id=1, replica_groups={{11,0,5,10,15,4,9,14,3,8,13,2,7,12,1,6},{27,16,21,26,31,20,25,30,19,24,..., dimensions={0} | all-to-all | bytes 1048576 | tf_op jit(solution)/shard_map/all_to_all | solution.py:52
  22.2 0.3 shard_map.128
  22.5 0.0 copy-start
  22.6 12.1 %all_to_all.16.returned = bf16[16,64,128]{2,1,0:T(8,128)(2,1)S(1)} all-to-all(bf16[16,64,128]{2,1,0:T(8,128)(2,1)S(1)} %shard_map.128), channel_id=1, replica_groups={{11,15,14,13,12,10,9,8,7,6,5,4,3,2,1,0},{27,31,30,29,28,26,25,24,23,22,..., dimensions={0} | all-to-all | bytes 524288 | tf_op jit(solution)/shard_map/all_to_all | solution.py:52
  34.7 0.0 copy-done
  34.7 0.9 %shard_map.129 = (f32[8,128,128]{2,1,0:T(8,128)S(1)}, bf16[8,128,128]{2,1,0:T(8,128)(2,1)S(1)}, bf16[16,32,128]{2,1,0:T(8,128)(2,1)S(1)}) custom-call(bf16[16,64,128]{2,1,0:T(8,128)(2,1)S(1)} %all_to_all.16.returned, f32[8,128,128]{2,1,0:T(8,128)S(1)} %get-tuple-element.18.gate, bf16[8,128,128]{2,1,0:T(8,128)(2,1)S(1)} %copy-done, ...), custom_call_target="tpu_custom_call" | custom-call | flops 33554432 | bytes 1082368 | tf_op jit(solution)/shard_map/pallas_call | solution.py:338
  35.6 10.0 %all_to_all.17.refs_1_ = bf16[16,32,128]{2,1,0:T(8,128)(2,1)S(1)} all-to-all(bf16[16,32,128]{2,1,0:T(8,128)(2,1)S(1)} %get-tuple-element.27), channel_id=1, replica_groups={{11,0,5,10,15,4,9,14,3,8,13,2,7,12,1,6},{27,16,21,26,31,20,25,30,19,24,..., dimensions={0} | all-to-all | bytes 262144 | tf_op jit(solution)/shard_map/all_to_all | solution.py:52
  45.6 2.2 %shard_map.130 = bf16[8,128,128]{2,1,0:T(8,128)(2,1)} custom-call(bf16[8,128,128]{2,1,0:T(8,128)(2,1)S(1)} %get-tuple-element.21.att_norm, bf16[128,128]{1,0:T(8,128)(2,1)S(1)} %get-tuple-element.22.w_query, bf16[128,128]{1,0:T(8,128)(2,1)S(1)} %get-tuple-element.23.w_key, bf16[128,128]{1,0:T(8,128)(2,1)S(1)} %get-tuple-element.24.w_value, ...), custom_call_target="tpu_custom_call" | custom-call | flops 201326592 | bytes 1081344 | tf_op jit(solution)/shard_map/pallas_call | solution.py:338
Async XLA Ops:
  22.5 12.2 %copy-start = (bf16[8,128,128]{2,1,0:T(8,128)(2,1)S(1)}, bf16[8,128,128]{2,1,0:T(8,128)(2,1)}, u32[]{:S(2)}) copy-start(bf16[8,128,128]{2,1,0:T(8,128)(2,1)} %pair.1) | copy-start | bytes 786436

commit v26 on v22

--- a/solution.py
+++ b/solution.py
@@ -83,7 +83,7 @@
 
 def pipeline(rows, *steps):
     for tick in range(len(rows) + len(steps) - 1):
-        for late, step in enumerate(steps):
+        for late, step in reversed(list(enumerate(steps))):
             if 0 <= tick - late < len(rows):
                 step(rows[tick - late])
 

time: 47.9 us -> 48.4 us (1.010)
  Pallas kernels: 5.39 us -> 5.88 us
    pallas_call x4, Pallas kernels: 5.39 us -> 5.88 us  [call(): pl.pallas_call(kernel, out_shape=shapes, in_specs=[far] * fetched + [vmem...]
where the time goes in v26:
time: 48.4 us; the launch traced here: 48.2 us
  blocking collectives  42.3 us (87%)
  Pallas kernels  5.88 us (12%)
    all_to_all x3, blocking collectives, swap(): lax.all_to_all(blocks, 'row', split_axis=0, concat_axis=0, axis_index_gro...  42.3 us
    pallas_call x4, Pallas kernels, call(): pl.pallas_call(kernel, out_shape=shapes, in_specs=[far] * fetched + [vmem...  5.88 us

profile of v26, /device:TPU:0, one launch (start us, length us, event | category | flops | bytes accessed | tf_op | source)
XLA Modules:
  0.0 48.2 jit_solution(13202532643340929570)
XLA Ops:
  0.0 2.1 %shard_map.127 = (bf16[16,128,128]{2,1,0:T(8,128)(2,1)S(1)}, f32[8,128,128]{2,1,0:T(8,128)S(1)}, bf16[128,128]{1,0:T(8,128)(2,1)S(1)}, bf16[128,128]{1,0:T(8,128...) custom-call(bf16[8,128,128]{2,1,0:T(8,128)(2,1)} %pair.1, ...), custom_call_target="tpu_custom_call" | custom-call | flops 167772160 | bytes 623616 | tf_op jit(solution)/shard_map/pallas_call | solution.py:328
  2.1 20.1 %all_to_all.15.edges = bf16[16,128,128]{2,1,0:T(8,128)(2,1)S(1)} all-to-all(bf16[16,128,128]{2,1,0:T(8,128)(2,1)S(1)} %get-tuple-element.17), channel_id=1, replica_groups={{11,0,5,10,15,4,9,14,3,8,13,2,7,12,1,6},{27,16,21,26,31,20,25,30,19,24,..., dimensions={0} | all-to-all | bytes 1048576 | tf_op jit(solution)/shard_map/all_to_all | solution.py:51
  22.2 0.3 shard_map.128
  22.5 0.0 copy-start
  22.6 12.1 %all_to_all.16.returned = bf16[16,64,128]{2,1,0:T(8,128)(2,1)S(1)} all-to-all(bf16[16,64,128]{2,1,0:T(8,128)(2,1)S(1)} %shard_map.128), channel_id=1, replica_groups={{11,15,14,13,12,10,9,8,7,6,5,4,3,2,1,0},{27,31,30,29,28,26,25,24,23,22,..., dimensions={0} | all-to-all | bytes 524288 | tf_op jit(solution)/shard_map/all_to_all | solution.py:51
  34.7 0.0 copy-done
  34.7 0.9 %shard_map.129 = (f32[8,128,128]{2,1,0:T(8,128)S(1)}, bf16[8,128,128]{2,1,0:T(8,128)(2,1)S(1)}, bf16[16,32,128]{2,1,0:T(8,128)(2,1)S(1)}) custom-call(bf16[16,64,128]{2,1,0:T(8,128)(2,1)S(1)} %all_to_all.16.returned, f32[8,128,128]{2,1,0:T(8,128)S(1)} %get-tuple-element.18.gate, bf16[8,128,128]{2,1,0:T(8,128)(2,1)S(1)} %copy-done, ...), custom_call_target="tpu_custom_call" | custom-call | flops 33554432 | bytes 1082368 | tf_op jit(solution)/shard_map/pallas_call | solution.py:328
  35.6 10.0 %all_to_all.17.refs_1_ = bf16[16,32,128]{2,1,0:T(8,128)(2,1)S(1)} all-to-all(bf16[16,32,128]{2,1,0:T(8,128)(2,1)S(1)} %get-tuple-element.27), channel_id=1, replica_groups={{11,0,5,10,15,4,9,14,3,8,13,2,7,12,1,6},{27,16,21,26,31,20,25,30,19,24,..., dimensions={0} | all-to-all | bytes 262144 | tf_op jit(solution)/shard_map/all_to_all | solution.py:51
  45.6 2.6 %shard_map.130 = bf16[8,128,128]{2,1,0:T(8,128)(2,1)} custom-call(bf16[8,128,128]{2,1,0:T(8,128)(2,1)S(1)} %get-tuple-element.21.att_norm, bf16[128,128]{1,0:T(8,128)(2,1)S(1)} %get-tuple-element.22.w_query, bf16[128,128]{1,0:T(8,128)(2,1)S(1)} %get-tuple-element.23.w_key, bf16[128,128]{1,0:T(8,128)(2,1)S(1)} %get-tuple-element.24.w_value, ...), custom_call_target="tpu_custom_call" | custom-call | flops 201326592 | bytes 1081344 | tf_op jit(solution)/shard_map/pallas_call | solution.py:328
Async XLA Ops:
  22.5 12.2 %copy-start = (bf16[8,128,128]{2,1,0:T(8,128)(2,1)S(1)}, bf16[8,128,128]{2,1,0:T(8,128)(2,1)}, u32[]{:S(2)}) copy-start(bf16[8,128,128]{2,1,0:T(8,128)(2,1)} %pair.1) | copy-start | bytes 786436

commit v27 on v22

--- a/solution.py
+++ b/solution.py
@@ -111,6 +111,7 @@
 
     def project(i):
         both = dot(turned, jnp.concatenate([normed[i], normed[i + 1]], axis=0), NT)
+        gates = dot(side_by_side(normed, i), gate_weight)
         for side in range(2):
             base = 2 * side * channels
             act = sigmoid(both[base + channels : base + 2 * channels]) * both[base : base + channels]
@@ -118,7 +119,7 @@
                 row, part = divmod(tile, cols // LANES)
                 place = pl.ds(side * rows + i + row, channels, stride=2 * rows)
                 held[part, place, :] = act[:, lanes]
-        opened = sigmoid(dot(side_by_side(normed, i), gate_weight))
+        opened = sigmoid(gates)
         gate[i] = opened[:, :width]
         gate[i + 1] = opened[:, width:]
 

time: 47.9 us -> 47.9 us (level)
  no operation moved by 1% of the time
where the time goes in v27:
time: 47.9 us; the launch traced here: 47.7 us
  blocking collectives  42.3 us (88%)
  Pallas kernels  5.39 us (11%)
    all_to_all x3, blocking collectives, swap(): lax.all_to_all(blocks, 'row', split_axis=0, concat_axis=0, axis_index_gro...  42.3 us
    pallas_call x4, Pallas kernels, call(): pl.pallas_call(kernel, out_shape=shapes, in_specs=[far] * fetched + [vmem...  5.39 us

profile of v27, /device:TPU:0, one launch (start us, length us, event | category | flops | bytes accessed | tf_op | source)
XLA Modules:
  0.0 47.7 jit_solution(9494831563822386739)
XLA Ops:
  0.0 2.1 %shard_map.127 = (bf16[16,128,128]{2,1,0:T(8,128)(2,1)S(1)}, f32[8,128,128]{2,1,0:T(8,128)S(1)}, bf16[128,128]{1,0:T(8,128)(2,1)S(1)}, bf16[128,128]{1,0:T(8,128...) custom-call(bf16[8,128,128]{2,1,0:T(8,128)(2,1)} %pair.1, ...), custom_call_target="tpu_custom_call" | custom-call | flops 167772160 | bytes 623616 | tf_op jit(solution)/shard_map/pallas_call | solution.py:329
  2.1 20.1 %all_to_all.15.edges = bf16[16,128,128]{2,1,0:T(8,128)(2,1)S(1)} all-to-all(bf16[16,128,128]{2,1,0:T(8,128)(2,1)S(1)} %get-tuple-element.17), channel_id=1, replica_groups={{11,0,5,10,15,4,9,14,3,8,13,2,7,12,1,6},{27,16,21,26,31,20,25,30,19,24,..., dimensions={0} | all-to-all | bytes 1048576 | tf_op jit(solution)/shard_map/all_to_all | solution.py:51
  22.2 0.3 shard_map.128
  22.5 0.0 copy-start
  22.6 12.1 %all_to_all.16.returned = bf16[16,64,128]{2,1,0:T(8,128)(2,1)S(1)} all-to-all(bf16[16,64,128]{2,1,0:T(8,128)(2,1)S(1)} %shard_map.128), channel_id=1, replica_groups={{11,15,14,13,12,10,9,8,7,6,5,4,3,2,1,0},{27,31,30,29,28,26,25,24,23,22,..., dimensions={0} | all-to-all | bytes 524288 | tf_op jit(solution)/shard_map/all_to_all | solution.py:51
  34.7 0.0 copy-done
  34.7 0.9 %shard_map.129 = (f32[8,128,128]{2,1,0:T(8,128)S(1)}, bf16[8,128,128]{2,1,0:T(8,128)(2,1)S(1)}, bf16[16,32,128]{2,1,0:T(8,128)(2,1)S(1)}) custom-call(bf16[16,64,128]{2,1,0:T(8,128)(2,1)S(1)} %all_to_all.16.returned, f32[8,128,128]{2,1,0:T(8,128)S(1)} %get-tuple-element.18.gate, bf16[8,128,128]{2,1,0:T(8,128)(2,1)S(1)} %copy-done, ...), custom_call_target="tpu_custom_call" | custom-call | flops 33554432 | bytes 1082368 | tf_op jit(solution)/shard_map/pallas_call | solution.py:329
  35.6 10.0 %all_to_all.17.refs_1_ = bf16[16,32,128]{2,1,0:T(8,128)(2,1)S(1)} all-to-all(bf16[16,32,128]{2,1,0:T(8,128)(2,1)S(1)} %get-tuple-element.27), channel_id=1, replica_groups={{11,0,5,10,15,4,9,14,3,8,13,2,7,12,1,6},{27,16,21,26,31,20,25,30,19,24,..., dimensions={0} | all-to-all | bytes 262144 | tf_op jit(solution)/shard_map/all_to_all | solution.py:51
  45.6 2.1 %shard_map.130 = bf16[8,128,128]{2,1,0:T(8,128)(2,1)} custom-call(bf16[8,128,128]{2,1,0:T(8,128)(2,1)S(1)} %get-tuple-element.21.att_norm, bf16[128,128]{1,0:T(8,128)(2,1)S(1)} %get-tuple-element.22.w_query, bf16[128,128]{1,0:T(8,128)(2,1)S(1)} %get-tuple-element.23.w_key, bf16[128,128]{1,0:T(8,128)(2,1)S(1)} %get-tuple-element.24.w_value, ...), custom_call_target="tpu_custom_call" | custom-call | flops 201326592 | bytes 1081344 | tf_op jit(solution)/shard_map/pallas_call | solution.py:329
Async XLA Ops:
  22.5 12.2 %copy-start = (bf16[8,128,128]{2,1,0:T(8,128)(2,1)S(1)}, bf16[8,128,128]{2,1,0:T(8,128)(2,1)}, u32[]{:S(2)}) copy-start(bf16[8,128,128]{2,1,0:T(8,128)(2,1)} %pair.1) | copy-start | bytes 786436

commit v28 on v27

--- a/solution.py
+++ b/solution.py
@@ -95,10 +95,12 @@
         pltpu.make_async_copy(source, target, sems.at[n])
         for n, (source, target) in enumerate(zip(given, targets))
     ]
-    for copy in copies:
+    for copy in copies[:6]:
         copy.start()
     for copy in copies[:6]:
         copy.wait()
+    for copy in copies[6:]:
+        copy.start()
     rows, width = pair.shape[0], pair.shape[2]
     channels = weights.shape[2]
     cols = pair.shape[1]

time: 47.9 us -> 47.9 us (level)
  no operation moved by 1% of the time
where the time goes in v28:
time: 47.9 us; the launch traced here: 47.7 us
  blocking collectives  42.3 us (88%)
  Pallas kernels  5.39 us (11%)
    all_to_all x3, blocking collectives, swap(): lax.all_to_all(blocks, 'row', split_axis=0, concat_axis=0, axis_index_gro...  42.3 us
    pallas_call x4, Pallas kernels, call(): pl.pallas_call(kernel, out_shape=shapes, in_specs=[far] * fetched + [vmem...  5.39 us

profile of v28, /device:TPU:0, one launch (start us, length us, event | category | flops | bytes accessed | tf_op | source)
XLA Modules:
  0.0 47.7 jit_solution(10794290283014883518)
XLA Ops:
  0.0 2.1 %shard_map.127 = (bf16[16,128,128]{2,1,0:T(8,128)(2,1)S(1)}, f32[8,128,128]{2,1,0:T(8,128)S(1)}, bf16[128,128]{1,0:T(8,128)(2,1)S(1)}, bf16[128,128]{1,0:T(8,128...) custom-call(bf16[8,128,128]{2,1,0:T(8,128)(2,1)} %pair.1, ...), custom_call_target="tpu_custom_call" | custom-call | flops 167772160 | bytes 623616 | tf_op jit(solution)/shard_map/pallas_call | solution.py:331
  2.1 20.1 %all_to_all.15.edges = bf16[16,128,128]{2,1,0:T(8,128)(2,1)S(1)} all-to-all(bf16[16,128,128]{2,1,0:T(8,128)(2,1)S(1)} %get-tuple-element.17), channel_id=1, replica_groups={{11,0,5,10,15,4,9,14,3,8,13,2,7,12,1,6},{27,16,21,26,31,20,25,30,19,24,..., dimensions={0} | all-to-all | bytes 1048576 | tf_op jit(solution)/shard_map/all_to_all | solution.py:51
  22.2 0.3 shard_map.128
  22.5 0.0 copy-start
  22.6 12.1 %all_to_all.16.returned = bf16[16,64,128]{2,1,0:T(8,128)(2,1)S(1)} all-to-all(bf16[16,64,128]{2,1,0:T(8,128)(2,1)S(1)} %shard_map.128), channel_id=1, replica_groups={{11,15,14,13,12,10,9,8,7,6,5,4,3,2,1,0},{27,31,30,29,28,26,25,24,23,22,..., dimensions={0} | all-to-all | bytes 524288 | tf_op jit(solution)/shard_map/all_to_all | solution.py:51
  34.7 0.0 copy-done
  34.7 0.9 %shard_map.129 = (f32[8,128,128]{2,1,0:T(8,128)S(1)}, bf16[8,128,128]{2,1,0:T(8,128)(2,1)S(1)}, bf16[16,32,128]{2,1,0:T(8,128)(2,1)S(1)}) custom-call(bf16[16,64,128]{2,1,0:T(8,128)(2,1)S(1)} %all_to_all.16.returned, f32[8,128,128]{2,1,0:T(8,128)S(1)} %get-tuple-element.18.gate, bf16[8,128,128]{2,1,0:T(8,128)(2,1)S(1)} %copy-done, ...), custom_call_target="tpu_custom_call" | custom-call | flops 33554432 | bytes 1082368 | tf_op jit(solution)/shard_map/pallas_call | solution.py:331
  35.6 10.0 %all_to_all.17.refs_1_ = bf16[16,32,128]{2,1,0:T(8,128)(2,1)S(1)} all-to-all(bf16[16,32,128]{2,1,0:T(8,128)(2,1)S(1)} %get-tuple-element.27), channel_id=1, replica_groups={{11,0,5,10,15,4,9,14,3,8,13,2,7,12,1,6},{27,16,21,26,31,20,25,30,19,24,..., dimensions={0} | all-to-all | bytes 262144 | tf_op jit(solution)/shard_map/all_to_all | solution.py:51
  45.6 2.1 %shard_map.130 = bf16[8,128,128]{2,1,0:T(8,128)(2,1)} custom-call(bf16[8,128,128]{2,1,0:T(8,128)(2,1)S(1)} %get-tuple-element.21.att_norm, bf16[128,128]{1,0:T(8,128)(2,1)S(1)} %get-tuple-element.22.w_query, bf16[128,128]{1,0:T(8,128)(2,1)S(1)} %get-tuple-element.23.w_key, bf16[128,128]{1,0:T(8,128)(2,1)S(1)} %get-tuple-element.24.w_value, ...), custom_call_target="tpu_custom_call" | custom-call | flops 201326592 | bytes 1081344 | tf_op jit(solution)/shard_map/pallas_call | solution.py:331
Async XLA Ops:
  22.5 12.2 %copy-start = (bf16[8,128,128]{2,1,0:T(8,128)(2,1)S(1)}, bf16[8,128,128]{2,1,0:T(8,128)(2,1)}, u32[]{:S(2)}) copy-start(bf16[8,128,128]{2,1,0:T(8,128)(2,1)} %pair.1) | copy-start | bytes 786436
